TPU v7x, 256 devices: a whole 4x4x8 slice. The times are simulated.
256 devices in a mesh: tm: 16 (over x, z_hi), view: 16 (over z_lo, y, core).
Axes of the slice: x: 4, y: 4, z: 8 (z_hi: 4, z_lo: 2; z = z_hi * 2 + z_lo), core: 2. Of those that a mesh axis runs over, the one named last changes fastest.
Arguments:
- queries: bfloat16 [16, 16, 128, 1280], P('tm', 'view'), may hold values from -32 to 32, as said below
- keys: bfloat16 [16, 16, 128, 1280], P('tm', 'view'), may hold values from -32 to 32
- values: bfloat16 [16, 16, 128, 1280], P('tm', 'view'), may hold values from -6 to 6
- view_mask: int32 [8, 32, 32], replicated, may hold values from 0 to 1, as said below
- frame_times: int32 [8], replicated, may hold values from 0 to 11, as said below
- out_weight: bfloat16 [1280, 1280], replicated, may hold values from -0.15625 to 0.15625
Outputs:
- attended: bfloat16 [16, 16, 128, 1280], P('tm', 'view')
Inputs may be any that keep to these rules, and one draw needn't show every extreme that they name: `queries`: in the hidden and the shown draw alike, entries lie within the stated range. 0 or 1; view_mask[f, v, v] = 1 for every frame and view. frame_times[0] = 0; the steps from one frame to the next are four steps of 1, one step of 3 and 2 steps of 2, in any order.
All inputs are finite; a program needn't handle non-finite values.
Results may differ from a plain program's by a relative error of at most 0.014.
Values may be sent and summed in bfloat16 or wider, within the bound.
No kernel may reach another device: no remote copies, remote signals or barrier semaphores. Data moves between devices by JAX's collectives and lax.ppermute only.
A program may use at most 128 MiB of HBM per device.

v0:
```python
import jax
import jax.numpy as jnp
from jax import lax
from jax.sharding import PartitionSpec as P

HEADS = 20
REACH = 4
FRAMES = 8


lowest = -1e30


def from_behind(array, axis, by):
    length = lax.axis_size(axis)
    pairs = [(i, i + by) for i in range(length) if 0 <= i + by < length]
    return lax.ppermute(array, axis, pairs)


def partner_2(array, axis, apart):
    return lax.ppermute(array, axis, [(i, i ^ 1 << apart) for i in range(lax.axis_size(axis))])


def attend_group(state_now, query_rows, key_block, value_block, permit):
    row_max, row_sum, summed = state_now
    group_size, cells, head_count, head_size = key_block.shape
    scale = head_size ** (-0.5)
    scores = (
        jnp.einsum("phd,gkhd->hpgk", query_rows, key_block, preferred_element_type=jnp.float32)
        * scale
    )
    scores = scores.reshape(head_count, cells, group_size * cells)
    visible = jnp.broadcast_to(permit[:, None], (group_size, cells)).reshape(group_size * cells)
    masked = jnp.where(visible, scores, lowest)
    new_max = jnp.maximum(row_max, jnp.max(masked, -1))
    weights = jnp.where(visible, jnp.exp(scores - new_max[:, :, None]), 0.0)
    rescale = jnp.exp(row_max - new_max)
    new_sum = row_sum * rescale + jnp.sum(weights, -1)
    value_rows = value_block.reshape(group_size * cells, head_count, head_size)
    product = jnp.einsum(
        "hpk,khd->hpd", weights.astype(jnp.bfloat16), value_rows, preferred_element_type=jnp.float32
    )
    return (new_max, new_sum, summed * rescale[:, :, None] + product)


def attend_all(state_now, query_rows, blocks, permit):
    head_count, cells, head_size = state_now[2].shape
    block_total = blocks.shape[1]
    group_size = 2
    group_count = block_total // group_size
    key_groups = blocks[0].reshape(group_count, group_size, cells, head_count, head_size)
    value_groups = blocks[1].reshape(group_count, group_size, cells, head_count, head_size)
    permit_groups = permit.reshape(group_count, group_size)

    def advance(carried, block_item):
        key_block, value_block, allowed = block_item
        return (attend_group(carried, query_rows, key_block, value_block, allowed), None)

    final_state, unused = lax.scan(advance, state_now, (key_groups, value_groups, permit_groups))
    return final_state


def local(queries, keys, values, view_mask, frame_times, out_weight):
    cells = queries.shape[2]
    model_width = queries.shape[3]
    head_size = model_width // HEADS
    slot_id = lax.axis_index("tm")
    frame_id = slot_id % FRAMES
    group_id = slot_id // FRAMES
    group_total = lax.axis_size("tm") // FRAMES
    group_width = lax.axis_size("view")
    my_view = group_id * group_width + lax.axis_index("view")
    query_rows = queries[0, 0].reshape(cells, HEADS, head_size)
    stacked = jnp.stack([keys[:, 0], values[:, 0]])
    state_now = (
        jnp.full((HEADS, cells), lowest, jnp.float32),
        jnp.zeros((HEADS, cells), jnp.float32),
        jnp.zeros((HEADS, cells, head_size), jnp.float32),
    )
    offset_list = list(range(-REACH, 0)) + list(range(1, REACH + 1))
    received = []
    for offset_value in offset_list:
        received.append(from_behind(stacked, "tm", -offset_value))
    neighbours = jnp.concatenate(received, 1)
    offsets = jnp.array(offset_list, dtype=jnp.int32)
    other_frame = frame_id + offsets
    inside = (other_frame >= 0) & (other_frame < FRAMES)
    my_clock = lax.dynamic_index_in_dim(frame_times, frame_id, 0, False)
    their_clock = jnp.take(frame_times, jnp.clip(other_frame, 0, FRAMES - 1))
    nearby = inside & (jnp.abs(their_clock - my_clock) <= REACH)
    state_now = attend_all(state_now, query_rows, neighbours, nearby)
    partner = partner_2(stacked, "tm", FRAMES.bit_length() - 1)
    collected = jnp.where(
        group_id == 1,
        jnp.concatenate([partner, stacked], 1),
        jnp.concatenate([stacked, partner], 1),
    )
    frame_rows = lax.dynamic_index_in_dim(view_mask, frame_id, 0, False)
    allowed_row = lax.dynamic_index_in_dim(frame_rows, my_view, 0, False)
    allowed_views = allowed_row.reshape(group_total, group_width).T.reshape(-1)
    everyone = lax.all_gather(collected, "view", axis=1, tiled=True)
    state_now = attend_all(state_now, query_rows, everyone, allowed_views == 1)
    row_max, row_sum, summed = state_now
    heads_out = (
        (summed / row_sum[:, :, None])
        .transpose(1, 0, 2)
        .reshape(cells, model_width)
        .astype(jnp.bfloat16)
    )
    result = jnp.dot(heads_out, out_weight, preferred_element_type=jnp.float32).astype(jnp.bfloat16)
    return result.reshape(1, 1, cells, model_width)


def solution(mesh):
    return jax.shard_map(
        local,
        mesh=mesh,
        in_specs=(
            P("tm", "view", None, None),
            P("tm", "view", None, None),
            P("tm", "view", None, None),
            P(),
            P(),
            P(),
        ),
        out_specs=P("tm", "view", None, None),
        check_vma=False,
    )
```

profile of v0, /device:TPU:88, one launch (start us, length us, event | category | flops | bytes accessed | tf_op | source)
XLA Modules:
  0.0 572.0 jit_solution(3914078910995842579)
XLA Ops:
  12.4 3.0 collective-permute-start.8
  15.5 15.3 %collective-permute-done.8 = bf16[2,1,128,1280]{2,3,1,0:T(8,128)(2,1)} collective-permute-done((bf16[2,1,128,1280]{2,3,1,0:T(8,128)(2,1)}, bf16[2,1,128,1280]{2,3,1,0:T(8,128)(2,1)}, u32[]{:S(2)}, u32[]{:S(2)}) %collective-permute-start.8) | collective-permute-done | bytes 655392 | tf_op jit(solution)/shard_map/ppermute | solution.py:21
  30.7 3.0 maximum_select_fusion
  33.8 4.3 collective-permute-start
  40.6 9.1 %collective-permute-start.2 = (bf16[2,1,128,1280]{2,3,1,0:T(8,128)(2,1)}, bf16[2,1,128,1280]{2,3,1,0:T(8,128)(2,1)}, u32[]{:S(2)}, u32[]{:S(2)}) collective-permute-start(bf16[2,1,128,1280]{2,3,1,0:T(8,128)(2,1)} %pad_maximum_fusion), channel_id=1, source_target_pairs={{0,32},{16,48},{32,64},{48,80},{64,96},{80,112},{96,128},{112,144}... | collective-permute-start | bytes 1966088 | tf_op jit(solution)/shard_map/ppermute | solution.py:17
  49.7 3.7 collective-permute-start.3
  53.4 3.8 collective-permute-start.4
  62.0 8.3 %collective-permute-done = bf16[2,1,128,1280]{2,3,1,0:T(8,128)(2,1)} collective-permute-done((bf16[2,1,128,1280]{2,3,1,0:T(8,128)(2,1)}, bf16[2,1,128,1280]{2,3,1,0:T(8,128)(2,1)}, u32[]{:S(2)}, u32[]{:S(2)}) %collective-permute-start) | collective-permute-done | bytes 655392 | tf_op jit(solution)/shard_map/ppermute | solution.py:17
  75.2 30.3 %collective-permute-done.2 = bf16[2,1,128,1280]{2,3,1,0:T(8,128)(2,1)} collective-permute-done((bf16[2,1,128,1280]{2,3,1,0:T(8,128)(2,1)}, bf16[2,1,128,1280]{2,3,1,0:T(8,128)(2,1)}, u32[]{:S(2)}, u32[]{:S(2)}) %collective-permute-start.2) | collective-permute-done | bytes 655392 | tf_op jit(solution)/shard_map/ppermute | solution.py:17
  108.2 49.2 %collective-permute-done.3 = bf16[2,1,128,1280]{2,3,1,0:T(8,128)(2,1)} collective-permute-done((bf16[2,1,128,1280]{2,3,1,0:T(8,128)(2,1)}, bf16[2,1,128,1280]{2,3,1,0:T(8,128)(2,1)}, u32[]{:S(2)}, u32[]{:S(2)}) %collective-permute-start.3) | collective-permute-done | bytes 655392 | tf_op jit(solution)/shard_map/ppermute | solution.py:17
  159.8 15.8 %collective-permute-done.5 = bf16[2,1,128,1280]{2,3,1,0:T(8,128)(2,1)S(1)} collective-permute-done((bf16[2,1,128,1280]{2,3,1,0:T(8,128)(2,1)}, bf16[2,1,128,1280]{2,3,1,0:T(8,128)(2,1)S(1)}, u32[]{:S(2)}, u32[]{:S(2)}) %collective-permute-start.5) | collective-permute-done | bytes 655392 | tf_op jit(solution)/shard_map/ppermute | solution.py:17
  175.6 42.8 %collective-permute-done.6 = bf16[2,1,128,1280]{2,3,1,0:T(8,128)(2,1)S(1)} collective-permute-done((bf16[2,1,128,1280]{2,3,1,0:T(8,128)(2,1)}, bf16[2,1,128,1280]{2,3,1,0:T(8,128)(2,1)S(1)}, u32[]{:S(2)}, u32[]{:S(2)}) %collective-permute-start.6) | collective-permute-done | bytes 655392 | tf_op jit(solution)/shard_map/ppermute | solution.py:17
  221.3 72.1 %while.30 = (s32[]{:T(128)}, f32[20,128]{1,0:T(8,128)S(1)}, f32[20,128]{1,0:T(8,128)S(1)}, f32[20,128,64]{1,2,0:T(8,128)}, pred[4,2]{1,0:T(4,128)(4,1)S(1)}, /*i...) while((s32[]{:T(128)}, f32[20,128]{1,0:T(8,128)S(1)}, ...), condition=%wide.region_3.4_spmd.clone, body=%wide.region_0.3_spmd.clone.sunk | while | flops 174174720 | bytes 25395908 | solution.py:59
  232.5 3.2 copy.50
  235.8 3.4 fusion.47
  250.4 3.2 copy.50
  253.7 3.6 fusion.47
  268.4 3.2 copy.50
  271.8 3.6 fusion.47
  286.5 3.2 copy.50
  289.8 3.6 fusion.47
  293.4 18.6 %fusion.24 = (bf16[1,32,128,1280]{2,3,1,0:T(8,128)(2,1)}, bf16[1,32,128,1280]{2,3,1,0:T(8,128)(2,1)}) fusion(bf16[2,32,128,1280]{2,3,1,0:T(8,128)(2,1)} %all-gather.2.cloned.1.call-done), kind=kLoop, calls=%fused_computation.67 | loop fusion | bytes 41943040 | tf_op jit(solution)/shard_map/slice | solution.py:52
  312.0 250.6 %while.29 = (s32[]{:T(128)}, f32[20,128]{1,0:T(8,128)S(1)}, f32[20,128]{1,0:T(8,128)S(1)}, f32[20,128,64]{1,2,0:T(8,128)}, pred[16,2]{0,1:T(4,128)(4,1)S(1)}, /*...) while((s32[]{:T(128)}, f32[20,128]{1,0:T(8,128)S(1)}, ...), condition=%wide.region_7.8_spmd, body=%wide.region_4.7_spmd.sunk | while | flops 174003200 | bytes 33260212 | solution.py:59
  317.9 2.9 reshape.83
  320.8 3.2 copy.47
  324.1 3.6 fusion.42
  333.6 2.9 reshape.83
  336.4 3.2 copy.47
  339.8 3.6 fusion.42
  349.2 2.9 reshape.83
  352.1 3.2 copy.47
  355.4 3.6 fusion.42
  364.9 2.9 reshape.83
  367.8 3.2 copy.47
  371.1 3.6 fusion.42
  380.6 2.9 reshape.83
  383.4 3.2 copy.47
  386.8 3.6 fusion.42
  396.2 2.9 reshape.83
  399.1 3.2 copy.47
  402.4 3.6 fusion.42
  411.9 2.9 reshape.83
  414.8 3.2 copy.47
  418.1 3.6 fusion.42
  427.5 2.9 reshape.83
  430.4 3.2 copy.47
  433.7 3.6 fusion.42
  446.1 3.2 copy.47
  449.4 3.6 fusion.42
  461.7 3.2 copy.47
  465.1 3.6 fusion.42
  477.4 3.2 copy.47
  480.7 3.6 fusion.42
  493.1 3.2 copy.47
  496.4 3.6 fusion.42
  505.9 2.9 reshape.83
  508.7 3.2 copy.47
  512.1 3.6 fusion.42
  524.4 3.2 copy.47
  527.7 3.6 fusion.42
  540.1 3.2 copy.47
  543.4 3.6 fusion.42
  555.7 3.2 copy.47
  559.0 3.6 fusion.42
  (329 shorter events, 187.5 us)
Async XLA Ops:
  6.5 557.3 %copy-start = (bf16[1280,1280]{1,0:T(8,128)(2,1)S(1)}, bf16[1280,1280]{1,0:T(8,128)(2,1)}, u32[]{:S(2)}) copy-start(bf16[1280,1280]{1,0:T(8,128)(2,1)} %param.16) | copy-start | bytes 9830404
  6.5 286.9 %all-gather.2.cloned.1.call-start = ((), (), s32[]{:S(2)}) async-start(), calls=%async_computation | async-start | bytes 22282240 | tf_op jit(solution)/shard_map/all_gather | solution.py:101
  10.4 46.8 %copy-start.6 = (s32[8]{0:T(128)S(1)}, s32[8]{0:T(128)}, u32[]{:S(2)}) copy-start(s32[8]{0:T(128)} %constant.129.clone) | copy-start | bytes 100
  10.4 46.9 %copy-start.2 = (s32[8]{0:T(128)S(1)}, s32[8]{0:T(128)}, u32[]{:S(2)}) copy-start(s32[8]{0:T(128)} %param.15) | copy-start | bytes 100
  12.4 18.3 %collective-permute-start.8 = (bf16[2,1,128,1280]{2,3,1,0:T(8,128)(2,1)}, bf16[2,1,128,1280]{2,3,1,0:T(8,128)(2,1)}, u32[]{:S(2)}, u32[]{:S(2)}) collective-permute-start(bf16[2,1,128,1280]{2,3,1,0:T(8,128)(2,1)} %pad_maximum_fusion), channel_id=1, source_target_pairs={{0,128},{16,144},{32,160},{48,176},{64,192},{80,208},{96,224},{112... | collective-permute-start | bytes 1966088 | tf_op jit(solution)/shard_map/ppermute | solution.py:21
  33.8 36.5 %collective-permute-start = (bf16[2,1,128,1280]{2,3,1,0:T(8,128)(2,1)}, bf16[2,1,128,1280]{2,3,1,0:T(8,128)(2,1)}, u32[]{:S(2)}, u32[]{:S(2)}) collective-permute-start(bf16[2,1,128,1280]{2,3,1,0:T(8,128)(2,1)} %pad_maximum_fusion), channel_id=1, source_target_pairs={{0,64},{16,80},{32,96},{48,112},{64,128},{80,144},{96,160},{112,17... | collective-permute-start | bytes 1966088 | tf_op jit(solution)/shard_map/ppermute | solution.py:17
  38.1 34.7 %collective-permute-start.1 = (bf16[2,1,128,1280]{2,3,1,0:T(8,128)(2,1)}, bf16[2,1,128,1280]{2,3,1,0:T(8,128)(2,1)}, u32[]{:S(2)}, u32[]{:S(2)}) collective-permute-start(bf16[2,1,128,1280]{2,3,1,0:T(8,128)(2,1)} %pad_maximum_fusion), channel_id=1, source_target_pairs={{0,48},{16,64},{32,80},{48,96},{64,112},{80,128},{96,144},{112,160... | collective-permute-start | bytes 1966088 | tf_op jit(solution)/shard_map/ppermute | solution.py:17
  40.6 65.0 %collective-permute-start.2 = (bf16[2,1,128,1280]{2,3,1,0:T(8,128)(2,1)}, bf16[2,1,128,1280]{2,3,1,0:T(8,128)(2,1)}, u32[]{:S(2)}, u32[]{:S(2)}) collective-permute-start(bf16[2,1,128,1280]{2,3,1,0:T(8,128)(2,1)} %pad_maximum_fusion), channel_id=1, source_target_pairs={{0,32},{16,48},{32,64},{48,80},{64,96},{80,112},{96,128},{112,144}... | collective-permute-start | bytes 1966088 | tf_op jit(solution)/shard_map/ppermute | solution.py:17
  49.7 107.7 %collective-permute-start.3 = (bf16[2,1,128,1280]{2,3,1,0:T(8,128)(2,1)}, bf16[2,1,128,1280]{2,3,1,0:T(8,128)(2,1)}, u32[]{:S(2)}, u32[]{:S(2)}) collective-permute-start(bf16[2,1,128,1280]{2,3,1,0:T(8,128)(2,1)} %pad_maximum_fusion), channel_id=1, source_target_pairs={{0,16},{16,32},{32,48},{48,64},{64,80},{80,96},{96,112},{112,128},... | collective-permute-start | bytes 1966088 | tf_op jit(solution)/shard_map/ppermute | solution.py:17
  53.4 105.2 %collective-permute-start.4 = (bf16[2,1,128,1280]{2,3,1,0:T(8,128)(2,1)}, bf16[2,1,128,1280]{2,3,1,0:T(8,128)(2,1)}, u32[]{:S(2)}, u32[]{:S(2)}) collective-permute-start(bf16[2,1,128,1280]{2,3,1,0:T(8,128)(2,1)} %pad_maximum_fusion), channel_id=1, source_target_pairs={{16,0},{32,16},{48,32},{64,48},{80,64},{96,80},{112,96},{128,112},... | collective-permute-start | bytes 1966088 | tf_op jit(solution)/shard_map/ppermute | solution.py:17
  70.3 105.2 %collective-permute-start.5 = (bf16[2,1,128,1280]{2,3,1,0:T(8,128)(2,1)}, bf16[2,1,128,1280]{2,3,1,0:T(8,128)(2,1)S(1)}, u32[]{:S(2)}, u32[]{:S(2)}) collective-permute-start(bf16[2,1,128,1280]{2,3,1,0:T(8,128)(2,1)} %pad_maximum_fusion), channel_id=1, source_target_pairs={{32,0},{48,16},{64,32},{80,48},{96,64},{112,80},{128,96},{144,112}... | collective-permute-start | bytes 1966088 | tf_op jit(solution)/shard_map/ppermute | solution.py:17
  72.7 145.6 %collective-permute-start.6 = (bf16[2,1,128,1280]{2,3,1,0:T(8,128)(2,1)}, bf16[2,1,128,1280]{2,3,1,0:T(8,128)(2,1)S(1)}, u32[]{:S(2)}, u32[]{:S(2)}) collective-permute-start(bf16[2,1,128,1280]{2,3,1,0:T(8,128)(2,1)} %pad_maximum_fusion), channel_id=1, source_target_pairs={{48,0},{64,16},{80,32},{96,48},{112,64},{128,80},{144,96},{160,112... | collective-permute-start | bytes 1966088 | tf_op jit(solution)/shard_map/ppermute | solution.py:17
  105.5 112.9 %collective-permute-start.7 = (bf16[2,1,128,1280]{2,3,1,0:T(8,128)(2,1)}, bf16[2,1,128,1280]{2,3,1,0:T(8,128)(2,1)S(1)}, u32[]{:S(2)}, u32[]{:S(2)}) collective-permute-start(bf16[2,1,128,1280]{2,3,1,0:T(8,128)(2,1)} %pad_maximum_fusion), channel_id=1, source_target_pairs={{64,0},{80,16},{96,32},{112,48},{128,64},{144,80},{160,96},{176,11... | collective-permute-start | bytes 1966088 | tf_op jit(solution)/shard_map/ppermute | solution.py:17
  221.3 2.3 copy-start.4
  225.8 2.3 copy-start.3
  239.2 2.3 copy-start.4
  243.6 2.3 copy-start.3
  257.3 2.3 copy-start.4
  261.7 2.3 copy-start.3
  275.4 2.3 copy-start.4
  279.8 2.3 copy-start.3
  312.2 1.5 copy-start.5
  314.3 1.5 copy-start.1
  327.9 1.5 copy-start.5
  330.0 1.5 copy-start.1
  343.6 1.5 copy-start.5
  345.7 1.5 copy-start.1
  359.2 1.5 copy-start.5
  361.3 1.5 copy-start.1
  374.9 1.5 copy-start.5
  377.0 1.5 copy-start.1
  390.5 1.5 copy-start.5
  392.7 1.5 copy-start.1
  406.2 1.5 copy-start.5
  408.3 1.5 copy-start.1
  421.9 1.5 copy-start.5
  424.0 1.5 copy-start.1
  437.5 1.5 copy-start.5
  439.7 1.5 copy-start.1
  453.2 1.5 copy-start.5
  455.3 1.5 copy-start.1
  468.9 1.5 copy-start.5
  471.0 1.5 copy-start.1
  484.5 1.5 copy-start.5
  486.6 1.5 copy-start.1
  500.2 1.5 copy-start.5
  502.3 1.5 copy-start.1
  515.8 1.5 copy-start.5
  518.0 1.5 copy-start.1
  531.5 1.5 copy-start.5
  533.6 1.5 copy-start.1
  547.2 1.5 copy-start.5
  549.3 1.5 copy-start.1
Sparse Core Ops, SparseCore 0:
  33.9 205.5 all-gather.1
where the time goes:
time: 574 us; the launch traced here: 572 us
  local copies, waits for them, and re-layouts  248 us (43%)
  waiting for transfers between devices  162 us (28%)
  matrix products  92.1 us (16%)
  starting transfers between devices  30.5 us (5%)
  other arithmetic  25 us (4%)
  between operations  13.6 us (2%)
    ppermute x8, waiting for transfers between devices, from_behind(): return lax.ppermute(array, axis, pairs)  146 us
    dot_general x20, matrix products, attend_group(): jnp.einsum('hpk,khd->hpd', weights.astype(jnp.bfloat16), value_rows, pref...  72 us
    dynamic_slice x72, local copies, waits for them, and re-layouts, attend_all(): lax.scan(advance, state_now, (key_groups, value_groups, permit_groups))  65.9 us
    reshape x20, local copies, waits for them, and re-layouts, attend_group(): scores = scores.reshape(head_count, cells, group_size * cells)  64.9 us
    reshape x20, local copies, waits for them, and re-layouts, attend_group(): value_rows = value_block.reshape(group_size * cells, head_count, head_size)  57.3 us
    ppermute x8, starting transfers between devices, from_behind(): return lax.ppermute(array, axis, pairs)  27.5 us
    while x100, local copies, waits for them, and re-layouts  23.9 us
    slice x2, local copies, waits for them, and re-layouts, attend_all(): blocks[1].reshape(group_count, group_size, cells, head_count, head_size)  21.4 us
  transfers between devices with their start and end apart: 10, of which 6 were waited for; matrix products, arithmetic and copies ran while one was open for 15% of the time, Pallas kernels for 0%

commit v1 on v0

v1 whole, which is shorter than its diff:
```python
import jax
import jax.numpy as jnp
from jax import lax
from jax.experimental import pallas as pl
from jax.experimental.pallas import tpu as pltpu
from jax.sharding import Mesh, PartitionSpec as P

HEADS = 20
REACH = 4
FRAMES = 8
HEAD = 64
CELLS = 128
MAIN = 16
RING = 4
NEG = -(2.0**30)
LOG2E = 1.4426950408889634
RATE = HEAD**-0.5 * LOG2E
TILE = 256
CHUNK = 512
Z_ROWS = 960
X_ROWS = 448
T_ROWS = 208
O_ROWS = 144
F32 = jnp.float32
BF16 = jnp.bfloat16
VMEM = pl.BlockSpec(memory_space=pltpu.VMEM)
SMEM = pl.BlockSpec(memory_space=pltpu.SMEM)


def lanes(shape):
    return lax.broadcasted_iota(jnp.int32, shape, len(shape) - 1)


def rows_of(shape):
    return lax.broadcasted_iota(jnp.int32, shape, len(shape) - 2)


def swap_halves(x):
    return pltpu.roll(x, HEAD, 1)


def params(mib):
    return pltpu.CompilerParams(vmem_limit_bytes=mib * 1024 * 1024)


def pack_kernel(q_ref, k_ref, v_ref, view_ref, ring_ref, z0, z1, z2, z3, parts):
    frame = lax.axis_index("f")
    half = frame // 4
    place = frame % 4

    def pair(a_ref, a, b_ref, b):
        left = a_ref[:, a * HEAD : (a + 1) * HEAD]
        right = b_ref[:, b * HEAD : (b + 1) * HEAD]
        return jnp.concatenate([left, right], axis=1)

    for t in range(MAIN):
        view_ref[t, 0:CELLS] = pair(k_ref, t, v_ref, t)
        view_ref[t, CELLS : 2 * CELLS] = pair(q_ref, t, q_ref, MAIN + t % RING)
    for y in range(RING):
        ring_ref[y] = pair(k_ref, MAIN + y, v_ref, MAIN + y)
    for j in range(4):
        base = 5 * j
        first = [pair(k_ref, base, v_ref, base), pair(k_ref, base + 1, v_ref, base + 1)]
        first.append(pair(q_ref, base, q_ref, base + 1))
        second = [pair(k_ref, base + 2, v_ref, base + 2), pair(k_ref, base + 3, v_ref, base + 3)]
        second.append(pair(q_ref, base + 2, q_ref, base + 3))
        for i in range(3):
            a, b = first[i].astype(F32), second[i].astype(F32)
            parts[j, i * CELLS : (i + 1) * CELLS] = jnp.where(half == 0, a, b).astype(BF16)
            parts[j, 576 + i * CELLS : 576 + (i + 1) * CELLS] = jnp.where(half == 0, b, a).astype(BF16)
        parts[j, 384:512] = pair(k_ref, base + 4, v_ref, base + 4)
        last = q_ref[:, (base + 4) * HEAD : (base + 5) * HEAD]
        parts[j, 512:576] = jnp.concatenate([last[0:64], last[64:128]], axis=1)
    for k, out in enumerate((z0, z1, z2, z3)):
        out[...] = parts[place ^ k]


def pack(q, k, v):
    block = jax.ShapeDtypeStruct((Z_ROWS, CELLS), BF16)
    return pl.pallas_call(
        pack_kernel,
        out_shape=[
            jax.ShapeDtypeStruct((MAIN, 2 * CELLS, CELLS), BF16),
            jax.ShapeDtypeStruct((RING, CELLS, CELLS), BF16),
            block,
            block,
            block,
            block,
        ],
        in_specs=[VMEM] * 3,
        out_specs=[VMEM] * 6,
        scratch_shapes=[pltpu.VMEM((4, Z_ROWS, CELLS), BF16)],
        compiler_params=params(32),
        name="pack",
    )(q, k, v)


def score_tile(q, key_ref, score_ref, count):
    best = None
    for start in range(0, count, CHUNK):
        s = lax.dot_general(
            q, key_ref[start : start + CHUNK], (((1,), (1,)), ((), ())), preferred_element_type=F32
        )
        score_ref[:, start : start + CHUNK] = s
        for lane in range(0, CHUNK, 128):
            part = s[:, lane : lane + 128]
            best = part if best is None else jnp.maximum(best, part)
    return jnp.max(best, axis=1, keepdims=True)


def weigh_tile(score_ref, row_max, value_ref, count):
    total = None
    for start in range(0, count, CHUNK):
        s = score_ref[:, start : start + CHUNK]
        w = jnp.exp2((s - row_max) * RATE).astype(BF16)
        part = jnp.dot(w, value_ref[start : start + CHUNK], preferred_element_type=F32)
        total = part if total is None else total + part
    return total


def split3(x):
    high = x.astype(BF16).astype(F32)
    middle = (x - high).astype(BF16).astype(F32)
    low = (x - high - middle).astype(BF16).astype(F32)
    return [high, middle, low]


def level_rows(levels, lane):
    columns = [part for level in levels for part in split3(level)]
    table = jnp.zeros_like(columns[0])
    for i, column in enumerate(columns):
        table = jnp.where(lane == i, column, table)
    return table


def keys_with_mask(kv, mask_row, lane):
    return jnp.where(lane < HEAD, kv, mask_row).astype(BF16)


def view_kernel(own_ref, other_ref, ring_ref, mask_ref, out_ref, key_s, value_s, rkey_s, rvalue_s, s_a, s_b, r_s):
    frame = lax.axis_index("f")
    core = lax.axis_index("c")
    y = lax.axis_index("y")
    ring = lax.axis_index("g") * 2 + lax.axis_index("zl")
    lane = lanes((CELLS, CELLS))

    seen = mask_ref[frame].astype(F32)
    b32, u32 = rows_of((32, 32)), lanes((32, 32))
    key_view = jnp.where(b32 < 16, 2 * b32 + core, 2 * (b32 - 16) + 1 - core)
    pick = (u32 == key_view).astype(F32)
    v128, l128 = rows_of((32, 128)), lanes((32, 128))
    query_pick = ((l128 >= HEAD) & (l128 < HEAD + 16) & (v128 == 2 * (l128 - HEAD) + core)).astype(F32)
    by_key = lax.dot_general(pick, seen, (((1,), (1,)), ((), ())), preferred_element_type=F32)
    allowed = jnp.dot(by_key, query_pick, preferred_element_type=F32)
    bias = jnp.where((l128 >= HEAD) & (l128 < HEAD + 16) & (allowed < 0.5), NEG, 0.0)
    r8, ru8 = rows_of((8, 32)), lanes((8, 32))
    ring_pick = (ru8 == ring * 8 + r8).astype(F32)
    by_ring = lax.dot_general(ring_pick, seen, (((1,), (1,)), ((), ())), preferred_element_type=F32)
    ring_allowed = jnp.dot(by_ring, query_pick, preferred_element_type=F32)
    l8 = lanes((8, 128))
    ring_bias = jnp.where((l8 >= HEAD) & (l8 < HEAD + 16) & (ring_allowed < 0.5), NEG, 0.0)

    for b in range(32):
        kv = (own_ref[b, 0:CELLS] if b < 16 else other_ref[b - 16, 0:CELLS]).astype(F32)
        rows = slice(b * CELLS, (b + 1) * CELLS)
        key_s[rows] = keys_with_mask(kv, bias[b : b + 1], lane)
        value_s[rows] = jnp.where(lane < HEAD, swap_halves(kv), 1.0).astype(BF16)
    for b in range(8):
        kv = ring_ref[b, y].astype(F32)
        rows = slice(b * CELLS, (b + 1) * CELLS)
        rkey_s[rows] = keys_with_mask(kv, ring_bias[b : b + 1], lane)
        rvalue_s[rows] = jnp.where(lane < HEAD, 1.0, kv).astype(BF16)

    def queries(j):
        qq = own_ref[j, CELLS : 2 * CELLS].astype(F32)
        hot = (lane == HEAD + j).astype(F32)
        main = jnp.where(lane < HEAD, qq, hot).astype(BF16)
        ring_q = jnp.where(lane < HEAD, swap_halves(qq), hot).astype(BF16)
        return main, ring_q

    def tile(i):
        a, b = queries(2 * i), queries(2 * i + 1)
        return jnp.concatenate([a[0], b[0]], axis=0), jnp.concatenate([a[1], b[1]], axis=0)

    wide = lanes((TILE, CELLS))

    def finish(i, score_ref, row_max, ring_q):
        ring_max = score_tile(ring_q, rkey_s, r_s, 1024)
        main = weigh_tile(score_ref, row_max, value_s, 4096)
        part = weigh_tile(r_s, ring_max, rvalue_s, 1024)
        main_sum = swap_halves(main)
        heads = jnp.where(wide < HEAD, main / main_sum, part / swap_halves(part))
        main_level = row_max * RATE + jnp.log2(jnp.where(wide < HEAD, main_sum, 1.0))
        ring_level = ring_max * RATE + jnp.log2(jnp.where(wide < HEAD, part, 1.0))
        table = level_rows([main_level, ring_level], wide)
        for n in range(2):
            rows = slice(n * CELLS, (n + 1) * CELLS)
            out_ref[2 * i + n, 0:CELLS] = heads[rows].astype(BF16)
            out_ref[2 * i + n, CELLS:O_ROWS] = table[rows].T[0:16].astype(BF16)

    q0, rq0 = tile(0)
    m0 = score_tile(q0, key_s, s_a, 4096)

    def body(step, carry):
        m_a, rq_a = carry
        q_b, rq_b = tile(2 * step + 1)
        m_b = score_tile(q_b, key_s, s_b, 4096)
        finish(2 * step, s_a, m_a, rq_a)
        q_a, rq_next = tile(jnp.minimum(2 * step + 2, 7))
        m_next = score_tile(q_a, key_s, s_a, 4096)
        finish(2 * step + 1, s_b, m_b, rq_b)
        return m_next, rq_next

    lax.fori_loop(0, 4, body, (m0, rq0))


def view_attention(own, other, ring, view_mask):
    return pl.pallas_call(
        view_kernel,
        out_shape=jax.ShapeDtypeStruct((MAIN, O_ROWS, CELLS), BF16),
        in_specs=[VMEM] * 4,
        out_specs=VMEM,
        scratch_shapes=[
            pltpu.VMEM((4096, CELLS), BF16),
            pltpu.VMEM((4096, CELLS), BF16),
            pltpu.VMEM((1024, CELLS), BF16),
            pltpu.VMEM((1024, CELLS), BF16),
            pltpu.VMEM((TILE, 4096), F32),
            pltpu.VMEM((TILE, 4096), F32),
            pltpu.VMEM((TILE, 1024), F32),
        ],
        compiler_params=params(48),
        cost_estimate=pl.CostEstimate(flops=2700000000, bytes_accessed=4000000, transcendentals=11000000),
        name="view_attention",
    )(own, other, ring, view_mask)


def time_kernel(z0, z1, z2, z3, x_ref, times_ref, o0, o1, o2, o3, o4, o5, o6, o7, key_s, value_s, q_s, s_ref):
    frame = lax.axis_index("f")
    lane = lanes((CELLS, CELLS))
    own = (z0, z1, z2, z3)
    outs = (o0, o1, o2, o3, o4, o5, o6, o7)

    l8, r8 = lanes((8, 128)), rows_of((8, 128))
    query_time = jnp.zeros((8, 128), jnp.int32)
    key_time = jnp.zeros((8, 128), jnp.int32)
    for k in range(FRAMES):
        now = times_ref[frame ^ k]
        query_time = jnp.where(l8 == HEAD + k, now, query_time)
        key_time = jnp.where(r8 == k, now, key_time)
    near = (jnp.abs(query_time - key_time) <= REACH) & (l8 - HEAD != r8)
    bias = jnp.where((l8 >= HEAD) & (l8 < HEAD + 8) & jnp.logical_not(near), NEG, 0.0)

    for head in range(3):
        slots = 8 if head < 2 else 4
        for k in range(slots):
            if head == 2:
                kv = own[k][384:512]
            elif k < 4:
                kv = own[k][head * CELLS : (head + 1) * CELLS]
            else:
                kv = x_ref[k - 4, 64 + head * CELLS : 64 + (head + 1) * CELLS]
            kv = kv.astype(F32)
            rows = slice(k * CELLS, (k + 1) * CELLS)
            key_s[head, rows] = keys_with_mask(kv, bias[k : k + 1], lane)
            value_s[head, rows] = jnp.where(lane < HEAD, swap_halves(kv), 1.0).astype(BF16)
        for k in range(8):
            hot = jnp.where(lane == HEAD + k, 1.0, 0.0)
            rows = slice(k * CELLS, (k + 1) * CELLS)
            if head < 2:
                qq = (own[k][256:384] if k < 4 else x_ref[k - 4, 320:448]).astype(F32)
                qq = swap_halves(qq) if head == 1 else qq
            else:
                packed = (own[k][512:576] if k < 4 else x_ref[k - 4, 0:64]).astype(F32)
                qq = jnp.concatenate([packed, swap_halves(packed)], axis=0)
            q_s[head, rows] = jnp.where(lane < HEAD, qq, hot).astype(BF16)

    wide = lanes((TILE, CELLS))
    for i in range(4):
        heads, levels = [], []
        for head in range(3):
            count = 1024 if head < 2 else 512
            q = q_s[head, i * TILE : (i + 1) * TILE]
            score = s_ref.at[(3 * i + head) % 2]
            row_max = score_tile(q, key_s.at[head], score, count)
            total = weigh_tile(score, row_max, value_s.at[head], count)
            sums = swap_halves(total)
            heads.append(jnp.where(wide < HEAD, total / sums, 0.0))
            levels.append(row_max * RATE + jnp.log2(jnp.where(wide < HEAD, sums, 1.0)))
        both = heads[0] + swap_halves(heads[1])
        table = level_rows(levels, wide)
        for n in range(2):
            rows = slice(n * CELLS, (n + 1) * CELLS)
            out = outs[2 * i + n]
            out[0:128] = both[rows].astype(BF16)
            last = heads[2][rows]
            out[128:192] = (last[0:64] + swap_halves(last[64:128])).astype(BF16)
            out[192:208] = table[rows].T[0:16].astype(BF16)


def time_attention(own, crossed, frame_times):
    return pl.pallas_call(
        time_kernel,
        out_shape=[jax.ShapeDtypeStruct((T_ROWS, CELLS), BF16)] * 8,
        in_specs=[VMEM] * 5 + [SMEM],
        out_specs=[VMEM] * 8,
        scratch_shapes=[
            pltpu.VMEM((3, 1024, CELLS), BF16),
            pltpu.VMEM((3, 1024, CELLS), BF16),
            pltpu.VMEM((3, 1024, CELLS), BF16),
            pltpu.VMEM((2, TILE, 1024), F32),
        ],
        compiler_params=params(40),
        cost_estimate=pl.CostEstimate(flops=700000000, bytes_accessed=2000000, transcendentals=2700000),
        name="time_attention",
    )(*own, crossed, frame_times)


def join_kernel(view_ref, t0, t1, t2, t3, t4, t5, t6, t7, weight_ref, out_ref, times, heads_s):
    frame = lax.axis_index("f")
    for k, piece in enumerate((t0, t1, t2, t3, t4, t5, t6, t7)):
        times[frame ^ k] = piece[...]

    def level(block, i):
        parts = block[3 * i : 3 * i + 3].astype(F32)
        return parts[0:1] + parts[1:2] + parts[2:3]

    sources = []
    view_levels = [view_ref[t, CELLS:O_ROWS].astype(F32) for t in range(MAIN)]
    time_levels = [times[d, 192:208].astype(F32) for d in range(8)]
    for head in range(HEADS):
        found = []
        if head < MAIN:
            found.append((("view", head, 0), level(view_levels[head], 0)))
        else:
            for ring in range(4):
                t = 4 * ring + head - MAIN
                found.append((("view", t, 1), level(view_levels[t], 1)))
        group, i = head // 5, head % 5
        if i < 4:
            d = (i // 2) * 4 + group
            found.append((("time", d, i % 2), level(time_levels[d], i % 2)))
        else:
            for side in range(2):
                d = side * 4 + group
                found.append((("time", d, 2), level(time_levels[d], 2)))
        sources.append(found)

    columns = []
    for found in sources:
        best = found[0][1]
        for _, value in found[1:]:
            best = jnp.maximum(best, value)
        powers = [jnp.exp2(value - best) for _, value in found]
        total = powers[0]
        for power in powers[1:]:
            total = total + power
        columns.extend(power / total for power in powers)
    columns.extend([jnp.zeros((128 - len(columns), CELLS), F32)])
    table = jnp.concatenate(columns, axis=0).T

    def block(kind, at, i):
        if kind == "view":
            return view_ref[at, 0:CELLS, i * HEAD : (i + 1) * HEAD].astype(F32)
        if i < 2:
            return times[at, 0:CELLS, i * HEAD : (i + 1) * HEAD].astype(F32)
        packed = times[at, 128:192].astype(F32)
        return jnp.concatenate([packed[:, 0:HEAD], packed[:, HEAD:128]], axis=0)

    position = 0
    for head, found in enumerate(sources):
        total = None
        for which, _ in found:
            part = block(*which) * table[:, position : position + 1]
            total = part if total is None else total + part
            position += 1
        heads_s[:, head * HEAD : (head + 1) * HEAD] = total.astype(BF16)
    out_ref[...] = jnp.dot(heads_s[...], weight_ref[...], preferred_element_type=F32).astype(BF16)


def join(view_out, pieces, out_weight):
    return pl.pallas_call(
        join_kernel,
        out_shape=jax.ShapeDtypeStruct((CELLS, HEADS * HEAD), BF16),
        in_specs=[VMEM] * 10,
        out_specs=VMEM,
        scratch_shapes=[pltpu.VMEM((8, T_ROWS, CELLS), BF16), pltpu.VMEM((CELLS, HEADS * HEAD), BF16)],
        compiler_params=params(32),
        name="join",
    )(view_out, *pieces, out_weight)


def across(array, k):
    return lax.ppermute(array, "f", [(i, i ^ k) for i in range(FRAMES)])


def after(array, *others):
    return lax.optimization_barrier((array,) + others)[0]


def local(queries, keys, values, view_mask, frame_times, out_weight):
    model = queries.shape[3]
    q, k, v = (a.reshape(CELLS, model) for a in (queries, keys, values))
    to_view, to_ring, *z = pack(q, k, v)
    ring = lax.all_gather(to_ring, ("y", "c"), axis=0, tiled=False)
    z = [z[0]] + [across(z[i], i) for i in (1, 2, 3)]
    own = lax.all_to_all(to_view, ("g", "zl", "y"), 0, 0)
    other = lax.ppermute(own, "c", [(0, 1), (1, 0)])
    crossed = across(jnp.stack([a[512:960] for a in z]), 4)
    view_out = view_attention(own, other, ring, view_mask)
    pieces = time_attention(z, crossed, frame_times)
    pieces = [pieces[0]] + [across(pieces[i], i) for i in range(1, 8)]
    view_back = lax.all_to_all(view_out, ("g", "zl", "y"), 0, 0)
    result = join(view_back, pieces, out_weight)
    return result.reshape(1, 1, CELLS, model)


def solution(mesh):
    fine = Mesh(mesh.devices.reshape(2, 8, 2, 4, 2), ("g", "f", "zl", "y", "c"))
    blocks = P(("g", "f"), ("zl", "y", "c"), None, None)
    return jax.shard_map(
        local,
        mesh=fine,
        in_specs=(blocks, blocks, blocks, P(), P(), P()),
        out_specs=blocks,
        check_vma=False,
    )
```

time: 574 us -> 149 us (0.26)
  the two profiles are of different devices: /device:TPU:88 before, /device:TPU:8 now
where the time goes in v1:
time: 149 us; the launch traced here: 148 us
  waiting for transfers between devices  53 us (36%)
  starting transfers between devices  39.1 us (26%)
  Pallas kernels  28.6 us (19%)
  between operations  13.5 us (9%)
  local copies, waits for them, and re-layouts  12.7 us (9%)
    ppermute x11, waiting for transfers between devices, across(): return lax.ppermute(array, 'f', [(i, i ^ k) for i in range(FRAMES)])  36.1 us
    ppermute x11, starting transfers between devices, across(): return lax.ppermute(array, 'f', [(i, i ^ k) for i in range(FRAMES)])  24.6 us
    all_to_all x1, waiting for transfers between devices, local(): own = lax.all_to_all(to_view, ('g', 'zl', 'y'), 0, 0)  16.2 us
    pallas_call x1, Pallas kernels, view_attention(): pl.pallas_call(view_kernel, out_shape=jax.ShapeDtypeStruct((MAIN, O_ROWS,...  15.2 us
    unnamed x30, local copies, waits for them, and re-layouts  9.39 us
    all_to_all x1, starting transfers between devices, local(): own = lax.all_to_all(to_view, ('g', 'zl', 'y'), 0, 0)  8.75 us
    pallas_call x1, Pallas kernels, time_attention(): pl.pallas_call(time_kernel, out_shape=[jax.ShapeDtypeStruct((T_ROWS, CELL...  7.04 us
    all_to_all x1, starting transfers between devices, local(): view_back = lax.all_to_all(view_out, ('g', 'zl', 'y'), 0, 0)  5.66 us
  transfers between devices with their start and end apart: 15, of which 5 were waited for; matrix products, arithmetic and copies ran while one was open for 3% of the time, Pallas kernels for 15%

profile of v1, /device:TPU:8, one launch (start us, length us, event | category | flops | bytes accessed | tf_op | source)
XLA Modules:
  0.0 147.8 jit_solution(16062509619723529139)
XLA Ops:
  6.5 0.0 copy-start.1
  6.5 1.0 copy-done.1
  7.5 0.0 copy-start.2
  7.5 1.0 copy-done.2
  8.5 0.0 copy-start.3
  8.5 1.0 copy-done.3
  9.5 1.6 %pack.1 = (bf16[16,256,128]{2,1,0:T(8,128)(2,1)}, bf16[4,128,128]{2,1,0:T(8,128)(2,1)}, bf16[960,128]{1,0:T(8,128)(2,1)S(1)}, bf16[960,128]{1,0:T(8,128)(2,1)S(1...) custom-call(bf16[128,1280]{1,0:T(8,128)(2,1)S(1)} %bitcast.13, bf16[128,1280]{1,0:T(8,128)(2,1)S(1)} %bitcast.14, ...), custom_call_target="tpu_custom_call" | custom-call | tf_op jit(solution)/shard_map/pack/pallas_call | solution.py:80
  11.0 8.7 %all-to-all-start = ((bf16[16,256,128]{2,1,0:T(8,128)(2,1)}), bf16[16,256,128]{2,1,0:T(8,128)(2,1)S(1)}, u32[]{:S(2)}, u32[]{:S(2)}) async-start(bf16[16,256,128]{2,1,0:T(8,128)(2,1)} %get-tuple-element.19), calls=%async_computation | async-start | bytes 2097152 | tf_op jit(solution)/shard_map/all_to_all | solution.py:407
  19.8 0.0 all-gather.3.cloned.1.call-start
  19.8 0.7 all-gather.3.cloned.1.call-update
  20.5 16.2 %all-to-all-done.own_ref = bf16[16,256,128]{2,1,0:T(8,128)(2,1)S(1)} async-done(((bf16[16,256,128]{2,1,0:T(8,128)(2,1)}), bf16[16,256,128]{2,1,0:T(8,128)(2,1)S(1)}, u32[]{:S(2)}, u32[]{:S(2)}) %all-to-all-start) | async-done | bytes 1048608 | tf_op jit(solution)/shard_map/all_to_all | solution.py:407
  36.7 0.0 collective-permute-start
  36.7 3.3 %collective-permute-start.1 = (bf16[960,128]{1,0:T(8,128)(2,1)S(1)}, bf16[960,128]{1,0:T(8,128)(2,1)S(1)}, u32[]{:S(2)}, u32[]{:S(2)}) collective-permute-start(bf16[960,128]{1,0:T(8,128)(2,1)S(1)} %get-tuple-element.22), channel_id=1, source_target_pairs={{0,16},{16,0},{32,48},{48,32},{64,80},{80,64},{96,112},{112,96},{1... | collective-permute-start | bytes 737288 | tf_op jit(solution)/shard_map/ppermute | solution.py:394
  40.0 4.5 %collective-permute-start.2 = (bf16[960,128]{1,0:T(8,128)(2,1)}, bf16[960,128]{1,0:T(8,128)(2,1)}, u32[]{:S(2)}, u32[]{:S(2)}) collective-permute-start(bf16[960,128]{1,0:T(8,128)(2,1)} %get-tuple-element.23), channel_id=1, source_target_pairs={{0,32},{16,48},{32,0},{48,16},{64,96},{80,112},{96,64},{112,80},{1... | collective-permute-start | bytes 737288 | tf_op jit(solution)/shard_map/ppermute | solution.py:394
  44.5 0.0 collective-permute-start.3
  44.5 0.7 slice_bitcast_fusion.3
  45.2 15.8 %collective-permute-done.1.z1 = bf16[960,128]{1,0:T(8,128)(2,1)S(1)} collective-permute-done((bf16[960,128]{1,0:T(8,128)(2,1)S(1)}, bf16[960,128]{1,0:T(8,128)(2,1)S(1)}, u32[]{:S(2)}, u32[]{:S(2)}) %collective-permute-start.1) | collective-permute-done | bytes 245792 | tf_op jit(solution)/shard_map/ppermute | solution.py:394
  60.9 0.0 copy-start.4
  60.9 0.7 slice_bitcast_fusion.2
  61.6 0.0 all-gather.3.cloned.1.call-done
  61.6 0.0 collective-permute-done.other_ref
  61.6 0.0 copy-done.13
  61.6 0.0 copy-start.12
  61.6 1.2 copy-done.12
  62.9 0.0 copy-start.14
  62.9 15.2 %view_attention.1 = bf16[16,144,128]{2,1,0:T(8,128)(2,1)} custom-call(bf16[16,256,128]{2,1,0:T(8,128)(2,1)S(1)} %all-to-all-done.own_ref, bf16[16,256,128]{2,1,0:T(8,128)(2,1)S(1)} %collective-permute-done.other_ref, bf16[8,4,128,128]{3,2,1,0:T(8,128)(2,1)S(1)} %bitcast.16, s32[8,32,32]{2,1,0:T(8,128)S(1)} %copy-done.13), custom_call_target="tpu_custom_call" | custom-call | flops 2700000000 | bytes 4000000 | tf_op jit(solution)/shard_map/view_attention/pallas_call | solution.py:218
  78.0 0.0 copy-done.4
  78.0 5.7 %all-to-all-start.1 = ((bf16[16,144,128]{2,1,0:T(8,128)(2,1)}), bf16[16,144,128]{2,1,0:T(8,128)(2,1)}, u32[]{:S(2)}, u32[]{:S(2)}) async-start(bf16[16,144,128]{2,1,0:T(8,128)(2,1)} %view_attention.1), calls=%async_computation.1 | async-start | bytes 1179648 | tf_op jit(solution)/shard_map/all_to_all | solution.py:413
  83.7 0.0 copy-start
  83.7 0.0 collective-permute-done.2.z2
  83.7 1.1 slice_bitcast_fusion.1
  84.8 0.0 collective-permute-done.3.z3
  84.8 0.9 slice_bitcast_fusion
  85.7 1.0 pad_maximum_fusion
  86.7 0.9 collective-permute-start.4
  87.6 13.7 %collective-permute-done.4.x_ref = bf16[4,448,128]{2,1,0:T(8,128)(2,1)S(1)} collective-permute-done((bf16[4,448,128]{2,1,0:T(8,128)(2,1)S(1)}, bf16[4,448,128]{2,1,0:T(8,128)(2,1)S(1)}, u32[]{:S(2)}, u32[]{:S(2)}) %collective-permute-start.4) | collective-permute-done | bytes 458784 | tf_op jit(solution)/shard_map/ppermute | solution.py:394
  101.3 0.0 copy-done.14
  101.3 0.0 copy-start.5
  101.3 0.9 copy-done.5
  102.3 7.0 %time_attention.1 = (bf16[208,128]{1,0:T(8,128)(2,1)S(1)}, bf16[208,128]{1,0:T(8,128)(2,1)S(1)}, bf16[208,128]{1,0:T(8,128)(2,1)S(1)}, bf16[208,128]{1,0:T(8,128...) custom-call(bf16[960,128]{1,0:T(8,128)(2,1)S(1)} %get-tuple-element., ...), custom_call_target="tpu_custom_call" | custom-call | flops 700000000 | bytes 2000000 | tf_op jit(solution)/shard_map/time_attention/pallas_call | solution.py:302
  109.3 0.0 copy-start.6
  109.3 0.6 copy-done.6
  109.9 2.7 %collective-permute-start.5 = (bf16[208,128]{1,0:T(8,128)(2,1)S(1)}, bf16[208,128]{1,0:T(8,128)(2,1)S(1)}, u32[]{:S(2)}, u32[]{:S(2)}) collective-permute-start(bf16[208,128]{1,0:T(8,128)(2,1)S(1)} %get-tuple-element.26), channel_id=1, source_target_pairs={{0,16},{16,0},{32,48},{48,32},{64,80},{80,64},{96,112},{112,96},{1... | collective-permute-start | bytes 159752 | tf_op jit(solution)/shard_map/ppermute | solution.py:394
  112.6 4.5 %collective-permute-start.6 = (bf16[208,128]{1,0:T(8,128)(2,1)S(1)}, bf16[208,128]{1,0:T(8,128)(2,1)S(1)}, u32[]{:S(2)}, u32[]{:S(2)}) collective-permute-start(bf16[208,128]{1,0:T(8,128)(2,1)S(1)} %get-tuple-element.27), channel_id=1, source_target_pairs={{0,32},{16,48},{32,0},{48,16},{64,96},{80,112},{96,64},{112,80},{1... | collective-permute-start | bytes 159752 | tf_op jit(solution)/shard_map/ppermute | solution.py:394
  117.1 0.0 collective-permute-start.7
  117.1 1.4 collective-permute-start.8
  118.5 2.1 %collective-permute-start.9 = (bf16[208,128]{1,0:T(8,128)(2,1)S(1)}, bf16[208,128]{1,0:T(8,128)(2,1)S(1)}, u32[]{:S(2)}, u32[]{:S(2)}) collective-permute-start(bf16[208,128]{1,0:T(8,128)(2,1)S(1)} %get-tuple-element.30), channel_id=1, source_target_pairs={{0,80},{16,64},{32,112},{48,96},{64,16},{80,0},{96,48},{112,32},{1... | collective-permute-start | bytes 159752 | tf_op jit(solution)/shard_map/ppermute | solution.py:394
  120.6 0.0 collective-permute-done.5.t1
  120.6 5.3 %collective-permute-start.10 = (bf16[208,128]{1,0:T(8,128)(2,1)S(1)}, bf16[208,128]{1,0:T(8,128)(2,1)S(1)}, u32[]{:S(2)}, u32[]{:S(2)}) collective-permute-start(bf16[208,128]{1,0:T(8,128)(2,1)S(1)} %get-tuple-element.31), channel_id=1, source_target_pairs={{0,96},{16,112},{32,64},{48,80},{64,32},{80,48},{96,0},{112,16},{1... | collective-permute-start | bytes 159752 | tf_op jit(solution)/shard_map/ppermute | solution.py:394
  125.9 0.0 collective-permute-done.6.t2
  125.9 0.0 collective-permute-start.11
  126.0 0.0 collective-permute-done.7.t3
  126.0 0.0 collective-permute-done.8.t4
  126.0 0.0 collective-permute-done.9.t5
  126.0 4.1 %collective-permute-done.10.t6 = bf16[208,128]{1,0:T(8,128)(2,1)S(1)} collective-permute-done((bf16[208,128]{1,0:T(8,128)(2,1)S(1)}, bf16[208,128]{1,0:T(8,128)(2,1)S(1)}, u32[]{:S(2)}, u32[]{:S(2)}) %collective-permute-start.10) | collective-permute-done | bytes 53280 | tf_op jit(solution)/shard_map/ppermute | solution.py:394
  130.1 0.6 copy-done.8
  130.7 2.4 %collective-permute-done.11.t7 = bf16[208,128]{1,0:T(8,128)(2,1)S(1)} collective-permute-done((bf16[208,128]{1,0:T(8,128)(2,1)S(1)}, bf16[208,128]{1,0:T(8,128)(2,1)S(1)}, u32[]{:S(2)}, u32[]{:S(2)}) %collective-permute-start.11) | collective-permute-done | bytes 53280 | tf_op jit(solution)/shard_map/ppermute | solution.py:394
  133.1 0.6 copy-done.10
  133.8 0.0 all-to-all-done.1.view_ref
  133.8 0.0 copy-done
  133.8 0.8 copy-done.7
  134.6 0.8 copy-done.9
  135.4 0.8 copy-done.11
  136.2 4.8 %join.1 = bf16[128,1280]{1,0:T(8,128)(2,1)} custom-call(bf16[16,144,128]{2,1,0:T(8,128)(2,1)} %all-to-all-done.1.view_ref, bf16[208,128]{1,0:T(8,128)(2,1)S(1)} %copy-done.7, bf16[208,128]{1,0:T(8,128)(2,1)S(1)} %collective-permute-done.5.t1, bf16[208,128]{1,0:T(8,128)(2,1)S(1)} %collective-permute-done.6.t2, ...), custom_call_target="tpu_custom_call" | custom-call | tf_op jit(solution)/shard_map/join/pallas_call | solution.py:382
  (6 shorter events, 0.0 us)
Async XLA Ops:
  6.5 1.0 copy-start.1
  7.5 1.0 copy-start.2
  8.5 1.0 copy-start.3
  9.5 52.2 %copy-start.13 = (s32[8,32,32]{2,1,0:T(8,128)S(1)}, s32[8,32,32]{2,1,0:T(8,128)}, u32[]{:S(2)}) copy-start(s32[8,32,32]{2,1,0:T(8,128)} %mask_ref.1) | copy-start | bytes 98308
  11.0 25.7 %all-to-all-start = ((bf16[16,256,128]{2,1,0:T(8,128)(2,1)}), bf16[16,256,128]{2,1,0:T(8,128)(2,1)S(1)}, u32[]{:S(2)}, u32[]{:S(2)}) async-start(bf16[16,256,128]{2,1,0:T(8,128)(2,1)} %get-tuple-element.19), calls=%async_computation | async-start | bytes 2097152 | tf_op jit(solution)/shard_map/all_to_all | solution.py:407
  19.8 41.8 %all-gather.3.cloned.1.call-start = ((), (), s32[]{:S(2)}) async-start(), calls=%async_computation.2 | async-start | bytes 1179648 | tf_op jit(solution)/shard_map/all_gather | solution.py:405
  36.7 24.9 %collective-permute-start = (bf16[16,256,128]{2,1,0:T(8,128)(2,1)S(1)}, bf16[16,256,128]{2,1,0:T(8,128)(2,1)S(1)}, u32[]{:S(2)}, u32[]{:S(2)}) collective-permute-start(bf16[16,256,128]{2,1,0:T(8,128)(2,1)S(1)} %all-to-all-done.own_ref), channel_id=1, source_target_pairs={{0,1},{1,0},{2,3},{3,2},{4,5},{5,4},{6,7},{7,6},{8,9},{9,8},{10,11... | collective-permute-start | bytes 3145736 | tf_op jit(solution)/shard_map/ppermute | solution.py:408
  36.7 24.2 %collective-permute-start.1 = (bf16[960,128]{1,0:T(8,128)(2,1)S(1)}, bf16[960,128]{1,0:T(8,128)(2,1)S(1)}, u32[]{:S(2)}, u32[]{:S(2)}) collective-permute-start(bf16[960,128]{1,0:T(8,128)(2,1)S(1)} %get-tuple-element.22), channel_id=1, source_target_pairs={{0,16},{16,0},{32,48},{48,32},{64,80},{80,64},{96,112},{112,96},{1... | collective-permute-start | bytes 737288 | tf_op jit(solution)/shard_map/ppermute | solution.py:394
  40.0 43.7 %collective-permute-start.2 = (bf16[960,128]{1,0:T(8,128)(2,1)}, bf16[960,128]{1,0:T(8,128)(2,1)}, u32[]{:S(2)}, u32[]{:S(2)}) collective-permute-start(bf16[960,128]{1,0:T(8,128)(2,1)} %get-tuple-element.23), channel_id=1, source_target_pairs={{0,32},{16,48},{32,0},{48,16},{64,96},{80,112},{96,64},{112,80},{1... | collective-permute-start | bytes 737288 | tf_op jit(solution)/shard_map/ppermute | solution.py:394
  44.5 40.3 %collective-permute-start.3 = (bf16[960,128]{1,0:T(8,128)(2,1)}, bf16[960,128]{1,0:T(8,128)(2,1)}, u32[]{:S(2)}, u32[]{:S(2)}) collective-permute-start(bf16[960,128]{1,0:T(8,128)(2,1)} %get-tuple-element.24), channel_id=1, source_target_pairs={{0,48},{16,32},{32,16},{48,0},{64,112},{80,96},{96,80},{112,64},{1... | collective-permute-start | bytes 737288 | tf_op jit(solution)/shard_map/ppermute | solution.py:394
  60.9 17.1 %copy-start.4 = (bf16[960,128]{1,0:T(8,128)(2,1)}, bf16[960,128]{1,0:T(8,128)(2,1)S(1)}, u32[]{:S(2)}) copy-start(bf16[960,128]{1,0:T(8,128)(2,1)S(1)} %collective-permute-done.1.z1) | copy-start | bytes 737284
  61.6 1.2 copy-start.12
  62.9 38.5 %copy-start.14 = (s32[8]{0:T(128)S(1)}, s32[8]{0:T(128)}, u32[]{:S(2)}) copy-start(s32[8]{0:T(128)} %times_ref.1) | copy-start | bytes 100
  78.0 55.7 %all-to-all-start.1 = ((bf16[16,144,128]{2,1,0:T(8,128)(2,1)}), bf16[16,144,128]{2,1,0:T(8,128)(2,1)}, u32[]{:S(2)}, u32[]{:S(2)}) async-start(bf16[16,144,128]{2,1,0:T(8,128)(2,1)} %view_attention.1), calls=%async_computation.1 | async-start | bytes 1179648 | tf_op jit(solution)/shard_map/all_to_all | solution.py:413
  83.7 50.1 %copy-start = (bf16[1280,1280]{1,0:T(8,128)(2,1)S(1)}, bf16[1280,1280]{1,0:T(8,128)(2,1)}, u32[]{:S(2)}) copy-start(bf16[1280,1280]{1,0:T(8,128)(2,1)} %weight_ref.1) | copy-start | bytes 9830404
  86.7 14.6 %collective-permute-start.4 = (bf16[4,448,128]{2,1,0:T(8,128)(2,1)S(1)}, bf16[4,448,128]{2,1,0:T(8,128)(2,1)S(1)}, u32[]{:S(2)}, u32[]{:S(2)}) collective-permute-start(bf16[4,448,128]{2,1,0:T(8,128)(2,1)S(1)} %pad_maximum_fusion), channel_id=1, source_target_pairs={{0,64},{16,80},{32,96},{48,112},{64,0},{80,16},{96,32},{112,48},{1... | collective-permute-start | bytes 1376264 | tf_op jit(solution)/shard_map/ppermute | solution.py:394
  101.3 0.9 copy-start.5
  109.3 0.6 copy-start.6
  109.9 10.7 %collective-permute-start.5 = (bf16[208,128]{1,0:T(8,128)(2,1)S(1)}, bf16[208,128]{1,0:T(8,128)(2,1)S(1)}, u32[]{:S(2)}, u32[]{:S(2)}) collective-permute-start(bf16[208,128]{1,0:T(8,128)(2,1)S(1)} %get-tuple-element.26), channel_id=1, source_target_pairs={{0,16},{16,0},{32,48},{48,32},{64,80},{80,64},{96,112},{112,96},{1... | collective-permute-start | bytes 159752 | tf_op jit(solution)/shard_map/ppermute | solution.py:394
  112.6 13.3 %collective-permute-start.6 = (bf16[208,128]{1,0:T(8,128)(2,1)S(1)}, bf16[208,128]{1,0:T(8,128)(2,1)S(1)}, u32[]{:S(2)}, u32[]{:S(2)}) collective-permute-start(bf16[208,128]{1,0:T(8,128)(2,1)S(1)} %get-tuple-element.27), channel_id=1, source_target_pairs={{0,32},{16,48},{32,0},{48,16},{64,96},{80,112},{96,64},{112,80},{1... | collective-permute-start | bytes 159752 | tf_op jit(solution)/shard_map/ppermute | solution.py:394
  117.1 8.9 %collective-permute-start.7 = (bf16[208,128]{1,0:T(8,128)(2,1)S(1)}, bf16[208,128]{1,0:T(8,128)(2,1)S(1)}, u32[]{:S(2)}, u32[]{:S(2)}) collective-permute-start(bf16[208,128]{1,0:T(8,128)(2,1)S(1)} %get-tuple-element.28), channel_id=1, source_target_pairs={{0,48},{16,32},{32,16},{48,0},{64,112},{80,96},{96,80},{112,64},{1... | collective-permute-start | bytes 159752 | tf_op jit(solution)/shard_map/ppermute | solution.py:394
  117.1 8.9 %collective-permute-start.8 = (bf16[208,128]{1,0:T(8,128)(2,1)S(1)}, bf16[208,128]{1,0:T(8,128)(2,1)S(1)}, u32[]{:S(2)}, u32[]{:S(2)}) collective-permute-start(bf16[208,128]{1,0:T(8,128)(2,1)S(1)} %get-tuple-element.29), channel_id=1, source_target_pairs={{0,64},{16,80},{32,96},{48,112},{64,0},{80,16},{96,32},{112,48},{1... | collective-permute-start | bytes 159752 | tf_op jit(solution)/shard_map/ppermute | solution.py:394
  118.5 7.4 %collective-permute-start.9 = (bf16[208,128]{1,0:T(8,128)(2,1)S(1)}, bf16[208,128]{1,0:T(8,128)(2,1)S(1)}, u32[]{:S(2)}, u32[]{:S(2)}) collective-permute-start(bf16[208,128]{1,0:T(8,128)(2,1)S(1)} %get-tuple-element.30), channel_id=1, source_target_pairs={{0,80},{16,64},{32,112},{48,96},{64,16},{80,0},{96,48},{112,32},{1... | collective-permute-start | bytes 159752 | tf_op jit(solution)/shard_map/ppermute | solution.py:394
  120.6 9.5 %collective-permute-start.10 = (bf16[208,128]{1,0:T(8,128)(2,1)S(1)}, bf16[208,128]{1,0:T(8,128)(2,1)S(1)}, u32[]{:S(2)}, u32[]{:S(2)}) collective-permute-start(bf16[208,128]{1,0:T(8,128)(2,1)S(1)} %get-tuple-element.31), channel_id=1, source_target_pairs={{0,96},{16,112},{32,64},{48,80},{64,32},{80,48},{96,0},{112,16},{1... | collective-permute-start | bytes 159752 | tf_op jit(solution)/shard_map/ppermute | solution.py:394
  125.9 7.2 %collective-permute-start.11 = (bf16[208,128]{1,0:T(8,128)(2,1)S(1)}, bf16[208,128]{1,0:T(8,128)(2,1)S(1)}, u32[]{:S(2)}, u32[]{:S(2)}) collective-permute-start(bf16[208,128]{1,0:T(8,128)(2,1)S(1)} %get-tuple-element.32), channel_id=1, source_target_pairs={{0,112},{16,96},{32,80},{48,64},{64,48},{80,32},{96,16},{112,0},{1... | collective-permute-start | bytes 159752 | tf_op jit(solution)/shard_map/ppermute | solution.py:394
  130.1 0.6 copy-start.8
  133.1 0.6 copy-start.10
  133.8 0.8 copy-start.7
  134.6 0.8 copy-start.9
  135.4 0.8 copy-start.11
Sparse Core Ops, SparseCore 0:
  22.5 26.1 all-gather.2

commit v2 on v0

v2 whole, which is shorter than its diff:
```python
import jax
import jax.numpy as jnp
from jax import lax
from jax.experimental import pallas as pl
from jax.experimental.pallas import tpu as pltpu
from jax.sharding import Mesh, PartitionSpec as P

HEADS = 20
REACH = 4
FRAMES = 8
HEAD = 64
CELLS = 128
MAIN = 16
RING = 4
NEG = -(2.0**30)
LOG2E = 1.4426950408889634
RATE = HEAD**-0.5 * LOG2E
TILE = 256
CHUNK = 512
Z_ROWS = 960
X_ROWS = 640
T_ROWS = 336
O_ROWS = 144
F32 = jnp.float32
BF16 = jnp.bfloat16
ANY = pl.BlockSpec(memory_space=pl.ANY)
VMEM = pl.BlockSpec(memory_space=pltpu.VMEM)
SMEM = pl.BlockSpec(memory_space=pltpu.SMEM)


def lanes(shape):
    return lax.broadcasted_iota(jnp.int32, shape, len(shape) - 1)


def rows_of(shape):
    return lax.broadcasted_iota(jnp.int32, shape, len(shape) - 2)


def swap_halves(x):
    return pltpu.roll(x, HEAD, 1)


def params(mib):
    return pltpu.CompilerParams(vmem_limit_bytes=mib * 1024 * 1024)


def turned(index, k):
    return (index, index + 1 - 2 * (index % 2), (index + 2) % 4, 3 - index)[k]


def copy_all(moves, sems):
    copies = [pltpu.make_async_copy(source, target, sems.at[i]) for i, (source, target) in enumerate(moves)]
    for copy in copies:
        copy.start()
    for copy in copies:
        copy.wait()


def pair(a_ref, a, b_ref, b):
    left = a_ref[:, a * HEAD : (a + 1) * HEAD]
    right = b_ref[:, b * HEAD : (b + 1) * HEAD]
    return jnp.concatenate([left, right], axis=1)


def pack_time_kernel(q_hbm, k_hbm, v_hbm, z0, z1, z2, z3, ring_ref, q_ref, k_ref, v_ref, sems, parts):
    place = lax.axis_index("f") % 4
    copy_all([(k_hbm, k_ref), (v_hbm, v_ref), (q_hbm, q_ref)], sems)
    for j in range(4):
        base = 5 * j
        for i in range(5):
            parts[j, i * CELLS : (i + 1) * CELLS] = pair(k_ref, base + i, v_ref, base + i)
        for i in range(2):
            rows = slice((5 + i) * CELLS, (6 + i) * CELLS)
            parts[j, rows] = pair(q_ref, base + 2 * i, q_ref, base + 2 * i + 1)
        last = q_ref[:, (base + 4) * HEAD : (base + 5) * HEAD]
        parts[j, 896:960] = jnp.concatenate([last[0:64], last[64:128]], axis=1)
    keep = pltpu.make_async_copy(parts.at[place], z0, sems.at[3])
    keep.start()
    for k, out in enumerate((z1, z2, z3)):
        out[...] = parts[turned(place, k + 1)]
    for y in range(RING):
        ring_ref[y] = pair(k_ref, MAIN + y, v_ref, MAIN + y)
    keep.wait()


def in_hbm(x):
    return pltpu.with_memory_space_constraint(x, pltpu.HBM)


def pack_time(q, k, v):
    block = jax.ShapeDtypeStruct((Z_ROWS, CELLS), BF16)
    whole = jax.ShapeDtypeStruct((CELLS, HEADS * HEAD), BF16)
    return pl.pallas_call(
        pack_time_kernel,
        out_shape=[pltpu.HBM((Z_ROWS, CELLS), BF16)] + [block] * 3 + [jax.ShapeDtypeStruct((RING, CELLS, CELLS), BF16)] + [whole] * 3,
        in_specs=[ANY] * 3,
        out_specs=[ANY] + [VMEM] * 7,
        scratch_shapes=[pltpu.SemaphoreType.DMA((4,)), pltpu.VMEM((4, Z_ROWS, CELLS), BF16)],
        compiler_params=params(16),
        name="pack_time",
    )(in_hbm(q), in_hbm(k), in_hbm(v))


def pack_view_kernel(q_ref, k_ref, v_ref, view_ref):
    for t in range(MAIN):
        view_ref[t, 0:CELLS] = pair(k_ref, t, v_ref, t)
        view_ref[t, CELLS : 2 * CELLS] = pair(q_ref, t, q_ref, MAIN + t % RING)


def pack_view(q, k, v):
    return pl.pallas_call(
        pack_view_kernel,
        out_shape=jax.ShapeDtypeStruct((MAIN, 2 * CELLS, CELLS), BF16),
        in_specs=[VMEM] * 3,
        out_specs=VMEM,
        compiler_params=params(16),
        cost_estimate=pl.CostEstimate(flops=4000000000, bytes_accessed=2000000, transcendentals=0),
        name="pack_view",
    )(q, k, v)


def stack_kernel(z0, z1, z2, z3, own_ref, ring_ref, sibling_ref, out_ref, kv_ref, r0, r1, r2, r3, sems):
    y = lax.axis_index("y")
    moves = [(piece.at[pl.ds(0, X_ROWS)], out_ref.at[k]) for k, piece in enumerate((z0, z1, z2, z3))]
    moves.append((own_ref.at[:, pl.ds(0, CELLS)], kv_ref))
    for k, out in enumerate((r0, r1, r2, r3)):
        moves.append((ring_ref.at[turned(y, k)], out.at[0]))
        moves.append((sibling_ref.at[turned(y, k)], out.at[1]))
    copy_all(moves, sems)


def stack(z, own, ring, other):
    block = jax.ShapeDtypeStruct((2, CELLS, CELLS), BF16)
    return pl.pallas_call(
        stack_kernel,
        out_shape=[
            jax.ShapeDtypeStruct((4, X_ROWS, CELLS), BF16),
            jax.ShapeDtypeStruct((MAIN, CELLS, CELLS), BF16),
        ]
        + [block] * 4,
        in_specs=[ANY] * 7,
        out_specs=[ANY] * 6,
        scratch_shapes=[pltpu.SemaphoreType.DMA((13,))],
        compiler_params=params(4),
        name="stack",
    )(*z, own, ring, other)


def score_tile(q, key_ref, score_ref, count):
    best = None
    for start in range(0, count, CHUNK):
        s = lax.dot_general(
            q, key_ref[start : start + CHUNK], (((1,), (1,)), ((), ())), preferred_element_type=F32
        )
        score_ref[:, start : start + CHUNK] = s
        for lane in range(0, CHUNK, 128):
            part = s[:, lane : lane + 128]
            best = part if best is None else jnp.maximum(best, part)
    return jnp.max(best, axis=1, keepdims=True)


def weigh_tile(score_ref, row_max, value_ref, count):
    total = None
    for start in range(0, count, CHUNK):
        s = score_ref[:, start : start + CHUNK]
        w = jnp.exp2((s - row_max) * RATE).astype(BF16)
        part = jnp.dot(w, value_ref[start : start + CHUNK], preferred_element_type=F32)
        total = part if total is None else total + part
    return total


def split3(x):
    high = x.astype(BF16).astype(F32)
    middle = (x - high).astype(BF16).astype(F32)
    low = (x - high - middle).astype(BF16).astype(F32)
    return [high, middle, low]


def level_rows(levels, lane, at=0):
    columns = [part for level in levels for part in split3(level)]
    table = jnp.zeros_like(columns[0])
    for i, column in enumerate(columns):
        table = jnp.where(lane == at + i, column, table)
    return table


def row(x):
    return x.astype(BF16)


def seen_bias(mask_ref, key_view, count):
    core = lax.axis_index("c")
    seen = mask_ref[lax.axis_index("f")].astype(F32)
    pick = (lanes((count, 32)) == key_view).astype(F32)
    view, column = rows_of((32, 128)), lanes((32, 128)) - HEAD
    query_pick = ((column >= 0) & (column < 16) & (view == 2 * column + core)).astype(F32)
    by_key = lax.dot_general(pick, seen, (((1,), (1,)), ((), ())), preferred_element_type=F32)
    allowed = jnp.dot(by_key, query_pick, preferred_element_type=F32)
    column = lanes((count, 128)) - HEAD
    return row(jnp.where((column >= 0) & (column < 16) & (allowed < 0.5), NEG, 0.0))


def fill(key_s, value_s, at, kv, bias):
    rows = slice(at * CELLS, (at + 1) * CELLS)
    low = row(jnp.where(lanes((1, CELLS)) < HEAD, 1.0, 0.0))
    key_s[rows] = kv * low + bias
    value_s[rows] = kv * (1 - low) + low


def view_kernel(own_ref, other_ref, mask_ref, order_ref, out_ref, key_s, value_s, s_a, s_b):
    del order_ref
    core = lax.axis_index("c")
    lane = lanes((CELLS, CELLS))
    block = rows_of((32, 32))
    bias = seen_bias(mask_ref, jnp.where(block < 16, 2 * block + core, 2 * (block - 16) + 1 - core), 32)
    for b in range(32):
        kv = own_ref[b, 0:CELLS] if b < 16 else other_ref[b - 16]
        fill(key_s, value_s, b, kv, bias[b : b + 1])

    def query(j):
        qq = own_ref[j, CELLS : 2 * CELLS].astype(F32)
        return jnp.where(lane < HEAD, qq, (lane == HEAD + j).astype(F32)).astype(BF16)

    def tile(i):
        return jnp.concatenate([query(2 * i), query(2 * i + 1)], axis=0)

    wide = lanes((TILE, CELLS))

    def finish(i, score_ref, row_max):
        main = weigh_tile(score_ref, row_max, value_s, 4096)
        heads = jnp.where(wide < HEAD, swap_halves(main) / main, 0.0)
        table = level_rows([row_max * RATE + jnp.log2(jnp.where(wide < HEAD, main, 1.0))], wide)
        for n in range(2):
            rows = slice(n * CELLS, (n + 1) * CELLS)
            out_ref[2 * i + n, 0:CELLS] = heads[rows].astype(BF16)
            out_ref[2 * i + n, CELLS:O_ROWS] = table[rows].T[0:16].astype(BF16)

    first = score_tile(tile(0), key_s, s_a, 4096)

    def body(step, m_a):
        m_b = score_tile(tile(2 * step + 1), key_s, s_b, 4096)
        finish(2 * step, s_a, m_a)
        m_next = score_tile(tile(jnp.minimum(2 * step + 2, 7)), key_s, s_a, 4096)
        finish(2 * step + 1, s_b, m_b)
        return m_next

    lax.fori_loop(0, 4, body, first)


def view_attention(own, other, view_mask, order):
    return pl.pallas_call(
        view_kernel,
        out_shape=jax.ShapeDtypeStruct((MAIN, O_ROWS, CELLS), BF16),
        in_specs=[VMEM] * 3 + [ANY],
        out_specs=VMEM,
        scratch_shapes=[
            pltpu.VMEM((4096, CELLS), BF16),
            pltpu.VMEM((4096, CELLS), BF16),
            pltpu.VMEM((TILE, 4096), F32),
            pltpu.VMEM((TILE, 4096), F32),
        ],
        compiler_params=params(20),
        cost_estimate=pl.CostEstimate(flops=8000000000, bytes_accessed=4000000, transcendentals=9000000),
        name="view_attention",
    )(own, other, view_mask, order)


def ring_kernel(main_ref, own_ref, r0, r1, r2, r3, mask_ref, order_ref, out_hbm, out_ref, sems, key_s, value_s, s_ref):
    del order_ref
    core = lax.axis_index("c")
    y = lax.axis_index("y")
    ring = lax.axis_index("g") * 2 + lax.axis_index("zl")
    lane = lanes((CELLS, CELLS))
    block = rows_of((8, 32))
    side = jnp.where(block % 2 == 0, core, 1 - core)
    bias = seen_bias(mask_ref, ring * 8 + 2 * (y ^ (block // 2)) + side, 8)
    for k, piece in enumerate((r0, r1, r2, r3)):
        for n in range(2):
            fill(key_s, value_s, 2 * k + n, piece[n], bias[2 * k + n : 2 * k + n + 1])

    def query(j):
        qq = swap_halves(own_ref[j, CELLS : 2 * CELLS].astype(F32))
        return jnp.where(lane < HEAD, qq, (lane == HEAD + j).astype(F32)).astype(BF16)

    wide = lanes((TILE, CELLS))

    def begin(i):
        tile = jnp.concatenate([query(2 * i), query(2 * i + 1)], axis=0)
        return score_tile(tile, key_s, s_ref.at[i % 2], 1024)

    row_max = begin(0)
    copies = []
    for i in range(8):
        following = begin(i + 1) if i < 7 else None
        part = weigh_tile(s_ref.at[i % 2], row_max, value_s, 1024)
        heads = jnp.where(wide < HEAD, 0.0, part / swap_halves(part)).astype(BF16)
        level = row_max * RATE + jnp.log2(jnp.where(wide < HEAD, part, 1.0))
        table = level_rows([level], wide, 3)
        for n in range(2):
            rows = slice(n * CELLS, (n + 1) * CELLS)
            j = 2 * i + n
            out_ref[j, 0:CELLS] = main_ref[j, 0:CELLS] + heads[rows]
            out_ref[j, CELLS:O_ROWS] = main_ref[j, CELLS:O_ROWS] + table[rows].T[0:16].astype(BF16)
        copies.append(pltpu.make_async_copy(out_ref.at[pl.ds(2 * i, 2)], out_hbm.at[pl.ds(2 * i, 2)], sems.at[i]))
        copies[-1].start()
        row_max = following
    for copy in copies:
        copy.wait()


def ring_attention(main, own, pieces, view_mask, order):
    return pl.pallas_call(
        ring_kernel,
        out_shape=pltpu.HBM((MAIN, O_ROWS, CELLS), BF16),
        in_specs=[VMEM] * 7 + [ANY],
        out_specs=ANY,
        scratch_shapes=[
            pltpu.VMEM((MAIN, O_ROWS, CELLS), BF16),
            pltpu.SemaphoreType.DMA((8,)),
            pltpu.VMEM((1024, CELLS), BF16),
            pltpu.VMEM((1024, CELLS), BF16),
            pltpu.VMEM((2, TILE, 1024), F32),
        ],
        compiler_params=params(12),
        cost_estimate=pl.CostEstimate(flops=500000000, bytes_accessed=2000000, transcendentals=2000000),
        name="ring_attention",
    )(main, own, *pieces, view_mask, order)


def time_kernel(z0, z1, z2, z3, x_any, times_ref, o_hbm, o1, o2, o3, o0, z_s, x_ref, sems, key_s, value_s, q_s, s_ref):
    frame = lax.axis_index("f")
    lane = lanes((CELLS, CELLS))
    own = [z_s.at[k] for k in range(4)]
    outs = (o0, o1, o2, o3)

    l8, r8 = lanes((8, 128)), rows_of((8, 128))
    query_time = jnp.zeros((8, 128), jnp.int32)
    key_time = jnp.zeros((8, 128), jnp.int32)
    for k in range(FRAMES):
        now = times_ref[frame ^ k]
        query_time = jnp.where(l8 == HEAD + k, now, query_time)
        key_time = jnp.where(r8 == k, now, key_time)
    near = (jnp.abs(query_time - key_time) <= REACH) & (l8 - HEAD != r8)
    bias = row(jnp.where((l8 >= HEAD) & (l8 < HEAD + 4) & jnp.logical_not(near), NEG, 0.0))
    low = row(jnp.where(lanes((1, CELLS)) < HEAD, 1.0, 0.0))
    high = row(jnp.where(lanes((1, CELLS)) < HEAD, 0.0, 1.0))

    copy_all(list(zip((z0, z1, z2, z3, x_any), own + [x_ref])), sems)

    for head in range(5):
        for k in range(8):
            at = slice(head * CELLS, (head + 1) * CELLS)
            kv = own[k][at] if k < 4 else x_ref[k - 4, at]
            rows = slice(k * CELLS, (k + 1) * CELLS)
            key_s[head, rows] = kv * low + bias[k : k + 1]
            value_s[head, rows] = kv * high + low
    for k in range(4):
        rows = slice(k * CELLS, (k + 1) * CELLS)
        hot = jnp.where(lane == HEAD + k, 1.0, 0.0)
        for i in range(2):
            qq = own[k][(5 + i) * CELLS : (6 + i) * CELLS].astype(F32)
            q_s[2 * i, rows] = jnp.where(lane < HEAD, qq, hot).astype(BF16)
            q_s[2 * i + 1, rows] = jnp.where(lane < HEAD, swap_halves(qq), hot).astype(BF16)
        packed = own[k][896:960].astype(F32)
        qq = jnp.concatenate([packed, swap_halves(packed)], axis=0)
        q_s[4, rows] = jnp.where(lane < HEAD, qq, hot).astype(BF16)

    wide = lanes((TILE, CELLS))
    work = [(i, head) for i in range(2) for head in range(5)]

    def begin(n):
        i, head = work[n]
        return score_tile(q_s[head, i * TILE : (i + 1) * TILE], key_s.at[head], s_ref.at[n % 2], 1024)

    row_max = begin(0)
    heads, levels = [], []
    for n, (i, head) in enumerate(work):
        following = begin(n + 1) if n + 1 < len(work) else None
        total = weigh_tile(s_ref.at[n % 2], row_max, value_s.at[head], 1024)
        sums = swap_halves(total)
        if head % 2 == 0:
            heads.append(jnp.where(wide < HEAD, sums / total, 0.0))
        else:
            heads.append(jnp.where(wide < HEAD, 0.0, total / sums))
        levels.append(row_max * RATE + jnp.log2(jnp.where(wide < HEAD, total, 1.0)))
        row_max = following
        if head < 4:
            continue
        table = level_rows(levels, wide)
        for m in range(2):
            rows = slice(m * CELLS, (m + 1) * CELLS)
            out = outs[2 * i + m]
            out[0:128] = (heads[0] + heads[1])[rows].astype(BF16)
            out[128:256] = (heads[2] + heads[3])[rows].astype(BF16)
            last = heads[4][rows]
            out[256:320] = (last[0:64] + swap_halves(last[64:128])).astype(BF16)
            out[320:336] = table[rows].T[0:16].astype(BF16)
        if i == 0:
            keep = pltpu.make_async_copy(o0, o_hbm, sems.at[5])
            keep.start()
        heads, levels = [], []
    keep.wait()


def time_attention(own, crossed, frame_times):
    return pl.pallas_call(
        time_kernel,
        out_shape=[pltpu.HBM((T_ROWS, CELLS), BF16)] + [jax.ShapeDtypeStruct((T_ROWS, CELLS), BF16)] * 3,
        in_specs=[ANY] * 5 + [SMEM],
        out_specs=[ANY] + [VMEM] * 3,
        scratch_shapes=[
            pltpu.VMEM((T_ROWS, CELLS), BF16),
            pltpu.VMEM((4, Z_ROWS, CELLS), BF16),
            pltpu.VMEM((4, X_ROWS, CELLS), BF16),
            pltpu.SemaphoreType.DMA((6,)),
            pltpu.VMEM((5, 1024, CELLS), BF16),
            pltpu.VMEM((5, 1024, CELLS), BF16),
            pltpu.VMEM((5, 512, CELLS), BF16),
            pltpu.VMEM((2, TILE, 1024), F32),
        ],
        compiler_params=params(16),
        cost_estimate=pl.CostEstimate(flops=700000000, bytes_accessed=2000000, transcendentals=2700000),
        name="time_attention",
    )(*own, crossed, frame_times)


def join_kernel(view_any, t0, t1, t2, t3, weight_any, out_ref, view_ref, times, weight_ref, heads_s, sems):
    place = lax.axis_index("f") % 4
    load = pltpu.make_async_copy(weight_any, weight_ref, sems.at[5])
    moves = [(piece, times.at[turned(place, k)]) for k, piece in enumerate((t0, t1, t2, t3))]
    copies = [pltpu.make_async_copy(*move, sems.at[i]) for i, move in enumerate([*moves, (view_any, view_ref)])]
    for copy in copies:
        copy.start()
    load.start()
    for copy in copies:
        copy.wait()

    view_rows = jnp.concatenate([view_ref[t, CELLS:O_ROWS] for t in range(MAIN)], axis=0)
    time_rows = jnp.concatenate([times[j, 320:336] for j in range(4)], axis=0)

    def levels(rows, picked):
        pick = jnp.where(picked, 1.0, 0.0).astype(BF16)
        return lax.dot_general(rows, pick, (((0,), (0,)), ((), ())), preferred_element_type=F32)

    at, head = rows_of((256, 128)), lanes((256, 128))
    source, part = at // 16, at % 16
    found = []
    for ring in range(4):
        picked = (head >= MAIN) & (source == 4 * ring + head - MAIN) & (part >= 3) & (part < 6)
        if ring == 0:
            picked = picked | ((head < MAIN) & (source == head) & (part < 3))
        found.append(levels(view_rows, picked))
    at, head = rows_of((64, 128)), lanes((64, 128))
    offset = at % 16 - 3 * (head - 5 * (at // 16))
    inside = (head >= 5 * (at // 16)) & (head < 5 * (at // 16) + 5)
    found.append(levels(time_rows, inside & (offset >= 0) & (offset < 3)))
    column = lanes((CELLS, CELLS))
    for ring in range(1, 4):
        found[ring] = jnp.where(column < MAIN, -1e30, found[ring])
    best = found[0]
    for value in found[1:]:
        best = jnp.maximum(best, value)
    powers = [jnp.exp2(value - best) for value in found]
    total = powers[0]
    for power in powers[1:]:
        total = total + power
    shares = [power / total for power in powers]

    def time_block(head):
        j, i = head // 5, head % 5
        if i < 4:
            rows = slice((i // 2) * CELLS, (i // 2 + 1) * CELLS)
            return times[j, rows, (i % 2) * HEAD : (i % 2 + 1) * HEAD].astype(F32)
        packed = times[j, 256:320].astype(F32)
        return jnp.concatenate([packed[:, 0:HEAD], packed[:, HEAD:128]], axis=0)

    load.wait()
    result = None
    for first in range(0, HEADS, 4):
        for h in range(first, first + 4):
            mixed = time_block(h) * shares[4][:, h : h + 1]
            if h < MAIN:
                mixed += view_ref[h, 0:CELLS, 0:HEAD].astype(F32) * shares[0][:, h : h + 1]
            else:
                for ring in range(4):
                    block = view_ref[4 * ring + h - MAIN, 0:CELLS, HEAD:128].astype(F32)
                    mixed += block * shares[ring][:, h : h + 1]
            heads_s[:, h * HEAD : (h + 1) * HEAD] = mixed.astype(BF16)
        columns = slice(first * HEAD, (first + 4) * HEAD)
        product = jnp.dot(heads_s[:, columns], weight_ref[columns], preferred_element_type=F32)
        result = product if result is None else result + product
    out_ref[...] = result.astype(BF16)


def join(view_out, pieces, out_weight):
    return pl.pallas_call(
        join_kernel,
        out_shape=jax.ShapeDtypeStruct((CELLS, HEADS * HEAD), BF16),
        in_specs=[ANY] * 6,
        out_specs=VMEM,
        scratch_shapes=[
            pltpu.VMEM((MAIN, O_ROWS, CELLS), BF16),
            pltpu.VMEM((4, T_ROWS, CELLS), BF16),
            pltpu.VMEM((HEADS * HEAD, HEADS * HEAD), BF16),
            pltpu.VMEM((CELLS, HEADS * HEAD), BF16),
            pltpu.SemaphoreType.DMA((6,)),
        ],
        compiler_params=params(16),
        name="join",
    )(view_out, *pieces, in_hbm(out_weight))


def across(array, k):
    return lax.ppermute(array, "f", [(i, i ^ k) for i in range(FRAMES)])


def around(array, k):
    return lax.ppermute(array, "y", [(i, i ^ k) for i in range(RING)])


def sibling(array):
    return lax.ppermute(array, "c", [(0, 1), (1, 0)])


def local(queries, keys, values, view_mask, frame_times, out_weight):
    model = queries.shape[3]
    q, k, v = (a.reshape(CELLS, model) for a in (queries, keys, values))
    *z, to_ring, q, k, v = pack_time(q, k, v)
    z = [in_hbm(z[0])] + [across(z[i], i) for i in (1, 2, 3)]
    beside = sibling(to_ring)
    own = lax.all_to_all(pack_view(q, k, v), ("g", "zl", "y"), 0, 0)
    stacked, kv, *ring = stack(z, own, to_ring, beside)
    ring = [ring[0]] + [around(ring[i], i) for i in (1, 2, 3)]
    crossed = across(stacked, 4)
    main_out = view_attention(own, sibling(kv), view_mask, stacked)
    view_out = ring_attention(main_out, own, ring, view_mask, crossed)
    view_back = lax.all_to_all(view_out, ("g", "zl", "y"), 0, 0)
    pieces = time_attention([in_hbm(a) for a in z], in_hbm(crossed), frame_times)
    pieces = [in_hbm(pieces[0])] + [across(pieces[i], i) for i in (1, 2, 3)]
    result = join(view_back, pieces, out_weight)
    return result.reshape(1, 1, CELLS, model)


def solution(mesh):
    fine = Mesh(mesh.devices.reshape(2, 8, 2, 4, 2), ("g", "f", "zl", "y", "c"))
    blocks = P(("g", "f"), ("zl", "y", "c"), None, None)
    return jax.shard_map(
        local,
        mesh=fine,
        in_specs=(blocks, blocks, blocks, P(), P(), P()),
        out_specs=blocks,
        check_vma=False,
    )
```

time: 574 us -> 110 us (0.19)
  the two profiles are of different devices: /device:TPU:88 before, /device:TPU:8 now
where the time goes in v2:
time: 110 us; the launch traced here: 109 us
  waiting for transfers between devices  40.4 us (37%)
  starting transfers between devices  35.6 us (32%)
  Pallas kernels  33 us (30%)
    ppermute x7, waiting for transfers between devices, across(): return lax.ppermute(array, 'f', [(i, i ^ k) for i in range(FRAMES)])  39 us
    ppermute x7, starting transfers between devices, across(): return lax.ppermute(array, 'f', [(i, i ^ k) for i in range(FRAMES)])  14.9 us
    pallas_call x1, Pallas kernels, view_attention(): pl.pallas_call(view_kernel, out_shape=jax.ShapeDtypeStruct((MAIN, O_ROWS,...  11.7 us
    all_to_all x1, starting transfers between devices, local(): own = lax.all_to_all(pack_view(q, k, v), ('g', 'zl', 'y'), 0, 0)  8.88 us
    all_to_all x1, starting transfers between devices, local(): view_back = lax.all_to_all(view_out, ('g', 'zl', 'y'), 0, 0)  8.16 us
    pallas_call x1, Pallas kernels, time_attention(): pl.pallas_call(time_kernel, out_shape=[pltpu.HBM((T_ROWS, CELLS), BF16)]...  6.75 us
    pallas_call x1, Pallas kernels, join(): pl.pallas_call(join_kernel, out_shape=jax.ShapeDtypeStruct((CELLS, HEADS...  5.91 us
    pallas_call x1, Pallas kernels, ring_attention(): pl.pallas_call(ring_kernel, out_shape=pltpu.HBM((MAIN, O_ROWS, CELLS), BF...  3.94 us
  transfers between devices with their start and end apart: 14, of which 7 were waited for; matrix products, arithmetic and copies ran while one was open for 0% of the time, Pallas kernels for 17%

profile of v2, /device:TPU:8, one launch (start us, length us, event | category | flops | bytes accessed | tf_op | source)
XLA Modules:
  0.0 109.4 jit_solution(10516132723650420737)
XLA Ops:
  0.0 2.2 %pack_time.1 = (bf16[960,128]{1,0:T(8,128)(2,1)}, bf16[960,128]{1,0:T(8,128)(2,1)S(1)}, bf16[960,128]{1,0:T(8,128)(2,1)S(1)}, bf16[960,128]{1,0:T(8,128)(2,1)S(1...) custom-call(bf16[128,1280]{1,0:T(8,128)(2,1)} %bitcast.4, ...), custom_call_target="tpu_custom_call" | custom-call | tf_op jit(solution)/shard_map/pack_time/pallas_call | solution.py:93
  2.2 1.3 %pack_view.1 = bf16[16,256,128]{2,1,0:T(8,128)(2,1)} custom-call(bf16[128,1280]{1,0:T(8,128)(2,1)S(1)} %get-tuple-element.23.q_ref, bf16[128,1280]{1,0:T(8,128)(2,1)S(1)} %get-tuple-element.24.k_ref, bf16[128,1280]{1,0:T(8,128)(2,1)S(1)} %get-tuple-element.25.v_ref), custom_call_target="tpu_custom_call" | custom-call | flops 4000000000 | bytes 2000000 | tf_op jit(solution)/shard_map/pack_view/pallas_call | solution.py:111
  3.6 0.0 copy-start.4
  3.6 8.9 %all-to-all-start = ((bf16[16,256,128]{2,1,0:T(8,128)(2,1)}), bf16[16,256,128]{2,1,0:T(8,128)(2,1)S(1)}, u32[]{:S(2)}, u32[]{:S(2)}) async-start(bf16[16,256,128]{2,1,0:T(8,128)(2,1)} %pack_view.1), calls=%async_computation | async-start | bytes 2097152 | tf_op jit(solution)/shard_map/all_to_all | solution.py:531
  12.4 3.3 %collective-permute-start = (bf16[960,128]{1,0:T(8,128)(2,1)S(1)}, bf16[960,128]{1,0:T(8,128)(2,1)S(1)}, u32[]{:S(2)}, u32[]{:S(2)}) collective-permute-start(bf16[960,128]{1,0:T(8,128)(2,1)S(1)} %get-tuple-element.27), channel_id=1, source_target_pairs={{0,16},{16,0},{32,48},{48,32},{64,80},{80,64},{96,112},{112,96},{1... | collective-permute-start | bytes 737288 | tf_op jit(solution)/shard_map/ppermute | solution.py:514
  15.7 4.5 %collective-permute-start.1 = (bf16[960,128]{1,0:T(8,128)(2,1)S(1)}, bf16[960,128]{1,0:T(8,128)(2,1)S(1)}, u32[]{:S(2)}, u32[]{:S(2)}) collective-permute-start(bf16[960,128]{1,0:T(8,128)(2,1)S(1)} %get-tuple-element.28), channel_id=1, source_target_pairs={{0,32},{16,48},{32,0},{48,16},{64,96},{80,112},{96,64},{112,80},{1... | collective-permute-start | bytes 737288 | tf_op jit(solution)/shard_map/ppermute | solution.py:514
  20.2 0.0 collective-permute-start.2
  20.2 0.0 collective-permute-start.3
  20.2 1.3 %collective-permute-done.3.sibling_ref = bf16[4,128,128]{2,1,0:T(8,128)(2,1)S(1)} collective-permute-done((bf16[4,128,128]{2,1,0:T(8,128)(2,1)S(1)}, bf16[4,128,128]{2,1,0:T(8,128)(2,1)S(1)}, u32[]{:S(2)}, u32[]{:S(2)}) %collective-permute-start.3) | collective-permute-done | bytes 131104 | tf_op jit(solution)/shard_map/ppermute | solution.py:522
  21.6 19.1 %collective-permute-done.z1 = bf16[960,128]{1,0:T(8,128)(2,1)S(1)} collective-permute-done((bf16[960,128]{1,0:T(8,128)(2,1)S(1)}, bf16[960,128]{1,0:T(8,128)(2,1)S(1)}, u32[]{:S(2)}, u32[]{:S(2)}) %collective-permute-start) | collective-permute-done | bytes 245792 | tf_op jit(solution)/shard_map/ppermute | solution.py:514
  40.7 0.0 copy-start
  40.7 10.7 %collective-permute-done.1.z2 = bf16[960,128]{1,0:T(8,128)(2,1)S(1)} collective-permute-done((bf16[960,128]{1,0:T(8,128)(2,1)S(1)}, bf16[960,128]{1,0:T(8,128)(2,1)S(1)}, u32[]{:S(2)}, u32[]{:S(2)}) %collective-permute-start.1) | collective-permute-done | bytes 245792 | tf_op jit(solution)/shard_map/ppermute | solution.py:514
  51.4 0.0 copy-start.1
  51.4 0.0 collective-permute-done.2.z3
  51.4 0.0 copy-start.2
  51.4 0.0 all-to-all-done.own_ref
  51.4 1.2 %stack.1 = (bf16[4,640,128]{2,1,0:T(8,128)(2,1)S(1)}, bf16[16,128,128]{2,1,0:T(8,128)(2,1)S(1)}, bf16[2,128,128]{2,1,0:T(8,128)(2,1)S(1)}, bf16[2,128,128]{2,1,0...) custom-call(bf16[960,128]{1,0:T(8,128)(2,1)} %get-tuple-element.26.z0, ...), custom_call_target="tpu_custom_call" | custom-call | tf_op jit(solution)/shard_map/stack/pallas_call | solution.py:134
  52.6 0.1 collective-permute-start.4
  52.7 0.4 collective-permute-start.5
  53.1 2.6 %collective-permute-start.6 = (bf16[2,128,128]{2,1,0:T(8,128)(2,1)S(1)}, bf16[2,128,128]{2,1,0:T(8,128)(2,1)S(1)}, u32[]{:S(2)}, u32[]{:S(2)}) collective-permute-start(bf16[2,128,128]{2,1,0:T(8,128)(2,1)S(1)} %get-tuple-element.35), channel_id=1, source_target_pairs={{0,4},{2,6},{4,0},{6,2},{1,5},{3,7},{5,1},{7,3},{8,12},{10,14},{12... | collective-permute-start | bytes 196616 | tf_op jit(solution)/shard_map/ppermute | solution.py:518
  55.7 0.6 collective-permute-start.7
  56.3 0.6 collective-permute-start.8
  56.9 0.0 collective-permute-done.4.other_ref
  56.9 0.0 copy-done.4
  56.9 11.7 %view_attention.1.main_ref = bf16[16,144,128]{2,1,0:T(8,128)(2,1)S(1)} custom-call(bf16[16,256,128]{2,1,0:T(8,128)(2,1)S(1)} %all-to-all-done.own_ref, bf16[16,128,128]{2,1,0:T(8,128)(2,1)S(1)} %collective-permute-done.4.other_ref, s32[8,32,32]{2,1,0:T(8,128)S(1)} %copy-done.4, bf16[4,640,128]{2,1,0:T(8,128)(2,1)S(1)} %get-tuple-element.32.order_ref), custom_call_target="tpu_custom_call" | custom-call | flops 8000000000 | bytes 4000000 | tf_op jit(solution)/shard_map/view_attention/pallas_call | solution.py:251
  68.5 0.0 copy-done
  68.5 0.0 copy-done.1
  68.6 0.0 copy-done.2
  68.6 0.0 copy-start.5
  68.6 0.0 collective-permute-done.5.r1
  68.6 0.0 collective-permute-done.6.r2
  68.6 0.0 collective-permute-done.7.r3
  68.6 3.9 %collective-permute-done.8.order_ref.x_any = bf16[4,640,128]{2,1,0:T(8,128)(2,1)S(1)} collective-permute-done((bf16[4,640,128]{2,1,0:T(8,128)(2,1)S(1)}, bf16[4,640,128]{2,1,0:T(8,128)(2,1)S(1)}, u32[]{:S(2)}, u32[]{:S(2)}) %collective-permute-start.8) | collective-permute-done | bytes 655392 | tf_op jit(solution)/shard_map/ppermute | solution.py:514
  72.5 0.0 copy-start.3
  72.5 3.9 %ring_attention.1 = bf16[16,144,128]{2,1,0:T(8,128)(2,1)} custom-call(bf16[16,144,128]{2,1,0:T(8,128)(2,1)S(1)} %view_attention.1.main_ref, bf16[16,256,128]{2,1,0:T(8,128)(2,1)S(1)} %all-to-all-done.own_ref, bf16[2,128,128]{2,1,0:T(8,128)(2,1)S(1)} %get-tuple-element.33.r0, bf16[2,128,128]{2,1,0:T(8,128)(2,1)S(1)} %collective-permute-done.5.r1, ...), custom_call_target="tpu_custom_call" | custom-call | flops 500000000 | bytes 2000000 | tf_op jit(solution)/shard_map/ring_attention/pallas_call | solution.py:312
  76.5 8.2 %all-to-all-start.1 = ((bf16[16,144,128]{2,1,0:T(8,128)(2,1)}), bf16[16,144,128]{2,1,0:T(8,128)(2,1)S(1)}, u32[]{:S(2)}, u32[]{:S(2)}) async-start(bf16[16,144,128]{2,1,0:T(8,128)(2,1)} %ring_attention.1), calls=%async_computation.1 | async-start | bytes 1179648 | tf_op jit(solution)/shard_map/all_to_all | solution.py:537
  84.6 0.0 copy-done.3
  84.6 0.0 copy-done.5
  84.6 6.7 %time_attention.1 = (bf16[336,128]{1,0:T(8,128)(2,1)}, bf16[336,128]{1,0:T(8,128)(2,1)S(1)}, bf16[336,128]{1,0:T(8,128)(2,1)S(1)}, bf16[336,128]{1,0:T(8,128)(2,1)S(1)}) custom-call(bf16[960,128]{1,0:T(8,128)(2,1)} %get-tuple-element.26.z0, bf16[960,128]{1,0:T(8,128)(2,1)} %copy-done, bf16[960,128]{1,0:T(8,128)(2,1)} %copy-done.1, ...), custom_call_target="tpu_custom_call" | custom-call | flops 700000000 | bytes 2000000 | tf_op jit(solution)/shard_map/time_attention/pallas_call | solution.py:406
  91.4 2.5 %collective-permute-start.9 = (bf16[336,128]{1,0:T(8,128)(2,1)S(1)}, bf16[336,128]{1,0:T(8,128)(2,1)S(1)}, u32[]{:S(2)}, u32[]{:S(2)}) collective-permute-start(bf16[336,128]{1,0:T(8,128)(2,1)S(1)} %get-tuple-element.38), channel_id=1, source_target_pairs={{0,16},{16,0},{32,48},{48,32},{64,80},{80,64},{96,112},{112,96},{1... | collective-permute-start | bytes 258056 | tf_op jit(solution)/shard_map/ppermute | solution.py:514
  93.8 1.4 %collective-permute-start.10 = (bf16[336,128]{1,0:T(8,128)(2,1)S(1)}, bf16[336,128]{1,0:T(8,128)(2,1)S(1)}, u32[]{:S(2)}, u32[]{:S(2)}) collective-permute-start(bf16[336,128]{1,0:T(8,128)(2,1)S(1)} %get-tuple-element.39), channel_id=1, source_target_pairs={{0,32},{16,48},{32,0},{48,16},{64,96},{80,112},{96,64},{112,80},{1... | collective-permute-start | bytes 258056 | tf_op jit(solution)/shard_map/ppermute | solution.py:514
  95.3 2.7 %collective-permute-start.11 = (bf16[336,128]{1,0:T(8,128)(2,1)S(1)}, bf16[336,128]{1,0:T(8,128)(2,1)S(1)}, u32[]{:S(2)}, u32[]{:S(2)}) collective-permute-start(bf16[336,128]{1,0:T(8,128)(2,1)S(1)} %get-tuple-element.40), channel_id=1, source_target_pairs={{0,48},{16,32},{32,16},{48,0},{64,112},{80,96},{96,80},{112,64},{1... | collective-permute-start | bytes 258056 | tf_op jit(solution)/shard_map/ppermute | solution.py:514
  98.0 0.1 collective-permute-done.9.t1
  98.1 4.6 %collective-permute-done.10.t2 = bf16[336,128]{1,0:T(8,128)(2,1)S(1)} collective-permute-done((bf16[336,128]{1,0:T(8,128)(2,1)S(1)}, bf16[336,128]{1,0:T(8,128)(2,1)S(1)}, u32[]{:S(2)}, u32[]{:S(2)}) %collective-permute-start.10) | collective-permute-done | bytes 86048 | tf_op jit(solution)/shard_map/ppermute | solution.py:514
  102.7 0.6 collective-permute-done.11.t3
  103.3 0.0 all-to-all-done.1.view_any
  103.3 5.9 %join.1 = bf16[128,1280]{1,0:T(8,128)(2,1)} custom-call(bf16[16,144,128]{2,1,0:T(8,128)(2,1)S(1)} %all-to-all-done.1.view_any, bf16[336,128]{1,0:T(8,128)(2,1)} %get-tuple-element.37.t0, bf16[336,128]{1,0:T(8,128)(2,1)S(1)} %collective-permute-done.9.t1, bf16[336,128]{1,0:T(8,128)(2,1)S(1)} %collective-permute-done.10.t2, ...), custom_call_target="tpu_custom_call" | custom-call | tf_op jit(solution)/shard_map/join/pallas_call | solution.py:496
Async XLA Ops:
  3.6 53.3 %copy-start.4 = (s32[8,32,32]{2,1,0:T(8,128)S(1)}, s32[8,32,32]{2,1,0:T(8,128)}, u32[]{:S(2)}) copy-start(s32[8,32,32]{2,1,0:T(8,128)} %mask_ref.3) | copy-start | bytes 98308
  3.6 47.8 %all-to-all-start = ((bf16[16,256,128]{2,1,0:T(8,128)(2,1)}), bf16[16,256,128]{2,1,0:T(8,128)(2,1)S(1)}, u32[]{:S(2)}, u32[]{:S(2)}) async-start(bf16[16,256,128]{2,1,0:T(8,128)(2,1)} %pack_view.1), calls=%async_computation | async-start | bytes 2097152 | tf_op jit(solution)/shard_map/all_to_all | solution.py:531
  12.4 28.2 %collective-permute-start = (bf16[960,128]{1,0:T(8,128)(2,1)S(1)}, bf16[960,128]{1,0:T(8,128)(2,1)S(1)}, u32[]{:S(2)}, u32[]{:S(2)}) collective-permute-start(bf16[960,128]{1,0:T(8,128)(2,1)S(1)} %get-tuple-element.27), channel_id=1, source_target_pairs={{0,16},{16,0},{32,48},{48,32},{64,80},{80,64},{96,112},{112,96},{1... | collective-permute-start | bytes 737288 | tf_op jit(solution)/shard_map/ppermute | solution.py:514
  15.7 35.6 %collective-permute-start.1 = (bf16[960,128]{1,0:T(8,128)(2,1)S(1)}, bf16[960,128]{1,0:T(8,128)(2,1)S(1)}, u32[]{:S(2)}, u32[]{:S(2)}) collective-permute-start(bf16[960,128]{1,0:T(8,128)(2,1)S(1)} %get-tuple-element.28), channel_id=1, source_target_pairs={{0,32},{16,48},{32,0},{48,16},{64,96},{80,112},{96,64},{112,80},{1... | collective-permute-start | bytes 737288 | tf_op jit(solution)/shard_map/ppermute | solution.py:514
  20.2 31.2 %collective-permute-start.2 = (bf16[960,128]{1,0:T(8,128)(2,1)S(1)}, bf16[960,128]{1,0:T(8,128)(2,1)S(1)}, u32[]{:S(2)}, u32[]{:S(2)}) collective-permute-start(bf16[960,128]{1,0:T(8,128)(2,1)S(1)} %get-tuple-element.29), channel_id=1, source_target_pairs={{0,48},{16,32},{32,16},{48,0},{64,112},{80,96},{96,80},{112,64},{1... | collective-permute-start | bytes 737288 | tf_op jit(solution)/shard_map/ppermute | solution.py:514
  20.2 1.3 %collective-permute-start.3 = (bf16[4,128,128]{2,1,0:T(8,128)(2,1)S(1)}, bf16[4,128,128]{2,1,0:T(8,128)(2,1)S(1)}, u32[]{:S(2)}, u32[]{:S(2)}) collective-permute-start(bf16[4,128,128]{2,1,0:T(8,128)(2,1)S(1)} %get-tuple-element.30.ring_ref), channel_id=1, source_target_pairs={{0,1},{1,0},{2,3},{3,2},{4,5},{5,4},{6,7},{7,6},{8,9},{9,8},{10,11... | collective-permute-start | bytes 393224 | tf_op jit(solution)/shard_map/ppermute | solution.py:522
  40.7 27.9 %copy-start = (bf16[960,128]{1,0:T(8,128)(2,1)}, bf16[960,128]{1,0:T(8,128)(2,1)S(1)}, u32[]{:S(2)}) copy-start(bf16[960,128]{1,0:T(8,128)(2,1)S(1)} %collective-permute-done.z1) | copy-start | bytes 737284
  51.4 17.2 %copy-start.1 = (bf16[960,128]{1,0:T(8,128)(2,1)}, bf16[960,128]{1,0:T(8,128)(2,1)S(1)}, u32[]{:S(2)}) copy-start(bf16[960,128]{1,0:T(8,128)(2,1)S(1)} %collective-permute-done.1.z2) | copy-start | bytes 737284
  51.4 17.2 %copy-start.2 = (bf16[960,128]{1,0:T(8,128)(2,1)}, bf16[960,128]{1,0:T(8,128)(2,1)S(1)}, u32[]{:S(2)}) copy-start(bf16[960,128]{1,0:T(8,128)(2,1)S(1)} %collective-permute-done.2.z3) | copy-start | bytes 737284
  52.6 4.3 %collective-permute-start.4 = (bf16[16,128,128]{2,1,0:T(8,128)(2,1)S(1)}, bf16[16,128,128]{2,1,0:T(8,128)(2,1)S(1)}, u32[]{:S(2)}, u32[]{:S(2)}) collective-permute-start(bf16[16,128,128]{2,1,0:T(8,128)(2,1)S(1)} %get-tuple-element.31), channel_id=1, source_target_pairs={{0,1},{1,0},{2,3},{3,2},{4,5},{5,4},{6,7},{7,6},{8,9},{9,8},{10,11... | collective-permute-start | bytes 1572872 | tf_op jit(solution)/shard_map/ppermute | solution.py:522
  52.7 15.9 %collective-permute-start.5 = (bf16[2,128,128]{2,1,0:T(8,128)(2,1)S(1)}, bf16[2,128,128]{2,1,0:T(8,128)(2,1)S(1)}, u32[]{:S(2)}, u32[]{:S(2)}) collective-permute-start(bf16[2,128,128]{2,1,0:T(8,128)(2,1)S(1)} %get-tuple-element.34), channel_id=1, source_target_pairs={{0,2},{2,0},{4,6},{6,4},{1,3},{3,1},{5,7},{7,5},{8,10},{10,8},{12,... | collective-permute-start | bytes 196616 | tf_op jit(solution)/shard_map/ppermute | solution.py:518
  53.1 15.5 %collective-permute-start.6 = (bf16[2,128,128]{2,1,0:T(8,128)(2,1)S(1)}, bf16[2,128,128]{2,1,0:T(8,128)(2,1)S(1)}, u32[]{:S(2)}, u32[]{:S(2)}) collective-permute-start(bf16[2,128,128]{2,1,0:T(8,128)(2,1)S(1)} %get-tuple-element.35), channel_id=1, source_target_pairs={{0,4},{2,6},{4,0},{6,2},{1,5},{3,7},{5,1},{7,3},{8,12},{10,14},{12... | collective-permute-start | bytes 196616 | tf_op jit(solution)/shard_map/ppermute | solution.py:518
  55.7 12.9 %collective-permute-start.7 = (bf16[2,128,128]{2,1,0:T(8,128)(2,1)S(1)}, bf16[2,128,128]{2,1,0:T(8,128)(2,1)S(1)}, u32[]{:S(2)}, u32[]{:S(2)}) collective-permute-start(bf16[2,128,128]{2,1,0:T(8,128)(2,1)S(1)} %get-tuple-element.36), channel_id=1, source_target_pairs={{0,6},{2,4},{4,2},{6,0},{1,7},{3,5},{5,3},{7,1},{8,14},{10,12},{12... | collective-permute-start | bytes 196616 | tf_op jit(solution)/shard_map/ppermute | solution.py:518
  56.3 16.2 %collective-permute-start.8 = (bf16[4,640,128]{2,1,0:T(8,128)(2,1)S(1)}, bf16[4,640,128]{2,1,0:T(8,128)(2,1)S(1)}, u32[]{:S(2)}, u32[]{:S(2)}) collective-permute-start(bf16[4,640,128]{2,1,0:T(8,128)(2,1)S(1)} %get-tuple-element.32.order_ref), channel_id=1, source_target_pairs={{0,64},{16,80},{32,96},{48,112},{64,0},{80,16},{96,32},{112,48},{1... | collective-permute-start | bytes 1966088 | tf_op jit(solution)/shard_map/ppermute | solution.py:514
  68.6 16.1 %copy-start.5 = (s32[8]{0:T(128)S(1)}, s32[8]{0:T(128)}, u32[]{:S(2)}) copy-start(s32[8]{0:T(128)} %times_ref.1) | copy-start | bytes 100
  72.5 12.1 %copy-start.3 = (bf16[4,640,128]{2,1,0:T(8,128)(2,1)}, bf16[4,640,128]{2,1,0:T(8,128)(2,1)S(1)}, u32[]{:S(2)}) copy-start(bf16[4,640,128]{2,1,0:T(8,128)(2,1)S(1)} %collective-permute-done.8.order_ref.x_any) | copy-start | bytes 1966084
  76.5 26.8 %all-to-all-start.1 = ((bf16[16,144,128]{2,1,0:T(8,128)(2,1)}), bf16[16,144,128]{2,1,0:T(8,128)(2,1)S(1)}, u32[]{:S(2)}, u32[]{:S(2)}) async-start(bf16[16,144,128]{2,1,0:T(8,128)(2,1)} %ring_attention.1), calls=%async_computation.1 | async-start | bytes 1179648 | tf_op jit(solution)/shard_map/all_to_all | solution.py:537
  91.4 6.7 %collective-permute-start.9 = (bf16[336,128]{1,0:T(8,128)(2,1)S(1)}, bf16[336,128]{1,0:T(8,128)(2,1)S(1)}, u32[]{:S(2)}, u32[]{:S(2)}) collective-permute-start(bf16[336,128]{1,0:T(8,128)(2,1)S(1)} %get-tuple-element.38), channel_id=1, source_target_pairs={{0,16},{16,0},{32,48},{48,32},{64,80},{80,64},{96,112},{112,96},{1... | collective-permute-start | bytes 258056 | tf_op jit(solution)/shard_map/ppermute | solution.py:514
  93.8 8.8 %collective-permute-start.10 = (bf16[336,128]{1,0:T(8,128)(2,1)S(1)}, bf16[336,128]{1,0:T(8,128)(2,1)S(1)}, u32[]{:S(2)}, u32[]{:S(2)}) collective-permute-start(bf16[336,128]{1,0:T(8,128)(2,1)S(1)} %get-tuple-element.39), channel_id=1, source_target_pairs={{0,32},{16,48},{32,0},{48,16},{64,96},{80,112},{96,64},{112,80},{1... | collective-permute-start | bytes 258056 | tf_op jit(solution)/shard_map/ppermute | solution.py:514
  95.3 8.0 %collective-permute-start.11 = (bf16[336,128]{1,0:T(8,128)(2,1)S(1)}, bf16[336,128]{1,0:T(8,128)(2,1)S(1)}, u32[]{:S(2)}, u32[]{:S(2)}) collective-permute-start(bf16[336,128]{1,0:T(8,128)(2,1)S(1)} %get-tuple-element.40), channel_id=1, source_target_pairs={{0,48},{16,32},{32,16},{48,0},{64,112},{80,96},{96,80},{112,64},{1... | collective-permute-start | bytes 258056 | tf_op jit(solution)/shard_map/ppermute | solution.py:514

commit v3 on v2

--- a/solution.py
+++ b/solution.py
@@ -62,7 +62,7 @@
     return jnp.concatenate([left, right], axis=1)
 
 
-def pack_time_kernel(q_hbm, k_hbm, v_hbm, z0, z1, z2, z3, ring_ref, q_ref, k_ref, v_ref, sems, parts):
+def pack_time_kernel(q_hbm, k_hbm, v_hbm, z0, z1, z2, z3, q_ref, k_ref, v_ref, sems, parts):
     place = lax.axis_index("f") % 4
     copy_all([(k_hbm, k_ref), (v_hbm, v_ref), (q_hbm, q_ref)], sems)
     for j in range(4):
@@ -78,8 +78,6 @@
     keep.start()
     for k, out in enumerate((z1, z2, z3)):
         out[...] = parts[turned(place, k + 1)]
-    for y in range(RING):
-        ring_ref[y] = pair(k_ref, MAIN + y, v_ref, MAIN + y)
     keep.wait()
 
 
@@ -89,61 +87,101 @@
 
 def pack_time(q, k, v):
     block = jax.ShapeDtypeStruct((Z_ROWS, CELLS), BF16)
-    whole = jax.ShapeDtypeStruct((CELLS, HEADS * HEAD), BF16)
+    whole = pltpu.VMEM((CELLS, HEADS * HEAD), BF16)
     return pl.pallas_call(
         pack_time_kernel,
-        out_shape=[pltpu.HBM((Z_ROWS, CELLS), BF16)] + [block] * 3 + [jax.ShapeDtypeStruct((RING, CELLS, CELLS), BF16)] + [whole] * 3,
+        out_shape=[block] * 4,
         in_specs=[ANY] * 3,
-        out_specs=[ANY] + [VMEM] * 7,
-        scratch_shapes=[pltpu.SemaphoreType.DMA((4,)), pltpu.VMEM((4, Z_ROWS, CELLS), BF16)],
+        out_specs=[ANY] + [VMEM] * 3,
+        scratch_shapes=[whole] * 3 + [pltpu.SemaphoreType.DMA((4,)), pltpu.VMEM((4, Z_ROWS, CELLS), BF16)],
         compiler_params=params(16),
         name="pack_time",
     )(in_hbm(q), in_hbm(k), in_hbm(v))
 
 
-def pack_view_kernel(q_ref, k_ref, v_ref, view_ref):
+def pack_view_kernel(q_hbm, k_hbm, v_hbm, view_ref, ring_ref, q_ref, k_ref, v_ref, sems):
+    load = pltpu.make_async_copy(q_hbm, q_ref, sems.at[2])
+    load.start()
+    copy_all([(k_hbm, k_ref), (v_hbm, v_ref)], sems)
     for t in range(MAIN):
         view_ref[t, 0:CELLS] = pair(k_ref, t, v_ref, t)
+    for y in range(RING):
+        ring_ref[y] = pair(k_ref, MAIN + y, v_ref, MAIN + y)
+    load.wait()
+    for t in range(MAIN):
         view_ref[t, CELLS : 2 * CELLS] = pair(q_ref, t, q_ref, MAIN + t % RING)
 
 
 def pack_view(q, k, v):
+    whole = pltpu.VMEM((CELLS, HEADS * HEAD), BF16)
     return pl.pallas_call(
         pack_view_kernel,
-        out_shape=jax.ShapeDtypeStruct((MAIN, 2 * CELLS, CELLS), BF16),
-        in_specs=[VMEM] * 3,
-        out_specs=VMEM,
+        out_shape=[
+            jax.ShapeDtypeStruct((MAIN, 2 * CELLS, CELLS), BF16),
+            jax.ShapeDtypeStruct((RING, CELLS, CELLS), BF16),
+        ],
+        in_specs=[ANY] * 3,
+        out_specs=[VMEM] * 2,
+        scratch_shapes=[whole] * 3 + [pltpu.SemaphoreType.DMA((3,))],
         compiler_params=params(16),
-        cost_estimate=pl.CostEstimate(flops=4000000000, bytes_accessed=2000000, transcendentals=0),
         name="pack_view",
-    )(q, k, v)
-
-
-def stack_kernel(z0, z1, z2, z3, own_ref, ring_ref, sibling_ref, out_ref, kv_ref, r0, r1, r2, r3, sems):
+    )(in_hbm(q), in_hbm(k), in_hbm(v))
+
+
+def ring_pack_kernel(ring_ref, sibling_ref, r0, r1, r2, r3):
     y = lax.axis_index("y")
-    moves = [(piece.at[pl.ds(0, X_ROWS)], out_ref.at[k]) for k, piece in enumerate((z0, z1, z2, z3))]
-    moves.append((own_ref.at[:, pl.ds(0, CELLS)], kv_ref))
     for k, out in enumerate((r0, r1, r2, r3)):
-        moves.append((ring_ref.at[turned(y, k)], out.at[0]))
-        moves.append((sibling_ref.at[turned(y, k)], out.at[1]))
+        out[0] = ring_ref[turned(y, k)]
+        out[1] = sibling_ref[turned(y, k)]
+
+
+def ring_pack(ring, other):
+    return pl.pallas_call(
+        ring_pack_kernel,
+        out_shape=[jax.ShapeDtypeStruct((2, CELLS, CELLS), BF16)] * 4,
+        in_specs=[VMEM] * 2,
+        out_specs=[VMEM] * 4,
+        compiler_params=params(4),
+        name="ring_pack",
+    )(ring, other)
+
+
+def stack_kernel(own_ref, z0, z1, z3, *refs):
+    kv_ref, out_ref, sems = refs[-3:]
+    moves = [(own_ref.at[:, pl.ds(0, CELLS)], kv_ref)]
+    moves += [(piece.at[pl.ds(0, X_ROWS)], out_ref.at[k]) for k, piece in enumerate((z0, z1, z3))]
     copy_all(moves, sems)
 
 
-def stack(z, own, ring, other):
-    block = jax.ShapeDtypeStruct((2, CELLS, CELLS), BF16)
+def stack(own, z0, z1, z3, order):
     return pl.pallas_call(
         stack_kernel,
         out_shape=[
-            jax.ShapeDtypeStruct((4, X_ROWS, CELLS), BF16),
             jax.ShapeDtypeStruct((MAIN, CELLS, CELLS), BF16),
-        ]
-        + [block] * 4,
-        in_specs=[ANY] * 7,
-        out_specs=[ANY] * 6,
-        scratch_shapes=[pltpu.SemaphoreType.DMA((13,))],
+            jax.ShapeDtypeStruct((3, X_ROWS, CELLS), BF16),
+        ],
+        in_specs=[ANY] * (4 + len(order)),
+        out_specs=[ANY] * 2,
+        scratch_shapes=[pltpu.SemaphoreType.DMA((4,))],
         compiler_params=params(4),
         name="stack",
-    )(*z, own, ring, other)
+    )(own, z0, z1, z3, *order)
+
+
+def strip_kernel(z_ref, order_ref, out_ref):
+    del order_ref
+    out_ref[...] = z_ref[0:X_ROWS]
+
+
+def strip(z, order):
+    return pl.pallas_call(
+        strip_kernel,
+        out_shape=jax.ShapeDtypeStruct((X_ROWS, CELLS), BF16),
+        in_specs=[VMEM, ANY],
+        out_specs=VMEM,
+        compiler_params=params(4),
+        name="strip",
+    )(z, order)
 
 
 def score_tile(q, key_ref, score_ref, count):
@@ -207,15 +245,9 @@
     value_s[rows] = kv * (1 - low) + low
 
 
-def view_kernel(own_ref, other_ref, mask_ref, order_ref, out_ref, key_s, value_s, s_a, s_b):
-    del order_ref
-    core = lax.axis_index("c")
+def attend_views(own_ref, ring_ref, key_s, value_s, s_a, s_b, first, write):
     lane = lanes((CELLS, CELLS))
-    block = rows_of((32, 32))
-    bias = seen_bias(mask_ref, jnp.where(block < 16, 2 * block + core, 2 * (block - 16) + 1 - core), 32)
-    for b in range(32):
-        kv = own_ref[b, 0:CELLS] if b < 16 else other_ref[b - 16]
-        fill(key_s, value_s, b, kv, bias[b : b + 1])
+    wide = lanes((TILE, CELLS))
 
     def query(j):
         qq = own_ref[j, CELLS : 2 * CELLS].astype(F32)
@@ -223,8 +255,6 @@
 
     def tile(i):
         return jnp.concatenate([query(2 * i), query(2 * i + 1)], axis=0)
-
-    wide = lanes((TILE, CELLS))
 
     def finish(i, score_ref, row_max):
         main = weigh_tile(score_ref, row_max, value_s, 4096)
@@ -232,41 +262,87 @@
         table = level_rows([row_max * RATE + jnp.log2(jnp.where(wide < HEAD, main, 1.0))], wide)
         for n in range(2):
             rows = slice(n * CELLS, (n + 1) * CELLS)
-            out_ref[2 * i + n, 0:CELLS] = heads[rows].astype(BF16)
-            out_ref[2 * i + n, CELLS:O_ROWS] = table[rows].T[0:16].astype(BF16)
-
-    first = score_tile(tile(0), key_s, s_a, 4096)
+            j = 2 * i + n
+            head_rows = ring_ref[j, 0:CELLS] + heads[rows].astype(BF16)
+            write(j, head_rows, ring_ref[j, CELLS:O_ROWS] + table[rows].T[0:16].astype(BF16))
+
+    start = score_tile(tile(first), key_s, s_a, 4096)
 
     def body(step, m_a):
-        m_b = score_tile(tile(2 * step + 1), key_s, s_b, 4096)
-        finish(2 * step, s_a, m_a)
-        m_next = score_tile(tile(jnp.minimum(2 * step + 2, 7)), key_s, s_a, 4096)
-        finish(2 * step + 1, s_b, m_b)
+        i = first + 2 * step
+        m_b = score_tile(tile(i + 1), key_s, s_b, 4096)
+        finish(i, s_a, m_a)
+        m_next = score_tile(tile(jnp.minimum(i + 2, first + 3)), key_s, s_a, 4096)
+        finish(i + 1, s_b, m_b)
         return m_next
 
-    lax.fori_loop(0, 4, body, first)
-
-
-def view_attention(own, other, view_mask, order):
+    lax.fori_loop(0, 2, body, start)
+
+
+def view_kernel(own_ref, other_ref, ring_ref, mask_ref, out_ref, key_s, value_s, s_a, s_b):
+    core = lax.axis_index("c")
+    block = rows_of((32, 32))
+    bias = seen_bias(mask_ref, jnp.where(block < 16, 2 * block + core, 2 * (block - 16) + 1 - core), 32)
+    for b in range(32):
+        kv = own_ref[b, 0:CELLS] if b < 16 else other_ref[b - 16]
+        fill(key_s, value_s, b, kv, bias[b : b + 1])
+
+    def write(j, head_rows, level_part):
+        out_ref[j, 0:CELLS] = head_rows
+        out_ref[j, CELLS:O_ROWS] = level_part
+
+    attend_views(own_ref, ring_ref, key_s, value_s, s_a, s_b, 0, write)
+
+
+def view_rest_kernel(own_ref, ring_ref, half_ref, key_s, value_s, out_hbm, out_ref, sems, s_a, s_b):
+    early = pltpu.make_async_copy(half_ref, out_hbm.at[pl.ds(0, 8)], sems.at[8])
+    early.start()
+
+    def away(j):
+        return pltpu.make_async_copy(out_ref.at[j], out_hbm.at[j], sems.at[j - 8])
+
+    def write(j, head_rows, level_part):
+        out_ref[j, 0:CELLS] = head_rows
+        out_ref[j, CELLS:O_ROWS] = level_part
+        away(j).start()
+
+    attend_views(own_ref, ring_ref, key_s, value_s, s_a, s_b, 4, write)
+    for j in range(8, 16):
+        away(j).wait()
+    early.wait()
+
+
+SCORES = [pltpu.VMEM((TILE, 4096), F32)] * 2
+
+
+def view_attention(own, other, ring_out, view_mask):
+    filled = jax.ShapeDtypeStruct((4096, CELLS), BF16)
     return pl.pallas_call(
         view_kernel,
-        out_shape=jax.ShapeDtypeStruct((MAIN, O_ROWS, CELLS), BF16),
-        in_specs=[VMEM] * 3 + [ANY],
-        out_specs=VMEM,
-        scratch_shapes=[
-            pltpu.VMEM((4096, CELLS), BF16),
-            pltpu.VMEM((4096, CELLS), BF16),
-            pltpu.VMEM((TILE, 4096), F32),
-            pltpu.VMEM((TILE, 4096), F32),
-        ],
-        compiler_params=params(20),
-        cost_estimate=pl.CostEstimate(flops=8000000000, bytes_accessed=4000000, transcendentals=9000000),
+        out_shape=[jax.ShapeDtypeStruct((8, O_ROWS, CELLS), BF16), filled, filled],
+        in_specs=[VMEM] * 4,
+        out_specs=[VMEM] * 3,
+        scratch_shapes=SCORES,
+        compiler_params=params(16),
+        cost_estimate=pl.CostEstimate(flops=1000000, bytes_accessed=100000, transcendentals=0),
         name="view_attention",
-    )(own, other, view_mask, order)
-
-
-def ring_kernel(main_ref, own_ref, r0, r1, r2, r3, mask_ref, order_ref, out_hbm, out_ref, sems, key_s, value_s, s_ref):
-    del order_ref
+    )(own, other, ring_out, view_mask)
+
+
+def view_attention_rest(own, ring_out, half, key_rows, value_rows):
+    return pl.pallas_call(
+        view_rest_kernel,
+        out_shape=pltpu.HBM((MAIN, O_ROWS, CELLS), BF16),
+        in_specs=[VMEM] * 5,
+        out_specs=ANY,
+        scratch_shapes=[pltpu.VMEM((MAIN, O_ROWS, CELLS), BF16), pltpu.SemaphoreType.DMA((9,))] + SCORES,
+        compiler_params=params(16),
+        cost_estimate=pl.CostEstimate(flops=1000000, bytes_accessed=100000, transcendentals=0),
+        name="view_attention_rest",
+    )(own, ring_out, half, key_rows, value_rows)
+
+
+def ring_kernel(own_ref, r0, r1, r2, r3, mask_ref, out_ref, key_s, value_s, s_ref):
     core = lax.axis_index("c")
     y = lax.axis_index("y")
     ring = lax.axis_index("g") * 2 + lax.axis_index("zl")
@@ -289,7 +365,6 @@
         return score_tile(tile, key_s, s_ref.at[i % 2], 1024)
 
     row_max = begin(0)
-    copies = []
     for i in range(8):
         following = begin(i + 1) if i < 7 else None
         part = weigh_tile(s_ref.at[i % 2], row_max, value_s, 1024)
@@ -299,38 +374,33 @@
         for n in range(2):
             rows = slice(n * CELLS, (n + 1) * CELLS)
             j = 2 * i + n
-            out_ref[j, 0:CELLS] = main_ref[j, 0:CELLS] + heads[rows]
-            out_ref[j, CELLS:O_ROWS] = main_ref[j, CELLS:O_ROWS] + table[rows].T[0:16].astype(BF16)
-        copies.append(pltpu.make_async_copy(out_ref.at[pl.ds(2 * i, 2)], out_hbm.at[pl.ds(2 * i, 2)], sems.at[i]))
-        copies[-1].start()
+            out_ref[j, 0:CELLS] = heads[rows]
+            out_ref[j, CELLS:O_ROWS] = table[rows].T[0:16].astype(BF16)
         row_max = following
-    for copy in copies:
-        copy.wait()
-
-
-def ring_attention(main, own, pieces, view_mask, order):
+
+
+def ring_attention(own, pieces, view_mask):
     return pl.pallas_call(
         ring_kernel,
-        out_shape=pltpu.HBM((MAIN, O_ROWS, CELLS), BF16),
-        in_specs=[VMEM] * 7 + [ANY],
-        out_specs=ANY,
+        out_shape=jax.ShapeDtypeStruct((MAIN, O_ROWS, CELLS), BF16),
+        in_specs=[VMEM] * 6,
+        out_specs=VMEM,
         scratch_shapes=[
-            pltpu.VMEM((MAIN, O_ROWS, CELLS), BF16),
-            pltpu.SemaphoreType.DMA((8,)),
             pltpu.VMEM((1024, CELLS), BF16),
             pltpu.VMEM((1024, CELLS), BF16),
             pltpu.VMEM((2, TILE, 1024), F32),
         ],
         compiler_params=params(12),
-        cost_estimate=pl.CostEstimate(flops=500000000, bytes_accessed=2000000, transcendentals=2000000),
+        cost_estimate=pl.CostEstimate(flops=1000000, bytes_accessed=100000, transcendentals=0),
         name="ring_attention",
-    )(main, own, *pieces, view_mask, order)
-
-
-def time_kernel(z0, z1, z2, z3, x_any, times_ref, o_hbm, o1, o2, o3, o0, z_s, x_ref, sems, key_s, value_s, q_s, s_ref):
+    )(own, *pieces, view_mask)
+
+
+def time_kernel(z0, z1, z2, z3, x_ref, x2_ref, times_ref, o0, o1, o2, o3, key_s, value_s, q_s, s_ref):
     frame = lax.axis_index("f")
     lane = lanes((CELLS, CELLS))
-    own = [z_s.at[k] for k in range(4)]
+    own = (z0, z1, z2, z3)
+    far = (x_ref.at[0], x_ref.at[1], x2_ref, x_ref.at[2])
     outs = (o0, o1, o2, o3)
 
     l8, r8 = lanes((8, 128)), rows_of((8, 128))
@@ -345,12 +415,10 @@
     low = row(jnp.where(lanes((1, CELLS)) < HEAD, 1.0, 0.0))
     high = row(jnp.where(lanes((1, CELLS)) < HEAD, 0.0, 1.0))
 
-    copy_all(list(zip((z0, z1, z2, z3, x_any), own + [x_ref])), sems)
-
     for head in range(5):
         for k in range(8):
             at = slice(head * CELLS, (head + 1) * CELLS)
-            kv = own[k][at] if k < 4 else x_ref[k - 4, at]
+            kv = (own + far)[k][at]
             rows = slice(k * CELLS, (k + 1) * CELLS)
             key_s[head, rows] = kv * low + bias[k : k + 1]
             value_s[head, rows] = kv * high + low
@@ -395,24 +463,16 @@
             last = heads[4][rows]
             out[256:320] = (last[0:64] + swap_halves(last[64:128])).astype(BF16)
             out[320:336] = table[rows].T[0:16].astype(BF16)
-        if i == 0:
-            keep = pltpu.make_async_copy(o0, o_hbm, sems.at[5])
-            keep.start()
         heads, levels = [], []
-    keep.wait()
 
 
 def time_attention(own, crossed, frame_times):
     return pl.pallas_call(
         time_kernel,
-        out_shape=[pltpu.HBM((T_ROWS, CELLS), BF16)] + [jax.ShapeDtypeStruct((T_ROWS, CELLS), BF16)] * 3,
-        in_specs=[ANY] * 5 + [SMEM],
-        out_specs=[ANY] + [VMEM] * 3,
+        out_shape=[jax.ShapeDtypeStruct((T_ROWS, CELLS), BF16)] * 4,
+        in_specs=[VMEM] * 6 + [SMEM],
+        out_specs=[VMEM] * 4,
         scratch_shapes=[
-            pltpu.VMEM((T_ROWS, CELLS), BF16),
-            pltpu.VMEM((4, Z_ROWS, CELLS), BF16),
-            pltpu.VMEM((4, X_ROWS, CELLS), BF16),
-            pltpu.SemaphoreType.DMA((6,)),
             pltpu.VMEM((5, 1024, CELLS), BF16),
             pltpu.VMEM((5, 1024, CELLS), BF16),
             pltpu.VMEM((5, 512, CELLS), BF16),
@@ -421,19 +481,31 @@
         compiler_params=params(16),
         cost_estimate=pl.CostEstimate(flops=700000000, bytes_accessed=2000000, transcendentals=2700000),
         name="time_attention",
-    )(*own, crossed, frame_times)
-
-
-def join_kernel(view_any, t0, t1, t2, t3, weight_any, out_ref, view_ref, times, weight_ref, heads_s, sems):
+    )(*own, *crossed, frame_times)
+
+
+def pass_kernel(*refs):
+    del refs
+
+
+def pass_after(array, others):
+    return pl.pallas_call(
+        pass_kernel,
+        out_shape=pltpu.HBM(array.shape, array.dtype),
+        in_specs=[ANY] * (1 + len(others)),
+        out_specs=ANY,
+        input_output_aliases={0: 0},
+        compiler_params=params(4),
+        name="pass_after",
+    )(in_hbm(array), *others)
+
+
+def join_kernel(view_ref, t0, t1, t2, t3, weight_any, out_ref, times, heads_s, weight_ref, sems):
+    load = pltpu.make_async_copy(weight_any, weight_ref, sems.at[0])
+    load.start()
     place = lax.axis_index("f") % 4
-    load = pltpu.make_async_copy(weight_any, weight_ref, sems.at[5])
-    moves = [(piece, times.at[turned(place, k)]) for k, piece in enumerate((t0, t1, t2, t3))]
-    copies = [pltpu.make_async_copy(*move, sems.at[i]) for i, move in enumerate([*moves, (view_any, view_ref)])]
-    for copy in copies:
-        copy.start()
-    load.start()
-    for copy in copies:
-        copy.wait()
+    for k, piece in enumerate((t0, t1, t2, t3)):
+        times[turned(place, k)] = piece[...]
 
     view_rows = jnp.concatenate([view_ref[t, CELLS:O_ROWS] for t in range(MAIN)], axis=0)
     time_rows = jnp.concatenate([times[j, 320:336] for j in range(4)], axis=0)
@@ -496,14 +568,13 @@
     return pl.pallas_call(
         join_kernel,
         out_shape=jax.ShapeDtypeStruct((CELLS, HEADS * HEAD), BF16),
-        in_specs=[ANY] * 6,
+        in_specs=[VMEM] * 5 + [ANY],
         out_specs=VMEM,
         scratch_shapes=[
-            pltpu.VMEM((MAIN, O_ROWS, CELLS), BF16),
             pltpu.VMEM((4, T_ROWS, CELLS), BF16),
+            pltpu.VMEM((CELLS, HEADS * HEAD), BF16),
             pltpu.VMEM((HEADS * HEAD, HEADS * HEAD), BF16),
-            pltpu.VMEM((CELLS, HEADS * HEAD), BF16),
-            pltpu.SemaphoreType.DMA((6,)),
+            pltpu.SemaphoreType.DMA((1,)),
         ],
         compiler_params=params(16),
         name="join",
@@ -525,18 +596,21 @@
 def local(queries, keys, values, view_mask, frame_times, out_weight):
     model = queries.shape[3]
     q, k, v = (a.reshape(CELLS, model) for a in (queries, keys, values))
-    *z, to_ring, q, k, v = pack_time(q, k, v)
-    z = [in_hbm(z[0])] + [across(z[i], i) for i in (1, 2, 3)]
-    beside = sibling(to_ring)
-    own = lax.all_to_all(pack_view(q, k, v), ("g", "zl", "y"), 0, 0)
-    stacked, kv, *ring = stack(z, own, to_ring, beside)
+    to_view, to_ring = pack_view(q, k, v)
+    own = lax.all_to_all(to_view, ("g", "zl", "y"), 0, 0)
+    ring = ring_pack(to_ring, sibling(to_ring))
     ring = [ring[0]] + [around(ring[i], i) for i in (1, 2, 3)]
-    crossed = across(stacked, 4)
-    main_out = view_attention(own, sibling(kv), view_mask, stacked)
-    view_out = ring_attention(main_out, own, ring, view_mask, crossed)
+    z0, z1, z2, z3 = pack_time(q, k, v)
+    z1, z2, z3 = across(z1, 1), across(z2, 2), across(z3, 3)
+    kv, some = stack(own, z0, z1, z3, ring[1:])
+    ring_out = ring_attention(own, ring, view_mask)
+    half, *filled = view_attention(own, sibling(kv), ring_out, view_mask)
+    crossed = (across(some, 4), across(strip(z2, half), 4))
+    view_out = view_attention_rest(own, ring_out, half, *filled)
+    view_out = pass_after(view_out, crossed)
     view_back = lax.all_to_all(view_out, ("g", "zl", "y"), 0, 0)
-    pieces = time_attention([in_hbm(a) for a in z], in_hbm(crossed), frame_times)
-    pieces = [in_hbm(pieces[0])] + [across(pieces[i], i) for i in (1, 2, 3)]
+    pieces = time_attention((z0, z1, z2, z3), crossed, frame_times)
+    pieces = [pieces[0]] + [across(pieces[i], i) for i in (1, 2, 3)]
     result = join(view_back, pieces, out_weight)
     return result.reshape(1, 1, CELLS, model)
 

time: 110 us -> 96.5 us (0.88)
  waiting for transfers between devices: 40.4 us -> 25.6 us
  starting transfers between devices: 35.6 us -> 37.7 us
    ppermute x7 -> x8, waiting for transfers between devices: 39 us -> 18.8 us  [across(): return lax.ppermute(array, 'f', [(i, i ^ k) for i in range(FRAMES)])]
    ppermute x3, waiting for transfers between devices: 0.01 us -> 5.51 us  [around(): return lax.ppermute(array, 'y', [(i, i ^ k) for i in range(RING)])]
    ppermute x7 -> x8, starting transfers between devices: 14.9 us -> 18.2 us  [across(): return lax.ppermute(array, 'f', [(i, i ^ k) for i in range(FRAMES)])]
    pallas_call x6 -> x10, Pallas kernels: 27.1 us -> 26.6 us  [the longest x1 6.76 us: view_attention_rest(): pl.pallas_call(view_rest_kernel, out_shape=pltpu.HBM((MAIN, O_ROWS, CELLS...]
  transfers between devices with their start and end apart: 14 -> 15, of which waited for: 7 -> 10; matrix products, arithmetic and copies ran while one was open for 0% -> 0% of each run, Pallas kernels for 17% -> 24%
where the time goes in v3:
time: 96.5 us; the launch traced here: 95.6 us
  starting transfers between devices  37.7 us (39%)
  Pallas kernels  32.1 us (33%)
  waiting for transfers between devices  25.6 us (27%)
    ppermute x8, waiting for transfers between devices, across(): return lax.ppermute(array, 'f', [(i, i ^ k) for i in range(FRAMES)])  18.8 us
    ppermute x8, starting transfers between devices, across(): return lax.ppermute(array, 'f', [(i, i ^ k) for i in range(FRAMES)])  18.2 us
    all_to_all x1, starting transfers between devices, local(): own = lax.all_to_all(to_view, ('g', 'zl', 'y'), 0, 0)  8.76 us
    all_to_all x1, starting transfers between devices, local(): view_back = lax.all_to_all(view_out, ('g', 'zl', 'y'), 0, 0)  7.07 us
    pallas_call x1, Pallas kernels, view_attention_rest(): pl.pallas_call(view_rest_kernel, out_shape=pltpu.HBM((MAIN, O_ROWS, CELLS...  6.76 us
    pallas_call x1, Pallas kernels, view_attention(): pl.pallas_call(view_kernel, out_shape=[jax.ShapeDtypeStruct((8, O_ROWS, C...  6.41 us
    ppermute x3, waiting for transfers between devices, around(): return lax.ppermute(array, 'y', [(i, i ^ k) for i in range(RING)])  5.51 us
    pallas_call x1, Pallas kernels, join(): pl.pallas_call(join_kernel, out_shape=jax.ShapeDtypeStruct((CELLS, HEADS...  5.49 us
  transfers between devices with their start and end apart: 15, of which 10 were waited for; matrix products, arithmetic and copies ran while one was open for 0% of the time, Pallas kernels for 24%

profile of v3, /device:TPU:8, one launch (start us, length us, event | category | flops | bytes accessed | tf_op | source)
XLA Modules:
  0.0 95.6 jit_solution(14003299871120002636)
XLA Ops:
  0.0 0.0 copy-start
  0.0 2.7 %pack_view.1 = (bf16[16,256,128]{2,1,0:T(8,128)(2,1)}, bf16[4,128,128]{2,1,0:T(8,128)(2,1)S(1)}) custom-call(bf16[128,1280]{1,0:T(8,128)(2,1)} %bitcast.4, bf16[128,1280]{1,0:T(8,128)(2,1)} %bitcast.6, bf16[128,1280]{1,0:T(8,128)(2,1)} %bitcast.8), custom_call_target="tpu_custom_call" | custom-call | tf_op jit(solution)/shard_map/pack_view/pallas_call | solution.py:117
  2.7 8.8 %all-to-all-start = ((bf16[16,256,128]{2,1,0:T(8,128)(2,1)}), bf16[16,256,128]{2,1,0:T(8,128)(2,1)S(1)}, u32[]{:S(2)}, u32[]{:S(2)}) async-start(bf16[16,256,128]{2,1,0:T(8,128)(2,1)} %get-tuple-element.24), calls=%async_computation | async-start | bytes 2097152 | tf_op jit(solution)/shard_map/all_to_all | solution.py:600
  11.4 1.9 %pack_time.1 = (bf16[960,128]{1,0:T(8,128)(2,1)S(1)}, bf16[960,128]{1,0:T(8,128)(2,1)S(1)}, bf16[960,128]{1,0:T(8,128)(2,1)S(1)}, bf16[960,128]{1,0:T(8,128)(2,1)S(1)}) custom-call(bf16[128,1280]{1,0:T(8,128)(2,1)} %bitcast.5, bf16[128,1280]{1,0:T(8,128)(2,1)} %bitcast.7, bf16[128,1280]{1,0:T(8,128)(2,1)} %bitcast.9), custom_call_target="tpu_custom_call" | custom-call | tf_op jit(solution)/shard_map/pack_time/pallas_call | solution.py:91
  13.3 3.4 %collective-permute-start.4 = (bf16[960,128]{1,0:T(8,128)(2,1)S(1)}, bf16[960,128]{1,0:T(8,128)(2,1)S(1)}, u32[]{:S(2)}, u32[]{:S(2)}) collective-permute-start(bf16[960,128]{1,0:T(8,128)(2,1)S(1)} %get-tuple-element.31), channel_id=1, source_target_pairs={{0,16},{16,0},{32,48},{48,32},{64,80},{80,64},{96,112},{112,96},{1... | collective-permute-start | bytes 737288 | tf_op jit(solution)/shard_map/ppermute | solution.py:585
  16.7 3.6 %collective-permute-start.5 = (bf16[960,128]{1,0:T(8,128)(2,1)S(1)}, bf16[960,128]{1,0:T(8,128)(2,1)S(1)}, u32[]{:S(2)}, u32[]{:S(2)}) collective-permute-start(bf16[960,128]{1,0:T(8,128)(2,1)S(1)} %get-tuple-element.32), channel_id=1, source_target_pairs={{0,48},{16,32},{32,16},{48,0},{64,112},{80,96},{96,80},{112,64},{1... | collective-permute-start | bytes 737288 | tf_op jit(solution)/shard_map/ppermute | solution.py:585
  20.3 0.0 collective-permute-start
  20.3 1.3 %collective-permute-done.sibling_ref = bf16[4,128,128]{2,1,0:T(8,128)(2,1)S(1)} collective-permute-done((bf16[4,128,128]{2,1,0:T(8,128)(2,1)S(1)}, bf16[4,128,128]{2,1,0:T(8,128)(2,1)S(1)}, u32[]{:S(2)}, u32[]{:S(2)}) %collective-permute-start) | collective-permute-done | bytes 131104 | tf_op jit(solution)/shard_map/ppermute | solution.py:593
  21.7 0.2 collective-permute-start.1
  21.9 2.8 %collective-permute-start.2 = (bf16[2,128,128]{2,1,0:T(8,128)(2,1)S(1)}, bf16[2,128,128]{2,1,0:T(8,128)(2,1)S(1)}, u32[]{:S(2)}, u32[]{:S(2)}) collective-permute-start(bf16[2,128,128]{2,1,0:T(8,128)(2,1)S(1)} %get-tuple-element.28), channel_id=1, source_target_pairs={{0,4},{2,6},{4,0},{6,2},{1,5},{3,7},{5,1},{7,3},{8,12},{10,14},{12... | collective-permute-start | bytes 196616 | tf_op jit(solution)/shard_map/ppermute | solution.py:589
  24.7 0.6 collective-permute-start.3
  25.2 3.3 %collective-permute-done.1.r1.refs_0_ = bf16[2,128,128]{2,1,0:T(8,128)(2,1)S(1)} collective-permute-done((bf16[2,128,128]{2,1,0:T(8,128)(2,1)S(1)}, bf16[2,128,128]{2,1,0:T(8,128)(2,1)S(1)}, u32[]{:S(2)}, u32[]{:S(2)}) %collective-permute-start.1) | collective-permute-done | bytes 65568 | tf_op jit(solution)/shard_map/ppermute | solution.py:589
  28.5 1.7 %collective-permute-done.2.r2.refs_1_ = bf16[2,128,128]{2,1,0:T(8,128)(2,1)S(1)} collective-permute-done((bf16[2,128,128]{2,1,0:T(8,128)(2,1)S(1)}, bf16[2,128,128]{2,1,0:T(8,128)(2,1)S(1)}, u32[]{:S(2)}, u32[]{:S(2)}) %collective-permute-start.2) | collective-permute-done | bytes 65568 | tf_op jit(solution)/shard_map/ppermute | solution.py:589
  30.1 0.6 collective-permute-done.3.r3.refs_2_
  30.7 2.3 %collective-permute-done.4.z1 = bf16[960,128]{1,0:T(8,128)(2,1)S(1)} collective-permute-done((bf16[960,128]{1,0:T(8,128)(2,1)S(1)}, bf16[960,128]{1,0:T(8,128)(2,1)S(1)}, u32[]{:S(2)}, u32[]{:S(2)}) %collective-permute-start.4) | collective-permute-done | bytes 245792 | tf_op jit(solution)/shard_map/ppermute | solution.py:585
  33.1 5.9 %collective-permute-done.5.z3 = bf16[960,128]{1,0:T(8,128)(2,1)S(1)} collective-permute-done((bf16[960,128]{1,0:T(8,128)(2,1)S(1)}, bf16[960,128]{1,0:T(8,128)(2,1)S(1)}, u32[]{:S(2)}, u32[]{:S(2)}) %collective-permute-start.5) | collective-permute-done | bytes 245792 | tf_op jit(solution)/shard_map/ppermute | solution.py:585
  38.9 0.0 all-to-all-done.own_ref
  38.9 0.7 stack.1
  39.6 0.1 collective-permute-start.6
  39.7 0.7 collective-permute-start.7
  40.4 2.5 %collective-permute-start.8 = (bf16[960,128]{1,0:T(8,128)(2,1)S(1)}, bf16[960,128]{1,0:T(8,128)(2,1)S(1)}, u32[]{:S(2)}, u32[]{:S(2)}) collective-permute-start(bf16[960,128]{1,0:T(8,128)(2,1)S(1)} %get-tuple-element.38), channel_id=1, source_target_pairs={{0,32},{16,48},{32,0},{48,16},{64,96},{80,112},{96,64},{112,80},{1... | collective-permute-start | bytes 737288 | tf_op jit(solution)/shard_map/ppermute | solution.py:585
  42.9 0.0 copy-done
  42.9 3.2 %ring_attention.1.ring_ref = bf16[16,144,128]{2,1,0:T(8,128)(2,1)S(1)} custom-call(bf16[16,256,128]{2,1,0:T(8,128)(2,1)S(1)} %all-to-all-done.own_ref, bf16[2,128,128]{2,1,0:T(8,128)(2,1)S(1)} %get-tuple-element.26.r0, bf16[2,128,128]{2,1,0:T(8,128)(2,1)S(1)} %collective-permute-done.1.r1.refs_0_, ...), custom_call_target="tpu_custom_call" | custom-call | flops 1000000 | bytes 100000 | tf_op jit(solution)/shard_map/ring_attention/pallas_call | solution.py:383
  46.1 0.0 collective-permute-done.6.other_ref
  46.1 6.4 %view_attention.1 = (bf16[8,144,128]{2,1,0:T(8,128)(2,1)S(1)}, bf16[4096,128]{1,0:T(8,128)(2,1)S(1)}, bf16[4096,128]{1,0:T(8,128)(2,1)S(1)}) custom-call(bf16[16,256,128]{2,1,0:T(8,128)(2,1)S(1)} %all-to-all-done.own_ref, bf16[16,128,128]{2,1,0:T(8,128)(2,1)S(1)} %collective-permute-done.6.other_ref, bf16[16,144,128]{2,1,0:T(8,128)(2,1)S(1)} %ring_attention.1.ring_ref, ...), custom_call_target="tpu_custom_call" | custom-call | flops 1000000 | bytes 100000 | tf_op jit(solution)/shard_map/view_attention/pallas_call | solution.py:320
  52.5 5.2 %collective-permute-done.8.z_ref.z2 = bf16[960,128]{1,0:T(8,128)(2,1)S(1)} collective-permute-done((bf16[960,128]{1,0:T(8,128)(2,1)S(1)}, bf16[960,128]{1,0:T(8,128)(2,1)S(1)}, u32[]{:S(2)}, u32[]{:S(2)}) %collective-permute-start.8) | collective-permute-done | bytes 245792 | tf_op jit(solution)/shard_map/ppermute | solution.py:585
  57.7 1.5 %collective-permute-start.9 = (bf16[640,128]{1,0:T(8,128)(2,1)S(1)}, bf16[640,128]{1,0:T(8,128)(2,1)S(1)}, u32[]{:S(2)}, u32[]{:S(2)}) collective-permute-start(bf16[640,128]{1,0:T(8,128)(2,1)S(1)} %strip.1), channel_id=1, source_target_pairs={{0,64},{16,80},{32,96},{48,112},{64,0},{80,16},{96,32},{112,48},{1... | collective-permute-start | bytes 491528 | tf_op jit(solution)/shard_map/ppermute | solution.py:585
  59.2 0.0 copy-start.1
  59.2 6.8 %view_attention_rest.1.refs_0_ = bf16[16,144,128]{2,1,0:T(8,128)(2,1)} custom-call(bf16[16,256,128]{2,1,0:T(8,128)(2,1)S(1)} %all-to-all-done.own_ref, bf16[16,144,128]{2,1,0:T(8,128)(2,1)S(1)} %ring_attention.1.ring_ref, bf16[8,144,128]{2,1,0:T(8,128)(2,1)S(1)} %get-tuple-element.34.half_ref.order_ref, bf16[4096,128]{1,0:T(8,128)(2,1)S(1)} %get-tuple-element.35.key_s, ...), custom_call_target="tpu_custom_call" | custom-call | flops 1000000 | bytes 100000 | tf_op jit(solution)/shard_map/view_attention_rest/pallas_call | solution.py:333
  66.0 0.0 collective-permute-done.7.refs_1_.x_ref
  66.0 0.0 collective-permute-done.9.refs_2_.x2_ref
  66.0 7.1 %all-to-all-start.1 = ((bf16[16,144,128]{2,1,0:T(8,128)(2,1)}), bf16[16,144,128]{2,1,0:T(8,128)(2,1)S(1)}, u32[]{:S(2)}, u32[]{:S(2)}) async-start(bf16[16,144,128]{2,1,0:T(8,128)(2,1)} %pass_after.1), calls=%async_computation.1 | async-start | bytes 1179648 | tf_op jit(solution)/shard_map/all_to_all | solution.py:611
  73.1 0.0 copy-done.1
  73.1 4.9 %time_attention.1 = (bf16[336,128]{1,0:T(8,128)(2,1)S(1)}, bf16[336,128]{1,0:T(8,128)(2,1)S(1)}, bf16[336,128]{1,0:T(8,128)(2,1)S(1)}, bf16[336,128]{1,0:T(8,128)(2,1)S(1)}) custom-call(bf16[960,128]{1,0:T(8,128)(2,1)S(1)} %get-tuple-element.30.z0, bf16[960,128]{1,0:T(8,128)(2,1)S(1)} %collective-permute-done.4.z1, ...), custom_call_target="tpu_custom_call" | custom-call | flops 700000000 | bytes 2000000 | tf_op jit(solution)/shard_map/time_attention/pallas_call | solution.py:470
  78.0 2.6 %collective-permute-start.10 = (bf16[336,128]{1,0:T(8,128)(2,1)S(1)}, bf16[336,128]{1,0:T(8,128)(2,1)S(1)}, u32[]{:S(2)}, u32[]{:S(2)}) collective-permute-start(bf16[336,128]{1,0:T(8,128)(2,1)S(1)} %get-tuple-element.40), channel_id=1, source_target_pairs={{0,16},{16,0},{32,48},{48,32},{64,80},{80,64},{96,112},{112,96},{1... | collective-permute-start | bytes 258056 | tf_op jit(solution)/shard_map/ppermute | solution.py:585
  80.6 1.4 %collective-permute-start.11 = (bf16[336,128]{1,0:T(8,128)(2,1)S(1)}, bf16[336,128]{1,0:T(8,128)(2,1)S(1)}, u32[]{:S(2)}, u32[]{:S(2)}) collective-permute-start(bf16[336,128]{1,0:T(8,128)(2,1)S(1)} %get-tuple-element.41), channel_id=1, source_target_pairs={{0,32},{16,48},{32,0},{48,16},{64,96},{80,112},{96,64},{112,80},{1... | collective-permute-start | bytes 258056 | tf_op jit(solution)/shard_map/ppermute | solution.py:585
  82.0 2.6 %collective-permute-start.12 = (bf16[336,128]{1,0:T(8,128)(2,1)S(1)}, bf16[336,128]{1,0:T(8,128)(2,1)S(1)}, u32[]{:S(2)}, u32[]{:S(2)}) collective-permute-start(bf16[336,128]{1,0:T(8,128)(2,1)S(1)} %get-tuple-element.42), channel_id=1, source_target_pairs={{0,48},{16,32},{32,16},{48,0},{64,112},{80,96},{96,80},{112,64},{1... | collective-permute-start | bytes 258056 | tf_op jit(solution)/shard_map/ppermute | solution.py:585
  84.5 1.3 %collective-permute-done.10.t1 = bf16[336,128]{1,0:T(8,128)(2,1)S(1)} collective-permute-done((bf16[336,128]{1,0:T(8,128)(2,1)S(1)}, bf16[336,128]{1,0:T(8,128)(2,1)S(1)}, u32[]{:S(2)}, u32[]{:S(2)}) %collective-permute-start.10) | collective-permute-done | bytes 86048 | tf_op jit(solution)/shard_map/ppermute | solution.py:585
  85.8 3.7 %collective-permute-done.11.t2 = bf16[336,128]{1,0:T(8,128)(2,1)S(1)} collective-permute-done((bf16[336,128]{1,0:T(8,128)(2,1)S(1)}, bf16[336,128]{1,0:T(8,128)(2,1)S(1)}, u32[]{:S(2)}, u32[]{:S(2)}) %collective-permute-start.11) | collective-permute-done | bytes 86048 | tf_op jit(solution)/shard_map/ppermute | solution.py:585
  89.5 0.5 collective-permute-done.12.t3
  90.0 0.0 all-to-all-done.1.view_ref
  90.0 5.5 %join.1 = bf16[128,1280]{1,0:T(8,128)(2,1)} custom-call(bf16[16,144,128]{2,1,0:T(8,128)(2,1)S(1)} %all-to-all-done.1.view_ref, bf16[336,128]{1,0:T(8,128)(2,1)S(1)} %get-tuple-element.39.t0, bf16[336,128]{1,0:T(8,128)(2,1)S(1)} %collective-permute-done.10.t1, bf16[336,128]{1,0:T(8,128)(2,1)S(1)} %collective-permute-done.11.t2, ...), custom_call_target="tpu_custom_call" | custom-call | tf_op jit(solution)/shard_map/join/pallas_call | solution.py:568
  (3 shorter events, 0.0 us)
Async XLA Ops:
  0.0 42.9 %copy-start = (s32[8,32,32]{2,1,0:T(8,128)S(1)}, s32[8,32,32]{2,1,0:T(8,128)}, u32[]{:S(2)}) copy-start(s32[8,32,32]{2,1,0:T(8,128)} %mask_ref.3) | copy-start | bytes 98308
  2.7 36.3 %all-to-all-start = ((bf16[16,256,128]{2,1,0:T(8,128)(2,1)}), bf16[16,256,128]{2,1,0:T(8,128)(2,1)S(1)}, u32[]{:S(2)}, u32[]{:S(2)}) async-start(bf16[16,256,128]{2,1,0:T(8,128)(2,1)} %get-tuple-element.24), calls=%async_computation | async-start | bytes 2097152 | tf_op jit(solution)/shard_map/all_to_all | solution.py:600
  13.3 19.7 %collective-permute-start.4 = (bf16[960,128]{1,0:T(8,128)(2,1)S(1)}, bf16[960,128]{1,0:T(8,128)(2,1)S(1)}, u32[]{:S(2)}, u32[]{:S(2)}) collective-permute-start(bf16[960,128]{1,0:T(8,128)(2,1)S(1)} %get-tuple-element.31), channel_id=1, source_target_pairs={{0,16},{16,0},{32,48},{48,32},{64,80},{80,64},{96,112},{112,96},{1... | collective-permute-start | bytes 737288 | tf_op jit(solution)/shard_map/ppermute | solution.py:585
  16.7 22.2 %collective-permute-start.5 = (bf16[960,128]{1,0:T(8,128)(2,1)S(1)}, bf16[960,128]{1,0:T(8,128)(2,1)S(1)}, u32[]{:S(2)}, u32[]{:S(2)}) collective-permute-start(bf16[960,128]{1,0:T(8,128)(2,1)S(1)} %get-tuple-element.32), channel_id=1, source_target_pairs={{0,48},{16,32},{32,16},{48,0},{64,112},{80,96},{96,80},{112,64},{1... | collective-permute-start | bytes 737288 | tf_op jit(solution)/shard_map/ppermute | solution.py:585
  20.3 1.3 %collective-permute-start = (bf16[4,128,128]{2,1,0:T(8,128)(2,1)S(1)}, bf16[4,128,128]{2,1,0:T(8,128)(2,1)S(1)}, u32[]{:S(2)}, u32[]{:S(2)}) collective-permute-start(bf16[4,128,128]{2,1,0:T(8,128)(2,1)S(1)} %get-tuple-element.25.ring_ref), channel_id=1, source_target_pairs={{0,1},{1,0},{2,3},{3,2},{4,5},{5,4},{6,7},{7,6},{8,9},{9,8},{10,11... | collective-permute-start | bytes 393224 | tf_op jit(solution)/shard_map/ppermute | solution.py:593
  21.7 6.8 %collective-permute-start.1 = (bf16[2,128,128]{2,1,0:T(8,128)(2,1)S(1)}, bf16[2,128,128]{2,1,0:T(8,128)(2,1)S(1)}, u32[]{:S(2)}, u32[]{:S(2)}) collective-permute-start(bf16[2,128,128]{2,1,0:T(8,128)(2,1)S(1)} %get-tuple-element.27), channel_id=1, source_target_pairs={{0,2},{2,0},{4,6},{6,4},{1,3},{3,1},{5,7},{7,5},{8,10},{10,8},{12,... | collective-permute-start | bytes 196616 | tf_op jit(solution)/shard_map/ppermute | solution.py:589
  21.9 8.3 %collective-permute-start.2 = (bf16[2,128,128]{2,1,0:T(8,128)(2,1)S(1)}, bf16[2,128,128]{2,1,0:T(8,128)(2,1)S(1)}, u32[]{:S(2)}, u32[]{:S(2)}) collective-permute-start(bf16[2,128,128]{2,1,0:T(8,128)(2,1)S(1)} %get-tuple-element.28), channel_id=1, source_target_pairs={{0,4},{2,6},{4,0},{6,2},{1,5},{3,7},{5,1},{7,3},{8,12},{10,14},{12... | collective-permute-start | bytes 196616 | tf_op jit(solution)/shard_map/ppermute | solution.py:589
  24.7 6.1 %collective-permute-start.3 = (bf16[2,128,128]{2,1,0:T(8,128)(2,1)S(1)}, bf16[2,128,128]{2,1,0:T(8,128)(2,1)S(1)}, u32[]{:S(2)}, u32[]{:S(2)}) collective-permute-start(bf16[2,128,128]{2,1,0:T(8,128)(2,1)S(1)} %get-tuple-element.29), channel_id=1, source_target_pairs={{0,6},{2,4},{4,2},{6,0},{1,7},{3,5},{5,3},{7,1},{8,14},{10,12},{12... | collective-permute-start | bytes 196616 | tf_op jit(solution)/shard_map/ppermute | solution.py:589
  39.6 6.4 %collective-permute-start.6 = (bf16[16,128,128]{2,1,0:T(8,128)(2,1)S(1)}, bf16[16,128,128]{2,1,0:T(8,128)(2,1)S(1)}, u32[]{:S(2)}, u32[]{:S(2)}) collective-permute-start(bf16[16,128,128]{2,1,0:T(8,128)(2,1)S(1)} %get-tuple-element.33), channel_id=1, source_target_pairs={{0,1},{1,0},{2,3},{3,2},{4,5},{5,4},{6,7},{7,6},{8,9},{9,8},{10,11... | collective-permute-start | bytes 1572872 | tf_op jit(solution)/shard_map/ppermute | solution.py:593
  39.7 26.2 %collective-permute-start.7 = (bf16[3,640,128]{2,1,0:T(8,128)(2,1)S(1)}, bf16[3,640,128]{2,1,0:T(8,128)(2,1)S(1)}, u32[]{:S(2)}, u32[]{:S(2)}) collective-permute-start(bf16[3,640,128]{2,1,0:T(8,128)(2,1)S(1)} %get-tuple-element.37), channel_id=1, source_target_pairs={{0,64},{16,80},{32,96},{48,112},{64,0},{80,16},{96,32},{112,48},{1... | collective-permute-start | bytes 1474568 | tf_op jit(solution)/shard_map/ppermute | solution.py:585
  40.4 17.2 %collective-permute-start.8 = (bf16[960,128]{1,0:T(8,128)(2,1)S(1)}, bf16[960,128]{1,0:T(8,128)(2,1)S(1)}, u32[]{:S(2)}, u32[]{:S(2)}) collective-permute-start(bf16[960,128]{1,0:T(8,128)(2,1)S(1)} %get-tuple-element.38), channel_id=1, source_target_pairs={{0,32},{16,48},{32,0},{48,16},{64,96},{80,112},{96,64},{112,80},{1... | collective-permute-start | bytes 737288 | tf_op jit(solution)/shard_map/ppermute | solution.py:585
  57.7 8.3 %collective-permute-start.9 = (bf16[640,128]{1,0:T(8,128)(2,1)S(1)}, bf16[640,128]{1,0:T(8,128)(2,1)S(1)}, u32[]{:S(2)}, u32[]{:S(2)}) collective-permute-start(bf16[640,128]{1,0:T(8,128)(2,1)S(1)} %strip.1), channel_id=1, source_target_pairs={{0,64},{16,80},{32,96},{48,112},{64,0},{80,16},{96,32},{112,48},{1... | collective-permute-start | bytes 491528 | tf_op jit(solution)/shard_map/ppermute | solution.py:585
  59.2 13.9 %copy-start.1 = (s32[8]{0:T(128)S(1)}, s32[8]{0:T(128)}, u32[]{:S(2)}) copy-start(s32[8]{0:T(128)} %times_ref.1) | copy-start | bytes 100
  66.0 24.0 %all-to-all-start.1 = ((bf16[16,144,128]{2,1,0:T(8,128)(2,1)}), bf16[16,144,128]{2,1,0:T(8,128)(2,1)S(1)}, u32[]{:S(2)}, u32[]{:S(2)}) async-start(bf16[16,144,128]{2,1,0:T(8,128)(2,1)} %pass_after.1), calls=%async_computation.1 | async-start | bytes 1179648 | tf_op jit(solution)/shard_map/all_to_all | solution.py:611
  78.0 7.8 %collective-permute-start.10 = (bf16[336,128]{1,0:T(8,128)(2,1)S(1)}, bf16[336,128]{1,0:T(8,128)(2,1)S(1)}, u32[]{:S(2)}, u32[]{:S(2)}) collective-permute-start(bf16[336,128]{1,0:T(8,128)(2,1)S(1)} %get-tuple-element.40), channel_id=1, source_target_pairs={{0,16},{16,0},{32,48},{48,32},{64,80},{80,64},{96,112},{112,96},{1... | collective-permute-start | bytes 258056 | tf_op jit(solution)/shard_map/ppermute | solution.py:585
  80.6 9.0 %collective-permute-start.11 = (bf16[336,128]{1,0:T(8,128)(2,1)S(1)}, bf16[336,128]{1,0:T(8,128)(2,1)S(1)}, u32[]{:S(2)}, u32[]{:S(2)}) collective-permute-start(bf16[336,128]{1,0:T(8,128)(2,1)S(1)} %get-tuple-element.41), channel_id=1, source_target_pairs={{0,32},{16,48},{32,0},{48,16},{64,96},{80,112},{96,64},{112,80},{1... | collective-permute-start | bytes 258056 | tf_op jit(solution)/shard_map/ppermute | solution.py:585
  82.0 8.0 %collective-permute-start.12 = (bf16[336,128]{1,0:T(8,128)(2,1)S(1)}, bf16[336,128]{1,0:T(8,128)(2,1)S(1)}, u32[]{:S(2)}, u32[]{:S(2)}) collective-permute-start(bf16[336,128]{1,0:T(8,128)(2,1)S(1)} %get-tuple-element.42), channel_id=1, source_target_pairs={{0,48},{16,32},{32,16},{48,0},{64,112},{80,96},{96,80},{112,64},{1... | collective-permute-start | bytes 258056 | tf_op jit(solution)/shard_map/ppermute | solution.py:585

commit v4 on v3

--- a/solution.py
+++ b/solution.py
@@ -62,69 +62,51 @@
     return jnp.concatenate([left, right], axis=1)
 
 
-def pack_time_kernel(q_hbm, k_hbm, v_hbm, z0, z1, z2, z3, q_ref, k_ref, v_ref, sems, parts):
+def in_hbm(x):
+    return pltpu.with_memory_space_constraint(x, pltpu.HBM)
+
+
+def pack_kernel(q_hbm, k_hbm, v_hbm, z0, z1, z2, z3, ring_ref, view_ref, q_ref, k_ref, v_ref, sems, parts):
     place = lax.axis_index("f") % 4
-    copy_all([(k_hbm, k_ref), (v_hbm, v_ref), (q_hbm, q_ref)], sems)
+    load = pltpu.make_async_copy(q_hbm, q_ref, sems.at[2])
+    load.start()
+    copy_all([(k_hbm, k_ref), (v_hbm, v_ref)], sems)
+    for j in range(4):
+        for i in range(5):
+            parts[j, i * CELLS : (i + 1) * CELLS] = pair(k_ref, 5 * j + i, v_ref, 5 * j + i)
+    for t in range(MAIN):
+        view_ref[t, 0:CELLS] = pair(k_ref, t, v_ref, t)
+    for y in range(RING):
+        ring_ref[y] = pair(k_ref, MAIN + y, v_ref, MAIN + y)
+    load.wait()
     for j in range(4):
         base = 5 * j
-        for i in range(5):
-            parts[j, i * CELLS : (i + 1) * CELLS] = pair(k_ref, base + i, v_ref, base + i)
         for i in range(2):
             rows = slice((5 + i) * CELLS, (6 + i) * CELLS)
             parts[j, rows] = pair(q_ref, base + 2 * i, q_ref, base + 2 * i + 1)
         last = q_ref[:, (base + 4) * HEAD : (base + 5) * HEAD]
         parts[j, 896:960] = jnp.concatenate([last[0:64], last[64:128]], axis=1)
-    keep = pltpu.make_async_copy(parts.at[place], z0, sems.at[3])
-    keep.start()
-    for k, out in enumerate((z1, z2, z3)):
-        out[...] = parts[turned(place, k + 1)]
-    keep.wait()
-
-
-def in_hbm(x):
-    return pltpu.with_memory_space_constraint(x, pltpu.HBM)
-
-
-def pack_time(q, k, v):
+    for k, out in enumerate((z0, z1, z2, z3)):
+        out[...] = parts[turned(place, k)]
+    for t in range(MAIN):
+        view_ref[t, CELLS : 2 * CELLS] = pair(q_ref, t, q_ref, MAIN + t % RING)
+
+
+def pack(q, k, v):
     block = jax.ShapeDtypeStruct((Z_ROWS, CELLS), BF16)
     whole = pltpu.VMEM((CELLS, HEADS * HEAD), BF16)
     return pl.pallas_call(
-        pack_time_kernel,
-        out_shape=[block] * 4,
-        in_specs=[ANY] * 3,
-        out_specs=[ANY] + [VMEM] * 3,
-        scratch_shapes=[whole] * 3 + [pltpu.SemaphoreType.DMA((4,)), pltpu.VMEM((4, Z_ROWS, CELLS), BF16)],
-        compiler_params=params(16),
-        name="pack_time",
-    )(in_hbm(q), in_hbm(k), in_hbm(v))
-
-
-def pack_view_kernel(q_hbm, k_hbm, v_hbm, view_ref, ring_ref, q_ref, k_ref, v_ref, sems):
-    load = pltpu.make_async_copy(q_hbm, q_ref, sems.at[2])
-    load.start()
-    copy_all([(k_hbm, k_ref), (v_hbm, v_ref)], sems)
-    for t in range(MAIN):
-        view_ref[t, 0:CELLS] = pair(k_ref, t, v_ref, t)
-    for y in range(RING):
-        ring_ref[y] = pair(k_ref, MAIN + y, v_ref, MAIN + y)
-    load.wait()
-    for t in range(MAIN):
-        view_ref[t, CELLS : 2 * CELLS] = pair(q_ref, t, q_ref, MAIN + t % RING)
-
-
-def pack_view(q, k, v):
-    whole = pltpu.VMEM((CELLS, HEADS * HEAD), BF16)
-    return pl.pallas_call(
-        pack_view_kernel,
-        out_shape=[
+        pack_kernel,
+        out_shape=[block] * 4
+        + [
+            jax.ShapeDtypeStruct((RING, CELLS, CELLS), BF16),
             jax.ShapeDtypeStruct((MAIN, 2 * CELLS, CELLS), BF16),
-            jax.ShapeDtypeStruct((RING, CELLS, CELLS), BF16),
         ],
         in_specs=[ANY] * 3,
-        out_specs=[VMEM] * 2,
-        scratch_shapes=[whole] * 3 + [pltpu.SemaphoreType.DMA((3,))],
+        out_specs=[VMEM] * 6,
+        scratch_shapes=[whole] * 3 + [pltpu.SemaphoreType.DMA((3,)), pltpu.VMEM((4, Z_ROWS, CELLS), BF16)],
         compiler_params=params(16),
-        name="pack_view",
+        name="pack",
     )(in_hbm(q), in_hbm(k), in_hbm(v))
 
 
@@ -146,42 +128,39 @@
     )(ring, other)
 
 
-def stack_kernel(own_ref, z0, z1, z3, *refs):
-    kv_ref, out_ref, sems = refs[-3:]
-    moves = [(own_ref.at[:, pl.ds(0, CELLS)], kv_ref)]
-    moves += [(piece.at[pl.ds(0, X_ROWS)], out_ref.at[k]) for k, piece in enumerate((z0, z1, z3))]
-    copy_all(moves, sems)
-
-
-def stack(own, z0, z1, z3, order):
+def stack_kernel(z0, z1, z2, z3, *refs):
+    out_ref = refs[-1]
+    for k, piece in enumerate((z0, z1, z2, z3)):
+        out_ref[k] = piece[0:X_ROWS]
+
+
+def stack(z, order):
     return pl.pallas_call(
         stack_kernel,
-        out_shape=[
-            jax.ShapeDtypeStruct((MAIN, CELLS, CELLS), BF16),
-            jax.ShapeDtypeStruct((3, X_ROWS, CELLS), BF16),
-        ],
-        in_specs=[ANY] * (4 + len(order)),
-        out_specs=[ANY] * 2,
-        scratch_shapes=[pltpu.SemaphoreType.DMA((4,))],
-        compiler_params=params(4),
-        name="stack",
-    )(own, z0, z1, z3, *order)
-
-
-def strip_kernel(z_ref, order_ref, out_ref):
-    del order_ref
-    out_ref[...] = z_ref[0:X_ROWS]
-
-
-def strip(z, order):
-    return pl.pallas_call(
-        strip_kernel,
-        out_shape=jax.ShapeDtypeStruct((X_ROWS, CELLS), BF16),
-        in_specs=[VMEM, ANY],
+        out_shape=jax.ShapeDtypeStruct((4, X_ROWS, CELLS), BF16),
+        in_specs=[VMEM] * 4 + [ANY] * len(order),
         out_specs=VMEM,
         compiler_params=params(4),
-        name="strip",
-    )(z, order)
+        cost_estimate=pl.CostEstimate(flops=18000000000, bytes_accessed=100000, transcendentals=0),
+        name="stack",
+    )(*z, *order)
+
+
+def keep_kernel(own_ref, *refs):
+    kv_ref, sems = refs[-2:]
+    copy_all([(own_ref.at[:, pl.ds(0, CELLS)], kv_ref)], sems)
+
+
+def keep(own, order):
+    return pl.pallas_call(
+        keep_kernel,
+        out_shape=jax.ShapeDtypeStruct((MAIN, CELLS, CELLS), BF16),
+        in_specs=[ANY] * (1 + len(order)),
+        out_specs=ANY,
+        scratch_shapes=[pltpu.SemaphoreType.DMA((1,))],
+        compiler_params=params(4),
+        name="keep",
+    )(own, *order)
 
 
 def score_tile(q, key_ref, score_ref, count):
@@ -245,7 +224,7 @@
     value_s[rows] = kv * (1 - low) + low
 
 
-def attend_views(own_ref, ring_ref, key_s, value_s, s_a, s_b, first, write):
+def attend_views(own_ref, ring_ref, key_s, value_s, s_a, s_b, write):
     lane = lanes((CELLS, CELLS))
     wide = lanes((TILE, CELLS))
 
@@ -266,20 +245,20 @@
             head_rows = ring_ref[j, 0:CELLS] + heads[rows].astype(BF16)
             write(j, head_rows, ring_ref[j, CELLS:O_ROWS] + table[rows].T[0:16].astype(BF16))
 
-    start = score_tile(tile(first), key_s, s_a, 4096)
+    start = score_tile(tile(0), key_s, s_a, 4096)
 
     def body(step, m_a):
-        i = first + 2 * step
+        i = 2 * step
         m_b = score_tile(tile(i + 1), key_s, s_b, 4096)
         finish(i, s_a, m_a)
-        m_next = score_tile(tile(jnp.minimum(i + 2, first + 3)), key_s, s_a, 4096)
+        m_next = score_tile(tile(jnp.minimum(i + 2, 7)), key_s, s_a, 4096)
         finish(i + 1, s_b, m_b)
         return m_next
 
-    lax.fori_loop(0, 2, body, start)
-
-
-def view_kernel(own_ref, other_ref, ring_ref, mask_ref, out_ref, key_s, value_s, s_a, s_b):
+    lax.fori_loop(0, 4, body, start)
+
+
+def view_kernel(own_ref, other_ref, ring_ref, mask_ref, out_hbm, out_ref, sems, key_s, value_s, s_a, s_b):
     core = lax.axis_index("c")
     block = rows_of((32, 32))
     bias = seen_bias(mask_ref, jnp.where(block < 16, 2 * block + core, 2 * (block - 16) + 1 - core), 32)
@@ -287,59 +266,39 @@
         kv = own_ref[b, 0:CELLS] if b < 16 else other_ref[b - 16]
         fill(key_s, value_s, b, kv, bias[b : b + 1])
 
-    def write(j, head_rows, level_part):
-        out_ref[j, 0:CELLS] = head_rows
-        out_ref[j, CELLS:O_ROWS] = level_part
-
-    attend_views(own_ref, ring_ref, key_s, value_s, s_a, s_b, 0, write)
-
-
-def view_rest_kernel(own_ref, ring_ref, half_ref, key_s, value_s, out_hbm, out_ref, sems, s_a, s_b):
-    early = pltpu.make_async_copy(half_ref, out_hbm.at[pl.ds(0, 8)], sems.at[8])
-    early.start()
-
     def away(j):
-        return pltpu.make_async_copy(out_ref.at[j], out_hbm.at[j], sems.at[j - 8])
+        return pltpu.make_async_copy(out_ref.at[j], out_hbm.at[j], sems.at[j])
 
     def write(j, head_rows, level_part):
         out_ref[j, 0:CELLS] = head_rows
         out_ref[j, CELLS:O_ROWS] = level_part
         away(j).start()
 
-    attend_views(own_ref, ring_ref, key_s, value_s, s_a, s_b, 4, write)
-    for j in range(8, 16):
+    attend_views(own_ref, ring_ref, key_s, value_s, s_a, s_b, write)
+    for j in range(MAIN):
         away(j).wait()
-    early.wait()
-
-
-SCORES = [pltpu.VMEM((TILE, 4096), F32)] * 2
 
 
 def view_attention(own, other, ring_out, view_mask):
-    filled = jax.ShapeDtypeStruct((4096, CELLS), BF16)
+    rows = pltpu.VMEM((4096, CELLS), BF16)
+    scores = pltpu.VMEM((TILE, 4096), F32)
     return pl.pallas_call(
         view_kernel,
-        out_shape=[jax.ShapeDtypeStruct((8, O_ROWS, CELLS), BF16), filled, filled],
+        out_shape=pltpu.HBM((MAIN, O_ROWS, CELLS), BF16),
         in_specs=[VMEM] * 4,
-        out_specs=[VMEM] * 3,
-        scratch_shapes=SCORES,
-        compiler_params=params(16),
+        out_specs=ANY,
+        scratch_shapes=[
+            pltpu.VMEM((MAIN, O_ROWS, CELLS), BF16),
+            pltpu.SemaphoreType.DMA((MAIN,)),
+            rows,
+            rows,
+            scores,
+            scores,
+        ],
+        compiler_params=params(20),
         cost_estimate=pl.CostEstimate(flops=1000000, bytes_accessed=100000, transcendentals=0),
         name="view_attention",
     )(own, other, ring_out, view_mask)
-
-
-def view_attention_rest(own, ring_out, half, key_rows, value_rows):
-    return pl.pallas_call(
-        view_rest_kernel,
-        out_shape=pltpu.HBM((MAIN, O_ROWS, CELLS), BF16),
-        in_specs=[VMEM] * 5,
-        out_specs=ANY,
-        scratch_shapes=[pltpu.VMEM((MAIN, O_ROWS, CELLS), BF16), pltpu.SemaphoreType.DMA((9,))] + SCORES,
-        compiler_params=params(16),
-        cost_estimate=pl.CostEstimate(flops=1000000, bytes_accessed=100000, transcendentals=0),
-        name="view_attention_rest",
-    )(own, ring_out, half, key_rows, value_rows)
 
 
 def ring_kernel(own_ref, r0, r1, r2, r3, mask_ref, out_ref, key_s, value_s, s_ref):
@@ -396,11 +355,11 @@
     )(own, *pieces, view_mask)
 
 
-def time_kernel(z0, z1, z2, z3, x_ref, x2_ref, times_ref, o0, o1, o2, o3, key_s, value_s, q_s, s_ref):
+def time_kernel(z0, z1, z2, z3, x_ref, times_ref, o0, o1, o2, o3, key_s, value_s, q_s, s_ref):
     frame = lax.axis_index("f")
     lane = lanes((CELLS, CELLS))
     own = (z0, z1, z2, z3)
-    far = (x_ref.at[0], x_ref.at[1], x2_ref, x_ref.at[2])
+    far = tuple(x_ref.at[k] for k in range(4))
     outs = (o0, o1, o2, o3)
 
     l8, r8 = lanes((8, 128)), rows_of((8, 128))
@@ -470,7 +429,7 @@
     return pl.pallas_call(
         time_kernel,
         out_shape=[jax.ShapeDtypeStruct((T_ROWS, CELLS), BF16)] * 4,
-        in_specs=[VMEM] * 6 + [SMEM],
+        in_specs=[VMEM] * 5 + [SMEM],
         out_specs=[VMEM] * 4,
         scratch_shapes=[
             pltpu.VMEM((5, 1024, CELLS), BF16),
@@ -481,7 +440,7 @@
         compiler_params=params(16),
         cost_estimate=pl.CostEstimate(flops=700000000, bytes_accessed=2000000, transcendentals=2700000),
         name="time_attention",
-    )(*own, *crossed, frame_times)
+    )(*own, crossed, frame_times)
 
 
 def pass_kernel(*refs):
@@ -596,20 +555,19 @@
 def local(queries, keys, values, view_mask, frame_times, out_weight):
     model = queries.shape[3]
     q, k, v = (a.reshape(CELLS, model) for a in (queries, keys, values))
-    to_view, to_ring = pack_view(q, k, v)
+    *z, to_ring, to_view = pack(q, k, v)
     own = lax.all_to_all(to_view, ("g", "zl", "y"), 0, 0)
+    z = [z[0]] + [across(z[i], i) for i in (1, 2, 3)]
     ring = ring_pack(to_ring, sibling(to_ring))
     ring = [ring[0]] + [around(ring[i], i) for i in (1, 2, 3)]
-    z0, z1, z2, z3 = pack_time(q, k, v)
-    z1, z2, z3 = across(z1, 1), across(z2, 2), across(z3, 3)
-    kv, some = stack(own, z0, z1, z3, ring[1:])
+    some = stack(z, ring[1:])
+    crossed = across(some, 4)
+    other = sibling(keep(own, [some]))
     ring_out = ring_attention(own, ring, view_mask)
-    half, *filled = view_attention(own, sibling(kv), ring_out, view_mask)
-    crossed = (across(some, 4), across(strip(z2, half), 4))
-    view_out = view_attention_rest(own, ring_out, half, *filled)
-    view_out = pass_after(view_out, crossed)
+    view_out = view_attention(own, other, ring_out, view_mask)
+    view_out = pass_after(view_out, (crossed,))
     view_back = lax.all_to_all(view_out, ("g", "zl", "y"), 0, 0)
-    pieces = time_attention((z0, z1, z2, z3), crossed, frame_times)
+    pieces = time_attention(z, crossed, frame_times)
     pieces = [pieces[0]] + [across(pieces[i], i) for i in (1, 2, 3)]
     result = join(view_back, pieces, out_weight)
     return result.reshape(1, 1, CELLS, model)

time: 96.5 us -> 94.7 us (0.981)
  waiting for transfers between devices: 25.6 us -> 29 us
  starting transfers between devices: 37.7 us -> 34.4 us
  Pallas kernels: 32.1 us -> 29.1 us
    all_to_all x1, waiting for transfers between devices: 0.01 us -> 12.2 us  [local(): own = lax.all_to_all(to_view, ('g', 'zl', 'y'), 0, 0)]
    ppermute x8 -> x7, waiting for transfers between devices: 18.8 us -> 8.85 us  [across(): return lax.ppermute(array, 'f', [(i, i ^ k) for i in range(FRAMES)])]
    pallas_call x6 -> x4, Pallas kernels: 18.5 us -> 15.4 us  [the longest x1 12.4 us: view_attention(): pl.pallas_call(view_kernel, out_shape=pltpu.HBM((MAIN, O_ROWS, CELLS), BF...]
    ppermute x3, waiting for transfers between devices: 5.51 us -> 7.97 us  [around(): return lax.ppermute(array, 'y', [(i, i ^ k) for i in range(RING)])]
    all_to_all x1, starting transfers between devices: 7.07 us -> 4.73 us  [local(): view_back = lax.all_to_all(view_out, ('g', 'zl', 'y'), 0, 0)]
    ppermute x8 -> x7, starting transfers between devices: 18.2 us -> 16.8 us  [across(): return lax.ppermute(array, 'f', [(i, i ^ k) for i in range(FRAMES)])]
    ppermute x2, waiting for transfers between devices: 1.35 us -> 0.01 us  [sibling(): return lax.ppermute(array, 'c', [(0, 1), (1, 0)])]
    ppermute x3, starting transfers between devices: 3.58 us -> 4.64 us  [around(): return lax.ppermute(array, 'y', [(i, i ^ k) for i in range(RING)])]
  transfers between devices with their start and end apart: 15 -> 14, of which waited for: 10 -> 8; matrix products, arithmetic and copies ran while one was open for 0% -> 0% of each run, Pallas kernels for 24% -> 22%
where the time goes in v4:
time: 94.7 us; the launch traced here: 93.4 us
  starting transfers between devices  34.4 us (36%)
  Pallas kernels  29.1 us (31%)
  waiting for transfers between devices  29 us (31%)
    ppermute x7, starting transfers between devices, across(): return lax.ppermute(array, 'f', [(i, i ^ k) for i in range(FRAMES)])  16.8 us
    pallas_call x1, Pallas kernels, view_attention(): pl.pallas_call(view_kernel, out_shape=pltpu.HBM((MAIN, O_ROWS, CELLS), BF...  12.4 us
    all_to_all x1, waiting for transfers between devices, local(): own = lax.all_to_all(to_view, ('g', 'zl', 'y'), 0, 0)  12.2 us
    ppermute x7, waiting for transfers between devices, across(): return lax.ppermute(array, 'f', [(i, i ^ k) for i in range(FRAMES)])  8.85 us
    ppermute x3, waiting for transfers between devices, around(): return lax.ppermute(array, 'y', [(i, i ^ k) for i in range(RING)])  7.97 us
    all_to_all x1, starting transfers between devices, local(): own = lax.all_to_all(to_view, ('g', 'zl', 'y'), 0, 0)  7.85 us
    pallas_call x1, Pallas kernels, join(): pl.pallas_call(join_kernel, out_shape=jax.ShapeDtypeStruct((CELLS, HEADS...  5.49 us
    pallas_call x1, Pallas kernels, time_attention(): pl.pallas_call(time_kernel, out_shape=[jax.ShapeDtypeStruct((T_ROWS, CELL...  4.92 us
  transfers between devices with their start and end apart: 14, of which 8 were waited for; matrix products, arithmetic and copies ran while one was open for 0% of the time, Pallas kernels for 22%

profile of v4, /device:TPU:8, one launch (start us, length us, event | category | flops | bytes accessed | tf_op | source)
XLA Modules:
  0.0 93.4 jit_solution(17185861147982442779)
XLA Ops:
  0.0 2.9 %pack.1 = (bf16[960,128]{1,0:T(8,128)(2,1)S(1)}, bf16[960,128]{1,0:T(8,128)(2,1)S(1)}, bf16[960,128]{1,0:T(8,128)(2,1)S(1)}, bf16[960,128]{1,0:T(8,128)(2,1)S(1)...) custom-call(bf16[128,1280]{1,0:T(8,128)(2,1)} %bitcast.4, bf16[128,1280]{1,0:T(8,128)(2,1)} %bitcast.5, ...), custom_call_target="tpu_custom_call" | custom-call | tf_op jit(solution)/shard_map/pack/pallas_call | solution.py:98
  3.0 0.1 collective-permute-start.3
  3.1 3.4 %collective-permute-start = (bf16[960,128]{1,0:T(8,128)(2,1)S(1)}, bf16[960,128]{1,0:T(8,128)(2,1)S(1)}, u32[]{:S(2)}, u32[]{:S(2)}) collective-permute-start(bf16[960,128]{1,0:T(8,128)(2,1)S(1)} %get-tuple-element.21), channel_id=1, source_target_pairs={{0,16},{16,0},{32,48},{48,32},{64,80},{80,64},{96,112},{112,96},{1... | collective-permute-start | bytes 737288 | tf_op jit(solution)/shard_map/ppermute | solution.py:544
  6.4 5.4 %collective-permute-start.1 = (bf16[960,128]{1,0:T(8,128)(2,1)S(1)}, bf16[960,128]{1,0:T(8,128)(2,1)S(1)}, u32[]{:S(2)}, u32[]{:S(2)}) collective-permute-start(bf16[960,128]{1,0:T(8,128)(2,1)S(1)} %get-tuple-element.22), channel_id=1, source_target_pairs={{0,32},{16,48},{32,0},{48,16},{64,96},{80,112},{96,64},{112,80},{1... | collective-permute-start | bytes 737288 | tf_op jit(solution)/shard_map/ppermute | solution.py:544
  11.8 0.0 collective-permute-start.2
  11.8 7.8 %all-to-all-start = ((bf16[16,256,128]{2,1,0:T(8,128)(2,1)}), bf16[16,256,128]{2,1,0:T(8,128)(2,1)S(1)}, u32[]{:S(2)}, u32[]{:S(2)}) async-start(bf16[16,256,128]{2,1,0:T(8,128)(2,1)} %get-tuple-element.19), calls=%async_computation | async-start | bytes 2097152 | tf_op jit(solution)/shard_map/all_to_all | solution.py:559
  19.7 0.0 collective-permute-done.3.sibling_ref
  19.7 0.2 collective-permute-start.4
  19.9 2.8 %collective-permute-start.5 = (bf16[2,128,128]{2,1,0:T(8,128)(2,1)S(1)}, bf16[2,128,128]{2,1,0:T(8,128)(2,1)S(1)}, u32[]{:S(2)}, u32[]{:S(2)}) collective-permute-start(bf16[2,128,128]{2,1,0:T(8,128)(2,1)S(1)} %get-tuple-element.26), channel_id=1, source_target_pairs={{0,4},{2,6},{4,0},{6,2},{1,5},{3,7},{5,1},{7,3},{8,12},{10,14},{12... | collective-permute-start | bytes 196616 | tf_op jit(solution)/shard_map/ppermute | solution.py:548
  22.7 5.3 %collective-permute-done.4.refs_0_.r1 = bf16[2,128,128]{2,1,0:T(8,128)(2,1)S(1)} collective-permute-done((bf16[2,128,128]{2,1,0:T(8,128)(2,1)S(1)}, bf16[2,128,128]{2,1,0:T(8,128)(2,1)S(1)}, u32[]{:S(2)}, u32[]{:S(2)}) %collective-permute-start.4) | collective-permute-done | bytes 65568 | tf_op jit(solution)/shard_map/ppermute | solution.py:548
  28.0 1.6 %collective-permute-start.6 = (bf16[2,128,128]{2,1,0:T(8,128)(2,1)S(1)}, bf16[2,128,128]{2,1,0:T(8,128)(2,1)S(1)}, u32[]{:S(2)}, u32[]{:S(2)}) collective-permute-start(bf16[2,128,128]{2,1,0:T(8,128)(2,1)S(1)} %get-tuple-element.27), channel_id=1, source_target_pairs={{0,6},{2,4},{4,2},{6,0},{1,7},{3,5},{5,3},{7,1},{8,14},{10,12},{12... | collective-permute-start | bytes 196616 | tf_op jit(solution)/shard_map/ppermute | solution.py:548
  29.7 0.8 collective-permute-done.5.refs_1_.r2
  30.5 1.8 %collective-permute-done.6.refs_2_.r3 = bf16[2,128,128]{2,1,0:T(8,128)(2,1)S(1)} collective-permute-done((bf16[2,128,128]{2,1,0:T(8,128)(2,1)S(1)}, bf16[2,128,128]{2,1,0:T(8,128)(2,1)S(1)}, u32[]{:S(2)}, u32[]{:S(2)}) %collective-permute-start.6) | collective-permute-done | bytes 65568 | tf_op jit(solution)/shard_map/ppermute | solution.py:548
  32.3 0.0 collective-permute-done.z1
  32.3 2.1 %collective-permute-done.1.z2 = bf16[960,128]{1,0:T(8,128)(2,1)S(1)} collective-permute-done((bf16[960,128]{1,0:T(8,128)(2,1)S(1)}, bf16[960,128]{1,0:T(8,128)(2,1)S(1)}, u32[]{:S(2)}, u32[]{:S(2)}) %collective-permute-start.1) | collective-permute-done | bytes 245792 | tf_op jit(solution)/shard_map/ppermute | solution.py:544
  34.4 0.0 collective-permute-done.2.z3
  34.4 0.0 copy-start
  34.4 0.0 copy-start.1
  34.5 0.7 copy-done.1
  35.1 1.5 %collective-permute-start.8 = (bf16[4,640,128]{2,1,0:T(8,128)(2,1)S(1)}, bf16[4,640,128]{2,1,0:T(8,128)(2,1)S(1)}, u32[]{:S(2)}, u32[]{:S(2)}) collective-permute-start(bf16[4,640,128]{2,1,0:T(8,128)(2,1)S(1)} %stack.1.refs_0_), channel_id=1, source_target_pairs={{0,64},{16,80},{32,96},{48,112},{64,0},{80,16},{96,32},{112,48},{1... | collective-permute-start | bytes 1966088 | tf_op jit(solution)/shard_map/ppermute | solution.py:544
  36.6 12.2 %all-to-all-done.own_ref = bf16[16,256,128]{2,1,0:T(8,128)(2,1)S(1)} async-done(((bf16[16,256,128]{2,1,0:T(8,128)(2,1)}), bf16[16,256,128]{2,1,0:T(8,128)(2,1)S(1)}, u32[]{:S(2)}, u32[]{:S(2)}) %all-to-all-start) | async-done | bytes 1048608 | tf_op jit(solution)/shard_map/all_to_all | solution.py:559
  48.8 0.3 collective-permute-start.7
  49.1 0.0 copy-done
  49.1 3.2 %ring_attention.1.ring_ref = bf16[16,144,128]{2,1,0:T(8,128)(2,1)S(1)} custom-call(bf16[16,256,128]{2,1,0:T(8,128)(2,1)S(1)} %all-to-all-done.own_ref, bf16[2,128,128]{2,1,0:T(8,128)(2,1)S(1)} %get-tuple-element.28.r0, bf16[2,128,128]{2,1,0:T(8,128)(2,1)S(1)} %collective-permute-done.4.refs_0_.r1, ...), custom_call_target="tpu_custom_call" | custom-call | flops 1000000 | bytes 100000 | tf_op jit(solution)/shard_map/ring_attention/pallas_call | solution.py:342
  52.3 0.0 copy-start.2
  52.3 0.0 copy-start.3
  52.3 0.0 collective-permute-done.7.other_ref
  52.3 12.4 %view_attention.1.refs_0_ = bf16[16,144,128]{2,1,0:T(8,128)(2,1)} custom-call(bf16[16,256,128]{2,1,0:T(8,128)(2,1)S(1)} %all-to-all-done.own_ref, bf16[16,128,128]{2,1,0:T(8,128)(2,1)S(1)} %collective-permute-done.7.other_ref, bf16[16,144,128]{2,1,0:T(8,128)(2,1)S(1)} %ring_attention.1.ring_ref, s32[8,32,32]{2,1,0:T(8,128)S(1)} %copy-done), custom_call_target="tpu_custom_call" | custom-call | flops 1000000 | bytes 100000 | tf_op jit(solution)/shard_map/view_attention/pallas_call | solution.py:285
  64.7 0.0 collective-permute-done.8.refs_1_.x_ref
  64.8 4.7 %all-to-all-start.1 = ((bf16[16,144,128]{2,1,0:T(8,128)(2,1)}), bf16[16,144,128]{2,1,0:T(8,128)(2,1)S(1)}, u32[]{:S(2)}, u32[]{:S(2)}) async-start(bf16[16,144,128]{2,1,0:T(8,128)(2,1)} %pass_after.1), calls=%async_computation.1 | async-start | bytes 1179648 | tf_op jit(solution)/shard_map/all_to_all | solution.py:569
  69.5 0.0 copy-done.2
  69.5 0.0 copy-done.3
  69.5 4.9 %time_attention.1 = (bf16[336,128]{1,0:T(8,128)(2,1)S(1)}, bf16[336,128]{1,0:T(8,128)(2,1)S(1)}, bf16[336,128]{1,0:T(8,128)(2,1)S(1)}, bf16[336,128]{1,0:T(8,128)(2,1)S(1)}) custom-call(bf16[960,128]{1,0:T(8,128)(2,1)S(1)} %get-tuple-element.20.z0, bf16[960,128]{1,0:T(8,128)(2,1)S(1)} %collective-permute-done.z1, ...), custom_call_target="tpu_custom_call" | custom-call | flops 700000000 | bytes 2000000 | tf_op jit(solution)/shard_map/time_attention/pallas_call | solution.py:429
  74.4 2.3 %collective-permute-start.10 = (bf16[336,128]{1,0:T(8,128)(2,1)S(1)}, bf16[336,128]{1,0:T(8,128)(2,1)S(1)}, u32[]{:S(2)}, u32[]{:S(2)}) collective-permute-start(bf16[336,128]{1,0:T(8,128)(2,1)S(1)} %get-tuple-element.31), channel_id=1, source_target_pairs={{0,32},{16,48},{32,0},{48,16},{64,96},{80,112},{96,64},{112,80},{1... | collective-permute-start | bytes 258056 | tf_op jit(solution)/shard_map/ppermute | solution.py:544
  76.7 3.2 %collective-permute-start.11 = (bf16[336,128]{1,0:T(8,128)(2,1)S(1)}, bf16[336,128]{1,0:T(8,128)(2,1)S(1)}, u32[]{:S(2)}, u32[]{:S(2)}) collective-permute-start(bf16[336,128]{1,0:T(8,128)(2,1)S(1)} %get-tuple-element.32), channel_id=1, source_target_pairs={{0,48},{16,32},{32,16},{48,0},{64,112},{80,96},{96,80},{112,64},{1... | collective-permute-start | bytes 258056 | tf_op jit(solution)/shard_map/ppermute | solution.py:544
  79.9 1.1 %collective-permute-start.9 = (bf16[336,128]{1,0:T(8,128)(2,1)S(1)}, bf16[336,128]{1,0:T(8,128)(2,1)S(1)}, u32[]{:S(2)}, u32[]{:S(2)}) collective-permute-start(bf16[336,128]{1,0:T(8,128)(2,1)S(1)} %get-tuple-element.30), channel_id=1, source_target_pairs={{0,16},{16,0},{32,48},{48,32},{64,80},{80,64},{96,112},{112,96},{1... | collective-permute-start | bytes 258056 | tf_op jit(solution)/shard_map/ppermute | solution.py:544
  81.0 4.0 %collective-permute-done.10.t2 = bf16[336,128]{1,0:T(8,128)(2,1)S(1)} collective-permute-done((bf16[336,128]{1,0:T(8,128)(2,1)S(1)}, bf16[336,128]{1,0:T(8,128)(2,1)S(1)}, u32[]{:S(2)}, u32[]{:S(2)}) %collective-permute-start.10) | collective-permute-done | bytes 86048 | tf_op jit(solution)/shard_map/ppermute | solution.py:544
  85.0 1.0 %collective-permute-done.11.t3 = bf16[336,128]{1,0:T(8,128)(2,1)S(1)} collective-permute-done((bf16[336,128]{1,0:T(8,128)(2,1)S(1)}, bf16[336,128]{1,0:T(8,128)(2,1)S(1)}, u32[]{:S(2)}, u32[]{:S(2)}) %collective-permute-start.11) | collective-permute-done | bytes 86048 | tf_op jit(solution)/shard_map/ppermute | solution.py:544
  86.1 1.7 %collective-permute-done.9.t1 = bf16[336,128]{1,0:T(8,128)(2,1)S(1)} collective-permute-done((bf16[336,128]{1,0:T(8,128)(2,1)S(1)}, bf16[336,128]{1,0:T(8,128)(2,1)S(1)}, u32[]{:S(2)}, u32[]{:S(2)}) %collective-permute-start.9) | collective-permute-done | bytes 86048 | tf_op jit(solution)/shard_map/ppermute | solution.py:544
  87.8 0.0 all-to-all-done.1.view_ref
  87.8 5.5 %join.1 = bf16[128,1280]{1,0:T(8,128)(2,1)} custom-call(bf16[16,144,128]{2,1,0:T(8,128)(2,1)S(1)} %all-to-all-done.1.view_ref, bf16[336,128]{1,0:T(8,128)(2,1)S(1)} %get-tuple-element.29.t0, bf16[336,128]{1,0:T(8,128)(2,1)S(1)} %collective-permute-done.9.t1, bf16[336,128]{1,0:T(8,128)(2,1)S(1)} %collective-permute-done.10.t2, ...), custom_call_target="tpu_custom_call" | custom-call | tf_op jit(solution)/shard_map/join/pallas_call | solution.py:527
  (4 shorter events, 0.1 us)
Async XLA Ops:
  3.0 16.7 %collective-permute-start.3 = (bf16[4,128,128]{2,1,0:T(8,128)(2,1)S(1)}, bf16[4,128,128]{2,1,0:T(8,128)(2,1)S(1)}, u32[]{:S(2)}, u32[]{:S(2)}) collective-permute-start(bf16[4,128,128]{2,1,0:T(8,128)(2,1)S(1)} %get-tuple-element.24.ring_ref), channel_id=1, source_target_pairs={{0,1},{1,0},{2,3},{3,2},{4,5},{5,4},{6,7},{7,6},{8,9},{9,8},{10,11... | collective-permute-start | bytes 393224 | tf_op jit(solution)/shard_map/ppermute | solution.py:552
  3.1 29.3 %collective-permute-start = (bf16[960,128]{1,0:T(8,128)(2,1)S(1)}, bf16[960,128]{1,0:T(8,128)(2,1)S(1)}, u32[]{:S(2)}, u32[]{:S(2)}) collective-permute-start(bf16[960,128]{1,0:T(8,128)(2,1)S(1)} %get-tuple-element.21), channel_id=1, source_target_pairs={{0,16},{16,0},{32,48},{48,32},{64,80},{80,64},{96,112},{112,96},{1... | collective-permute-start | bytes 737288 | tf_op jit(solution)/shard_map/ppermute | solution.py:544
  6.4 28.0 %collective-permute-start.1 = (bf16[960,128]{1,0:T(8,128)(2,1)S(1)}, bf16[960,128]{1,0:T(8,128)(2,1)S(1)}, u32[]{:S(2)}, u32[]{:S(2)}) collective-permute-start(bf16[960,128]{1,0:T(8,128)(2,1)S(1)} %get-tuple-element.22), channel_id=1, source_target_pairs={{0,32},{16,48},{32,0},{48,16},{64,96},{80,112},{96,64},{112,80},{1... | collective-permute-start | bytes 737288 | tf_op jit(solution)/shard_map/ppermute | solution.py:544
  11.8 22.6 %collective-permute-start.2 = (bf16[960,128]{1,0:T(8,128)(2,1)S(1)}, bf16[960,128]{1,0:T(8,128)(2,1)S(1)}, u32[]{:S(2)}, u32[]{:S(2)}) collective-permute-start(bf16[960,128]{1,0:T(8,128)(2,1)S(1)} %get-tuple-element.23), channel_id=1, source_target_pairs={{0,48},{16,32},{32,16},{48,0},{64,112},{80,96},{96,80},{112,64},{1... | collective-permute-start | bytes 737288 | tf_op jit(solution)/shard_map/ppermute | solution.py:544
  11.8 37.0 %all-to-all-start = ((bf16[16,256,128]{2,1,0:T(8,128)(2,1)}), bf16[16,256,128]{2,1,0:T(8,128)(2,1)S(1)}, u32[]{:S(2)}, u32[]{:S(2)}) async-start(bf16[16,256,128]{2,1,0:T(8,128)(2,1)} %get-tuple-element.19), calls=%async_computation | async-start | bytes 2097152 | tf_op jit(solution)/shard_map/all_to_all | solution.py:559
  19.7 8.3 %collective-permute-start.4 = (bf16[2,128,128]{2,1,0:T(8,128)(2,1)S(1)}, bf16[2,128,128]{2,1,0:T(8,128)(2,1)S(1)}, u32[]{:S(2)}, u32[]{:S(2)}) collective-permute-start(bf16[2,128,128]{2,1,0:T(8,128)(2,1)S(1)} %get-tuple-element.25), channel_id=1, source_target_pairs={{0,2},{2,0},{4,6},{6,4},{1,3},{3,1},{5,7},{7,5},{8,10},{10,8},{12,... | collective-permute-start | bytes 196616 | tf_op jit(solution)/shard_map/ppermute | solution.py:548
  19.9 10.6 %collective-permute-start.5 = (bf16[2,128,128]{2,1,0:T(8,128)(2,1)S(1)}, bf16[2,128,128]{2,1,0:T(8,128)(2,1)S(1)}, u32[]{:S(2)}, u32[]{:S(2)}) collective-permute-start(bf16[2,128,128]{2,1,0:T(8,128)(2,1)S(1)} %get-tuple-element.26), channel_id=1, source_target_pairs={{0,4},{2,6},{4,0},{6,2},{1,5},{3,7},{5,1},{7,3},{8,12},{10,14},{12... | collective-permute-start | bytes 196616 | tf_op jit(solution)/shard_map/ppermute | solution.py:548
  28.0 4.3 %collective-permute-start.6 = (bf16[2,128,128]{2,1,0:T(8,128)(2,1)S(1)}, bf16[2,128,128]{2,1,0:T(8,128)(2,1)S(1)}, u32[]{:S(2)}, u32[]{:S(2)}) collective-permute-start(bf16[2,128,128]{2,1,0:T(8,128)(2,1)S(1)} %get-tuple-element.27), channel_id=1, source_target_pairs={{0,6},{2,4},{4,2},{6,0},{1,7},{3,5},{5,3},{7,1},{8,14},{10,12},{12... | collective-permute-start | bytes 196616 | tf_op jit(solution)/shard_map/ppermute | solution.py:548
  34.4 14.7 %copy-start = (s32[8,32,32]{2,1,0:T(8,128)S(1)}, s32[8,32,32]{2,1,0:T(8,128)}, u32[]{:S(2)}) copy-start(s32[8,32,32]{2,1,0:T(8,128)} %mask_ref.3) | copy-start | bytes 98308
  34.4 0.7 copy-start.1
  35.1 29.6 %collective-permute-start.8 = (bf16[4,640,128]{2,1,0:T(8,128)(2,1)S(1)}, bf16[4,640,128]{2,1,0:T(8,128)(2,1)S(1)}, u32[]{:S(2)}, u32[]{:S(2)}) collective-permute-start(bf16[4,640,128]{2,1,0:T(8,128)(2,1)S(1)} %stack.1.refs_0_), channel_id=1, source_target_pairs={{0,64},{16,80},{32,96},{48,112},{64,0},{80,16},{96,32},{112,48},{1... | collective-permute-start | bytes 1966088 | tf_op jit(solution)/shard_map/ppermute | solution.py:544
  48.8 3.5 %collective-permute-start.7 = (bf16[16,128,128]{2,1,0:T(8,128)(2,1)S(1)}, bf16[16,128,128]{2,1,0:T(8,128)(2,1)S(1)}, u32[]{:S(2)}, u32[]{:S(2)}) collective-permute-start(bf16[16,128,128]{2,1,0:T(8,128)(2,1)S(1)} %keep.1), channel_id=1, source_target_pairs={{0,1},{1,0},{2,3},{3,2},{4,5},{5,4},{6,7},{7,6},{8,9},{9,8},{10,11... | collective-permute-start | bytes 1572872 | tf_op jit(solution)/shard_map/ppermute | solution.py:552
  52.3 17.2 %copy-start.2 = (bf16[960,128]{1,0:T(8,128)(2,1)S(1)}, bf16[960,128]{1,0:T(8,128)(2,1)}, u32[]{:S(2)}) copy-start(bf16[960,128]{1,0:T(8,128)(2,1)} %copy-done.1) | copy-start | bytes 737284
  52.3 17.2 %copy-start.3 = (s32[8]{0:T(128)S(1)}, s32[8]{0:T(128)}, u32[]{:S(2)}) copy-start(s32[8]{0:T(128)} %times_ref.1) | copy-start | bytes 100
  64.8 23.0 %all-to-all-start.1 = ((bf16[16,144,128]{2,1,0:T(8,128)(2,1)}), bf16[16,144,128]{2,1,0:T(8,128)(2,1)S(1)}, u32[]{:S(2)}, u32[]{:S(2)}) async-start(bf16[16,144,128]{2,1,0:T(8,128)(2,1)} %pass_after.1), calls=%async_computation.1 | async-start | bytes 1179648 | tf_op jit(solution)/shard_map/all_to_all | solution.py:569
  74.4 10.6 %collective-permute-start.10 = (bf16[336,128]{1,0:T(8,128)(2,1)S(1)}, bf16[336,128]{1,0:T(8,128)(2,1)S(1)}, u32[]{:S(2)}, u32[]{:S(2)}) collective-permute-start(bf16[336,128]{1,0:T(8,128)(2,1)S(1)} %get-tuple-element.31), channel_id=1, source_target_pairs={{0,32},{16,48},{32,0},{48,16},{64,96},{80,112},{96,64},{112,80},{1... | collective-permute-start | bytes 258056 | tf_op jit(solution)/shard_map/ppermute | solution.py:544
  76.7 9.3 %collective-permute-start.11 = (bf16[336,128]{1,0:T(8,128)(2,1)S(1)}, bf16[336,128]{1,0:T(8,128)(2,1)S(1)}, u32[]{:S(2)}, u32[]{:S(2)}) collective-permute-start(bf16[336,128]{1,0:T(8,128)(2,1)S(1)} %get-tuple-element.32), channel_id=1, source_target_pairs={{0,48},{16,32},{32,16},{48,0},{64,112},{80,96},{96,80},{112,64},{1... | collective-permute-start | bytes 258056 | tf_op jit(solution)/shard_map/ppermute | solution.py:544
  79.9 7.9 %collective-permute-start.9 = (bf16[336,128]{1,0:T(8,128)(2,1)S(1)}, bf16[336,128]{1,0:T(8,128)(2,1)S(1)}, u32[]{:S(2)}, u32[]{:S(2)}) collective-permute-start(bf16[336,128]{1,0:T(8,128)(2,1)S(1)} %get-tuple-element.30), channel_id=1, source_target_pairs={{0,16},{16,0},{32,48},{48,32},{64,80},{80,64},{96,112},{112,96},{1... | collective-permute-start | bytes 258056 | tf_op jit(solution)/shard_map/ppermute | solution.py:544

commit v5 on v4

--- a/solution.py
+++ b/solution.py
@@ -66,7 +66,7 @@
     return pltpu.with_memory_space_constraint(x, pltpu.HBM)
 
 
-def pack_kernel(q_hbm, k_hbm, v_hbm, z0, z1, z2, z3, ring_ref, view_ref, q_ref, k_ref, v_ref, sems, parts):
+def pack_kernel(q_hbm, k_hbm, v_hbm, x0, z0, z1, z2, z3, ring_ref, view_ref, q_ref, k_ref, v_ref, sems, parts):
     place = lax.axis_index("f") % 4
     load = pltpu.make_async_copy(q_hbm, q_ref, sems.at[2])
     load.start()
@@ -88,6 +88,7 @@
         parts[j, 896:960] = jnp.concatenate([last[0:64], last[64:128]], axis=1)
     for k, out in enumerate((z0, z1, z2, z3)):
         out[...] = parts[turned(place, k)]
+    x0[...] = z0[0:X_ROWS]
     for t in range(MAIN):
         view_ref[t, CELLS : 2 * CELLS] = pair(q_ref, t, q_ref, MAIN + t % RING)
 
@@ -97,13 +98,14 @@
     whole = pltpu.VMEM((CELLS, HEADS * HEAD), BF16)
     return pl.pallas_call(
         pack_kernel,
-        out_shape=[block] * 4
+        out_shape=[jax.ShapeDtypeStruct((X_ROWS, CELLS), BF16)]
+        + [block] * 4
         + [
             jax.ShapeDtypeStruct((RING, CELLS, CELLS), BF16),
             jax.ShapeDtypeStruct((MAIN, 2 * CELLS, CELLS), BF16),
         ],
         in_specs=[ANY] * 3,
-        out_specs=[VMEM] * 6,
+        out_specs=[VMEM] * 7,
         scratch_shapes=[whole] * 3 + [pltpu.SemaphoreType.DMA((3,)), pltpu.VMEM((4, Z_ROWS, CELLS), BF16)],
         compiler_params=params(16),
         name="pack",
@@ -128,22 +130,19 @@
     )(ring, other)
 
 
-def stack_kernel(z0, z1, z2, z3, *refs):
-    out_ref = refs[-1]
-    for k, piece in enumerate((z0, z1, z2, z3)):
-        out_ref[k] = piece[0:X_ROWS]
-
-
-def stack(z, order):
-    return pl.pallas_call(
-        stack_kernel,
-        out_shape=jax.ShapeDtypeStruct((4, X_ROWS, CELLS), BF16),
-        in_specs=[VMEM] * 4 + [ANY] * len(order),
+def strip_kernel(z_ref, *refs):
+    refs[-1][...] = z_ref[0:X_ROWS]
+
+
+def strip(z, order=()):
+    return pl.pallas_call(
+        strip_kernel,
+        out_shape=jax.ShapeDtypeStruct((X_ROWS, CELLS), BF16),
+        in_specs=[VMEM] + [ANY] * len(order),
         out_specs=VMEM,
         compiler_params=params(4),
-        cost_estimate=pl.CostEstimate(flops=18000000000, bytes_accessed=100000, transcendentals=0),
-        name="stack",
-    )(*z, *order)
+        name="strip",
+    )(z, *order)
 
 
 def keep_kernel(own_ref, *refs):
@@ -355,11 +354,11 @@
     )(own, *pieces, view_mask)
 
 
-def time_kernel(z0, z1, z2, z3, x_ref, times_ref, o0, o1, o2, o3, key_s, value_s, q_s, s_ref):
+def time_kernel(z0, z1, z2, z3, x0, x1, x2, x3, times_ref, o0, o1, o2, o3, key_s, value_s, q_s, s_ref):
     frame = lax.axis_index("f")
     lane = lanes((CELLS, CELLS))
     own = (z0, z1, z2, z3)
-    far = tuple(x_ref.at[k] for k in range(4))
+    far = (x0, x1, x2, x3)
     outs = (o0, o1, o2, o3)
 
     l8, r8 = lanes((8, 128)), rows_of((8, 128))
@@ -429,7 +428,7 @@
     return pl.pallas_call(
         time_kernel,
         out_shape=[jax.ShapeDtypeStruct((T_ROWS, CELLS), BF16)] * 4,
-        in_specs=[VMEM] * 5 + [SMEM],
+        in_specs=[VMEM] * 8 + [SMEM],
         out_specs=[VMEM] * 4,
         scratch_shapes=[
             pltpu.VMEM((5, 1024, CELLS), BF16),
@@ -438,30 +437,16 @@
             pltpu.VMEM((2, TILE, 1024), F32),
         ],
         compiler_params=params(16),
-        cost_estimate=pl.CostEstimate(flops=700000000, bytes_accessed=2000000, transcendentals=2700000),
+        cost_estimate=pl.CostEstimate(flops=17000000000, bytes_accessed=2000000, transcendentals=2700000),
         name="time_attention",
-    )(*own, crossed, frame_times)
-
-
-def pass_kernel(*refs):
-    del refs
-
-
-def pass_after(array, others):
-    return pl.pallas_call(
-        pass_kernel,
-        out_shape=pltpu.HBM(array.shape, array.dtype),
-        in_specs=[ANY] * (1 + len(others)),
-        out_specs=ANY,
-        input_output_aliases={0: 0},
-        compiler_params=params(4),
-        name="pass_after",
-    )(in_hbm(array), *others)
+    )(*own, *crossed, frame_times)
 
 
 def join_kernel(view_ref, t0, t1, t2, t3, weight_any, out_ref, times, heads_s, weight_ref, sems):
-    load = pltpu.make_async_copy(weight_any, weight_ref, sems.at[0])
-    load.start()
+    chunks = [pl.ds(i * 256, 256) for i in range(5)]
+    loads = [pltpu.make_async_copy(weight_any.at[c], weight_ref.at[c], sems.at[i]) for i, c in enumerate(chunks)]
+    for load in loads:
+        load.start()
     place = lax.axis_index("f") % 4
     for k, piece in enumerate((t0, t1, t2, t3)):
         times[turned(place, k)] = piece[...]
@@ -497,28 +482,46 @@
         total = total + power
     shares = [power / total for power in powers]
 
-    def time_block(head):
+    def spread(share, first, count):
+        pick = lanes((CELLS, count * HEAD)) // HEAD + first == rows_of((CELLS, count * HEAD))
+        pick = jnp.where(pick, 1.0, 0.0).astype(BF16)
+        high = share.astype(BF16)
+        rest = (share - high.astype(F32)).astype(BF16)
+        return jnp.dot(high, pick, preferred_element_type=F32) + jnp.dot(rest, pick, preferred_element_type=F32)
+
+    view_share, time_share = spread(shares[0], 0, HEADS), spread(shares[4], 0, HEADS)
+    ring_share = [view_share[:, MAIN * HEAD :]] + [spread(shares[ring], MAIN, RING) for ring in (1, 2, 3)]
+    left = column < HEAD
+
+    def time_half(head, side):
         j, i = head // 5, head % 5
         if i < 4:
-            rows = slice((i // 2) * CELLS, (i // 2 + 1) * CELLS)
-            return times[j, rows, (i % 2) * HEAD : (i % 2 + 1) * HEAD].astype(F32)
+            block = times[j, (i // 2) * CELLS : (i // 2 + 1) * CELLS].astype(F32)
+            return block if i % 2 == side else swap_halves(block)
         packed = times[j, 256:320].astype(F32)
-        return jnp.concatenate([packed[:, 0:HEAD], packed[:, HEAD:128]], axis=0)
-
-    load.wait()
+        turn = swap_halves(packed)
+        return jnp.concatenate([turn, packed] if side else [packed, turn], axis=0)
+
+    def view_half(head, ring, side):
+        if head < MAIN:
+            block = view_ref[head, 0:CELLS].astype(F32)
+            return swap_halves(block) if side else block
+        block = view_ref[4 * ring + head - MAIN, 0:CELLS].astype(F32)
+        return block if side else swap_halves(block)
+
     result = None
-    for first in range(0, HEADS, 4):
-        for h in range(first, first + 4):
-            mixed = time_block(h) * shares[4][:, h : h + 1]
-            if h < MAIN:
-                mixed += view_ref[h, 0:CELLS, 0:HEAD].astype(F32) * shares[0][:, h : h + 1]
-            else:
-                for ring in range(4):
-                    block = view_ref[4 * ring + h - MAIN, 0:CELLS, HEAD:128].astype(F32)
-                    mixed += block * shares[ring][:, h : h + 1]
-            heads_s[:, h * HEAD : (h + 1) * HEAD] = mixed.astype(BF16)
-        columns = slice(first * HEAD, (first + 4) * HEAD)
-        product = jnp.dot(heads_s[:, columns], weight_ref[columns], preferred_element_type=F32)
+    for step in range(5):
+        for p in (2 * step, 2 * step + 1):
+            here = slice(p * CELLS, (p + 1) * CELLS)
+            mixed = jnp.where(left, time_half(2 * p, 0), time_half(2 * p + 1, 1)) * time_share[:, here]
+            for ring in range(1 if p < 8 else 4):
+                block = jnp.where(left, view_half(2 * p, ring, 0), view_half(2 * p + 1, ring, 1))
+                share = view_share[:, here] if p < 8 else ring_share[ring][:, (p - 8) * CELLS : (p - 7) * CELLS]
+                mixed += block * share
+            heads_s[:, here] = mixed.astype(BF16)
+        loads[step].wait()
+        rows = slice(step * 256, (step + 1) * 256)
+        product = jnp.dot(heads_s[:, rows], weight_ref[rows], preferred_element_type=F32)
         result = product if result is None else result + product
     out_ref[...] = result.astype(BF16)
 
@@ -533,7 +536,7 @@
             pltpu.VMEM((4, T_ROWS, CELLS), BF16),
             pltpu.VMEM((CELLS, HEADS * HEAD), BF16),
             pltpu.VMEM((HEADS * HEAD, HEADS * HEAD), BF16),
-            pltpu.SemaphoreType.DMA((1,)),
+            pltpu.SemaphoreType.DMA((5,)),
         ],
         compiler_params=params(16),
         name="join",
@@ -555,19 +558,17 @@
 def local(queries, keys, values, view_mask, frame_times, out_weight):
     model = queries.shape[3]
     q, k, v = (a.reshape(CELLS, model) for a in (queries, keys, values))
-    *z, to_ring, to_view = pack(q, k, v)
+    x0, *z, to_ring, to_view = pack(q, k, v)
     own = lax.all_to_all(to_view, ("g", "zl", "y"), 0, 0)
     z = [z[0]] + [across(z[i], i) for i in (1, 2, 3)]
     ring = ring_pack(to_ring, sibling(to_ring))
     ring = [ring[0]] + [around(ring[i], i) for i in (1, 2, 3)]
-    some = stack(z, ring[1:])
-    crossed = across(some, 4)
-    other = sibling(keep(own, [some]))
+    crossed = [across(x0, 4)] + [across(strip(z[i], ring[1:] if i == 1 else ()), 4) for i in (1, 2, 3)]
+    pieces = time_attention(z, crossed, frame_times)
+    other = sibling(keep(own, pieces[:1]))
     ring_out = ring_attention(own, ring, view_mask)
     view_out = view_attention(own, other, ring_out, view_mask)
-    view_out = pass_after(view_out, (crossed,))
     view_back = lax.all_to_all(view_out, ("g", "zl", "y"), 0, 0)
-    pieces = time_attention(z, crossed, frame_times)
     pieces = [pieces[0]] + [across(pieces[i], i) for i in (1, 2, 3)]
     result = join(view_back, pieces, out_weight)
     return result.reshape(1, 1, CELLS, model)

time: 94.7 us -> 104 us (1.098)
  waiting for transfers between devices: 29 us -> 35.8 us
  starting transfers between devices: 34.4 us -> 40 us
  Pallas kernels: 29.1 us -> 26.7 us
    ppermute x7 -> x10, waiting for transfers between devices: 8.85 us -> 28.4 us  [across(): return lax.ppermute(array, 'f', [(i, i ^ k) for i in range(FRAMES)])]
    all_to_all x1, waiting for transfers between devices: 12.2 us -> 0.01 us  [local(): own = lax.all_to_all(to_view, ('g', 'zl', 'y'), 0, 0)]
    all_to_all x1, starting transfers between devices: 4.73 us -> 8.43 us  [local(): view_back = lax.all_to_all(view_out, ('g', 'zl', 'y'), 0, 0)]
    pallas_call x1, Pallas kernels: 5.49 us -> 3.03 us  [join(): pl.pallas_call(join_kernel, out_shape=jax.ShapeDtypeStruct((CELLS, HEADS...]
    ppermute x7 -> x10, starting transfers between devices: 16.8 us -> 18.7 us  [across(): return lax.ppermute(array, 'f', [(i, i ^ k) for i in range(FRAMES)])]
    pallas_call x3 -> x4, Pallas kernels: 2.99 us -> 3 us  [the longest x1 2.97 us: pack(): pl.pallas_call(pack_kernel, out_shape=[jax.ShapeDtypeStruct((X_ROWS, CELL...]
  transfers between devices with their start and end apart: 14 -> 17, of which waited for: 8 -> 10; matrix products, arithmetic and copies ran while one was open for 0% -> 0% of each run, Pallas kernels for 22% -> 8%
where the time goes in v5:
time: 104 us; the launch traced here: 103 us
  starting transfers between devices  40 us (38%)
  waiting for transfers between devices  35.8 us (34%)
  Pallas kernels  26.7 us (26%)
    ppermute x10, waiting for transfers between devices, across(): return lax.ppermute(array, 'f', [(i, i ^ k) for i in range(FRAMES)])  28.4 us
    ppermute x10, starting transfers between devices, across(): return lax.ppermute(array, 'f', [(i, i ^ k) for i in range(FRAMES)])  18.7 us
    pallas_call x1, Pallas kernels, view_attention(): pl.pallas_call(view_kernel, out_shape=pltpu.HBM((MAIN, O_ROWS, CELLS), BF...  12.5 us
    all_to_all x1, starting transfers between devices, local(): view_back = lax.all_to_all(view_out, ('g', 'zl', 'y'), 0, 0)  8.43 us
    all_to_all x1, starting transfers between devices, local(): own = lax.all_to_all(to_view, ('g', 'zl', 'y'), 0, 0)  7.85 us
    ppermute x3, waiting for transfers between devices, around(): return lax.ppermute(array, 'y', [(i, i ^ k) for i in range(RING)])  7.38 us
    pallas_call x1, Pallas kernels, time_attention(): pl.pallas_call(time_kernel, out_shape=[jax.ShapeDtypeStruct((T_ROWS, CELL...  4.95 us
    ppermute x3, starting transfers between devices, around(): return lax.ppermute(array, 'y', [(i, i ^ k) for i in range(RING)])  4.64 us
  transfers between devices with their start and end apart: 17, of which 10 were waited for; matrix products, arithmetic and copies ran while one was open for 0% of the time, Pallas kernels for 8%

profile of v5, /device:TPU:8, one launch (start us, length us, event | category | flops | bytes accessed | tf_op | source)
XLA Modules:
  0.0 102.8 jit_solution(16339085415659776657)
XLA Ops:
  0.0 0.0 copy-start.1
  0.0 3.0 %pack.1 = (bf16[640,128]{1,0:T(8,128)(2,1)S(1)}, bf16[960,128]{1,0:T(8,128)(2,1)S(1)}, bf16[960,128]{1,0:T(8,128)(2,1)S(1)}, bf16[960,128]{1,0:T(8,128)(2,1)S(1)...) custom-call(bf16[128,1280]{1,0:T(8,128)(2,1)} %bitcast.4, ...), custom_call_target="tpu_custom_call" | custom-call | tf_op jit(solution)/shard_map/pack/pallas_call | solution.py:99
  3.0 0.1 collective-permute-start.4
  3.1 3.4 %collective-permute-start = (bf16[960,128]{1,0:T(8,128)(2,1)S(1)}, bf16[960,128]{1,0:T(8,128)(2,1)S(1)}, u32[]{:S(2)}, u32[]{:S(2)}) collective-permute-start(bf16[960,128]{1,0:T(8,128)(2,1)S(1)} %get-tuple-element.22), channel_id=1, source_target_pairs={{0,16},{16,0},{32,48},{48,32},{64,80},{80,64},{96,112},{112,96},{1... | collective-permute-start | bytes 737288 | tf_op jit(solution)/shard_map/ppermute | solution.py:547
  6.4 5.4 %collective-permute-start.1 = (bf16[960,128]{1,0:T(8,128)(2,1)S(1)}, bf16[960,128]{1,0:T(8,128)(2,1)S(1)}, u32[]{:S(2)}, u32[]{:S(2)}) collective-permute-start(bf16[960,128]{1,0:T(8,128)(2,1)S(1)} %get-tuple-element.23), channel_id=1, source_target_pairs={{0,32},{16,48},{32,0},{48,16},{64,96},{80,112},{96,64},{112,80},{1... | collective-permute-start | bytes 737288 | tf_op jit(solution)/shard_map/ppermute | solution.py:547
  11.8 0.0 collective-permute-start.2
  11.8 7.8 %all-to-all-start = ((bf16[16,256,128]{2,1,0:T(8,128)(2,1)}), bf16[16,256,128]{2,1,0:T(8,128)(2,1)S(1)}, u32[]{:S(2)}, u32[]{:S(2)}) async-start(bf16[16,256,128]{2,1,0:T(8,128)(2,1)} %get-tuple-element.20), calls=%async_computation | async-start | bytes 2097152 | tf_op jit(solution)/shard_map/all_to_all | solution.py:562
  19.7 0.0 collective-permute-done.4.sibling_ref
  19.7 0.2 collective-permute-start.5
  19.9 2.8 %collective-permute-start.6 = (bf16[2,128,128]{2,1,0:T(8,128)(2,1)S(1)}, bf16[2,128,128]{2,1,0:T(8,128)(2,1)S(1)}, u32[]{:S(2)}, u32[]{:S(2)}) collective-permute-start(bf16[2,128,128]{2,1,0:T(8,128)(2,1)S(1)} %get-tuple-element.28), channel_id=1, source_target_pairs={{0,4},{2,6},{4,0},{6,2},{1,5},{3,7},{5,1},{7,3},{8,12},{10,14},{12... | collective-permute-start | bytes 196616 | tf_op jit(solution)/shard_map/ppermute | solution.py:551
  22.7 5.3 %collective-permute-done.5.refs_0_.r1 = bf16[2,128,128]{2,1,0:T(8,128)(2,1)S(1)} collective-permute-done((bf16[2,128,128]{2,1,0:T(8,128)(2,1)S(1)}, bf16[2,128,128]{2,1,0:T(8,128)(2,1)S(1)}, u32[]{:S(2)}, u32[]{:S(2)}) %collective-permute-start.5) | collective-permute-done | bytes 65568 | tf_op jit(solution)/shard_map/ppermute | solution.py:551
  28.1 1.6 %collective-permute-start.7 = (bf16[2,128,128]{2,1,0:T(8,128)(2,1)S(1)}, bf16[2,128,128]{2,1,0:T(8,128)(2,1)S(1)}, u32[]{:S(2)}, u32[]{:S(2)}) collective-permute-start(bf16[2,128,128]{2,1,0:T(8,128)(2,1)S(1)} %get-tuple-element.29), channel_id=1, source_target_pairs={{0,6},{2,4},{4,2},{6,0},{1,7},{3,5},{5,3},{7,1},{8,14},{10,12},{12... | collective-permute-start | bytes 196616 | tf_op jit(solution)/shard_map/ppermute | solution.py:551
  29.7 0.8 collective-permute-done.6.refs_1_.r2
  30.5 0.6 collective-permute-start.3
  31.1 1.2 %collective-permute-done.7.refs_2_.r3 = bf16[2,128,128]{2,1,0:T(8,128)(2,1)S(1)} collective-permute-done((bf16[2,128,128]{2,1,0:T(8,128)(2,1)S(1)}, bf16[2,128,128]{2,1,0:T(8,128)(2,1)S(1)}, u32[]{:S(2)}, u32[]{:S(2)}) %collective-permute-start.7) | collective-permute-done | bytes 65568 | tf_op jit(solution)/shard_map/ppermute | solution.py:551
  32.3 0.0 collective-permute-done.z_ref.z1
  32.4 0.7 collective-permute-start.8
  33.0 1.4 %collective-permute-done.1.z_ref.z2 = bf16[960,128]{1,0:T(8,128)(2,1)S(1)} collective-permute-done((bf16[960,128]{1,0:T(8,128)(2,1)S(1)}, bf16[960,128]{1,0:T(8,128)(2,1)S(1)}, u32[]{:S(2)}, u32[]{:S(2)}) %collective-permute-start.1) | collective-permute-done | bytes 245792 | tf_op jit(solution)/shard_map/ppermute | solution.py:547
  34.4 1.6 %collective-permute-start.9 = (bf16[640,128]{1,0:T(8,128)(2,1)S(1)}, bf16[640,128]{1,0:T(8,128)(2,1)S(1)}, u32[]{:S(2)}, u32[]{:S(2)}) collective-permute-start(bf16[640,128]{1,0:T(8,128)(2,1)S(1)} %strip.4), channel_id=1, source_target_pairs={{0,64},{16,80},{32,96},{48,112},{64,0},{80,16},{96,32},{112,48},{1... | collective-permute-start | bytes 491528 | tf_op jit(solution)/shard_map/ppermute | solution.py:547
  36.0 0.0 collective-permute-done.2.z_ref.z3
  36.0 0.6 collective-permute-start.10
  36.6 5.7 %collective-permute-done.3.x0 = bf16[640,128]{1,0:T(8,128)(2,1)S(1)} collective-permute-done((bf16[640,128]{1,0:T(8,128)(2,1)S(1)}, bf16[640,128]{1,0:T(8,128)(2,1)S(1)}, u32[]{:S(2)}, u32[]{:S(2)}) %collective-permute-start.3) | collective-permute-done | bytes 163872 | tf_op jit(solution)/shard_map/ppermute | solution.py:547
  42.4 4.1 %collective-permute-done.8.x1 = bf16[640,128]{1,0:T(8,128)(2,1)S(1)} collective-permute-done((bf16[640,128]{1,0:T(8,128)(2,1)S(1)}, bf16[640,128]{1,0:T(8,128)(2,1)S(1)}, u32[]{:S(2)}, u32[]{:S(2)}) %collective-permute-start.8) | collective-permute-done | bytes 163872 | tf_op jit(solution)/shard_map/ppermute | solution.py:547
  46.4 2.3 %collective-permute-done.9.x2 = bf16[640,128]{1,0:T(8,128)(2,1)S(1)} collective-permute-done((bf16[640,128]{1,0:T(8,128)(2,1)S(1)}, bf16[640,128]{1,0:T(8,128)(2,1)S(1)}, u32[]{:S(2)}, u32[]{:S(2)}) %collective-permute-start.9) | collective-permute-done | bytes 163872 | tf_op jit(solution)/shard_map/ppermute | solution.py:547
  48.7 1.8 %collective-permute-done.10.x3 = bf16[640,128]{1,0:T(8,128)(2,1)S(1)} collective-permute-done((bf16[640,128]{1,0:T(8,128)(2,1)S(1)}, bf16[640,128]{1,0:T(8,128)(2,1)S(1)}, u32[]{:S(2)}, u32[]{:S(2)}) %collective-permute-start.10) | collective-permute-done | bytes 163872 | tf_op jit(solution)/shard_map/ppermute | solution.py:547
  50.5 0.0 copy-done.1
  50.5 0.0 copy-start
  50.5 5.0 %time_attention.1 = (bf16[336,128]{1,0:T(8,128)(2,1)S(1)}, bf16[336,128]{1,0:T(8,128)(2,1)S(1)}, bf16[336,128]{1,0:T(8,128)(2,1)S(1)}, bf16[336,128]{1,0:T(8,128)(2,1)S(1)}) custom-call(bf16[960,128]{1,0:T(8,128)(2,1)S(1)} %get-tuple-element.21.z0, bf16[960,128]{1,0:T(8,128)(2,1)S(1)} %collective-permute-done.z_ref.z1, ...), custom_call_target="tpu_custom_call" | custom-call | flops 16999999488 | bytes 2000000 | tf_op jit(solution)/shard_map/time_attention/pallas_call | solution.py:428
  55.4 0.0 all-to-all-done.own_ref
  55.4 0.1 keep.1
  55.5 0.3 collective-permute-start.11
  55.8 0.0 copy-done
  55.8 3.2 %ring_attention.1.ring_ref = bf16[16,144,128]{2,1,0:T(8,128)(2,1)S(1)} custom-call(bf16[16,256,128]{2,1,0:T(8,128)(2,1)S(1)} %all-to-all-done.own_ref, bf16[2,128,128]{2,1,0:T(8,128)(2,1)S(1)} %get-tuple-element.31.r0, bf16[2,128,128]{2,1,0:T(8,128)(2,1)S(1)} %collective-permute-done.5.refs_0_.r1, ...), custom_call_target="tpu_custom_call" | custom-call | flops 1000000 | bytes 100000 | tf_op jit(solution)/shard_map/ring_attention/pallas_call | solution.py:341
  59.0 0.0 collective-permute-done.11.other_ref
  59.0 12.5 %view_attention.1 = bf16[16,144,128]{2,1,0:T(8,128)(2,1)} custom-call(bf16[16,256,128]{2,1,0:T(8,128)(2,1)S(1)} %all-to-all-done.own_ref, bf16[16,128,128]{2,1,0:T(8,128)(2,1)S(1)} %collective-permute-done.11.other_ref, bf16[16,144,128]{2,1,0:T(8,128)(2,1)S(1)} %ring_attention.1.ring_ref, s32[8,32,32]{2,1,0:T(8,128)S(1)} %copy-done), custom_call_target="tpu_custom_call" | custom-call | flops 1000000 | bytes 100000 | tf_op jit(solution)/shard_map/view_attention/pallas_call | solution.py:284
  71.5 8.4 %all-to-all-start.1 = ((bf16[16,144,128]{2,1,0:T(8,128)(2,1)}), bf16[16,144,128]{2,1,0:T(8,128)(2,1)S(1)}, u32[]{:S(2)}, u32[]{:S(2)}) async-start(bf16[16,144,128]{2,1,0:T(8,128)(2,1)} %view_attention.1), calls=%async_computation.1 | async-start | bytes 1179648 | tf_op jit(solution)/shard_map/all_to_all | solution.py:571
  79.9 2.1 %collective-permute-start.12 = (bf16[336,128]{1,0:T(8,128)(2,1)S(1)}, bf16[336,128]{1,0:T(8,128)(2,1)S(1)}, u32[]{:S(2)}, u32[]{:S(2)}) collective-permute-start(bf16[336,128]{1,0:T(8,128)(2,1)S(1)} %get-tuple-element.32), channel_id=1, source_target_pairs={{0,16},{16,0},{32,48},{48,32},{64,80},{80,64},{96,112},{112,96},{1... | collective-permute-start | bytes 258056 | tf_op jit(solution)/shard_map/ppermute | solution.py:547
  82.0 4.4 %collective-permute-start.13 = (bf16[336,128]{1,0:T(8,128)(2,1)S(1)}, bf16[336,128]{1,0:T(8,128)(2,1)S(1)}, u32[]{:S(2)}, u32[]{:S(2)}) collective-permute-start(bf16[336,128]{1,0:T(8,128)(2,1)S(1)} %get-tuple-element.33), channel_id=1, source_target_pairs={{0,32},{16,48},{32,0},{48,16},{64,96},{80,112},{96,64},{112,80},{1... | collective-permute-start | bytes 258056 | tf_op jit(solution)/shard_map/ppermute | solution.py:547
  86.4 0.0 collective-permute-start.14
  86.4 2.9 %collective-permute-done.12.t1 = bf16[336,128]{1,0:T(8,128)(2,1)S(1)} collective-permute-done((bf16[336,128]{1,0:T(8,128)(2,1)S(1)}, bf16[336,128]{1,0:T(8,128)(2,1)S(1)}, u32[]{:S(2)}, u32[]{:S(2)}) %collective-permute-start.12) | collective-permute-done | bytes 86048 | tf_op jit(solution)/shard_map/ppermute | solution.py:547
  89.3 10.3 %collective-permute-done.13.t2 = bf16[336,128]{1,0:T(8,128)(2,1)S(1)} collective-permute-done((bf16[336,128]{1,0:T(8,128)(2,1)S(1)}, bf16[336,128]{1,0:T(8,128)(2,1)S(1)}, u32[]{:S(2)}, u32[]{:S(2)}) %collective-permute-start.13) | collective-permute-done | bytes 86048 | tf_op jit(solution)/shard_map/ppermute | solution.py:547
  99.6 0.0 collective-permute-done.14.t3
  99.6 0.0 all-to-all-done.1.view_ref
  99.6 3.0 %join.1 = bf16[128,1280]{1,0:T(8,128)(2,1)} custom-call(bf16[16,144,128]{2,1,0:T(8,128)(2,1)S(1)} %all-to-all-done.1.view_ref, bf16[336,128]{1,0:T(8,128)(2,1)S(1)} %get-tuple-element.30.refs_0_.t0, bf16[336,128]{1,0:T(8,128)(2,1)S(1)} %collective-permute-done.12.t1, bf16[336,128]{1,0:T(8,128)(2,1)S(1)} %collective-permute-done.13.t2, ...), custom_call_target="tpu_custom_call" | custom-call | tf_op jit(solution)/shard_map/join/pallas_call | solution.py:530
  (4 shorter events, 0.1 us)
Async XLA Ops:
  0.0 50.5 %copy-start.1 = (s32[8]{0:T(128)S(1)}, s32[8]{0:T(128)}, u32[]{:S(2)}) copy-start(s32[8]{0:T(128)} %times_ref.1) | copy-start | bytes 100
  3.0 16.7 %collective-permute-start.4 = (bf16[4,128,128]{2,1,0:T(8,128)(2,1)S(1)}, bf16[4,128,128]{2,1,0:T(8,128)(2,1)S(1)}, u32[]{:S(2)}, u32[]{:S(2)}) collective-permute-start(bf16[4,128,128]{2,1,0:T(8,128)(2,1)S(1)} %get-tuple-element.26.ring_ref), channel_id=1, source_target_pairs={{0,1},{1,0},{2,3},{3,2},{4,5},{5,4},{6,7},{7,6},{8,9},{9,8},{10,11... | collective-permute-start | bytes 393224 | tf_op jit(solution)/shard_map/ppermute | solution.py:555
  3.1 29.3 %collective-permute-start = (bf16[960,128]{1,0:T(8,128)(2,1)S(1)}, bf16[960,128]{1,0:T(8,128)(2,1)S(1)}, u32[]{:S(2)}, u32[]{:S(2)}) collective-permute-start(bf16[960,128]{1,0:T(8,128)(2,1)S(1)} %get-tuple-element.22), channel_id=1, source_target_pairs={{0,16},{16,0},{32,48},{48,32},{64,80},{80,64},{96,112},{112,96},{1... | collective-permute-start | bytes 737288 | tf_op jit(solution)/shard_map/ppermute | solution.py:547
  6.4 28.0 %collective-permute-start.1 = (bf16[960,128]{1,0:T(8,128)(2,1)S(1)}, bf16[960,128]{1,0:T(8,128)(2,1)S(1)}, u32[]{:S(2)}, u32[]{:S(2)}) collective-permute-start(bf16[960,128]{1,0:T(8,128)(2,1)S(1)} %get-tuple-element.23), channel_id=1, source_target_pairs={{0,32},{16,48},{32,0},{48,16},{64,96},{80,112},{96,64},{112,80},{1... | collective-permute-start | bytes 737288 | tf_op jit(solution)/shard_map/ppermute | solution.py:547
  11.8 24.2 %collective-permute-start.2 = (bf16[960,128]{1,0:T(8,128)(2,1)S(1)}, bf16[960,128]{1,0:T(8,128)(2,1)S(1)}, u32[]{:S(2)}, u32[]{:S(2)}) collective-permute-start(bf16[960,128]{1,0:T(8,128)(2,1)S(1)} %get-tuple-element.24), channel_id=1, source_target_pairs={{0,48},{16,32},{32,16},{48,0},{64,112},{80,96},{96,80},{112,64},{1... | collective-permute-start | bytes 737288 | tf_op jit(solution)/shard_map/ppermute | solution.py:547
  11.8 43.6 %all-to-all-start = ((bf16[16,256,128]{2,1,0:T(8,128)(2,1)}), bf16[16,256,128]{2,1,0:T(8,128)(2,1)S(1)}, u32[]{:S(2)}, u32[]{:S(2)}) async-start(bf16[16,256,128]{2,1,0:T(8,128)(2,1)} %get-tuple-element.20), calls=%async_computation | async-start | bytes 2097152 | tf_op jit(solution)/shard_map/all_to_all | solution.py:562
  19.7 8.3 %collective-permute-start.5 = (bf16[2,128,128]{2,1,0:T(8,128)(2,1)S(1)}, bf16[2,128,128]{2,1,0:T(8,128)(2,1)S(1)}, u32[]{:S(2)}, u32[]{:S(2)}) collective-permute-start(bf16[2,128,128]{2,1,0:T(8,128)(2,1)S(1)} %get-tuple-element.27), channel_id=1, source_target_pairs={{0,2},{2,0},{4,6},{6,4},{1,3},{3,1},{5,7},{7,5},{8,10},{10,8},{12,... | collective-permute-start | bytes 196616 | tf_op jit(solution)/shard_map/ppermute | solution.py:551
  19.9 10.6 %collective-permute-start.6 = (bf16[2,128,128]{2,1,0:T(8,128)(2,1)S(1)}, bf16[2,128,128]{2,1,0:T(8,128)(2,1)S(1)}, u32[]{:S(2)}, u32[]{:S(2)}) collective-permute-start(bf16[2,128,128]{2,1,0:T(8,128)(2,1)S(1)} %get-tuple-element.28), channel_id=1, source_target_pairs={{0,4},{2,6},{4,0},{6,2},{1,5},{3,7},{5,1},{7,3},{8,12},{10,14},{12... | collective-permute-start | bytes 196616 | tf_op jit(solution)/shard_map/ppermute | solution.py:551
  28.1 4.3 %collective-permute-start.7 = (bf16[2,128,128]{2,1,0:T(8,128)(2,1)S(1)}, bf16[2,128,128]{2,1,0:T(8,128)(2,1)S(1)}, u32[]{:S(2)}, u32[]{:S(2)}) collective-permute-start(bf16[2,128,128]{2,1,0:T(8,128)(2,1)S(1)} %get-tuple-element.29), channel_id=1, source_target_pairs={{0,6},{2,4},{4,2},{6,0},{1,7},{3,5},{5,3},{7,1},{8,14},{10,12},{12... | collective-permute-start | bytes 196616 | tf_op jit(solution)/shard_map/ppermute | solution.py:551
  30.5 11.8 %collective-permute-start.3 = (bf16[640,128]{1,0:T(8,128)(2,1)S(1)}, bf16[640,128]{1,0:T(8,128)(2,1)S(1)}, u32[]{:S(2)}, u32[]{:S(2)}) collective-permute-start(bf16[640,128]{1,0:T(8,128)(2,1)S(1)} %get-tuple-element.25), channel_id=1, source_target_pairs={{0,64},{16,80},{32,96},{48,112},{64,0},{80,16},{96,32},{112,48},{1... | collective-permute-start | bytes 491528 | tf_op jit(solution)/shard_map/ppermute | solution.py:547
  32.4 14.1 %collective-permute-start.8 = (bf16[640,128]{1,0:T(8,128)(2,1)S(1)}, bf16[640,128]{1,0:T(8,128)(2,1)S(1)}, u32[]{:S(2)}, u32[]{:S(2)}) collective-permute-start(bf16[640,128]{1,0:T(8,128)(2,1)S(1)} %strip.3), channel_id=1, source_target_pairs={{0,64},{16,80},{32,96},{48,112},{64,0},{80,16},{96,32},{112,48},{1... | collective-permute-start | bytes 491528 | tf_op jit(solution)/shard_map/ppermute | solution.py:547
  34.4 14.3 %collective-permute-start.9 = (bf16[640,128]{1,0:T(8,128)(2,1)S(1)}, bf16[640,128]{1,0:T(8,128)(2,1)S(1)}, u32[]{:S(2)}, u32[]{:S(2)}) collective-permute-start(bf16[640,128]{1,0:T(8,128)(2,1)S(1)} %strip.4), channel_id=1, source_target_pairs={{0,64},{16,80},{32,96},{48,112},{64,0},{80,16},{96,32},{112,48},{1... | collective-permute-start | bytes 491528 | tf_op jit(solution)/shard_map/ppermute | solution.py:547
  36.0 14.4 %collective-permute-start.10 = (bf16[640,128]{1,0:T(8,128)(2,1)S(1)}, bf16[640,128]{1,0:T(8,128)(2,1)S(1)}, u32[]{:S(2)}, u32[]{:S(2)}) collective-permute-start(bf16[640,128]{1,0:T(8,128)(2,1)S(1)} %strip.5), channel_id=1, source_target_pairs={{0,64},{16,80},{32,96},{48,112},{64,0},{80,16},{96,32},{112,48},{1... | collective-permute-start | bytes 491528 | tf_op jit(solution)/shard_map/ppermute | solution.py:547
  50.5 5.3 %copy-start = (s32[8,32,32]{2,1,0:T(8,128)S(1)}, s32[8,32,32]{2,1,0:T(8,128)}, u32[]{:S(2)}) copy-start(s32[8,32,32]{2,1,0:T(8,128)} %mask_ref.3) | copy-start | bytes 98308
  55.5 3.5 %collective-permute-start.11 = (bf16[16,128,128]{2,1,0:T(8,128)(2,1)S(1)}, bf16[16,128,128]{2,1,0:T(8,128)(2,1)S(1)}, u32[]{:S(2)}, u32[]{:S(2)}) collective-permute-start(bf16[16,128,128]{2,1,0:T(8,128)(2,1)S(1)} %keep.1), channel_id=1, source_target_pairs={{0,1},{1,0},{2,3},{3,2},{4,5},{5,4},{6,7},{7,6},{8,9},{9,8},{10,11... | collective-permute-start | bytes 1572872 | tf_op jit(solution)/shard_map/ppermute | solution.py:555
  71.5 28.2 %all-to-all-start.1 = ((bf16[16,144,128]{2,1,0:T(8,128)(2,1)}), bf16[16,144,128]{2,1,0:T(8,128)(2,1)S(1)}, u32[]{:S(2)}, u32[]{:S(2)}) async-start(bf16[16,144,128]{2,1,0:T(8,128)(2,1)} %view_attention.1), calls=%async_computation.1 | async-start | bytes 1179648 | tf_op jit(solution)/shard_map/all_to_all | solution.py:571
  79.9 9.4 %collective-permute-start.12 = (bf16[336,128]{1,0:T(8,128)(2,1)S(1)}, bf16[336,128]{1,0:T(8,128)(2,1)S(1)}, u32[]{:S(2)}, u32[]{:S(2)}) collective-permute-start(bf16[336,128]{1,0:T(8,128)(2,1)S(1)} %get-tuple-element.32), channel_id=1, source_target_pairs={{0,16},{16,0},{32,48},{48,32},{64,80},{80,64},{96,112},{112,96},{1... | collective-permute-start | bytes 258056 | tf_op jit(solution)/shard_map/ppermute | solution.py:547
  82.0 17.6 %collective-permute-start.13 = (bf16[336,128]{1,0:T(8,128)(2,1)S(1)}, bf16[336,128]{1,0:T(8,128)(2,1)S(1)}, u32[]{:S(2)}, u32[]{:S(2)}) collective-permute-start(bf16[336,128]{1,0:T(8,128)(2,1)S(1)} %get-tuple-element.33), channel_id=1, source_target_pairs={{0,32},{16,48},{32,0},{48,16},{64,96},{80,112},{96,64},{112,80},{1... | collective-permute-start | bytes 258056 | tf_op jit(solution)/shard_map/ppermute | solution.py:547
  86.4 13.2 %collective-permute-start.14 = (bf16[336,128]{1,0:T(8,128)(2,1)S(1)}, bf16[336,128]{1,0:T(8,128)(2,1)S(1)}, u32[]{:S(2)}, u32[]{:S(2)}) collective-permute-start(bf16[336,128]{1,0:T(8,128)(2,1)S(1)} %get-tuple-element.34), channel_id=1, source_target_pairs={{0,48},{16,32},{32,16},{48,0},{64,112},{80,96},{96,80},{112,64},{1... | collective-permute-start | bytes 258056 | tf_op jit(solution)/shard_map/ppermute | solution.py:547

commit v6 on v4

--- a/solution.py
+++ b/solution.py
@@ -460,8 +460,10 @@
 
 
 def join_kernel(view_ref, t0, t1, t2, t3, weight_any, out_ref, times, heads_s, weight_ref, sems):
-    load = pltpu.make_async_copy(weight_any, weight_ref, sems.at[0])
-    load.start()
+    chunks = [pl.ds(i * 256, 256) for i in range(5)]
+    loads = [pltpu.make_async_copy(weight_any.at[c], weight_ref.at[c], sems.at[i]) for i, c in enumerate(chunks)]
+    for load in loads:
+        load.start()
     place = lax.axis_index("f") % 4
     for k, piece in enumerate((t0, t1, t2, t3)):
         times[turned(place, k)] = piece[...]
@@ -497,28 +499,46 @@
         total = total + power
     shares = [power / total for power in powers]
 
-    def time_block(head):
+    def spread(share, first, count):
+        pick = lanes((CELLS, count * HEAD)) // HEAD + first == rows_of((CELLS, count * HEAD))
+        pick = jnp.where(pick, 1.0, 0.0).astype(BF16)
+        high = share.astype(BF16)
+        rest = (share - high.astype(F32)).astype(BF16)
+        return jnp.dot(high, pick, preferred_element_type=F32) + jnp.dot(rest, pick, preferred_element_type=F32)
+
+    view_share, time_share = spread(shares[0], 0, HEADS), spread(shares[4], 0, HEADS)
+    ring_share = [view_share[:, MAIN * HEAD :]] + [spread(shares[ring], MAIN, RING) for ring in (1, 2, 3)]
+    left = column < HEAD
+
+    def time_half(head, side):
         j, i = head // 5, head % 5
         if i < 4:
-            rows = slice((i // 2) * CELLS, (i // 2 + 1) * CELLS)
-            return times[j, rows, (i % 2) * HEAD : (i % 2 + 1) * HEAD].astype(F32)
+            block = times[j, (i // 2) * CELLS : (i // 2 + 1) * CELLS].astype(F32)
+            return block if i % 2 == side else swap_halves(block)
         packed = times[j, 256:320].astype(F32)
-        return jnp.concatenate([packed[:, 0:HEAD], packed[:, HEAD:128]], axis=0)
-
-    load.wait()
+        turn = swap_halves(packed)
+        return jnp.concatenate([turn, packed] if side else [packed, turn], axis=0)
+
+    def view_half(head, ring, side):
+        if head < MAIN:
+            block = view_ref[head, 0:CELLS].astype(F32)
+            return swap_halves(block) if side else block
+        block = view_ref[4 * ring + head - MAIN, 0:CELLS].astype(F32)
+        return block if side else swap_halves(block)
+
     result = None
-    for first in range(0, HEADS, 4):
-        for h in range(first, first + 4):
-            mixed = time_block(h) * shares[4][:, h : h + 1]
-            if h < MAIN:
-                mixed += view_ref[h, 0:CELLS, 0:HEAD].astype(F32) * shares[0][:, h : h + 1]
-            else:
-                for ring in range(4):
-                    block = view_ref[4 * ring + h - MAIN, 0:CELLS, HEAD:128].astype(F32)
-                    mixed += block * shares[ring][:, h : h + 1]
-            heads_s[:, h * HEAD : (h + 1) * HEAD] = mixed.astype(BF16)
-        columns = slice(first * HEAD, (first + 4) * HEAD)
-        product = jnp.dot(heads_s[:, columns], weight_ref[columns], preferred_element_type=F32)
+    for step in range(5):
+        for p in (2 * step, 2 * step + 1):
+            here = slice(p * CELLS, (p + 1) * CELLS)
+            mixed = jnp.where(left, time_half(2 * p, 0), time_half(2 * p + 1, 1)) * time_share[:, here]
+            for ring in range(1 if p < 8 else 4):
+                block = jnp.where(left, view_half(2 * p, ring, 0), view_half(2 * p + 1, ring, 1))
+                share = view_share[:, here] if p < 8 else ring_share[ring][:, (p - 8) * CELLS : (p - 7) * CELLS]
+                mixed += block * share
+            heads_s[:, here] = mixed.astype(BF16)
+        loads[step].wait()
+        rows = slice(step * 256, (step + 1) * 256)
+        product = jnp.dot(heads_s[:, rows], weight_ref[rows], preferred_element_type=F32)
         result = product if result is None else result + product
     out_ref[...] = result.astype(BF16)
 
@@ -533,7 +553,7 @@
             pltpu.VMEM((4, T_ROWS, CELLS), BF16),
             pltpu.VMEM((CELLS, HEADS * HEAD), BF16),
             pltpu.VMEM((HEADS * HEAD, HEADS * HEAD), BF16),
-            pltpu.SemaphoreType.DMA((1,)),
+            pltpu.SemaphoreType.DMA((5,)),
         ],
         compiler_params=params(16),
         name="join",

time: 94.7 us -> 92.2 us (0.974)
  Pallas kernels: 29.1 us -> 26.6 us
    pallas_call x1, Pallas kernels: 5.49 us -> 3.02 us  [join(): pl.pallas_call(join_kernel, out_shape=jax.ShapeDtypeStruct((CELLS, HEADS...]
  transfers between devices with their start and end apart: 14 -> 14, of which waited for: 8 -> 8; matrix products, arithmetic and copies ran while one was open for 0% -> 0% of each run, Pallas kernels for 22% -> 23%
where the time goes in v6:
time: 92.2 us; the launch traced here: 90.9 us
  starting transfers between devices  34.4 us (37%)
  waiting for transfers between devices  29 us (31%)
  Pallas kernels  26.6 us (29%)
    ppermute x7, starting transfers between devices, across(): return lax.ppermute(array, 'f', [(i, i ^ k) for i in range(FRAMES)])  16.8 us
    pallas_call x1, Pallas kernels, view_attention(): pl.pallas_call(view_kernel, out_shape=pltpu.HBM((MAIN, O_ROWS, CELLS), BF...  12.4 us
    all_to_all x1, waiting for transfers between devices, local(): own = lax.all_to_all(to_view, ('g', 'zl', 'y'), 0, 0)  12.2 us
    ppermute x7, waiting for transfers between devices, across(): return lax.ppermute(array, 'f', [(i, i ^ k) for i in range(FRAMES)])  8.85 us
    ppermute x3, waiting for transfers between devices, around(): return lax.ppermute(array, 'y', [(i, i ^ k) for i in range(RING)])  7.97 us
    all_to_all x1, starting transfers between devices, local(): own = lax.all_to_all(to_view, ('g', 'zl', 'y'), 0, 0)  7.85 us
    pallas_call x1, Pallas kernels, time_attention(): pl.pallas_call(time_kernel, out_shape=[jax.ShapeDtypeStruct((T_ROWS, CELL...  4.92 us
    all_to_all x1, starting transfers between devices, local(): view_back = lax.all_to_all(view_out, ('g', 'zl', 'y'), 0, 0)  4.73 us
  transfers between devices with their start and end apart: 14, of which 8 were waited for; matrix products, arithmetic and copies ran while one was open for 0% of the time, Pallas kernels for 23%

profile of v6, /device:TPU:8, one launch (start us, length us, event | category | flops | bytes accessed | tf_op | source)
XLA Modules:
  0.0 90.9 jit_solution(930117507288153535)
XLA Ops:
  0.0 2.9 %pack.1 = (bf16[960,128]{1,0:T(8,128)(2,1)S(1)}, bf16[960,128]{1,0:T(8,128)(2,1)S(1)}, bf16[960,128]{1,0:T(8,128)(2,1)S(1)}, bf16[960,128]{1,0:T(8,128)(2,1)S(1)...) custom-call(bf16[128,1280]{1,0:T(8,128)(2,1)} %bitcast.4, bf16[128,1280]{1,0:T(8,128)(2,1)} %bitcast.5, ...), custom_call_target="tpu_custom_call" | custom-call | tf_op jit(solution)/shard_map/pack/pallas_call | solution.py:98
  3.0 0.1 collective-permute-start.3
  3.1 3.4 %collective-permute-start = (bf16[960,128]{1,0:T(8,128)(2,1)S(1)}, bf16[960,128]{1,0:T(8,128)(2,1)S(1)}, u32[]{:S(2)}, u32[]{:S(2)}) collective-permute-start(bf16[960,128]{1,0:T(8,128)(2,1)S(1)} %get-tuple-element.21), channel_id=1, source_target_pairs={{0,16},{16,0},{32,48},{48,32},{64,80},{80,64},{96,112},{112,96},{1... | collective-permute-start | bytes 737288 | tf_op jit(solution)/shard_map/ppermute | solution.py:564
  6.4 5.4 %collective-permute-start.1 = (bf16[960,128]{1,0:T(8,128)(2,1)S(1)}, bf16[960,128]{1,0:T(8,128)(2,1)S(1)}, u32[]{:S(2)}, u32[]{:S(2)}) collective-permute-start(bf16[960,128]{1,0:T(8,128)(2,1)S(1)} %get-tuple-element.22), channel_id=1, source_target_pairs={{0,32},{16,48},{32,0},{48,16},{64,96},{80,112},{96,64},{112,80},{1... | collective-permute-start | bytes 737288 | tf_op jit(solution)/shard_map/ppermute | solution.py:564
  11.8 0.0 collective-permute-start.2
  11.8 7.8 %all-to-all-start = ((bf16[16,256,128]{2,1,0:T(8,128)(2,1)}), bf16[16,256,128]{2,1,0:T(8,128)(2,1)S(1)}, u32[]{:S(2)}, u32[]{:S(2)}) async-start(bf16[16,256,128]{2,1,0:T(8,128)(2,1)} %get-tuple-element.19), calls=%async_computation | async-start | bytes 2097152 | tf_op jit(solution)/shard_map/all_to_all | solution.py:579
  19.7 0.0 collective-permute-done.3.sibling_ref
  19.7 0.2 collective-permute-start.4
  19.9 2.8 %collective-permute-start.5 = (bf16[2,128,128]{2,1,0:T(8,128)(2,1)S(1)}, bf16[2,128,128]{2,1,0:T(8,128)(2,1)S(1)}, u32[]{:S(2)}, u32[]{:S(2)}) collective-permute-start(bf16[2,128,128]{2,1,0:T(8,128)(2,1)S(1)} %get-tuple-element.26), channel_id=1, source_target_pairs={{0,4},{2,6},{4,0},{6,2},{1,5},{3,7},{5,1},{7,3},{8,12},{10,14},{12... | collective-permute-start | bytes 196616 | tf_op jit(solution)/shard_map/ppermute | solution.py:568
  22.7 5.3 %collective-permute-done.4.refs_0_.r1 = bf16[2,128,128]{2,1,0:T(8,128)(2,1)S(1)} collective-permute-done((bf16[2,128,128]{2,1,0:T(8,128)(2,1)S(1)}, bf16[2,128,128]{2,1,0:T(8,128)(2,1)S(1)}, u32[]{:S(2)}, u32[]{:S(2)}) %collective-permute-start.4) | collective-permute-done | bytes 65568 | tf_op jit(solution)/shard_map/ppermute | solution.py:568
  28.0 1.6 %collective-permute-start.6 = (bf16[2,128,128]{2,1,0:T(8,128)(2,1)S(1)}, bf16[2,128,128]{2,1,0:T(8,128)(2,1)S(1)}, u32[]{:S(2)}, u32[]{:S(2)}) collective-permute-start(bf16[2,128,128]{2,1,0:T(8,128)(2,1)S(1)} %get-tuple-element.27), channel_id=1, source_target_pairs={{0,6},{2,4},{4,2},{6,0},{1,7},{3,5},{5,3},{7,1},{8,14},{10,12},{12... | collective-permute-start | bytes 196616 | tf_op jit(solution)/shard_map/ppermute | solution.py:568
  29.7 0.8 collective-permute-done.5.refs_1_.r2
  30.5 1.8 %collective-permute-done.6.refs_2_.r3 = bf16[2,128,128]{2,1,0:T(8,128)(2,1)S(1)} collective-permute-done((bf16[2,128,128]{2,1,0:T(8,128)(2,1)S(1)}, bf16[2,128,128]{2,1,0:T(8,128)(2,1)S(1)}, u32[]{:S(2)}, u32[]{:S(2)}) %collective-permute-start.6) | collective-permute-done | bytes 65568 | tf_op jit(solution)/shard_map/ppermute | solution.py:568
  32.3 0.0 collective-permute-done.z1
  32.3 2.1 %collective-permute-done.1.z2 = bf16[960,128]{1,0:T(8,128)(2,1)S(1)} collective-permute-done((bf16[960,128]{1,0:T(8,128)(2,1)S(1)}, bf16[960,128]{1,0:T(8,128)(2,1)S(1)}, u32[]{:S(2)}, u32[]{:S(2)}) %collective-permute-start.1) | collective-permute-done | bytes 245792 | tf_op jit(solution)/shard_map/ppermute | solution.py:564
  34.4 0.0 collective-permute-done.2.z3
  34.4 0.0 copy-start
  34.4 0.0 copy-start.1
  34.5 0.7 copy-done.1
  35.1 1.5 %collective-permute-start.8 = (bf16[4,640,128]{2,1,0:T(8,128)(2,1)S(1)}, bf16[4,640,128]{2,1,0:T(8,128)(2,1)S(1)}, u32[]{:S(2)}, u32[]{:S(2)}) collective-permute-start(bf16[4,640,128]{2,1,0:T(8,128)(2,1)S(1)} %stack.1.refs_0_), channel_id=1, source_target_pairs={{0,64},{16,80},{32,96},{48,112},{64,0},{80,16},{96,32},{112,48},{1... | collective-permute-start | bytes 1966088 | tf_op jit(solution)/shard_map/ppermute | solution.py:564
  36.6 12.2 %all-to-all-done.own_ref = bf16[16,256,128]{2,1,0:T(8,128)(2,1)S(1)} async-done(((bf16[16,256,128]{2,1,0:T(8,128)(2,1)}), bf16[16,256,128]{2,1,0:T(8,128)(2,1)S(1)}, u32[]{:S(2)}, u32[]{:S(2)}) %all-to-all-start) | async-done | bytes 1048608 | tf_op jit(solution)/shard_map/all_to_all | solution.py:579
  48.8 0.3 collective-permute-start.7
  49.1 0.0 copy-done
  49.1 3.2 %ring_attention.1.ring_ref = bf16[16,144,128]{2,1,0:T(8,128)(2,1)S(1)} custom-call(bf16[16,256,128]{2,1,0:T(8,128)(2,1)S(1)} %all-to-all-done.own_ref, bf16[2,128,128]{2,1,0:T(8,128)(2,1)S(1)} %get-tuple-element.28.r0, bf16[2,128,128]{2,1,0:T(8,128)(2,1)S(1)} %collective-permute-done.4.refs_0_.r1, ...), custom_call_target="tpu_custom_call" | custom-call | flops 1000000 | bytes 100000 | tf_op jit(solution)/shard_map/ring_attention/pallas_call | solution.py:342
  52.3 0.0 copy-start.2
  52.3 0.0 copy-start.3
  52.3 0.0 collective-permute-done.7.other_ref
  52.3 12.4 %view_attention.1.refs_0_ = bf16[16,144,128]{2,1,0:T(8,128)(2,1)} custom-call(bf16[16,256,128]{2,1,0:T(8,128)(2,1)S(1)} %all-to-all-done.own_ref, bf16[16,128,128]{2,1,0:T(8,128)(2,1)S(1)} %collective-permute-done.7.other_ref, bf16[16,144,128]{2,1,0:T(8,128)(2,1)S(1)} %ring_attention.1.ring_ref, s32[8,32,32]{2,1,0:T(8,128)S(1)} %copy-done), custom_call_target="tpu_custom_call" | custom-call | flops 1000000 | bytes 100000 | tf_op jit(solution)/shard_map/view_attention/pallas_call | solution.py:285
  64.7 0.0 collective-permute-done.8.refs_1_.x_ref
  64.8 4.7 %all-to-all-start.1 = ((bf16[16,144,128]{2,1,0:T(8,128)(2,1)}), bf16[16,144,128]{2,1,0:T(8,128)(2,1)S(1)}, u32[]{:S(2)}, u32[]{:S(2)}) async-start(bf16[16,144,128]{2,1,0:T(8,128)(2,1)} %pass_after.1), calls=%async_computation.1 | async-start | bytes 1179648 | tf_op jit(solution)/shard_map/all_to_all | solution.py:589
  69.5 0.0 copy-done.2
  69.5 0.0 copy-done.3
  69.5 4.9 %time_attention.1 = (bf16[336,128]{1,0:T(8,128)(2,1)S(1)}, bf16[336,128]{1,0:T(8,128)(2,1)S(1)}, bf16[336,128]{1,0:T(8,128)(2,1)S(1)}, bf16[336,128]{1,0:T(8,128)(2,1)S(1)}) custom-call(bf16[960,128]{1,0:T(8,128)(2,1)S(1)} %get-tuple-element.20.z0, bf16[960,128]{1,0:T(8,128)(2,1)S(1)} %collective-permute-done.z1, ...), custom_call_target="tpu_custom_call" | custom-call | flops 700000000 | bytes 2000000 | tf_op jit(solution)/shard_map/time_attention/pallas_call | solution.py:429
  74.4 2.3 %collective-permute-start.10 = (bf16[336,128]{1,0:T(8,128)(2,1)S(1)}, bf16[336,128]{1,0:T(8,128)(2,1)S(1)}, u32[]{:S(2)}, u32[]{:S(2)}) collective-permute-start(bf16[336,128]{1,0:T(8,128)(2,1)S(1)} %get-tuple-element.31), channel_id=1, source_target_pairs={{0,32},{16,48},{32,0},{48,16},{64,96},{80,112},{96,64},{112,80},{1... | collective-permute-start | bytes 258056 | tf_op jit(solution)/shard_map/ppermute | solution.py:564
  76.7 3.2 %collective-permute-start.11 = (bf16[336,128]{1,0:T(8,128)(2,1)S(1)}, bf16[336,128]{1,0:T(8,128)(2,1)S(1)}, u32[]{:S(2)}, u32[]{:S(2)}) collective-permute-start(bf16[336,128]{1,0:T(8,128)(2,1)S(1)} %get-tuple-element.32), channel_id=1, source_target_pairs={{0,48},{16,32},{32,16},{48,0},{64,112},{80,96},{96,80},{112,64},{1... | collective-permute-start | bytes 258056 | tf_op jit(solution)/shard_map/ppermute | solution.py:564
  79.9 1.1 %collective-permute-start.9 = (bf16[336,128]{1,0:T(8,128)(2,1)S(1)}, bf16[336,128]{1,0:T(8,128)(2,1)S(1)}, u32[]{:S(2)}, u32[]{:S(2)}) collective-permute-start(bf16[336,128]{1,0:T(8,128)(2,1)S(1)} %get-tuple-element.30), channel_id=1, source_target_pairs={{0,16},{16,0},{32,48},{48,32},{64,80},{80,64},{96,112},{112,96},{1... | collective-permute-start | bytes 258056 | tf_op jit(solution)/shard_map/ppermute | solution.py:564
  81.0 4.0 %collective-permute-done.10.t2 = bf16[336,128]{1,0:T(8,128)(2,1)S(1)} collective-permute-done((bf16[336,128]{1,0:T(8,128)(2,1)S(1)}, bf16[336,128]{1,0:T(8,128)(2,1)S(1)}, u32[]{:S(2)}, u32[]{:S(2)}) %collective-permute-start.10) | collective-permute-done | bytes 86048 | tf_op jit(solution)/shard_map/ppermute | solution.py:564
  85.0 1.0 %collective-permute-done.11.t3 = bf16[336,128]{1,0:T(8,128)(2,1)S(1)} collective-permute-done((bf16[336,128]{1,0:T(8,128)(2,1)S(1)}, bf16[336,128]{1,0:T(8,128)(2,1)S(1)}, u32[]{:S(2)}, u32[]{:S(2)}) %collective-permute-start.11) | collective-permute-done | bytes 86048 | tf_op jit(solution)/shard_map/ppermute | solution.py:564
  86.1 1.7 %collective-permute-done.9.t1 = bf16[336,128]{1,0:T(8,128)(2,1)S(1)} collective-permute-done((bf16[336,128]{1,0:T(8,128)(2,1)S(1)}, bf16[336,128]{1,0:T(8,128)(2,1)S(1)}, u32[]{:S(2)}, u32[]{:S(2)}) %collective-permute-start.9) | collective-permute-done | bytes 86048 | tf_op jit(solution)/shard_map/ppermute | solution.py:564
  87.8 0.0 all-to-all-done.1.view_ref
  87.8 3.0 %join.1 = bf16[128,1280]{1,0:T(8,128)(2,1)} custom-call(bf16[16,144,128]{2,1,0:T(8,128)(2,1)S(1)} %all-to-all-done.1.view_ref, bf16[336,128]{1,0:T(8,128)(2,1)S(1)} %get-tuple-element.29.t0, bf16[336,128]{1,0:T(8,128)(2,1)S(1)} %collective-permute-done.9.t1, bf16[336,128]{1,0:T(8,128)(2,1)S(1)} %collective-permute-done.10.t2, ...), custom_call_target="tpu_custom_call" | custom-call | tf_op jit(solution)/shard_map/join/pallas_call | solution.py:547
  (4 shorter events, 0.1 us)
Async XLA Ops:
  3.0 16.7 %collective-permute-start.3 = (bf16[4,128,128]{2,1,0:T(8,128)(2,1)S(1)}, bf16[4,128,128]{2,1,0:T(8,128)(2,1)S(1)}, u32[]{:S(2)}, u32[]{:S(2)}) collective-permute-start(bf16[4,128,128]{2,1,0:T(8,128)(2,1)S(1)} %get-tuple-element.24.ring_ref), channel_id=1, source_target_pairs={{0,1},{1,0},{2,3},{3,2},{4,5},{5,4},{6,7},{7,6},{8,9},{9,8},{10,11... | collective-permute-start | bytes 393224 | tf_op jit(solution)/shard_map/ppermute | solution.py:572
  3.1 29.3 %collective-permute-start = (bf16[960,128]{1,0:T(8,128)(2,1)S(1)}, bf16[960,128]{1,0:T(8,128)(2,1)S(1)}, u32[]{:S(2)}, u32[]{:S(2)}) collective-permute-start(bf16[960,128]{1,0:T(8,128)(2,1)S(1)} %get-tuple-element.21), channel_id=1, source_target_pairs={{0,16},{16,0},{32,48},{48,32},{64,80},{80,64},{96,112},{112,96},{1... | collective-permute-start | bytes 737288 | tf_op jit(solution)/shard_map/ppermute | solution.py:564
  6.4 28.0 %collective-permute-start.1 = (bf16[960,128]{1,0:T(8,128)(2,1)S(1)}, bf16[960,128]{1,0:T(8,128)(2,1)S(1)}, u32[]{:S(2)}, u32[]{:S(2)}) collective-permute-start(bf16[960,128]{1,0:T(8,128)(2,1)S(1)} %get-tuple-element.22), channel_id=1, source_target_pairs={{0,32},{16,48},{32,0},{48,16},{64,96},{80,112},{96,64},{112,80},{1... | collective-permute-start | bytes 737288 | tf_op jit(solution)/shard_map/ppermute | solution.py:564
  11.8 22.6 %collective-permute-start.2 = (bf16[960,128]{1,0:T(8,128)(2,1)S(1)}, bf16[960,128]{1,0:T(8,128)(2,1)S(1)}, u32[]{:S(2)}, u32[]{:S(2)}) collective-permute-start(bf16[960,128]{1,0:T(8,128)(2,1)S(1)} %get-tuple-element.23), channel_id=1, source_target_pairs={{0,48},{16,32},{32,16},{48,0},{64,112},{80,96},{96,80},{112,64},{1... | collective-permute-start | bytes 737288 | tf_op jit(solution)/shard_map/ppermute | solution.py:564
  11.8 37.0 %all-to-all-start = ((bf16[16,256,128]{2,1,0:T(8,128)(2,1)}), bf16[16,256,128]{2,1,0:T(8,128)(2,1)S(1)}, u32[]{:S(2)}, u32[]{:S(2)}) async-start(bf16[16,256,128]{2,1,0:T(8,128)(2,1)} %get-tuple-element.19), calls=%async_computation | async-start | bytes 2097152 | tf_op jit(solution)/shard_map/all_to_all | solution.py:579
  19.7 8.3 %collective-permute-start.4 = (bf16[2,128,128]{2,1,0:T(8,128)(2,1)S(1)}, bf16[2,128,128]{2,1,0:T(8,128)(2,1)S(1)}, u32[]{:S(2)}, u32[]{:S(2)}) collective-permute-start(bf16[2,128,128]{2,1,0:T(8,128)(2,1)S(1)} %get-tuple-element.25), channel_id=1, source_target_pairs={{0,2},{2,0},{4,6},{6,4},{1,3},{3,1},{5,7},{7,5},{8,10},{10,8},{12,... | collective-permute-start | bytes 196616 | tf_op jit(solution)/shard_map/ppermute | solution.py:568
  19.9 10.6 %collective-permute-start.5 = (bf16[2,128,128]{2,1,0:T(8,128)(2,1)S(1)}, bf16[2,128,128]{2,1,0:T(8,128)(2,1)S(1)}, u32[]{:S(2)}, u32[]{:S(2)}) collective-permute-start(bf16[2,128,128]{2,1,0:T(8,128)(2,1)S(1)} %get-tuple-element.26), channel_id=1, source_target_pairs={{0,4},{2,6},{4,0},{6,2},{1,5},{3,7},{5,1},{7,3},{8,12},{10,14},{12... | collective-permute-start | bytes 196616 | tf_op jit(solution)/shard_map/ppermute | solution.py:568
  28.0 4.3 %collective-permute-start.6 = (bf16[2,128,128]{2,1,0:T(8,128)(2,1)S(1)}, bf16[2,128,128]{2,1,0:T(8,128)(2,1)S(1)}, u32[]{:S(2)}, u32[]{:S(2)}) collective-permute-start(bf16[2,128,128]{2,1,0:T(8,128)(2,1)S(1)} %get-tuple-element.27), channel_id=1, source_target_pairs={{0,6},{2,4},{4,2},{6,0},{1,7},{3,5},{5,3},{7,1},{8,14},{10,12},{12... | collective-permute-start | bytes 196616 | tf_op jit(solution)/shard_map/ppermute | solution.py:568
  34.4 14.7 %copy-start = (s32[8,32,32]{2,1,0:T(8,128)S(1)}, s32[8,32,32]{2,1,0:T(8,128)}, u32[]{:S(2)}) copy-start(s32[8,32,32]{2,1,0:T(8,128)} %mask_ref.3) | copy-start | bytes 98308
  34.4 0.7 copy-start.1
  35.1 29.6 %collective-permute-start.8 = (bf16[4,640,128]{2,1,0:T(8,128)(2,1)S(1)}, bf16[4,640,128]{2,1,0:T(8,128)(2,1)S(1)}, u32[]{:S(2)}, u32[]{:S(2)}) collective-permute-start(bf16[4,640,128]{2,1,0:T(8,128)(2,1)S(1)} %stack.1.refs_0_), channel_id=1, source_target_pairs={{0,64},{16,80},{32,96},{48,112},{64,0},{80,16},{96,32},{112,48},{1... | collective-permute-start | bytes 1966088 | tf_op jit(solution)/shard_map/ppermute | solution.py:564
  48.8 3.5 %collective-permute-start.7 = (bf16[16,128,128]{2,1,0:T(8,128)(2,1)S(1)}, bf16[16,128,128]{2,1,0:T(8,128)(2,1)S(1)}, u32[]{:S(2)}, u32[]{:S(2)}) collective-permute-start(bf16[16,128,128]{2,1,0:T(8,128)(2,1)S(1)} %keep.1), channel_id=1, source_target_pairs={{0,1},{1,0},{2,3},{3,2},{4,5},{5,4},{6,7},{7,6},{8,9},{9,8},{10,11... | collective-permute-start | bytes 1572872 | tf_op jit(solution)/shard_map/ppermute | solution.py:572
  52.3 17.2 %copy-start.2 = (bf16[960,128]{1,0:T(8,128)(2,1)S(1)}, bf16[960,128]{1,0:T(8,128)(2,1)}, u32[]{:S(2)}) copy-start(bf16[960,128]{1,0:T(8,128)(2,1)} %copy-done.1) | copy-start | bytes 737284
  52.3 17.2 %copy-start.3 = (s32[8]{0:T(128)S(1)}, s32[8]{0:T(128)}, u32[]{:S(2)}) copy-start(s32[8]{0:T(128)} %times_ref.1) | copy-start | bytes 100
  64.8 23.0 %all-to-all-start.1 = ((bf16[16,144,128]{2,1,0:T(8,128)(2,1)}), bf16[16,144,128]{2,1,0:T(8,128)(2,1)S(1)}, u32[]{:S(2)}, u32[]{:S(2)}) async-start(bf16[16,144,128]{2,1,0:T(8,128)(2,1)} %pass_after.1), calls=%async_computation.1 | async-start | bytes 1179648 | tf_op jit(solution)/shard_map/all_to_all | solution.py:589
  74.4 10.6 %collective-permute-start.10 = (bf16[336,128]{1,0:T(8,128)(2,1)S(1)}, bf16[336,128]{1,0:T(8,128)(2,1)S(1)}, u32[]{:S(2)}, u32[]{:S(2)}) collective-permute-start(bf16[336,128]{1,0:T(8,128)(2,1)S(1)} %get-tuple-element.31), channel_id=1, source_target_pairs={{0,32},{16,48},{32,0},{48,16},{64,96},{80,112},{96,64},{112,80},{1... | collective-permute-start | bytes 258056 | tf_op jit(solution)/shard_map/ppermute | solution.py:564
  76.7 9.3 %collective-permute-start.11 = (bf16[336,128]{1,0:T(8,128)(2,1)S(1)}, bf16[336,128]{1,0:T(8,128)(2,1)S(1)}, u32[]{:S(2)}, u32[]{:S(2)}) collective-permute-start(bf16[336,128]{1,0:T(8,128)(2,1)S(1)} %get-tuple-element.32), channel_id=1, source_target_pairs={{0,48},{16,32},{32,16},{48,0},{64,112},{80,96},{96,80},{112,64},{1... | collective-permute-start | bytes 258056 | tf_op jit(solution)/shard_map/ppermute | solution.py:564
  79.9 7.9 %collective-permute-start.9 = (bf16[336,128]{1,0:T(8,128)(2,1)S(1)}, bf16[336,128]{1,0:T(8,128)(2,1)S(1)}, u32[]{:S(2)}, u32[]{:S(2)}) collective-permute-start(bf16[336,128]{1,0:T(8,128)(2,1)S(1)} %get-tuple-element.30), channel_id=1, source_target_pairs={{0,16},{16,0},{32,48},{48,32},{64,80},{80,64},{96,112},{112,96},{1... | collective-permute-start | bytes 258056 | tf_op jit(solution)/shard_map/ppermute | solution.py:564

commit v7 on v6

--- a/solution.py
+++ b/solution.py
@@ -20,6 +20,7 @@
 Z_ROWS = 960
 X_ROWS = 640
 T_ROWS = 336
+GATE_FLOPS = 19000000000
 O_ROWS = 144
 F32 = jnp.float32
 BF16 = jnp.bfloat16
@@ -128,6 +129,23 @@
     )(ring, other)
 
 
+def gate_kernel(*refs):
+    out_ref = refs[-1]
+    out_ref[...] = jnp.zeros_like(out_ref)
+
+
+def gate(arrays):
+    return pl.pallas_call(
+        gate_kernel,
+        out_shape=jax.ShapeDtypeStruct((16, CELLS), BF16),
+        in_specs=[ANY] * len(arrays),
+        out_specs=VMEM,
+        compiler_params=params(4),
+        cost_estimate=pl.CostEstimate(flops=GATE_FLOPS, bytes_accessed=100000, transcendentals=0),
+        name="gate",
+    )(*arrays)
+
+
 def stack_kernel(z0, z1, z2, z3, *refs):
     out_ref = refs[-1]
     for k, piece in enumerate((z0, z1, z2, z3)):
@@ -141,7 +159,6 @@
         in_specs=[VMEM] * 4 + [ANY] * len(order),
         out_specs=VMEM,
         compiler_params=params(4),
-        cost_estimate=pl.CostEstimate(flops=18000000000, bytes_accessed=100000, transcendentals=0),
         name="stack",
     )(*z, *order)
 
@@ -580,9 +597,9 @@
     z = [z[0]] + [across(z[i], i) for i in (1, 2, 3)]
     ring = ring_pack(to_ring, sibling(to_ring))
     ring = [ring[0]] + [around(ring[i], i) for i in (1, 2, 3)]
-    some = stack(z, ring[1:])
-    crossed = across(some, 4)
-    other = sibling(keep(own, [some]))
+    kept = keep(own, [gate(z[1:] + ring[1:])])
+    other = sibling(kept)
+    crossed = across(stack(z, [kept]), 4)
     ring_out = ring_attention(own, ring, view_mask)
     view_out = view_attention(own, other, ring_out, view_mask)
     view_out = pass_after(view_out, (crossed,))

time: 92.2 us -> 93 us (level)
  waiting for transfers between devices: 29 us -> 31 us
    all_to_all x1, waiting for transfers between devices: 12.2 us -> 14.2 us  [local(): own = lax.all_to_all(to_view, ('g', 'zl', 'y'), 0, 0)]
  transfers between devices with their start and end apart: 14 -> 14, of which waited for: 8 -> 8; matrix products, arithmetic and copies ran while one was open for 0% -> 0% of each run, Pallas kernels for 23% -> 22%
where the time goes in v7:
time: 93 us; the launch traced here: 91.8 us
  starting transfers between devices  33.9 us (36%)
  waiting for transfers between devices  31 us (33%)
  Pallas kernels  26.6 us (29%)
    ppermute x7, starting transfers between devices, across(): return lax.ppermute(array, 'f', [(i, i ^ k) for i in range(FRAMES)])  16.6 us
    all_to_all x1, waiting for transfers between devices, local(): own = lax.all_to_all(to_view, ('g', 'zl', 'y'), 0, 0)  14.2 us
    pallas_call x1, Pallas kernels, view_attention(): pl.pallas_call(view_kernel, out_shape=pltpu.HBM((MAIN, O_ROWS, CELLS), BF...  12.4 us
    ppermute x7, waiting for transfers between devices, across(): return lax.ppermute(array, 'f', [(i, i ^ k) for i in range(FRAMES)])  8.8 us
    ppermute x3, waiting for transfers between devices, around(): return lax.ppermute(array, 'y', [(i, i ^ k) for i in range(RING)])  7.97 us
    all_to_all x1, starting transfers between devices, local(): own = lax.all_to_all(to_view, ('g', 'zl', 'y'), 0, 0)  7.85 us
    pallas_call x1, Pallas kernels, time_attention(): pl.pallas_call(time_kernel, out_shape=[jax.ShapeDtypeStruct((T_ROWS, CELL...  4.92 us
    all_to_all x1, starting transfers between devices, local(): view_back = lax.all_to_all(view_out, ('g', 'zl', 'y'), 0, 0)  4.77 us
  transfers between devices with their start and end apart: 14, of which 8 were waited for; matrix products, arithmetic and copies ran while one was open for 0% of the time, Pallas kernels for 22%

profile of v7, /device:TPU:8, one launch (start us, length us, event | category | flops | bytes accessed | tf_op | source)
XLA Modules:
  0.0 91.8 jit_solution(1034261391215933188)
XLA Ops:
  0.0 2.9 %pack.1 = (bf16[960,128]{1,0:T(8,128)(2,1)S(1)}, bf16[960,128]{1,0:T(8,128)(2,1)S(1)}, bf16[960,128]{1,0:T(8,128)(2,1)S(1)}, bf16[960,128]{1,0:T(8,128)(2,1)S(1)...) custom-call(bf16[128,1280]{1,0:T(8,128)(2,1)} %bitcast.4, bf16[128,1280]{1,0:T(8,128)(2,1)} %bitcast.5, ...), custom_call_target="tpu_custom_call" | custom-call | tf_op jit(solution)/shard_map/pack/pallas_call | solution.py:99
  2.9 0.1 collective-permute-start.3
  3.0 3.4 %collective-permute-start = (bf16[960,128]{1,0:T(8,128)(2,1)S(1)}, bf16[960,128]{1,0:T(8,128)(2,1)S(1)}, u32[]{:S(2)}, u32[]{:S(2)}) collective-permute-start(bf16[960,128]{1,0:T(8,128)(2,1)S(1)} %get-tuple-element.20), channel_id=1, source_target_pairs={{0,16},{16,0},{32,48},{48,32},{64,80},{80,64},{96,112},{112,96},{1... | collective-permute-start | bytes 737288 | tf_op jit(solution)/shard_map/ppermute | solution.py:581
  6.4 5.4 %collective-permute-start.1 = (bf16[960,128]{1,0:T(8,128)(2,1)S(1)}, bf16[960,128]{1,0:T(8,128)(2,1)S(1)}, u32[]{:S(2)}, u32[]{:S(2)}) collective-permute-start(bf16[960,128]{1,0:T(8,128)(2,1)S(1)} %get-tuple-element.21), channel_id=1, source_target_pairs={{0,32},{16,48},{32,0},{48,16},{64,96},{80,112},{96,64},{112,80},{1... | collective-permute-start | bytes 737288 | tf_op jit(solution)/shard_map/ppermute | solution.py:581
  11.8 0.0 collective-permute-start.2
  11.8 7.8 %all-to-all-start = ((bf16[16,256,128]{2,1,0:T(8,128)(2,1)}), bf16[16,256,128]{2,1,0:T(8,128)(2,1)S(1)}, u32[]{:S(2)}, u32[]{:S(2)}) async-start(bf16[16,256,128]{2,1,0:T(8,128)(2,1)} %get-tuple-element.19), calls=%async_computation | async-start | bytes 2097152 | tf_op jit(solution)/shard_map/all_to_all | solution.py:596
  19.6 0.0 collective-permute-done.3.sibling_ref
  19.7 0.2 collective-permute-start.4
  19.9 2.8 %collective-permute-start.5 = (bf16[2,128,128]{2,1,0:T(8,128)(2,1)S(1)}, bf16[2,128,128]{2,1,0:T(8,128)(2,1)S(1)}, u32[]{:S(2)}, u32[]{:S(2)}) collective-permute-start(bf16[2,128,128]{2,1,0:T(8,128)(2,1)S(1)} %get-tuple-element.25), channel_id=1, source_target_pairs={{0,4},{2,6},{4,0},{6,2},{1,5},{3,7},{5,1},{7,3},{8,12},{10,14},{12... | collective-permute-start | bytes 196616 | tf_op jit(solution)/shard_map/ppermute | solution.py:585
  22.7 5.3 %collective-permute-done.4.refs_3_.r1 = bf16[2,128,128]{2,1,0:T(8,128)(2,1)S(1)} collective-permute-done((bf16[2,128,128]{2,1,0:T(8,128)(2,1)S(1)}, bf16[2,128,128]{2,1,0:T(8,128)(2,1)S(1)}, u32[]{:S(2)}, u32[]{:S(2)}) %collective-permute-start.4) | collective-permute-done | bytes 65568 | tf_op jit(solution)/shard_map/ppermute | solution.py:585
  28.0 1.6 %collective-permute-start.6 = (bf16[2,128,128]{2,1,0:T(8,128)(2,1)S(1)}, bf16[2,128,128]{2,1,0:T(8,128)(2,1)S(1)}, u32[]{:S(2)}, u32[]{:S(2)}) collective-permute-start(bf16[2,128,128]{2,1,0:T(8,128)(2,1)S(1)} %get-tuple-element.26), channel_id=1, source_target_pairs={{0,6},{2,4},{4,2},{6,0},{1,7},{3,5},{5,3},{7,1},{8,14},{10,12},{12... | collective-permute-start | bytes 196616 | tf_op jit(solution)/shard_map/ppermute | solution.py:585
  29.7 0.8 collective-permute-done.5.refs_4_.r2
  30.5 1.8 %collective-permute-done.6.refs_5_.r3 = bf16[2,128,128]{2,1,0:T(8,128)(2,1)S(1)} collective-permute-done((bf16[2,128,128]{2,1,0:T(8,128)(2,1)S(1)}, bf16[2,128,128]{2,1,0:T(8,128)(2,1)S(1)}, u32[]{:S(2)}, u32[]{:S(2)}) %collective-permute-start.6) | collective-permute-done | bytes 65568 | tf_op jit(solution)/shard_map/ppermute | solution.py:585
  32.3 0.0 collective-permute-done.refs_0_.z1
  32.3 2.1 %collective-permute-done.1.refs_1_.z2 = bf16[960,128]{1,0:T(8,128)(2,1)S(1)} collective-permute-done((bf16[960,128]{1,0:T(8,128)(2,1)S(1)}, bf16[960,128]{1,0:T(8,128)(2,1)S(1)}, u32[]{:S(2)}, u32[]{:S(2)}) %collective-permute-start.1) | collective-permute-done | bytes 245792 | tf_op jit(solution)/shard_map/ppermute | solution.py:581
  34.4 0.0 collective-permute-done.2.refs_2_.z3
  34.4 0.0 copy-start
  34.4 14.2 %all-to-all-done.own_ref = bf16[16,256,128]{2,1,0:T(8,128)(2,1)S(1)} async-done(((bf16[16,256,128]{2,1,0:T(8,128)(2,1)}), bf16[16,256,128]{2,1,0:T(8,128)(2,1)S(1)}, u32[]{:S(2)}, u32[]{:S(2)}) %all-to-all-start) | async-done | bytes 1048608 | tf_op jit(solution)/shard_map/all_to_all | solution.py:596
  48.7 0.7 collective-permute-start.8
  49.4 0.0 collective-permute-start.7
  49.4 0.0 copy-done
  49.4 3.2 %ring_attention.1.ring_ref = bf16[16,144,128]{2,1,0:T(8,128)(2,1)S(1)} custom-call(bf16[16,256,128]{2,1,0:T(8,128)(2,1)S(1)} %all-to-all-done.own_ref, bf16[2,128,128]{2,1,0:T(8,128)(2,1)S(1)} %get-tuple-element.27.r0, bf16[2,128,128]{2,1,0:T(8,128)(2,1)S(1)} %collective-permute-done.4.refs_3_.r1, ...), custom_call_target="tpu_custom_call" | custom-call | flops 1000000 | bytes 100000 | tf_op jit(solution)/shard_map/ring_attention/pallas_call | solution.py:359
  52.6 0.0 copy-start.1
  52.6 0.0 collective-permute-done.7.other_ref
  52.6 12.4 %view_attention.1.refs_0_ = bf16[16,144,128]{2,1,0:T(8,128)(2,1)} custom-call(bf16[16,256,128]{2,1,0:T(8,128)(2,1)S(1)} %all-to-all-done.own_ref, bf16[16,128,128]{2,1,0:T(8,128)(2,1)S(1)} %collective-permute-done.7.other_ref, bf16[16,144,128]{2,1,0:T(8,128)(2,1)S(1)} %ring_attention.1.ring_ref, s32[8,32,32]{2,1,0:T(8,128)S(1)} %copy-done), custom_call_target="tpu_custom_call" | custom-call | flops 1000000 | bytes 100000 | tf_op jit(solution)/shard_map/view_attention/pallas_call | solution.py:302
  65.0 0.0 collective-permute-done.8.refs_1_.x_ref
  65.0 4.8 %all-to-all-start.1 = ((bf16[16,144,128]{2,1,0:T(8,128)(2,1)}), bf16[16,144,128]{2,1,0:T(8,128)(2,1)S(1)}, u32[]{:S(2)}, u32[]{:S(2)}) async-start(bf16[16,144,128]{2,1,0:T(8,128)(2,1)} %pass_after.1), calls=%async_computation.1 | async-start | bytes 1179648 | tf_op jit(solution)/shard_map/all_to_all | solution.py:606
  69.8 0.0 copy-done.1
  69.8 4.9 %time_attention.1 = (bf16[336,128]{1,0:T(8,128)(2,1)S(1)}, bf16[336,128]{1,0:T(8,128)(2,1)S(1)}, bf16[336,128]{1,0:T(8,128)(2,1)S(1)}, bf16[336,128]{1,0:T(8,128)(2,1)S(1)}) custom-call(bf16[960,128]{1,0:T(8,128)(2,1)S(1)} %get-tuple-element.28.z0, bf16[960,128]{1,0:T(8,128)(2,1)S(1)} %collective-permute-done.refs_0_.z1, ...), custom_call_target="tpu_custom_call" | custom-call | flops 700000000 | bytes 2000000 | tf_op jit(solution)/shard_map/time_attention/pallas_call | solution.py:446
  74.7 2.5 %collective-permute-start.10 = (bf16[336,128]{1,0:T(8,128)(2,1)S(1)}, bf16[336,128]{1,0:T(8,128)(2,1)S(1)}, u32[]{:S(2)}, u32[]{:S(2)}) collective-permute-start(bf16[336,128]{1,0:T(8,128)(2,1)S(1)} %get-tuple-element.31), channel_id=1, source_target_pairs={{0,32},{16,48},{32,0},{48,16},{64,96},{80,112},{96,64},{112,80},{1... | collective-permute-start | bytes 258056 | tf_op jit(solution)/shard_map/ppermute | solution.py:581
  77.3 4.6 %collective-permute-start.11 = (bf16[336,128]{1,0:T(8,128)(2,1)S(1)}, bf16[336,128]{1,0:T(8,128)(2,1)S(1)}, u32[]{:S(2)}, u32[]{:S(2)}) collective-permute-start(bf16[336,128]{1,0:T(8,128)(2,1)S(1)} %get-tuple-element.32), channel_id=1, source_target_pairs={{0,48},{16,32},{32,16},{48,0},{64,112},{80,96},{96,80},{112,64},{1... | collective-permute-start | bytes 258056 | tf_op jit(solution)/shard_map/ppermute | solution.py:581
  81.9 0.0 collective-permute-start.9
  81.9 1.7 %collective-permute-done.10.t2 = bf16[336,128]{1,0:T(8,128)(2,1)S(1)} collective-permute-done((bf16[336,128]{1,0:T(8,128)(2,1)S(1)}, bf16[336,128]{1,0:T(8,128)(2,1)S(1)}, u32[]{:S(2)}, u32[]{:S(2)}) %collective-permute-start.10) | collective-permute-done | bytes 86048 | tf_op jit(solution)/shard_map/ppermute | solution.py:581
  83.6 4.0 %collective-permute-done.11.t3 = bf16[336,128]{1,0:T(8,128)(2,1)S(1)} collective-permute-done((bf16[336,128]{1,0:T(8,128)(2,1)S(1)}, bf16[336,128]{1,0:T(8,128)(2,1)S(1)}, u32[]{:S(2)}, u32[]{:S(2)}) %collective-permute-start.11) | collective-permute-done | bytes 86048 | tf_op jit(solution)/shard_map/ppermute | solution.py:581
  87.6 1.0 %collective-permute-done.9.t1 = bf16[336,128]{1,0:T(8,128)(2,1)S(1)} collective-permute-done((bf16[336,128]{1,0:T(8,128)(2,1)S(1)}, bf16[336,128]{1,0:T(8,128)(2,1)S(1)}, u32[]{:S(2)}, u32[]{:S(2)}) %collective-permute-start.9) | collective-permute-done | bytes 86048 | tf_op jit(solution)/shard_map/ppermute | solution.py:581
  88.6 0.0 all-to-all-done.1.view_ref
  88.6 3.0 %join.1 = bf16[128,1280]{1,0:T(8,128)(2,1)} custom-call(bf16[16,144,128]{2,1,0:T(8,128)(2,1)S(1)} %all-to-all-done.1.view_ref, bf16[336,128]{1,0:T(8,128)(2,1)S(1)} %get-tuple-element.29.t0, bf16[336,128]{1,0:T(8,128)(2,1)S(1)} %collective-permute-done.9.t1, bf16[336,128]{1,0:T(8,128)(2,1)S(1)} %collective-permute-done.10.t2, ...), custom_call_target="tpu_custom_call" | custom-call | tf_op jit(solution)/shard_map/join/pallas_call | solution.py:564
  (5 shorter events, 0.1 us)
Async XLA Ops:
  2.9 16.7 %collective-permute-start.3 = (bf16[4,128,128]{2,1,0:T(8,128)(2,1)S(1)}, bf16[4,128,128]{2,1,0:T(8,128)(2,1)S(1)}, u32[]{:S(2)}, u32[]{:S(2)}) collective-permute-start(bf16[4,128,128]{2,1,0:T(8,128)(2,1)S(1)} %get-tuple-element.23.ring_ref), channel_id=1, source_target_pairs={{0,1},{1,0},{2,3},{3,2},{4,5},{5,4},{6,7},{7,6},{8,9},{9,8},{10,11... | collective-permute-start | bytes 393224 | tf_op jit(solution)/shard_map/ppermute | solution.py:589
  3.0 29.3 %collective-permute-start = (bf16[960,128]{1,0:T(8,128)(2,1)S(1)}, bf16[960,128]{1,0:T(8,128)(2,1)S(1)}, u32[]{:S(2)}, u32[]{:S(2)}) collective-permute-start(bf16[960,128]{1,0:T(8,128)(2,1)S(1)} %get-tuple-element.20), channel_id=1, source_target_pairs={{0,16},{16,0},{32,48},{48,32},{64,80},{80,64},{96,112},{112,96},{1... | collective-permute-start | bytes 737288 | tf_op jit(solution)/shard_map/ppermute | solution.py:581
  6.4 28.0 %collective-permute-start.1 = (bf16[960,128]{1,0:T(8,128)(2,1)S(1)}, bf16[960,128]{1,0:T(8,128)(2,1)S(1)}, u32[]{:S(2)}, u32[]{:S(2)}) collective-permute-start(bf16[960,128]{1,0:T(8,128)(2,1)S(1)} %get-tuple-element.21), channel_id=1, source_target_pairs={{0,32},{16,48},{32,0},{48,16},{64,96},{80,112},{96,64},{112,80},{1... | collective-permute-start | bytes 737288 | tf_op jit(solution)/shard_map/ppermute | solution.py:581
  11.8 22.6 %collective-permute-start.2 = (bf16[960,128]{1,0:T(8,128)(2,1)S(1)}, bf16[960,128]{1,0:T(8,128)(2,1)S(1)}, u32[]{:S(2)}, u32[]{:S(2)}) collective-permute-start(bf16[960,128]{1,0:T(8,128)(2,1)S(1)} %get-tuple-element.22), channel_id=1, source_target_pairs={{0,48},{16,32},{32,16},{48,0},{64,112},{80,96},{96,80},{112,64},{1... | collective-permute-start | bytes 737288 | tf_op jit(solution)/shard_map/ppermute | solution.py:581
  11.8 36.8 %all-to-all-start = ((bf16[16,256,128]{2,1,0:T(8,128)(2,1)}), bf16[16,256,128]{2,1,0:T(8,128)(2,1)S(1)}, u32[]{:S(2)}, u32[]{:S(2)}) async-start(bf16[16,256,128]{2,1,0:T(8,128)(2,1)} %get-tuple-element.19), calls=%async_computation | async-start | bytes 2097152 | tf_op jit(solution)/shard_map/all_to_all | solution.py:596
  19.7 8.3 %collective-permute-start.4 = (bf16[2,128,128]{2,1,0:T(8,128)(2,1)S(1)}, bf16[2,128,128]{2,1,0:T(8,128)(2,1)S(1)}, u32[]{:S(2)}, u32[]{:S(2)}) collective-permute-start(bf16[2,128,128]{2,1,0:T(8,128)(2,1)S(1)} %get-tuple-element.24), channel_id=1, source_target_pairs={{0,2},{2,0},{4,6},{6,4},{1,3},{3,1},{5,7},{7,5},{8,10},{10,8},{12,... | collective-permute-start | bytes 196616 | tf_op jit(solution)/shard_map/ppermute | solution.py:585
  19.9 10.6 %collective-permute-start.5 = (bf16[2,128,128]{2,1,0:T(8,128)(2,1)S(1)}, bf16[2,128,128]{2,1,0:T(8,128)(2,1)S(1)}, u32[]{:S(2)}, u32[]{:S(2)}) collective-permute-start(bf16[2,128,128]{2,1,0:T(8,128)(2,1)S(1)} %get-tuple-element.25), channel_id=1, source_target_pairs={{0,4},{2,6},{4,0},{6,2},{1,5},{3,7},{5,1},{7,3},{8,12},{10,14},{12... | collective-permute-start | bytes 196616 | tf_op jit(solution)/shard_map/ppermute | solution.py:585
  28.0 4.3 %collective-permute-start.6 = (bf16[2,128,128]{2,1,0:T(8,128)(2,1)S(1)}, bf16[2,128,128]{2,1,0:T(8,128)(2,1)S(1)}, u32[]{:S(2)}, u32[]{:S(2)}) collective-permute-start(bf16[2,128,128]{2,1,0:T(8,128)(2,1)S(1)} %get-tuple-element.26), channel_id=1, source_target_pairs={{0,6},{2,4},{4,2},{6,0},{1,7},{3,5},{5,3},{7,1},{8,14},{10,12},{12... | collective-permute-start | bytes 196616 | tf_op jit(solution)/shard_map/ppermute | solution.py:585
  34.4 15.0 %copy-start = (s32[8,32,32]{2,1,0:T(8,128)S(1)}, s32[8,32,32]{2,1,0:T(8,128)}, u32[]{:S(2)}) copy-start(s32[8,32,32]{2,1,0:T(8,128)} %mask_ref.3) | copy-start | bytes 98308
  48.7 16.3 %collective-permute-start.8 = (bf16[4,640,128]{2,1,0:T(8,128)(2,1)S(1)}, bf16[4,640,128]{2,1,0:T(8,128)(2,1)S(1)}, u32[]{:S(2)}, u32[]{:S(2)}) collective-permute-start(bf16[4,640,128]{2,1,0:T(8,128)(2,1)S(1)} %stack.1), channel_id=1, source_target_pairs={{0,64},{16,80},{32,96},{48,112},{64,0},{80,16},{96,32},{112,48},{1... | collective-permute-start | bytes 1966088 | tf_op jit(solution)/shard_map/ppermute | solution.py:581
  49.4 3.2 %collective-permute-start.7 = (bf16[16,128,128]{2,1,0:T(8,128)(2,1)S(1)}, bf16[16,128,128]{2,1,0:T(8,128)(2,1)S(1)}, u32[]{:S(2)}, u32[]{:S(2)}) collective-permute-start(bf16[16,128,128]{2,1,0:T(8,128)(2,1)S(1)} %keep.1.refs_0_), channel_id=1, source_target_pairs={{0,1},{1,0},{2,3},{3,2},{4,5},{5,4},{6,7},{7,6},{8,9},{9,8},{10,11... | collective-permute-start | bytes 1572872 | tf_op jit(solution)/shard_map/ppermute | solution.py:589
  52.6 17.2 %copy-start.1 = (s32[8]{0:T(128)S(1)}, s32[8]{0:T(128)}, u32[]{:S(2)}) copy-start(s32[8]{0:T(128)} %times_ref.1) | copy-start | bytes 100
  65.0 23.6 %all-to-all-start.1 = ((bf16[16,144,128]{2,1,0:T(8,128)(2,1)}), bf16[16,144,128]{2,1,0:T(8,128)(2,1)S(1)}, u32[]{:S(2)}, u32[]{:S(2)}) async-start(bf16[16,144,128]{2,1,0:T(8,128)(2,1)} %pass_after.1), calls=%async_computation.1 | async-start | bytes 1179648 | tf_op jit(solution)/shard_map/all_to_all | solution.py:606
  74.7 8.9 %collective-permute-start.10 = (bf16[336,128]{1,0:T(8,128)(2,1)S(1)}, bf16[336,128]{1,0:T(8,128)(2,1)S(1)}, u32[]{:S(2)}, u32[]{:S(2)}) collective-permute-start(bf16[336,128]{1,0:T(8,128)(2,1)S(1)} %get-tuple-element.31), channel_id=1, source_target_pairs={{0,32},{16,48},{32,0},{48,16},{64,96},{80,112},{96,64},{112,80},{1... | collective-permute-start | bytes 258056 | tf_op jit(solution)/shard_map/ppermute | solution.py:581
  77.3 10.3 %collective-permute-start.11 = (bf16[336,128]{1,0:T(8,128)(2,1)S(1)}, bf16[336,128]{1,0:T(8,128)(2,1)S(1)}, u32[]{:S(2)}, u32[]{:S(2)}) collective-permute-start(bf16[336,128]{1,0:T(8,128)(2,1)S(1)} %get-tuple-element.32), channel_id=1, source_target_pairs={{0,48},{16,32},{32,16},{48,0},{64,112},{80,96},{96,80},{112,64},{1... | collective-permute-start | bytes 258056 | tf_op jit(solution)/shard_map/ppermute | solution.py:581
  81.9 6.7 %collective-permute-start.9 = (bf16[336,128]{1,0:T(8,128)(2,1)S(1)}, bf16[336,128]{1,0:T(8,128)(2,1)S(1)}, u32[]{:S(2)}, u32[]{:S(2)}) collective-permute-start(bf16[336,128]{1,0:T(8,128)(2,1)S(1)} %get-tuple-element.30), channel_id=1, source_target_pairs={{0,16},{16,0},{32,48},{48,32},{64,80},{80,64},{96,112},{112,96},{1... | collective-permute-start | bytes 258056 | tf_op jit(solution)/shard_map/ppermute | solution.py:581

commit v8 on v6

--- a/solution.py
+++ b/solution.py
@@ -20,6 +20,7 @@
 Z_ROWS = 960
 X_ROWS = 640
 T_ROWS = 336
+NEAR_FLOPS = 19000000000
 O_ROWS = 144
 F32 = jnp.float32
 BF16 = jnp.bfloat16
@@ -110,22 +111,31 @@
     )(in_hbm(q), in_hbm(k), in_hbm(v))
 
 
-def ring_pack_kernel(ring_ref, sibling_ref, r0, r1, r2, r3):
+def ring_pack_kernel(ring_ref, sibling_ref, mask_ref, r0, r1, r2, r3, bias_ref, ring_bias_ref):
+    core = lax.axis_index("c")
+    block = rows_of((32, 32))
+    bias_ref[...] = seen_bias(mask_ref, jnp.where(block < 16, 2 * block + core, 2 * (block - 16) + 1 - core), 32)
+    ring = lax.axis_index("g") * 2 + lax.axis_index("zl")
+    block = rows_of((8, 32))
+    side = jnp.where(block % 2 == 0, core, 1 - core)
+    bias = seen_bias(mask_ref, ring * 8 + 2 * (lax.axis_index("y") ^ (block // 2)) + side, 8)
+    ring_bias_ref[...] = jnp.concatenate([bias, jnp.zeros_like(bias)], axis=0)
     y = lax.axis_index("y")
     for k, out in enumerate((r0, r1, r2, r3)):
         out[0] = ring_ref[turned(y, k)]
         out[1] = sibling_ref[turned(y, k)]
 
 
-def ring_pack(ring, other):
+def ring_pack(ring, other, view_mask):
     return pl.pallas_call(
         ring_pack_kernel,
-        out_shape=[jax.ShapeDtypeStruct((2, CELLS, CELLS), BF16)] * 4,
-        in_specs=[VMEM] * 2,
-        out_specs=[VMEM] * 4,
+        out_shape=[jax.ShapeDtypeStruct((2, CELLS, CELLS), BF16)] * 4
+        + [jax.ShapeDtypeStruct((32, CELLS), BF16), jax.ShapeDtypeStruct((16, CELLS), BF16)],
+        in_specs=[VMEM] * 3,
+        out_specs=[VMEM] * 6,
         compiler_params=params(4),
         name="ring_pack",
-    )(ring, other)
+    )(ring, other, view_mask)
 
 
 def stack_kernel(z0, z1, z2, z3, *refs):
@@ -141,7 +151,6 @@
         in_specs=[VMEM] * 4 + [ANY] * len(order),
         out_specs=VMEM,
         compiler_params=params(4),
-        cost_estimate=pl.CostEstimate(flops=18000000000, bytes_accessed=100000, transcendentals=0),
         name="stack",
     )(*z, *order)
 
@@ -259,9 +268,7 @@
 
 
 def view_kernel(own_ref, other_ref, ring_ref, mask_ref, out_hbm, out_ref, sems, key_s, value_s, s_a, s_b):
-    core = lax.axis_index("c")
-    block = rows_of((32, 32))
-    bias = seen_bias(mask_ref, jnp.where(block < 16, 2 * block + core, 2 * (block - 16) + 1 - core), 32)
+    bias = mask_ref[...]
     for b in range(32):
         kv = own_ref[b, 0:CELLS] if b < 16 else other_ref[b - 16]
         fill(key_s, value_s, b, kv, bias[b : b + 1])
@@ -279,7 +286,7 @@
         away(j).wait()
 
 
-def view_attention(own, other, ring_out, view_mask):
+def view_attention(own, other, ring_out, bias):
     rows = pltpu.VMEM((4096, CELLS), BF16)
     scores = pltpu.VMEM((TILE, 4096), F32)
     return pl.pallas_call(
@@ -298,17 +305,12 @@
         compiler_params=params(20),
         cost_estimate=pl.CostEstimate(flops=1000000, bytes_accessed=100000, transcendentals=0),
         name="view_attention",
-    )(own, other, ring_out, view_mask)
+    )(own, other, ring_out, bias)
 
 
 def ring_kernel(own_ref, r0, r1, r2, r3, mask_ref, out_ref, key_s, value_s, s_ref):
-    core = lax.axis_index("c")
-    y = lax.axis_index("y")
-    ring = lax.axis_index("g") * 2 + lax.axis_index("zl")
     lane = lanes((CELLS, CELLS))
-    block = rows_of((8, 32))
-    side = jnp.where(block % 2 == 0, core, 1 - core)
-    bias = seen_bias(mask_ref, ring * 8 + 2 * (y ^ (block // 2)) + side, 8)
+    bias = mask_ref[...]
     for k, piece in enumerate((r0, r1, r2, r3)):
         for n in range(2):
             fill(key_s, value_s, 2 * k + n, piece[n], bias[2 * k + n : 2 * k + n + 1])
@@ -338,7 +340,7 @@
         row_max = following
 
 
-def ring_attention(own, pieces, view_mask):
+def ring_attention(own, pieces, bias):
     return pl.pallas_call(
         ring_kernel,
         out_shape=jax.ShapeDtypeStruct((MAIN, O_ROWS, CELLS), BF16),
@@ -352,16 +354,11 @@
         compiler_params=params(12),
         cost_estimate=pl.CostEstimate(flops=1000000, bytes_accessed=100000, transcendentals=0),
         name="ring_attention",
-    )(own, *pieces, view_mask)
-
-
-def time_kernel(z0, z1, z2, z3, x_ref, times_ref, o0, o1, o2, o3, key_s, value_s, q_s, s_ref):
+    )(own, *pieces, bias)
+
+
+def time_bias(times_ref):
     frame = lax.axis_index("f")
-    lane = lanes((CELLS, CELLS))
-    own = (z0, z1, z2, z3)
-    far = tuple(x_ref.at[k] for k in range(4))
-    outs = (o0, o1, o2, o3)
-
     l8, r8 = lanes((8, 128)), rows_of((8, 128))
     query_time = jnp.zeros((8, 128), jnp.int32)
     key_time = jnp.zeros((8, 128), jnp.int32)
@@ -370,17 +367,21 @@
         query_time = jnp.where(l8 == HEAD + k, now, query_time)
         key_time = jnp.where(r8 == k, now, key_time)
     near = (jnp.abs(query_time - key_time) <= REACH) & (l8 - HEAD != r8)
-    bias = row(jnp.where((l8 >= HEAD) & (l8 < HEAD + 4) & jnp.logical_not(near), NEG, 0.0))
-    low = row(jnp.where(lanes((1, CELLS)) < HEAD, 1.0, 0.0))
-    high = row(jnp.where(lanes((1, CELLS)) < HEAD, 0.0, 1.0))
-
+    return row(jnp.where((l8 >= HEAD) & (l8 < HEAD + 4) & jnp.logical_not(near), NEG, 0.0))
+
+
+WORK = [(i, head) for i in range(2) for head in range(5)]
+
+
+def near_kernel(z0, z1, z2, z3, times_ref, *refs):
+    state_ref, q_s, key_s, value_s, s_ref = refs[-5:]
+    lane = lanes((CELLS, CELLS))
+    own = (z0, z1, z2, z3)
+    bias = time_bias(times_ref)
     for head in range(5):
-        for k in range(8):
-            at = slice(head * CELLS, (head + 1) * CELLS)
-            kv = (own + far)[k][at]
-            rows = slice(k * CELLS, (k + 1) * CELLS)
-            key_s[head, rows] = kv * low + bias[k : k + 1]
-            value_s[head, rows] = kv * high + low
+        for k in range(4):
+            kv = own[k][head * CELLS : (head + 1) * CELLS]
+            fill(key_s.at[head], value_s.at[head], k, kv, bias[k : k + 1])
     for k in range(4):
         rows = slice(k * CELLS, (k + 1) * CELLS)
         hot = jnp.where(lane == HEAD + k, 1.0, 0.0)
@@ -393,24 +394,70 @@
         q_s[4, rows] = jnp.where(lane < HEAD, qq, hot).astype(BF16)
 
     wide = lanes((TILE, CELLS))
-    work = [(i, head) for i in range(2) for head in range(5)]
 
     def begin(n):
-        i, head = work[n]
-        return score_tile(q_s[head, i * TILE : (i + 1) * TILE], key_s.at[head], s_ref.at[n % 2], 1024)
+        i, head = WORK[n]
+        return score_tile(q_s[head, i * TILE : (i + 1) * TILE], key_s.at[head], s_ref.at[n % 2], 512)
 
     row_max = begin(0)
+    for n, (i, head) in enumerate(WORK):
+        following = begin(n + 1) if n + 1 < len(WORK) else None
+        total = weigh_tile(s_ref.at[n % 2], row_max, value_s.at[head], 512)
+        state_ref[head, i * TILE : (i + 1) * TILE] = jnp.where((wide >= 32) & (wide < HEAD), row_max, total)
+        row_max = following
+
+
+def time_near(own, frame_times, order):
+    return pl.pallas_call(
+        near_kernel,
+        out_shape=[jax.ShapeDtypeStruct((5, 512, CELLS), F32), jax.ShapeDtypeStruct((5, 512, CELLS), BF16)],
+        in_specs=[VMEM] * 4 + [SMEM] + [ANY] * len(order),
+        out_specs=[VMEM] * 2,
+        scratch_shapes=[
+            pltpu.VMEM((5, 512, CELLS), BF16),
+            pltpu.VMEM((5, 512, CELLS), BF16),
+            pltpu.VMEM((2, TILE, 512), F32),
+        ],
+        compiler_params=params(12),
+        cost_estimate=pl.CostEstimate(flops=NEAR_FLOPS, bytes_accessed=2000000, transcendentals=1300000),
+        name="time_near",
+    )(*own, frame_times, *order)
+
+
+def far_kernel(state_ref, q_any, x_ref, times_ref, o0, o1, o2, o3, q_ref, sems, key_s, value_s, s_ref):
+    load = pltpu.make_async_copy(q_any, q_ref, sems.at[0])
+    load.start()
+    outs = (o0, o1, o2, o3)
+    bias = time_bias(times_ref)
+    for head in range(5):
+        for k in range(4):
+            kv = x_ref[k, head * CELLS : (head + 1) * CELLS]
+            fill(key_s.at[head], value_s.at[head], k, kv, bias[k + 4 : k + 5])
+
+    wide = lanes((TILE, CELLS))
+
+    def begin(n):
+        i, head = WORK[n]
+        return score_tile(q_ref[head, i * TILE : (i + 1) * TILE], key_s.at[head], s_ref.at[n % 2], 512)
+
+    load.wait()
+    far_max = begin(0)
     heads, levels = [], []
-    for n, (i, head) in enumerate(work):
-        following = begin(n + 1) if n + 1 < len(work) else None
-        total = weigh_tile(s_ref.at[n % 2], row_max, value_s.at[head], 1024)
-        sums = swap_halves(total)
+    for n, (i, head) in enumerate(WORK):
+        following = begin(n + 1) if n + 1 < len(WORK) else None
+        state = state_ref[head, i * TILE : (i + 1) * TILE]
+        near_max = state[:, 32:33]
+        row_max = jnp.maximum(near_max, far_max)
+        total = weigh_tile(s_ref.at[n % 2], row_max, value_s.at[head], 512)
+        total = total + state * jnp.exp2((near_max - row_max) * RATE)
+        sums = total[:, 0:1]
+        normal = total / sums
         if head % 2 == 0:
-            heads.append(jnp.where(wide < HEAD, sums / total, 0.0))
+            heads.append(jnp.where(wide < HEAD, swap_halves(normal), 0.0))
         else:
-            heads.append(jnp.where(wide < HEAD, 0.0, total / sums))
-        levels.append(row_max * RATE + jnp.log2(jnp.where(wide < HEAD, total, 1.0)))
-        row_max = following
+            heads.append(jnp.where(wide < HEAD, 0.0, normal))
+        levels.append(row_max * RATE + jnp.log2(sums) + jnp.zeros((TILE, CELLS), F32))
+        far_max = following
         if head < 4:
             continue
         table = level_rows(levels, wide)
@@ -425,22 +472,23 @@
         heads, levels = [], []
 
 
-def time_attention(own, crossed, frame_times):
-    return pl.pallas_call(
-        time_kernel,
+def time_far(state, q, crossed, frame_times):
+    return pl.pallas_call(
+        far_kernel,
         out_shape=[jax.ShapeDtypeStruct((T_ROWS, CELLS), BF16)] * 4,
-        in_specs=[VMEM] * 5 + [SMEM],
+        in_specs=[VMEM, ANY, VMEM, SMEM],
         out_specs=[VMEM] * 4,
         scratch_shapes=[
-            pltpu.VMEM((5, 1024, CELLS), BF16),
-            pltpu.VMEM((5, 1024, CELLS), BF16),
             pltpu.VMEM((5, 512, CELLS), BF16),
-            pltpu.VMEM((2, TILE, 1024), F32),
+            pltpu.SemaphoreType.DMA((1,)),
+            pltpu.VMEM((5, 512, CELLS), BF16),
+            pltpu.VMEM((5, 512, CELLS), BF16),
+            pltpu.VMEM((2, TILE, 512), F32),
         ],
-        compiler_params=params(16),
-        cost_estimate=pl.CostEstimate(flops=700000000, bytes_accessed=2000000, transcendentals=2700000),
-        name="time_attention",
-    )(*own, crossed, frame_times)
+        compiler_params=params(12),
+        cost_estimate=pl.CostEstimate(flops=400000000, bytes_accessed=2000000, transcendentals=1300000),
+        name="time_far",
+    )(state, in_hbm(q), crossed, frame_times)
 
 
 def pass_kernel(*refs):
@@ -578,16 +626,17 @@
     *z, to_ring, to_view = pack(q, k, v)
     own = lax.all_to_all(to_view, ("g", "zl", "y"), 0, 0)
     z = [z[0]] + [across(z[i], i) for i in (1, 2, 3)]
-    ring = ring_pack(to_ring, sibling(to_ring))
+    *ring, bias, ring_bias = ring_pack(to_ring, sibling(to_ring), view_mask)
     ring = [ring[0]] + [around(ring[i], i) for i in (1, 2, 3)]
-    some = stack(z, ring[1:])
-    crossed = across(some, 4)
-    other = sibling(keep(own, [some]))
-    ring_out = ring_attention(own, ring, view_mask)
-    view_out = view_attention(own, other, ring_out, view_mask)
+    state, time_q = time_near(z, frame_times, ring[1:])
+    kept = keep(own, [state])
+    other = sibling(kept)
+    crossed = across(stack(z, [kept]), 4)
+    ring_out = ring_attention(own, ring, ring_bias)
+    view_out = view_attention(own, other, ring_out, bias)
     view_out = pass_after(view_out, (crossed,))
     view_back = lax.all_to_all(view_out, ("g", "zl", "y"), 0, 0)
-    pieces = time_attention(z, crossed, frame_times)
+    pieces = time_far(state, time_q, crossed, frame_times)
     pieces = [pieces[0]] + [across(pieces[i], i) for i in (1, 2, 3)]
     result = join(view_back, pieces, out_weight)
     return result.reshape(1, 1, CELLS, model)

time: 92.2 us -> 95.8 us (1.039)
  Pallas kernels: 26.6 us -> 32.6 us
  waiting for transfers between devices: 29 us -> 25.3 us
  local copies, waits for them, and re-layouts: 0.7 us -> 2.44 us
    pallas_call x1 -> x2, Pallas kernels: 4.92 us -> 11 us  [the longest x1 8.28 us: time_far(): pl.pallas_call(far_kernel, out_shape=[jax.ShapeDtypeStruct((T_ROWS, CELLS...]
    ppermute x3, waiting for transfers between devices: 7.97 us -> 5.7 us  [around(): return lax.ppermute(array, 'y', [(i, i ^ k) for i in range(RING)])]
    all_to_all x1, waiting for transfers between devices: 12.2 us -> 10 us  [local(): own = lax.all_to_all(to_view, ('g', 'zl', 'y'), 0, 0)]
    unnamed x8 -> x10, local copies, waits for them, and re-layouts: 0.7 us -> 2.44 us
  transfers between devices with their start and end apart: 14 -> 14, of which waited for: 8 -> 7; matrix products, arithmetic and copies ran while one was open for 0% -> 0% of each run, Pallas kernels for 23% -> 28%
where the time goes in v8:
time: 95.8 us; the launch traced here: 95.4 us
  starting transfers between devices  34.8 us (36%)
  Pallas kernels  32.6 us (34%)
  waiting for transfers between devices  25.3 us (26%)
  local copies, waits for them, and re-layouts  2.44 us (3%)
    ppermute x7, starting transfers between devices, across(): return lax.ppermute(array, 'f', [(i, i ^ k) for i in range(FRAMES)])  16.8 us
    pallas_call x1, Pallas kernels, view_attention(): pl.pallas_call(view_kernel, out_shape=pltpu.HBM((MAIN, O_ROWS, CELLS), BF...  12.2 us
    all_to_all x1, waiting for transfers between devices, local(): own = lax.all_to_all(to_view, ('g', 'zl', 'y'), 0, 0)  10 us
    ppermute x7, waiting for transfers between devices, across(): return lax.ppermute(array, 'f', [(i, i ^ k) for i in range(FRAMES)])  9.57 us
    pallas_call x1, Pallas kernels, time_far(): pl.pallas_call(far_kernel, out_shape=[jax.ShapeDtypeStruct((T_ROWS, CELLS...  8.28 us
    all_to_all x1, starting transfers between devices, local(): own = lax.all_to_all(to_view, ('g', 'zl', 'y'), 0, 0)  7.85 us
    ppermute x3, waiting for transfers between devices, around(): return lax.ppermute(array, 'y', [(i, i ^ k) for i in range(RING)])  5.7 us
    ppermute x3, starting transfers between devices, around(): return lax.ppermute(array, 'y', [(i, i ^ k) for i in range(RING)])  5.28 us
  transfers between devices with their start and end apart: 14, of which 7 were waited for; matrix products, arithmetic and copies ran while one was open for 0% of the time, Pallas kernels for 28%

profile of v8, /device:TPU:8, one launch (start us, length us, event | category | flops | bytes accessed | tf_op | source)
XLA Modules:
  0.0 95.4 jit_solution(2202914568488524259)
XLA Ops:
  0.0 0.0 copy-start.4
  0.0 2.9 %pack.1 = (bf16[960,128]{1,0:T(8,128)(2,1)S(1)}, bf16[960,128]{1,0:T(8,128)(2,1)S(1)}, bf16[960,128]{1,0:T(8,128)(2,1)S(1)}, bf16[960,128]{1,0:T(8,128)(2,1)S(1)...) custom-call(bf16[128,1280]{1,0:T(8,128)(2,1)} %bitcast.4, bf16[128,1280]{1,0:T(8,128)(2,1)} %bitcast.5, ...), custom_call_target="tpu_custom_call" | custom-call | tf_op jit(solution)/shard_map/pack/pallas_call | solution.py:99
  3.0 0.1 collective-permute-start.3
  3.1 3.4 %collective-permute-start = (bf16[960,128]{1,0:T(8,128)(2,1)S(1)}, bf16[960,128]{1,0:T(8,128)(2,1)S(1)}, u32[]{:S(2)}, u32[]{:S(2)}) collective-permute-start(bf16[960,128]{1,0:T(8,128)(2,1)S(1)} %get-tuple-element.25), channel_id=1, source_target_pairs={{0,16},{16,0},{32,48},{48,32},{64,80},{80,64},{96,112},{112,96},{1... | collective-permute-start | bytes 737288 | tf_op jit(solution)/shard_map/ppermute | solution.py:612
  6.4 5.4 %collective-permute-start.1 = (bf16[960,128]{1,0:T(8,128)(2,1)S(1)}, bf16[960,128]{1,0:T(8,128)(2,1)S(1)}, u32[]{:S(2)}, u32[]{:S(2)}) collective-permute-start(bf16[960,128]{1,0:T(8,128)(2,1)S(1)} %get-tuple-element.26), channel_id=1, source_target_pairs={{0,32},{16,48},{32,0},{48,16},{64,96},{80,112},{96,64},{112,80},{1... | collective-permute-start | bytes 737288 | tf_op jit(solution)/shard_map/ppermute | solution.py:612
  11.8 0.0 collective-permute-start.2
  11.8 7.8 %all-to-all-start = ((bf16[16,256,128]{2,1,0:T(8,128)(2,1)}), bf16[16,256,128]{2,1,0:T(8,128)(2,1)S(1)}, u32[]{:S(2)}, u32[]{:S(2)}) async-start(bf16[16,256,128]{2,1,0:T(8,128)(2,1)} %get-tuple-element.23), calls=%async_computation | async-start | bytes 2097152 | tf_op jit(solution)/shard_map/all_to_all | solution.py:627
  19.7 0.0 collective-permute-done.3.sibling_ref
  19.7 0.0 copy-start.1
  19.7 0.9 copy-done.1
  20.6 0.4 ring_pack.1
  20.9 0.1 collective-permute-start.4
  21.0 2.8 %collective-permute-start.5 = (bf16[2,128,128]{2,1,0:T(8,128)(2,1)S(1)}, bf16[2,128,128]{2,1,0:T(8,128)(2,1)S(1)}, u32[]{:S(2)}, u32[]{:S(2)}) collective-permute-start(bf16[2,128,128]{2,1,0:T(8,128)(2,1)S(1)} %get-tuple-element.30), channel_id=1, source_target_pairs={{0,4},{2,6},{4,0},{6,2},{1,5},{3,7},{5,1},{7,3},{8,12},{10,14},{12... | collective-permute-start | bytes 196616 | tf_op jit(solution)/shard_map/ppermute | solution.py:616
  23.9 3.5 %collective-permute-done.4.refs_0_.r1 = bf16[2,128,128]{2,1,0:T(8,128)(2,1)S(1)} collective-permute-done((bf16[2,128,128]{2,1,0:T(8,128)(2,1)S(1)}, bf16[2,128,128]{2,1,0:T(8,128)(2,1)S(1)}, u32[]{:S(2)}, u32[]{:S(2)}) %collective-permute-start.4) | collective-permute-done | bytes 65568 | tf_op jit(solution)/shard_map/ppermute | solution.py:616
  27.3 2.3 %collective-permute-start.6 = (bf16[2,128,128]{2,1,0:T(8,128)(2,1)S(1)}, bf16[2,128,128]{2,1,0:T(8,128)(2,1)S(1)}, u32[]{:S(2)}, u32[]{:S(2)}) collective-permute-start(bf16[2,128,128]{2,1,0:T(8,128)(2,1)S(1)} %get-tuple-element.31), channel_id=1, source_target_pairs={{0,6},{2,4},{4,2},{6,0},{1,7},{3,5},{5,3},{7,1},{8,14},{10,12},{12... | collective-permute-start | bytes 196616 | tf_op jit(solution)/shard_map/ppermute | solution.py:616
  29.7 0.8 collective-permute-done.5.refs_1_.r2
  30.5 1.4 %collective-permute-done.6.refs_2_.r3 = bf16[2,128,128]{2,1,0:T(8,128)(2,1)S(1)} collective-permute-done((bf16[2,128,128]{2,1,0:T(8,128)(2,1)S(1)}, bf16[2,128,128]{2,1,0:T(8,128)(2,1)S(1)}, u32[]{:S(2)}, u32[]{:S(2)}) %collective-permute-start.6) | collective-permute-done | bytes 65568 | tf_op jit(solution)/shard_map/ppermute | solution.py:616
  31.9 0.0 collective-permute-done.z1
  31.9 2.5 %collective-permute-done.1.z2 = bf16[960,128]{1,0:T(8,128)(2,1)S(1)} collective-permute-done((bf16[960,128]{1,0:T(8,128)(2,1)S(1)}, bf16[960,128]{1,0:T(8,128)(2,1)S(1)}, u32[]{:S(2)}, u32[]{:S(2)}) %collective-permute-start.1) | collective-permute-done | bytes 245792 | tf_op jit(solution)/shard_map/ppermute | solution.py:612
  34.4 0.0 collective-permute-done.2.z3
  34.4 0.0 copy-done.4
  34.4 2.7 %time_near.1 = (f32[5,512,128]{2,1,0:T(8,128)S(1)}, bf16[5,512,128]{2,1,0:T(8,128)(2,1)S(1)}) custom-call(bf16[960,128]{1,0:T(8,128)(2,1)S(1)} %get-tuple-element.24.z0, bf16[960,128]{1,0:T(8,128)(2,1)S(1)} %collective-permute-done.z1, bf16[960,128]{1,0:T(8,128)(2,1)S(1)} %collective-permute-done.1.z2, bf16[960,128]{1,0:T(8,128)(2,1)S(1)} %collective-permute-done.2.z3, ...), custom_call_target="tpu_custom_call" | custom-call | flops 19000000512 | bytes 2000000 | tf_op jit(solution)/shard_map/time_near/pallas_call | solution.py:411
  37.1 0.0 copy-start
  37.1 0.9 copy-done
  38.0 0.0 copy-start.2
  38.0 0.6 copy-done.2
  38.6 10.0 %all-to-all-done.own_ref = bf16[16,256,128]{2,1,0:T(8,128)(2,1)S(1)} async-done(((bf16[16,256,128]{2,1,0:T(8,128)(2,1)}), bf16[16,256,128]{2,1,0:T(8,128)(2,1)S(1)}, u32[]{:S(2)}, u32[]{:S(2)}) %all-to-all-start) | async-done | bytes 1048608 | tf_op jit(solution)/shard_map/all_to_all | solution.py:627
  48.6 0.0 copy-start.3
  48.8 0.7 collective-permute-start.8
  49.4 0.0 collective-permute-start.7
  49.4 0.0 copy-done.3
  49.5 3.0 %ring_attention.1.ring_ref = bf16[16,144,128]{2,1,0:T(8,128)(2,1)S(1)} custom-call(bf16[16,256,128]{2,1,0:T(8,128)(2,1)S(1)} %all-to-all-done.own_ref, bf16[2,128,128]{2,1,0:T(8,128)(2,1)S(1)} %get-tuple-element.33.r0, bf16[2,128,128]{2,1,0:T(8,128)(2,1)S(1)} %collective-permute-done.4.refs_0_.r1, ...), custom_call_target="tpu_custom_call" | custom-call | flops 1000000 | bytes 100000 | tf_op jit(solution)/shard_map/ring_attention/pallas_call | solution.py:344
  52.5 0.0 collective-permute-done.7.other_ref
  52.5 12.2 %view_attention.1.refs_0_ = bf16[16,144,128]{2,1,0:T(8,128)(2,1)} custom-call(bf16[16,256,128]{2,1,0:T(8,128)(2,1)S(1)} %all-to-all-done.own_ref, bf16[16,128,128]{2,1,0:T(8,128)(2,1)S(1)} %collective-permute-done.7.other_ref, bf16[16,144,128]{2,1,0:T(8,128)(2,1)S(1)} %ring_attention.1.ring_ref, bf16[32,128]{1,0:T(8,128)(2,1)S(1)} %get-tuple-element.35.mask_ref), custom_call_target="tpu_custom_call" | custom-call | flops 1000000 | bytes 100000 | tf_op jit(solution)/shard_map/view_attention/pallas_call | solution.py:292
  64.7 0.0 collective-permute-done.8.refs_1_.x_ref
  64.7 4.7 %all-to-all-start.1 = ((bf16[16,144,128]{2,1,0:T(8,128)(2,1)}), bf16[16,144,128]{2,1,0:T(8,128)(2,1)S(1)}, u32[]{:S(2)}, u32[]{:S(2)}) async-start(bf16[16,144,128]{2,1,0:T(8,128)(2,1)} %pass_after.1), calls=%async_computation.1 | async-start | bytes 1179648 | tf_op jit(solution)/shard_map/all_to_all | solution.py:638
  69.4 8.3 %time_far.1 = (bf16[336,128]{1,0:T(8,128)(2,1)S(1)}, bf16[336,128]{1,0:T(8,128)(2,1)S(1)}, bf16[336,128]{1,0:T(8,128)(2,1)S(1)}, bf16[336,128]{1,0:T(8,128)(2,1)S(1)}) custom-call(f32[5,512,128]{2,1,0:T(8,128)S(1)} %get-tuple-element.32.refs_0_.state_ref, bf16[5,512,128]{2,1,0:T(8,128)(2,1)} %copy-done, ...), custom_call_target="tpu_custom_call" | custom-call | flops 400000000 | bytes 2000000 | tf_op jit(solution)/shard_map/time_far/pallas_call | solution.py:476
  77.7 3.0 %collective-permute-start.10 = (bf16[336,128]{1,0:T(8,128)(2,1)S(1)}, bf16[336,128]{1,0:T(8,128)(2,1)S(1)}, u32[]{:S(2)}, u32[]{:S(2)}) collective-permute-start(bf16[336,128]{1,0:T(8,128)(2,1)S(1)} %get-tuple-element.39), channel_id=1, source_target_pairs={{0,32},{16,48},{32,0},{48,16},{64,96},{80,112},{96,64},{112,80},{1... | collective-permute-start | bytes 258056 | tf_op jit(solution)/shard_map/ppermute | solution.py:612
  80.7 4.4 %collective-permute-start.11 = (bf16[336,128]{1,0:T(8,128)(2,1)S(1)}, bf16[336,128]{1,0:T(8,128)(2,1)S(1)}, u32[]{:S(2)}, u32[]{:S(2)}) collective-permute-start(bf16[336,128]{1,0:T(8,128)(2,1)S(1)} %get-tuple-element.40), channel_id=1, source_target_pairs={{0,48},{16,32},{32,16},{48,0},{64,112},{80,96},{96,80},{112,64},{1... | collective-permute-start | bytes 258056 | tf_op jit(solution)/shard_map/ppermute | solution.py:612
  85.1 0.0 collective-permute-start.9
  85.1 2.7 %collective-permute-done.10.t2 = bf16[336,128]{1,0:T(8,128)(2,1)S(1)} collective-permute-done((bf16[336,128]{1,0:T(8,128)(2,1)S(1)}, bf16[336,128]{1,0:T(8,128)(2,1)S(1)}, u32[]{:S(2)}, u32[]{:S(2)}) %collective-permute-start.10) | collective-permute-done | bytes 86048 | tf_op jit(solution)/shard_map/ppermute | solution.py:612
  87.8 4.4 %collective-permute-done.11.t3 = bf16[336,128]{1,0:T(8,128)(2,1)S(1)} collective-permute-done((bf16[336,128]{1,0:T(8,128)(2,1)S(1)}, bf16[336,128]{1,0:T(8,128)(2,1)S(1)}, u32[]{:S(2)}, u32[]{:S(2)}) %collective-permute-start.11) | collective-permute-done | bytes 86048 | tf_op jit(solution)/shard_map/ppermute | solution.py:612
  92.2 0.0 collective-permute-done.9.t1
  92.2 0.0 all-to-all-done.1.view_ref
  92.2 3.0 %join.1 = bf16[128,1280]{1,0:T(8,128)(2,1)} custom-call(bf16[16,144,128]{2,1,0:T(8,128)(2,1)S(1)} %all-to-all-done.1.view_ref, bf16[336,128]{1,0:T(8,128)(2,1)S(1)} %get-tuple-element.37.t0, bf16[336,128]{1,0:T(8,128)(2,1)S(1)} %collective-permute-done.9.t1, bf16[336,128]{1,0:T(8,128)(2,1)S(1)} %collective-permute-done.10.t2, ...), custom_call_target="tpu_custom_call" | custom-call | tf_op jit(solution)/shard_map/join/pallas_call | solution.py:595
  (3 shorter events, 0.1 us)
Async XLA Ops:
  0.0 34.4 %copy-start.4 = (s32[8]{0:T(128)S(1)}, s32[8]{0:T(128)}, u32[]{:S(2)}) copy-start(s32[8]{0:T(128)} %times_ref.3) | copy-start | bytes 100
  3.0 16.7 %collective-permute-start.3 = (bf16[4,128,128]{2,1,0:T(8,128)(2,1)S(1)}, bf16[4,128,128]{2,1,0:T(8,128)(2,1)S(1)}, u32[]{:S(2)}, u32[]{:S(2)}) collective-permute-start(bf16[4,128,128]{2,1,0:T(8,128)(2,1)S(1)} %get-tuple-element.28.ring_ref), channel_id=1, source_target_pairs={{0,1},{1,0},{2,3},{3,2},{4,5},{5,4},{6,7},{7,6},{8,9},{9,8},{10,11... | collective-permute-start | bytes 393224 | tf_op jit(solution)/shard_map/ppermute | solution.py:620
  3.1 28.9 %collective-permute-start = (bf16[960,128]{1,0:T(8,128)(2,1)S(1)}, bf16[960,128]{1,0:T(8,128)(2,1)S(1)}, u32[]{:S(2)}, u32[]{:S(2)}) collective-permute-start(bf16[960,128]{1,0:T(8,128)(2,1)S(1)} %get-tuple-element.25), channel_id=1, source_target_pairs={{0,16},{16,0},{32,48},{48,32},{64,80},{80,64},{96,112},{112,96},{1... | collective-permute-start | bytes 737288 | tf_op jit(solution)/shard_map/ppermute | solution.py:612
  6.4 28.0 %collective-permute-start.1 = (bf16[960,128]{1,0:T(8,128)(2,1)S(1)}, bf16[960,128]{1,0:T(8,128)(2,1)S(1)}, u32[]{:S(2)}, u32[]{:S(2)}) collective-permute-start(bf16[960,128]{1,0:T(8,128)(2,1)S(1)} %get-tuple-element.26), channel_id=1, source_target_pairs={{0,32},{16,48},{32,0},{48,16},{64,96},{80,112},{96,64},{112,80},{1... | collective-permute-start | bytes 737288 | tf_op jit(solution)/shard_map/ppermute | solution.py:612
  11.8 22.6 %collective-permute-start.2 = (bf16[960,128]{1,0:T(8,128)(2,1)S(1)}, bf16[960,128]{1,0:T(8,128)(2,1)S(1)}, u32[]{:S(2)}, u32[]{:S(2)}) collective-permute-start(bf16[960,128]{1,0:T(8,128)(2,1)S(1)} %get-tuple-element.27), channel_id=1, source_target_pairs={{0,48},{16,32},{32,16},{48,0},{64,112},{80,96},{96,80},{112,64},{1... | collective-permute-start | bytes 737288 | tf_op jit(solution)/shard_map/ppermute | solution.py:612
  11.8 36.8 %all-to-all-start = ((bf16[16,256,128]{2,1,0:T(8,128)(2,1)}), bf16[16,256,128]{2,1,0:T(8,128)(2,1)S(1)}, u32[]{:S(2)}, u32[]{:S(2)}) async-start(bf16[16,256,128]{2,1,0:T(8,128)(2,1)} %get-tuple-element.23), calls=%async_computation | async-start | bytes 2097152 | tf_op jit(solution)/shard_map/all_to_all | solution.py:627
  19.7 0.9 copy-start.1
  20.9 6.4 %collective-permute-start.4 = (bf16[2,128,128]{2,1,0:T(8,128)(2,1)S(1)}, bf16[2,128,128]{2,1,0:T(8,128)(2,1)S(1)}, u32[]{:S(2)}, u32[]{:S(2)}) collective-permute-start(bf16[2,128,128]{2,1,0:T(8,128)(2,1)S(1)} %get-tuple-element.29), channel_id=1, source_target_pairs={{0,2},{2,0},{4,6},{6,4},{1,3},{3,1},{5,7},{7,5},{8,10},{10,8},{12,... | collective-permute-start | bytes 196616 | tf_op jit(solution)/shard_map/ppermute | solution.py:616
  21.0 9.5 %collective-permute-start.5 = (bf16[2,128,128]{2,1,0:T(8,128)(2,1)S(1)}, bf16[2,128,128]{2,1,0:T(8,128)(2,1)S(1)}, u32[]{:S(2)}, u32[]{:S(2)}) collective-permute-start(bf16[2,128,128]{2,1,0:T(8,128)(2,1)S(1)} %get-tuple-element.30), channel_id=1, source_target_pairs={{0,4},{2,6},{4,0},{6,2},{1,5},{3,7},{5,1},{7,3},{8,12},{10,14},{12... | collective-permute-start | bytes 196616 | tf_op jit(solution)/shard_map/ppermute | solution.py:616
  27.3 4.6 %collective-permute-start.6 = (bf16[2,128,128]{2,1,0:T(8,128)(2,1)S(1)}, bf16[2,128,128]{2,1,0:T(8,128)(2,1)S(1)}, u32[]{:S(2)}, u32[]{:S(2)}) collective-permute-start(bf16[2,128,128]{2,1,0:T(8,128)(2,1)S(1)} %get-tuple-element.31), channel_id=1, source_target_pairs={{0,6},{2,4},{4,2},{6,0},{1,7},{3,5},{5,3},{7,1},{8,14},{10,12},{12... | collective-permute-start | bytes 196616 | tf_op jit(solution)/shard_map/ppermute | solution.py:616
  37.1 0.9 copy-start
  38.0 0.6 copy-start.2
  48.6 0.8 copy-start.3
  48.8 15.9 %collective-permute-start.8 = (bf16[4,640,128]{2,1,0:T(8,128)(2,1)S(1)}, bf16[4,640,128]{2,1,0:T(8,128)(2,1)S(1)}, u32[]{:S(2)}, u32[]{:S(2)}) collective-permute-start(bf16[4,640,128]{2,1,0:T(8,128)(2,1)S(1)} %stack.1), channel_id=1, source_target_pairs={{0,64},{16,80},{32,96},{48,112},{64,0},{80,16},{96,32},{112,48},{1... | collective-permute-start | bytes 1966088 | tf_op jit(solution)/shard_map/ppermute | solution.py:612
  49.4 3.0 %collective-permute-start.7 = (bf16[16,128,128]{2,1,0:T(8,128)(2,1)S(1)}, bf16[16,128,128]{2,1,0:T(8,128)(2,1)S(1)}, u32[]{:S(2)}, u32[]{:S(2)}) collective-permute-start(bf16[16,128,128]{2,1,0:T(8,128)(2,1)S(1)} %keep.1.refs_0_), channel_id=1, source_target_pairs={{0,1},{1,0},{2,3},{3,2},{4,5},{5,4},{6,7},{7,6},{8,9},{9,8},{10,11... | collective-permute-start | bytes 1572872 | tf_op jit(solution)/shard_map/ppermute | solution.py:620
  64.7 27.5 %all-to-all-start.1 = ((bf16[16,144,128]{2,1,0:T(8,128)(2,1)}), bf16[16,144,128]{2,1,0:T(8,128)(2,1)S(1)}, u32[]{:S(2)}, u32[]{:S(2)}) async-start(bf16[16,144,128]{2,1,0:T(8,128)(2,1)} %pass_after.1), calls=%async_computation.1 | async-start | bytes 1179648 | tf_op jit(solution)/shard_map/all_to_all | solution.py:638
  77.7 10.1 %collective-permute-start.10 = (bf16[336,128]{1,0:T(8,128)(2,1)S(1)}, bf16[336,128]{1,0:T(8,128)(2,1)S(1)}, u32[]{:S(2)}, u32[]{:S(2)}) collective-permute-start(bf16[336,128]{1,0:T(8,128)(2,1)S(1)} %get-tuple-element.39), channel_id=1, source_target_pairs={{0,32},{16,48},{32,0},{48,16},{64,96},{80,112},{96,64},{112,80},{1... | collective-permute-start | bytes 258056 | tf_op jit(solution)/shard_map/ppermute | solution.py:612
  80.7 11.5 %collective-permute-start.11 = (bf16[336,128]{1,0:T(8,128)(2,1)S(1)}, bf16[336,128]{1,0:T(8,128)(2,1)S(1)}, u32[]{:S(2)}, u32[]{:S(2)}) collective-permute-start(bf16[336,128]{1,0:T(8,128)(2,1)S(1)} %get-tuple-element.40), channel_id=1, source_target_pairs={{0,48},{16,32},{32,16},{48,0},{64,112},{80,96},{96,80},{112,64},{1... | collective-permute-start | bytes 258056 | tf_op jit(solution)/shard_map/ppermute | solution.py:612
  85.1 7.1 %collective-permute-start.9 = (bf16[336,128]{1,0:T(8,128)(2,1)S(1)}, bf16[336,128]{1,0:T(8,128)(2,1)S(1)}, u32[]{:S(2)}, u32[]{:S(2)}) collective-permute-start(bf16[336,128]{1,0:T(8,128)(2,1)S(1)} %get-tuple-element.38), channel_id=1, source_target_pairs={{0,16},{16,0},{32,48},{48,32},{64,80},{80,64},{96,112},{112,96},{1... | collective-permute-start | bytes 258056 | tf_op jit(solution)/shard_map/ppermute | solution.py:612

commit v9 on v7

--- a/solution.py
+++ b/solution.py
@@ -20,7 +20,7 @@
 Z_ROWS = 960
 X_ROWS = 640
 T_ROWS = 336
-GATE_FLOPS = 19000000000
+GATE_FLOPS = 18000000000
 O_ROWS = 144
 F32 = jnp.float32
 BF16 = jnp.bfloat16
@@ -111,22 +111,31 @@
     )(in_hbm(q), in_hbm(k), in_hbm(v))
 
 
-def ring_pack_kernel(ring_ref, sibling_ref, r0, r1, r2, r3):
+def ring_pack_kernel(ring_ref, sibling_ref, mask_ref, r0, r1, r2, r3, bias_ref, ring_bias_ref):
+    core = lax.axis_index("c")
+    block = rows_of((32, 32))
+    bias_ref[...] = seen_bias(mask_ref, jnp.where(block < 16, 2 * block + core, 2 * (block - 16) + 1 - core), 32)
+    ring = lax.axis_index("g") * 2 + lax.axis_index("zl")
+    block = rows_of((8, 32))
+    side = jnp.where(block % 2 == 0, core, 1 - core)
+    bias = seen_bias(mask_ref, ring * 8 + 2 * (lax.axis_index("y") ^ (block // 2)) + side, 8)
+    ring_bias_ref[...] = jnp.concatenate([bias, jnp.zeros_like(bias)], axis=0)
     y = lax.axis_index("y")
     for k, out in enumerate((r0, r1, r2, r3)):
         out[0] = ring_ref[turned(y, k)]
         out[1] = sibling_ref[turned(y, k)]
 
 
-def ring_pack(ring, other):
+def ring_pack(ring, other, view_mask):
     return pl.pallas_call(
         ring_pack_kernel,
-        out_shape=[jax.ShapeDtypeStruct((2, CELLS, CELLS), BF16)] * 4,
-        in_specs=[VMEM] * 2,
-        out_specs=[VMEM] * 4,
+        out_shape=[jax.ShapeDtypeStruct((2, CELLS, CELLS), BF16)] * 4
+        + [jax.ShapeDtypeStruct((32, CELLS), BF16), jax.ShapeDtypeStruct((16, CELLS), BF16)],
+        in_specs=[VMEM] * 3,
+        out_specs=[VMEM] * 6,
         compiler_params=params(4),
         name="ring_pack",
-    )(ring, other)
+    )(ring, other, view_mask)
 
 
 def gate_kernel(*refs):
@@ -276,9 +285,7 @@
 
 
 def view_kernel(own_ref, other_ref, ring_ref, mask_ref, out_hbm, out_ref, sems, key_s, value_s, s_a, s_b):
-    core = lax.axis_index("c")
-    block = rows_of((32, 32))
-    bias = seen_bias(mask_ref, jnp.where(block < 16, 2 * block + core, 2 * (block - 16) + 1 - core), 32)
+    bias = mask_ref[...]
     for b in range(32):
         kv = own_ref[b, 0:CELLS] if b < 16 else other_ref[b - 16]
         fill(key_s, value_s, b, kv, bias[b : b + 1])
@@ -296,7 +303,7 @@
         away(j).wait()
 
 
-def view_attention(own, other, ring_out, view_mask):
+def view_attention(own, other, ring_out, bias):
     rows = pltpu.VMEM((4096, CELLS), BF16)
     scores = pltpu.VMEM((TILE, 4096), F32)
     return pl.pallas_call(
@@ -315,17 +322,12 @@
         compiler_params=params(20),
         cost_estimate=pl.CostEstimate(flops=1000000, bytes_accessed=100000, transcendentals=0),
         name="view_attention",
-    )(own, other, ring_out, view_mask)
+    )(own, other, ring_out, bias)
 
 
 def ring_kernel(own_ref, r0, r1, r2, r3, mask_ref, out_ref, key_s, value_s, s_ref):
-    core = lax.axis_index("c")
-    y = lax.axis_index("y")
-    ring = lax.axis_index("g") * 2 + lax.axis_index("zl")
     lane = lanes((CELLS, CELLS))
-    block = rows_of((8, 32))
-    side = jnp.where(block % 2 == 0, core, 1 - core)
-    bias = seen_bias(mask_ref, ring * 8 + 2 * (y ^ (block // 2)) + side, 8)
+    bias = mask_ref[...]
     for k, piece in enumerate((r0, r1, r2, r3)):
         for n in range(2):
             fill(key_s, value_s, 2 * k + n, piece[n], bias[2 * k + n : 2 * k + n + 1])
@@ -355,7 +357,7 @@
         row_max = following
 
 
-def ring_attention(own, pieces, view_mask):
+def ring_attention(own, pieces, bias):
     return pl.pallas_call(
         ring_kernel,
         out_shape=jax.ShapeDtypeStruct((MAIN, O_ROWS, CELLS), BF16),
@@ -369,7 +371,7 @@
         compiler_params=params(12),
         cost_estimate=pl.CostEstimate(flops=1000000, bytes_accessed=100000, transcendentals=0),
         name="ring_attention",
-    )(own, *pieces, view_mask)
+    )(own, *pieces, bias)
 
 
 def time_kernel(z0, z1, z2, z3, x_ref, times_ref, o0, o1, o2, o3, key_s, value_s, q_s, s_ref):
@@ -595,13 +597,13 @@
     *z, to_ring, to_view = pack(q, k, v)
     own = lax.all_to_all(to_view, ("g", "zl", "y"), 0, 0)
     z = [z[0]] + [across(z[i], i) for i in (1, 2, 3)]
-    ring = ring_pack(to_ring, sibling(to_ring))
+    *ring, bias, ring_bias = ring_pack(to_ring, sibling(to_ring), view_mask)
     ring = [ring[0]] + [around(ring[i], i) for i in (1, 2, 3)]
     kept = keep(own, [gate(z[1:] + ring[1:])])
     other = sibling(kept)
     crossed = across(stack(z, [kept]), 4)
-    ring_out = ring_attention(own, ring, view_mask)
-    view_out = view_attention(own, other, ring_out, view_mask)
+    ring_out = ring_attention(own, ring, ring_bias)
+    view_out = view_attention(own, other, ring_out, bias)
     view_out = pass_after(view_out, (crossed,))
     view_back = lax.all_to_all(view_out, ("g", "zl", "y"), 0, 0)
     pieces = time_attention(z, crossed, frame_times)

time: 93 us -> 96.6 us (1.039)
  waiting for transfers between devices: 31 us -> 33.5 us
    ppermute x7, waiting for transfers between devices: 8.8 us -> 24.4 us  [across(): return lax.ppermute(array, 'f', [(i, i ^ k) for i in range(FRAMES)])]
    all_to_all x1, waiting for transfers between devices: 14.2 us -> 0.01 us  [local(): own = lax.all_to_all(to_view, ('g', 'zl', 'y'), 0, 0)]
    all_to_all x1, starting transfers between devices: 4.77 us -> 7.85 us  [local(): view_back = lax.all_to_all(view_out, ('g', 'zl', 'y'), 0, 0)]
    ppermute x3, starting transfers between devices: 4.64 us -> 2.94 us  [around(): return lax.ppermute(array, 'y', [(i, i ^ k) for i in range(RING)])]
    ppermute x7, starting transfers between devices: 16.6 us -> 15.1 us  [across(): return lax.ppermute(array, 'f', [(i, i ^ k) for i in range(FRAMES)])]
    ppermute x3, waiting for transfers between devices: 7.97 us -> 9.11 us  [around(): return lax.ppermute(array, 'y', [(i, i ^ k) for i in range(RING)])]
  transfers between devices with their start and end apart: 14 -> 14, of which waited for: 8 -> 8; matrix products, arithmetic and copies ran while one was open for 0% -> 0% of each run, Pallas kernels for 22% -> 21%
where the time goes in v9:
time: 96.6 us; the launch traced here: 95.8 us
  starting transfers between devices  34.6 us (36%)
  waiting for transfers between devices  33.5 us (35%)
  Pallas kernels  26.5 us (27%)
    ppermute x7, waiting for transfers between devices, across(): return lax.ppermute(array, 'f', [(i, i ^ k) for i in range(FRAMES)])  24.4 us
    ppermute x7, starting transfers between devices, across(): return lax.ppermute(array, 'f', [(i, i ^ k) for i in range(FRAMES)])  15.1 us
    pallas_call x1, Pallas kernels, view_attention(): pl.pallas_call(view_kernel, out_shape=pltpu.HBM((MAIN, O_ROWS, CELLS), BF...  12.2 us
    ppermute x3, waiting for transfers between devices, around(): return lax.ppermute(array, 'y', [(i, i ^ k) for i in range(RING)])  9.11 us
    all_to_all x1, starting transfers between devices, local(): own = lax.all_to_all(to_view, ('g', 'zl', 'y'), 0, 0)  8.76 us
    all_to_all x1, starting transfers between devices, local(): view_back = lax.all_to_all(view_out, ('g', 'zl', 'y'), 0, 0)  7.85 us
    pallas_call x1, Pallas kernels, time_attention(): pl.pallas_call(time_kernel, out_shape=[jax.ShapeDtypeStruct((T_ROWS, CELL...  4.92 us
    pallas_call x1, Pallas kernels, join(): pl.pallas_call(join_kernel, out_shape=jax.ShapeDtypeStruct((CELLS, HEADS...  3.02 us
  transfers between devices with their start and end apart: 14, of which 8 were waited for; matrix products, arithmetic and copies ran while one was open for 0% of the time, Pallas kernels for 21%

profile of v9, /device:TPU:8, one launch (start us, length us, event | category | flops | bytes accessed | tf_op | source)
XLA Modules:
  0.0 95.8 jit_solution(7157344008902217777)
XLA Ops:
  0.0 2.9 %pack.1 = (bf16[960,128]{1,0:T(8,128)(2,1)S(1)}, bf16[960,128]{1,0:T(8,128)(2,1)S(1)}, bf16[960,128]{1,0:T(8,128)(2,1)S(1)}, bf16[960,128]{1,0:T(8,128)(2,1)S(1)...) custom-call(bf16[128,1280]{1,0:T(8,128)(2,1)} %bitcast.4, bf16[128,1280]{1,0:T(8,128)(2,1)} %bitcast.5, ...), custom_call_target="tpu_custom_call" | custom-call | tf_op jit(solution)/shard_map/pack/pallas_call | solution.py:99
  2.9 8.8 %all-to-all-start = ((bf16[16,256,128]{2,1,0:T(8,128)(2,1)}), bf16[16,256,128]{2,1,0:T(8,128)(2,1)S(1)}, u32[]{:S(2)}, u32[]{:S(2)}) async-start(bf16[16,256,128]{2,1,0:T(8,128)(2,1)} %get-tuple-element.21), calls=%async_computation | async-start | bytes 2097152 | tf_op jit(solution)/shard_map/all_to_all | solution.py:598
  11.7 0.0 collective-permute-start.3
  11.7 3.4 %collective-permute-start = (bf16[960,128]{1,0:T(8,128)(2,1)S(1)}, bf16[960,128]{1,0:T(8,128)(2,1)S(1)}, u32[]{:S(2)}, u32[]{:S(2)}) collective-permute-start(bf16[960,128]{1,0:T(8,128)(2,1)S(1)} %get-tuple-element.22), channel_id=1, source_target_pairs={{0,16},{16,0},{32,48},{48,32},{64,80},{80,64},{96,112},{112,96},{1... | collective-permute-start | bytes 737288 | tf_op jit(solution)/shard_map/ppermute | solution.py:583
  15.1 4.5 %collective-permute-start.1 = (bf16[960,128]{1,0:T(8,128)(2,1)S(1)}, bf16[960,128]{1,0:T(8,128)(2,1)S(1)}, u32[]{:S(2)}, u32[]{:S(2)}) collective-permute-start(bf16[960,128]{1,0:T(8,128)(2,1)S(1)} %get-tuple-element.23), channel_id=1, source_target_pairs={{0,32},{16,48},{32,0},{48,16},{64,96},{80,112},{96,64},{112,80},{1... | collective-permute-start | bytes 737288 | tf_op jit(solution)/shard_map/ppermute | solution.py:583
  19.6 0.0 collective-permute-start.2
  19.6 0.0 collective-permute-done.3.sibling_ref
  19.6 0.0 copy-start
  19.6 0.9 copy-done
  20.5 0.4 ring_pack.1
  20.8 0.2 collective-permute-start.4
  21.0 2.7 %collective-permute-start.5 = (bf16[2,128,128]{2,1,0:T(8,128)(2,1)S(1)}, bf16[2,128,128]{2,1,0:T(8,128)(2,1)S(1)}, u32[]{:S(2)}, u32[]{:S(2)}) collective-permute-start(bf16[2,128,128]{2,1,0:T(8,128)(2,1)S(1)} %get-tuple-element.27), channel_id=1, source_target_pairs={{0,4},{2,6},{4,0},{6,2},{1,5},{3,7},{5,1},{7,3},{8,12},{10,14},{12... | collective-permute-start | bytes 196616 | tf_op jit(solution)/shard_map/ppermute | solution.py:587
  23.8 4.6 %collective-permute-done.4.refs_3_.r1 = bf16[2,128,128]{2,1,0:T(8,128)(2,1)S(1)} collective-permute-done((bf16[2,128,128]{2,1,0:T(8,128)(2,1)S(1)}, bf16[2,128,128]{2,1,0:T(8,128)(2,1)S(1)}, u32[]{:S(2)}, u32[]{:S(2)}) %collective-permute-start.4) | collective-permute-done | bytes 65568 | tf_op jit(solution)/shard_map/ppermute | solution.py:587
  28.4 0.0 collective-permute-start.6
  28.4 0.2 collective-permute-done.5.refs_4_.r2
  28.6 4.3 %collective-permute-done.6.refs_5_.r3 = bf16[2,128,128]{2,1,0:T(8,128)(2,1)S(1)} collective-permute-done((bf16[2,128,128]{2,1,0:T(8,128)(2,1)S(1)}, bf16[2,128,128]{2,1,0:T(8,128)(2,1)S(1)}, u32[]{:S(2)}, u32[]{:S(2)}) %collective-permute-start.6) | collective-permute-done | bytes 65568 | tf_op jit(solution)/shard_map/ppermute | solution.py:587
  32.9 7.0 %collective-permute-done.refs_0_.z1 = bf16[960,128]{1,0:T(8,128)(2,1)S(1)} collective-permute-done((bf16[960,128]{1,0:T(8,128)(2,1)S(1)}, bf16[960,128]{1,0:T(8,128)(2,1)S(1)}, u32[]{:S(2)}, u32[]{:S(2)}) %collective-permute-start) | collective-permute-done | bytes 245792 | tf_op jit(solution)/shard_map/ppermute | solution.py:583
  39.9 10.7 %collective-permute-done.1.refs_1_.z2 = bf16[960,128]{1,0:T(8,128)(2,1)S(1)} collective-permute-done((bf16[960,128]{1,0:T(8,128)(2,1)S(1)}, bf16[960,128]{1,0:T(8,128)(2,1)S(1)}, u32[]{:S(2)}, u32[]{:S(2)}) %collective-permute-start.1) | collective-permute-done | bytes 245792 | tf_op jit(solution)/shard_map/ppermute | solution.py:583
  50.6 0.0 collective-permute-done.2.refs_2_.z3
  50.6 0.0 all-to-all-done.own_ref
  50.7 0.7 collective-permute-start.8
  51.4 0.0 collective-permute-start.7
  51.4 3.0 %ring_attention.1.ring_ref = bf16[16,144,128]{2,1,0:T(8,128)(2,1)S(1)} custom-call(bf16[16,256,128]{2,1,0:T(8,128)(2,1)S(1)} %all-to-all-done.own_ref, bf16[2,128,128]{2,1,0:T(8,128)(2,1)S(1)} %get-tuple-element.29.r0, bf16[2,128,128]{2,1,0:T(8,128)(2,1)S(1)} %collective-permute-done.4.refs_3_.r1, ...), custom_call_target="tpu_custom_call" | custom-call | flops 1000000 | bytes 100000 | tf_op jit(solution)/shard_map/ring_attention/pallas_call | solution.py:361
  54.4 0.0 copy-start.1
  54.4 0.0 collective-permute-done.7.other_ref
  54.4 12.2 %view_attention.1.refs_0_ = bf16[16,144,128]{2,1,0:T(8,128)(2,1)} custom-call(bf16[16,256,128]{2,1,0:T(8,128)(2,1)S(1)} %all-to-all-done.own_ref, bf16[16,128,128]{2,1,0:T(8,128)(2,1)S(1)} %collective-permute-done.7.other_ref, bf16[16,144,128]{2,1,0:T(8,128)(2,1)S(1)} %ring_attention.1.ring_ref, bf16[32,128]{1,0:T(8,128)(2,1)S(1)} %get-tuple-element.31.mask_ref), custom_call_target="tpu_custom_call" | custom-call | flops 1000000 | bytes 100000 | tf_op jit(solution)/shard_map/view_attention/pallas_call | solution.py:309
  66.6 0.0 collective-permute-done.8.refs_1_.x_ref
  66.6 7.8 %all-to-all-start.1 = ((bf16[16,144,128]{2,1,0:T(8,128)(2,1)}), bf16[16,144,128]{2,1,0:T(8,128)(2,1)S(1)}, u32[]{:S(2)}, u32[]{:S(2)}) async-start(bf16[16,144,128]{2,1,0:T(8,128)(2,1)} %pass_after.1), calls=%async_computation.1 | async-start | bytes 1179648 | tf_op jit(solution)/shard_map/all_to_all | solution.py:608
  74.5 0.0 copy-done.1
  74.5 4.9 %time_attention.1 = (bf16[336,128]{1,0:T(8,128)(2,1)S(1)}, bf16[336,128]{1,0:T(8,128)(2,1)S(1)}, bf16[336,128]{1,0:T(8,128)(2,1)S(1)}, bf16[336,128]{1,0:T(8,128)(2,1)S(1)}) custom-call(bf16[960,128]{1,0:T(8,128)(2,1)S(1)} %get-tuple-element.32.z0, bf16[960,128]{1,0:T(8,128)(2,1)S(1)} %collective-permute-done.refs_0_.z1, ...), custom_call_target="tpu_custom_call" | custom-call | flops 700000000 | bytes 2000000 | tf_op jit(solution)/shard_map/time_attention/pallas_call | solution.py:448
  79.4 0.6 collective-permute-start.10
  80.0 5.4 %collective-permute-start.11 = (bf16[336,128]{1,0:T(8,128)(2,1)S(1)}, bf16[336,128]{1,0:T(8,128)(2,1)S(1)}, u32[]{:S(2)}, u32[]{:S(2)}) collective-permute-start(bf16[336,128]{1,0:T(8,128)(2,1)S(1)} %get-tuple-element.36), channel_id=1, source_target_pairs={{0,48},{16,32},{32,16},{48,0},{64,112},{80,96},{96,80},{112,64},{1... | collective-permute-start | bytes 258056 | tf_op jit(solution)/shard_map/ppermute | solution.py:583
  85.4 0.6 collective-permute-start.9
  86.0 2.4 %collective-permute-done.10.t2 = bf16[336,128]{1,0:T(8,128)(2,1)S(1)} collective-permute-done((bf16[336,128]{1,0:T(8,128)(2,1)S(1)}, bf16[336,128]{1,0:T(8,128)(2,1)S(1)}, u32[]{:S(2)}, u32[]{:S(2)}) %collective-permute-start.10) | collective-permute-done | bytes 86048 | tf_op jit(solution)/shard_map/ppermute | solution.py:583
  88.3 3.6 %collective-permute-done.11.t3 = bf16[336,128]{1,0:T(8,128)(2,1)S(1)} collective-permute-done((bf16[336,128]{1,0:T(8,128)(2,1)S(1)}, bf16[336,128]{1,0:T(8,128)(2,1)S(1)}, u32[]{:S(2)}, u32[]{:S(2)}) %collective-permute-start.11) | collective-permute-done | bytes 86048 | tf_op jit(solution)/shard_map/ppermute | solution.py:583
  91.9 0.7 collective-permute-done.9.t1
  92.6 0.0 all-to-all-done.1.view_ref
  92.6 3.0 %join.1 = bf16[128,1280]{1,0:T(8,128)(2,1)} custom-call(bf16[16,144,128]{2,1,0:T(8,128)(2,1)S(1)} %all-to-all-done.1.view_ref, bf16[336,128]{1,0:T(8,128)(2,1)S(1)} %get-tuple-element.33.t0, bf16[336,128]{1,0:T(8,128)(2,1)S(1)} %collective-permute-done.9.t1, bf16[336,128]{1,0:T(8,128)(2,1)S(1)} %collective-permute-done.10.t2, ...), custom_call_target="tpu_custom_call" | custom-call | tf_op jit(solution)/shard_map/join/pallas_call | solution.py:566
  (4 shorter events, 0.1 us)
Async XLA Ops:
  2.9 47.7 %all-to-all-start = ((bf16[16,256,128]{2,1,0:T(8,128)(2,1)}), bf16[16,256,128]{2,1,0:T(8,128)(2,1)S(1)}, u32[]{:S(2)}, u32[]{:S(2)}) async-start(bf16[16,256,128]{2,1,0:T(8,128)(2,1)} %get-tuple-element.21), calls=%async_computation | async-start | bytes 2097152 | tf_op jit(solution)/shard_map/all_to_all | solution.py:598
  11.7 7.9 %collective-permute-start.3 = (bf16[4,128,128]{2,1,0:T(8,128)(2,1)S(1)}, bf16[4,128,128]{2,1,0:T(8,128)(2,1)S(1)}, u32[]{:S(2)}, u32[]{:S(2)}) collective-permute-start(bf16[4,128,128]{2,1,0:T(8,128)(2,1)S(1)} %get-tuple-element.25.ring_ref), channel_id=1, source_target_pairs={{0,1},{1,0},{2,3},{3,2},{4,5},{5,4},{6,7},{7,6},{8,9},{9,8},{10,11... | collective-permute-start | bytes 393224 | tf_op jit(solution)/shard_map/ppermute | solution.py:591
  11.7 28.2 %collective-permute-start = (bf16[960,128]{1,0:T(8,128)(2,1)S(1)}, bf16[960,128]{1,0:T(8,128)(2,1)S(1)}, u32[]{:S(2)}, u32[]{:S(2)}) collective-permute-start(bf16[960,128]{1,0:T(8,128)(2,1)S(1)} %get-tuple-element.22), channel_id=1, source_target_pairs={{0,16},{16,0},{32,48},{48,32},{64,80},{80,64},{96,112},{112,96},{1... | collective-permute-start | bytes 737288 | tf_op jit(solution)/shard_map/ppermute | solution.py:583
  15.1 35.5 %collective-permute-start.1 = (bf16[960,128]{1,0:T(8,128)(2,1)S(1)}, bf16[960,128]{1,0:T(8,128)(2,1)S(1)}, u32[]{:S(2)}, u32[]{:S(2)}) collective-permute-start(bf16[960,128]{1,0:T(8,128)(2,1)S(1)} %get-tuple-element.23), channel_id=1, source_target_pairs={{0,32},{16,48},{32,0},{48,16},{64,96},{80,112},{96,64},{112,80},{1... | collective-permute-start | bytes 737288 | tf_op jit(solution)/shard_map/ppermute | solution.py:583
  19.6 31.1 %collective-permute-start.2 = (bf16[960,128]{1,0:T(8,128)(2,1)S(1)}, bf16[960,128]{1,0:T(8,128)(2,1)S(1)}, u32[]{:S(2)}, u32[]{:S(2)}) collective-permute-start(bf16[960,128]{1,0:T(8,128)(2,1)S(1)} %get-tuple-element.24), channel_id=1, source_target_pairs={{0,48},{16,32},{32,16},{48,0},{64,112},{80,96},{96,80},{112,64},{1... | collective-permute-start | bytes 737288 | tf_op jit(solution)/shard_map/ppermute | solution.py:583
  19.6 0.9 copy-start
  20.8 7.5 %collective-permute-start.4 = (bf16[2,128,128]{2,1,0:T(8,128)(2,1)S(1)}, bf16[2,128,128]{2,1,0:T(8,128)(2,1)S(1)}, u32[]{:S(2)}, u32[]{:S(2)}) collective-permute-start(bf16[2,128,128]{2,1,0:T(8,128)(2,1)S(1)} %get-tuple-element.26), channel_id=1, source_target_pairs={{0,2},{2,0},{4,6},{6,4},{1,3},{3,1},{5,7},{7,5},{8,10},{10,8},{12,... | collective-permute-start | bytes 196616 | tf_op jit(solution)/shard_map/ppermute | solution.py:587
  21.0 7.6 %collective-permute-start.5 = (bf16[2,128,128]{2,1,0:T(8,128)(2,1)S(1)}, bf16[2,128,128]{2,1,0:T(8,128)(2,1)S(1)}, u32[]{:S(2)}, u32[]{:S(2)}) collective-permute-start(bf16[2,128,128]{2,1,0:T(8,128)(2,1)S(1)} %get-tuple-element.27), channel_id=1, source_target_pairs={{0,4},{2,6},{4,0},{6,2},{1,5},{3,7},{5,1},{7,3},{8,12},{10,14},{12... | collective-permute-start | bytes 196616 | tf_op jit(solution)/shard_map/ppermute | solution.py:587
  28.4 4.5 %collective-permute-start.6 = (bf16[2,128,128]{2,1,0:T(8,128)(2,1)S(1)}, bf16[2,128,128]{2,1,0:T(8,128)(2,1)S(1)}, u32[]{:S(2)}, u32[]{:S(2)}) collective-permute-start(bf16[2,128,128]{2,1,0:T(8,128)(2,1)S(1)} %get-tuple-element.28), channel_id=1, source_target_pairs={{0,6},{2,4},{4,2},{6,0},{1,7},{3,5},{5,3},{7,1},{8,14},{10,12},{12... | collective-permute-start | bytes 196616 | tf_op jit(solution)/shard_map/ppermute | solution.py:587
  50.7 15.9 %collective-permute-start.8 = (bf16[4,640,128]{2,1,0:T(8,128)(2,1)S(1)}, bf16[4,640,128]{2,1,0:T(8,128)(2,1)S(1)}, u32[]{:S(2)}, u32[]{:S(2)}) collective-permute-start(bf16[4,640,128]{2,1,0:T(8,128)(2,1)S(1)} %stack.1), channel_id=1, source_target_pairs={{0,64},{16,80},{32,96},{48,112},{64,0},{80,16},{96,32},{112,48},{1... | collective-permute-start | bytes 1966088 | tf_op jit(solution)/shard_map/ppermute | solution.py:583
  51.4 3.0 %collective-permute-start.7 = (bf16[16,128,128]{2,1,0:T(8,128)(2,1)S(1)}, bf16[16,128,128]{2,1,0:T(8,128)(2,1)S(1)}, u32[]{:S(2)}, u32[]{:S(2)}) collective-permute-start(bf16[16,128,128]{2,1,0:T(8,128)(2,1)S(1)} %keep.1.refs_0_), channel_id=1, source_target_pairs={{0,1},{1,0},{2,3},{3,2},{4,5},{5,4},{6,7},{7,6},{8,9},{9,8},{10,11... | collective-permute-start | bytes 1572872 | tf_op jit(solution)/shard_map/ppermute | solution.py:591
  54.4 20.1 %copy-start.1 = (s32[8]{0:T(128)S(1)}, s32[8]{0:T(128)}, u32[]{:S(2)}) copy-start(s32[8]{0:T(128)} %times_ref.1) | copy-start | bytes 100
  66.6 26.0 %all-to-all-start.1 = ((bf16[16,144,128]{2,1,0:T(8,128)(2,1)}), bf16[16,144,128]{2,1,0:T(8,128)(2,1)S(1)}, u32[]{:S(2)}, u32[]{:S(2)}) async-start(bf16[16,144,128]{2,1,0:T(8,128)(2,1)} %pass_after.1), calls=%async_computation.1 | async-start | bytes 1179648 | tf_op jit(solution)/shard_map/all_to_all | solution.py:608
  79.4 8.9 %collective-permute-start.10 = (bf16[336,128]{1,0:T(8,128)(2,1)S(1)}, bf16[336,128]{1,0:T(8,128)(2,1)S(1)}, u32[]{:S(2)}, u32[]{:S(2)}) collective-permute-start(bf16[336,128]{1,0:T(8,128)(2,1)S(1)} %get-tuple-element.35), channel_id=1, source_target_pairs={{0,32},{16,48},{32,0},{48,16},{64,96},{80,112},{96,64},{112,80},{1... | collective-permute-start | bytes 258056 | tf_op jit(solution)/shard_map/ppermute | solution.py:583
  80.0 11.9 %collective-permute-start.11 = (bf16[336,128]{1,0:T(8,128)(2,1)S(1)}, bf16[336,128]{1,0:T(8,128)(2,1)S(1)}, u32[]{:S(2)}, u32[]{:S(2)}) collective-permute-start(bf16[336,128]{1,0:T(8,128)(2,1)S(1)} %get-tuple-element.36), channel_id=1, source_target_pairs={{0,48},{16,32},{32,16},{48,0},{64,112},{80,96},{96,80},{112,64},{1... | collective-permute-start | bytes 258056 | tf_op jit(solution)/shard_map/ppermute | solution.py:583
  85.4 7.2 %collective-permute-start.9 = (bf16[336,128]{1,0:T(8,128)(2,1)S(1)}, bf16[336,128]{1,0:T(8,128)(2,1)S(1)}, u32[]{:S(2)}, u32[]{:S(2)}) collective-permute-start(bf16[336,128]{1,0:T(8,128)(2,1)S(1)} %get-tuple-element.34), channel_id=1, source_target_pairs={{0,16},{16,0},{32,48},{48,32},{64,80},{80,64},{96,112},{112,96},{1... | collective-permute-start | bytes 258056 | tf_op jit(solution)/shard_map/ppermute | solution.py:583

commit v10 on v9

--- a/solution.py
+++ b/solution.py
@@ -20,7 +20,7 @@
 Z_ROWS = 960
 X_ROWS = 640
 T_ROWS = 336
-GATE_FLOPS = 18000000000
+GATE_FLOPS = 19000000000
 O_ROWS = 144
 F32 = jnp.float32
 BF16 = jnp.bfloat16

time: 96.6 us -> 92.6 us (0.959)
  waiting for transfers between devices: 33.5 us -> 29.1 us
    ppermute x7, waiting for transfers between devices: 24.4 us -> 9.19 us  [across(): return lax.ppermute(array, 'f', [(i, i ^ k) for i in range(FRAMES)])]
    all_to_all x1, waiting for transfers between devices: 0.01 us -> 14.2 us  [local(): own = lax.all_to_all(to_view, ('g', 'zl', 'y'), 0, 0)]
    ppermute x3, waiting for transfers between devices: 9.11 us -> 5.7 us  [around(): return lax.ppermute(array, 'y', [(i, i ^ k) for i in range(RING)])]
    all_to_all x1, starting transfers between devices: 7.85 us -> 4.78 us  [local(): view_back = lax.all_to_all(view_out, ('g', 'zl', 'y'), 0, 0)]
    ppermute x3, starting transfers between devices: 2.94 us -> 5.28 us  [around(): return lax.ppermute(array, 'y', [(i, i ^ k) for i in range(RING)])]
    ppermute x7, starting transfers between devices: 15.1 us -> 16.6 us  [across(): return lax.ppermute(array, 'f', [(i, i ^ k) for i in range(FRAMES)])]
  transfers between devices with their start and end apart: 14 -> 14, of which waited for: 8 -> 8; matrix products, arithmetic and copies ran while one was open for 0% -> 0% of each run, Pallas kernels for 21% -> 22%
where the time goes in v10:
time: 92.6 us; the launch traced here: 91.4 us
  starting transfers between devices  34.6 us (37%)
  waiting for transfers between devices  29.1 us (31%)
  Pallas kernels  26.5 us (29%)
    ppermute x7, starting transfers between devices, across(): return lax.ppermute(array, 'f', [(i, i ^ k) for i in range(FRAMES)])  16.6 us
    all_to_all x1, waiting for transfers between devices, local(): own = lax.all_to_all(to_view, ('g', 'zl', 'y'), 0, 0)  14.2 us
    pallas_call x1, Pallas kernels, view_attention(): pl.pallas_call(view_kernel, out_shape=pltpu.HBM((MAIN, O_ROWS, CELLS), BF...  12.2 us
    ppermute x7, waiting for transfers between devices, across(): return lax.ppermute(array, 'f', [(i, i ^ k) for i in range(FRAMES)])  9.19 us
    all_to_all x1, starting transfers between devices, local(): own = lax.all_to_all(to_view, ('g', 'zl', 'y'), 0, 0)  7.85 us
    ppermute x3, waiting for transfers between devices, around(): return lax.ppermute(array, 'y', [(i, i ^ k) for i in range(RING)])  5.7 us
    ppermute x3, starting transfers between devices, around(): return lax.ppermute(array, 'y', [(i, i ^ k) for i in range(RING)])  5.28 us
    pallas_call x1, Pallas kernels, time_attention(): pl.pallas_call(time_kernel, out_shape=[jax.ShapeDtypeStruct((T_ROWS, CELL...  4.92 us
  transfers between devices with their start and end apart: 14, of which 8 were waited for; matrix products, arithmetic and copies ran while one was open for 0% of the time, Pallas kernels for 22%

profile of v10, /device:TPU:8, one launch (start us, length us, event | category | flops | bytes accessed | tf_op | source)
XLA Modules:
  0.0 91.4 jit_solution(2996794719310980256)
XLA Ops:
  0.0 2.9 %pack.1 = (bf16[960,128]{1,0:T(8,128)(2,1)S(1)}, bf16[960,128]{1,0:T(8,128)(2,1)S(1)}, bf16[960,128]{1,0:T(8,128)(2,1)S(1)}, bf16[960,128]{1,0:T(8,128)(2,1)S(1)...) custom-call(bf16[128,1280]{1,0:T(8,128)(2,1)} %bitcast.4, bf16[128,1280]{1,0:T(8,128)(2,1)} %bitcast.5, ...), custom_call_target="tpu_custom_call" | custom-call | tf_op jit(solution)/shard_map/pack/pallas_call | solution.py:99
  2.9 0.1 collective-permute-start.3
  3.0 3.4 %collective-permute-start = (bf16[960,128]{1,0:T(8,128)(2,1)S(1)}, bf16[960,128]{1,0:T(8,128)(2,1)S(1)}, u32[]{:S(2)}, u32[]{:S(2)}) collective-permute-start(bf16[960,128]{1,0:T(8,128)(2,1)S(1)} %get-tuple-element.22), channel_id=1, source_target_pairs={{0,16},{16,0},{32,48},{48,32},{64,80},{80,64},{96,112},{112,96},{1... | collective-permute-start | bytes 737288 | tf_op jit(solution)/shard_map/ppermute | solution.py:583
  6.4 5.4 %collective-permute-start.1 = (bf16[960,128]{1,0:T(8,128)(2,1)S(1)}, bf16[960,128]{1,0:T(8,128)(2,1)S(1)}, u32[]{:S(2)}, u32[]{:S(2)}) collective-permute-start(bf16[960,128]{1,0:T(8,128)(2,1)S(1)} %get-tuple-element.23), channel_id=1, source_target_pairs={{0,32},{16,48},{32,0},{48,16},{64,96},{80,112},{96,64},{112,80},{1... | collective-permute-start | bytes 737288 | tf_op jit(solution)/shard_map/ppermute | solution.py:583
  11.8 0.0 collective-permute-start.2
  11.8 7.8 %all-to-all-start = ((bf16[16,256,128]{2,1,0:T(8,128)(2,1)}), bf16[16,256,128]{2,1,0:T(8,128)(2,1)S(1)}, u32[]{:S(2)}, u32[]{:S(2)}) async-start(bf16[16,256,128]{2,1,0:T(8,128)(2,1)} %get-tuple-element.21), calls=%async_computation | async-start | bytes 2097152 | tf_op jit(solution)/shard_map/all_to_all | solution.py:598
  19.6 0.0 collective-permute-done.3.sibling_ref
  19.6 0.0 copy-start
  19.7 0.9 copy-done
  20.6 0.4 ring_pack.1
  20.9 0.1 collective-permute-start.4
  21.0 2.8 %collective-permute-start.5 = (bf16[2,128,128]{2,1,0:T(8,128)(2,1)S(1)}, bf16[2,128,128]{2,1,0:T(8,128)(2,1)S(1)}, u32[]{:S(2)}, u32[]{:S(2)}) collective-permute-start(bf16[2,128,128]{2,1,0:T(8,128)(2,1)S(1)} %get-tuple-element.27), channel_id=1, source_target_pairs={{0,4},{2,6},{4,0},{6,2},{1,5},{3,7},{5,1},{7,3},{8,12},{10,14},{12... | collective-permute-start | bytes 196616 | tf_op jit(solution)/shard_map/ppermute | solution.py:587
  23.9 3.5 %collective-permute-done.4.refs_3_.r1 = bf16[2,128,128]{2,1,0:T(8,128)(2,1)S(1)} collective-permute-done((bf16[2,128,128]{2,1,0:T(8,128)(2,1)S(1)}, bf16[2,128,128]{2,1,0:T(8,128)(2,1)S(1)}, u32[]{:S(2)}, u32[]{:S(2)}) %collective-permute-start.4) | collective-permute-done | bytes 65568 | tf_op jit(solution)/shard_map/ppermute | solution.py:587
  27.3 2.3 %collective-permute-start.6 = (bf16[2,128,128]{2,1,0:T(8,128)(2,1)S(1)}, bf16[2,128,128]{2,1,0:T(8,128)(2,1)S(1)}, u32[]{:S(2)}, u32[]{:S(2)}) collective-permute-start(bf16[2,128,128]{2,1,0:T(8,128)(2,1)S(1)} %get-tuple-element.28), channel_id=1, source_target_pairs={{0,6},{2,4},{4,2},{6,0},{1,7},{3,5},{5,3},{7,1},{8,14},{10,12},{12... | collective-permute-start | bytes 196616 | tf_op jit(solution)/shard_map/ppermute | solution.py:587
  29.7 0.8 collective-permute-done.5.refs_4_.r2
  30.5 1.4 %collective-permute-done.6.refs_5_.r3 = bf16[2,128,128]{2,1,0:T(8,128)(2,1)S(1)} collective-permute-done((bf16[2,128,128]{2,1,0:T(8,128)(2,1)S(1)}, bf16[2,128,128]{2,1,0:T(8,128)(2,1)S(1)}, u32[]{:S(2)}, u32[]{:S(2)}) %collective-permute-start.6) | collective-permute-done | bytes 65568 | tf_op jit(solution)/shard_map/ppermute | solution.py:587
  31.9 0.0 collective-permute-done.refs_0_.z1
  31.9 2.5 %collective-permute-done.1.refs_1_.z2 = bf16[960,128]{1,0:T(8,128)(2,1)S(1)} collective-permute-done((bf16[960,128]{1,0:T(8,128)(2,1)S(1)}, bf16[960,128]{1,0:T(8,128)(2,1)S(1)}, u32[]{:S(2)}, u32[]{:S(2)}) %collective-permute-start.1) | collective-permute-done | bytes 245792 | tf_op jit(solution)/shard_map/ppermute | solution.py:583
  34.4 0.0 collective-permute-done.2.refs_2_.z3
  34.4 14.2 %all-to-all-done.own_ref = bf16[16,256,128]{2,1,0:T(8,128)(2,1)S(1)} async-done(((bf16[16,256,128]{2,1,0:T(8,128)(2,1)}), bf16[16,256,128]{2,1,0:T(8,128)(2,1)S(1)}, u32[]{:S(2)}, u32[]{:S(2)}) %all-to-all-start) | async-done | bytes 1048608 | tf_op jit(solution)/shard_map/all_to_all | solution.py:598
  48.7 0.7 collective-permute-start.8
  49.4 0.0 collective-permute-start.7
  49.4 3.0 %ring_attention.1.ring_ref = bf16[16,144,128]{2,1,0:T(8,128)(2,1)S(1)} custom-call(bf16[16,256,128]{2,1,0:T(8,128)(2,1)S(1)} %all-to-all-done.own_ref, bf16[2,128,128]{2,1,0:T(8,128)(2,1)S(1)} %get-tuple-element.29.r0, bf16[2,128,128]{2,1,0:T(8,128)(2,1)S(1)} %collective-permute-done.4.refs_3_.r1, ...), custom_call_target="tpu_custom_call" | custom-call | flops 1000000 | bytes 100000 | tf_op jit(solution)/shard_map/ring_attention/pallas_call | solution.py:361
  52.4 0.0 copy-start.1
  52.4 0.0 collective-permute-done.7.other_ref
  52.4 12.2 %view_attention.1.refs_0_ = bf16[16,144,128]{2,1,0:T(8,128)(2,1)} custom-call(bf16[16,256,128]{2,1,0:T(8,128)(2,1)S(1)} %all-to-all-done.own_ref, bf16[16,128,128]{2,1,0:T(8,128)(2,1)S(1)} %collective-permute-done.7.other_ref, bf16[16,144,128]{2,1,0:T(8,128)(2,1)S(1)} %ring_attention.1.ring_ref, bf16[32,128]{1,0:T(8,128)(2,1)S(1)} %get-tuple-element.31.mask_ref), custom_call_target="tpu_custom_call" | custom-call | flops 1000000 | bytes 100000 | tf_op jit(solution)/shard_map/view_attention/pallas_call | solution.py:309
  64.6 0.0 collective-permute-done.8.refs_1_.x_ref
  64.6 4.8 %all-to-all-start.1 = ((bf16[16,144,128]{2,1,0:T(8,128)(2,1)}), bf16[16,144,128]{2,1,0:T(8,128)(2,1)S(1)}, u32[]{:S(2)}, u32[]{:S(2)}) async-start(bf16[16,144,128]{2,1,0:T(8,128)(2,1)} %pass_after.1), calls=%async_computation.1 | async-start | bytes 1179648 | tf_op jit(solution)/shard_map/all_to_all | solution.py:608
  69.4 0.0 copy-done.1
  69.4 4.9 %time_attention.1 = (bf16[336,128]{1,0:T(8,128)(2,1)S(1)}, bf16[336,128]{1,0:T(8,128)(2,1)S(1)}, bf16[336,128]{1,0:T(8,128)(2,1)S(1)}, bf16[336,128]{1,0:T(8,128)(2,1)S(1)}) custom-call(bf16[960,128]{1,0:T(8,128)(2,1)S(1)} %get-tuple-element.32.z0, bf16[960,128]{1,0:T(8,128)(2,1)S(1)} %collective-permute-done.refs_0_.z1, ...), custom_call_target="tpu_custom_call" | custom-call | flops 700000000 | bytes 2000000 | tf_op jit(solution)/shard_map/time_attention/pallas_call | solution.py:448
  74.3 2.8 %collective-permute-start.10 = (bf16[336,128]{1,0:T(8,128)(2,1)S(1)}, bf16[336,128]{1,0:T(8,128)(2,1)S(1)}, u32[]{:S(2)}, u32[]{:S(2)}) collective-permute-start(bf16[336,128]{1,0:T(8,128)(2,1)S(1)} %get-tuple-element.35), channel_id=1, source_target_pairs={{0,32},{16,48},{32,0},{48,16},{64,96},{80,112},{96,64},{112,80},{1... | collective-permute-start | bytes 258056 | tf_op jit(solution)/shard_map/ppermute | solution.py:583
  77.1 4.4 %collective-permute-start.11 = (bf16[336,128]{1,0:T(8,128)(2,1)S(1)}, bf16[336,128]{1,0:T(8,128)(2,1)S(1)}, u32[]{:S(2)}, u32[]{:S(2)}) collective-permute-start(bf16[336,128]{1,0:T(8,128)(2,1)S(1)} %get-tuple-element.36), channel_id=1, source_target_pairs={{0,48},{16,32},{32,16},{48,0},{64,112},{80,96},{96,80},{112,64},{1... | collective-permute-start | bytes 258056 | tf_op jit(solution)/shard_map/ppermute | solution.py:583
  81.5 0.0 collective-permute-start.9
  81.5 1.7 %collective-permute-done.10.t2 = bf16[336,128]{1,0:T(8,128)(2,1)S(1)} collective-permute-done((bf16[336,128]{1,0:T(8,128)(2,1)S(1)}, bf16[336,128]{1,0:T(8,128)(2,1)S(1)}, u32[]{:S(2)}, u32[]{:S(2)}) %collective-permute-start.10) | collective-permute-done | bytes 86048 | tf_op jit(solution)/shard_map/ppermute | solution.py:583
  83.2 3.9 %collective-permute-done.11.t3 = bf16[336,128]{1,0:T(8,128)(2,1)S(1)} collective-permute-done((bf16[336,128]{1,0:T(8,128)(2,1)S(1)}, bf16[336,128]{1,0:T(8,128)(2,1)S(1)}, u32[]{:S(2)}, u32[]{:S(2)}) %collective-permute-start.11) | collective-permute-done | bytes 86048 | tf_op jit(solution)/shard_map/ppermute | solution.py:583
  87.1 1.1 %collective-permute-done.9.t1 = bf16[336,128]{1,0:T(8,128)(2,1)S(1)} collective-permute-done((bf16[336,128]{1,0:T(8,128)(2,1)S(1)}, bf16[336,128]{1,0:T(8,128)(2,1)S(1)}, u32[]{:S(2)}, u32[]{:S(2)}) %collective-permute-start.9) | collective-permute-done | bytes 86048 | tf_op jit(solution)/shard_map/ppermute | solution.py:583
  88.2 0.0 all-to-all-done.1.view_ref
  88.2 3.0 %join.1 = bf16[128,1280]{1,0:T(8,128)(2,1)} custom-call(bf16[16,144,128]{2,1,0:T(8,128)(2,1)S(1)} %all-to-all-done.1.view_ref, bf16[336,128]{1,0:T(8,128)(2,1)S(1)} %get-tuple-element.33.t0, bf16[336,128]{1,0:T(8,128)(2,1)S(1)} %collective-permute-done.9.t1, bf16[336,128]{1,0:T(8,128)(2,1)S(1)} %collective-permute-done.10.t2, ...), custom_call_target="tpu_custom_call" | custom-call | tf_op jit(solution)/shard_map/join/pallas_call | solution.py:566
  (4 shorter events, 0.1 us)
Async XLA Ops:
  2.9 16.7 %collective-permute-start.3 = (bf16[4,128,128]{2,1,0:T(8,128)(2,1)S(1)}, bf16[4,128,128]{2,1,0:T(8,128)(2,1)S(1)}, u32[]{:S(2)}, u32[]{:S(2)}) collective-permute-start(bf16[4,128,128]{2,1,0:T(8,128)(2,1)S(1)} %get-tuple-element.25.ring_ref), channel_id=1, source_target_pairs={{0,1},{1,0},{2,3},{3,2},{4,5},{5,4},{6,7},{7,6},{8,9},{9,8},{10,11... | collective-permute-start | bytes 393224 | tf_op jit(solution)/shard_map/ppermute | solution.py:591
  3.0 28.9 %collective-permute-start = (bf16[960,128]{1,0:T(8,128)(2,1)S(1)}, bf16[960,128]{1,0:T(8,128)(2,1)S(1)}, u32[]{:S(2)}, u32[]{:S(2)}) collective-permute-start(bf16[960,128]{1,0:T(8,128)(2,1)S(1)} %get-tuple-element.22), channel_id=1, source_target_pairs={{0,16},{16,0},{32,48},{48,32},{64,80},{80,64},{96,112},{112,96},{1... | collective-permute-start | bytes 737288 | tf_op jit(solution)/shard_map/ppermute | solution.py:583
  6.4 28.0 %collective-permute-start.1 = (bf16[960,128]{1,0:T(8,128)(2,1)S(1)}, bf16[960,128]{1,0:T(8,128)(2,1)S(1)}, u32[]{:S(2)}, u32[]{:S(2)}) collective-permute-start(bf16[960,128]{1,0:T(8,128)(2,1)S(1)} %get-tuple-element.23), channel_id=1, source_target_pairs={{0,32},{16,48},{32,0},{48,16},{64,96},{80,112},{96,64},{112,80},{1... | collective-permute-start | bytes 737288 | tf_op jit(solution)/shard_map/ppermute | solution.py:583
  11.8 22.6 %collective-permute-start.2 = (bf16[960,128]{1,0:T(8,128)(2,1)S(1)}, bf16[960,128]{1,0:T(8,128)(2,1)S(1)}, u32[]{:S(2)}, u32[]{:S(2)}) collective-permute-start(bf16[960,128]{1,0:T(8,128)(2,1)S(1)} %get-tuple-element.24), channel_id=1, source_target_pairs={{0,48},{16,32},{32,16},{48,0},{64,112},{80,96},{96,80},{112,64},{1... | collective-permute-start | bytes 737288 | tf_op jit(solution)/shard_map/ppermute | solution.py:583
  11.8 36.8 %all-to-all-start = ((bf16[16,256,128]{2,1,0:T(8,128)(2,1)}), bf16[16,256,128]{2,1,0:T(8,128)(2,1)S(1)}, u32[]{:S(2)}, u32[]{:S(2)}) async-start(bf16[16,256,128]{2,1,0:T(8,128)(2,1)} %get-tuple-element.21), calls=%async_computation | async-start | bytes 2097152 | tf_op jit(solution)/shard_map/all_to_all | solution.py:598
  19.6 0.9 copy-start
  20.9 6.4 %collective-permute-start.4 = (bf16[2,128,128]{2,1,0:T(8,128)(2,1)S(1)}, bf16[2,128,128]{2,1,0:T(8,128)(2,1)S(1)}, u32[]{:S(2)}, u32[]{:S(2)}) collective-permute-start(bf16[2,128,128]{2,1,0:T(8,128)(2,1)S(1)} %get-tuple-element.26), channel_id=1, source_target_pairs={{0,2},{2,0},{4,6},{6,4},{1,3},{3,1},{5,7},{7,5},{8,10},{10,8},{12,... | collective-permute-start | bytes 196616 | tf_op jit(solution)/shard_map/ppermute | solution.py:587
  21.0 9.5 %collective-permute-start.5 = (bf16[2,128,128]{2,1,0:T(8,128)(2,1)S(1)}, bf16[2,128,128]{2,1,0:T(8,128)(2,1)S(1)}, u32[]{:S(2)}, u32[]{:S(2)}) collective-permute-start(bf16[2,128,128]{2,1,0:T(8,128)(2,1)S(1)} %get-tuple-element.27), channel_id=1, source_target_pairs={{0,4},{2,6},{4,0},{6,2},{1,5},{3,7},{5,1},{7,3},{8,12},{10,14},{12... | collective-permute-start | bytes 196616 | tf_op jit(solution)/shard_map/ppermute | solution.py:587
  27.3 4.6 %collective-permute-start.6 = (bf16[2,128,128]{2,1,0:T(8,128)(2,1)S(1)}, bf16[2,128,128]{2,1,0:T(8,128)(2,1)S(1)}, u32[]{:S(2)}, u32[]{:S(2)}) collective-permute-start(bf16[2,128,128]{2,1,0:T(8,128)(2,1)S(1)} %get-tuple-element.28), channel_id=1, source_target_pairs={{0,6},{2,4},{4,2},{6,0},{1,7},{3,5},{5,3},{7,1},{8,14},{10,12},{12... | collective-permute-start | bytes 196616 | tf_op jit(solution)/shard_map/ppermute | solution.py:587
  48.7 15.9 %collective-permute-start.8 = (bf16[4,640,128]{2,1,0:T(8,128)(2,1)S(1)}, bf16[4,640,128]{2,1,0:T(8,128)(2,1)S(1)}, u32[]{:S(2)}, u32[]{:S(2)}) collective-permute-start(bf16[4,640,128]{2,1,0:T(8,128)(2,1)S(1)} %stack.1), channel_id=1, source_target_pairs={{0,64},{16,80},{32,96},{48,112},{64,0},{80,16},{96,32},{112,48},{1... | collective-permute-start | bytes 1966088 | tf_op jit(solution)/shard_map/ppermute | solution.py:583
  49.4 3.0 %collective-permute-start.7 = (bf16[16,128,128]{2,1,0:T(8,128)(2,1)S(1)}, bf16[16,128,128]{2,1,0:T(8,128)(2,1)S(1)}, u32[]{:S(2)}, u32[]{:S(2)}) collective-permute-start(bf16[16,128,128]{2,1,0:T(8,128)(2,1)S(1)} %keep.1.refs_0_), channel_id=1, source_target_pairs={{0,1},{1,0},{2,3},{3,2},{4,5},{5,4},{6,7},{7,6},{8,9},{9,8},{10,11... | collective-permute-start | bytes 1572872 | tf_op jit(solution)/shard_map/ppermute | solution.py:591
  52.4 17.0 %copy-start.1 = (s32[8]{0:T(128)S(1)}, s32[8]{0:T(128)}, u32[]{:S(2)}) copy-start(s32[8]{0:T(128)} %times_ref.1) | copy-start | bytes 100
  64.6 23.6 %all-to-all-start.1 = ((bf16[16,144,128]{2,1,0:T(8,128)(2,1)}), bf16[16,144,128]{2,1,0:T(8,128)(2,1)S(1)}, u32[]{:S(2)}, u32[]{:S(2)}) async-start(bf16[16,144,128]{2,1,0:T(8,128)(2,1)} %pass_after.1), calls=%async_computation.1 | async-start | bytes 1179648 | tf_op jit(solution)/shard_map/all_to_all | solution.py:608
  74.3 8.9 %collective-permute-start.10 = (bf16[336,128]{1,0:T(8,128)(2,1)S(1)}, bf16[336,128]{1,0:T(8,128)(2,1)S(1)}, u32[]{:S(2)}, u32[]{:S(2)}) collective-permute-start(bf16[336,128]{1,0:T(8,128)(2,1)S(1)} %get-tuple-element.35), channel_id=1, source_target_pairs={{0,32},{16,48},{32,0},{48,16},{64,96},{80,112},{96,64},{112,80},{1... | collective-permute-start | bytes 258056 | tf_op jit(solution)/shard_map/ppermute | solution.py:583
  77.1 10.0 %collective-permute-start.11 = (bf16[336,128]{1,0:T(8,128)(2,1)S(1)}, bf16[336,128]{1,0:T(8,128)(2,1)S(1)}, u32[]{:S(2)}, u32[]{:S(2)}) collective-permute-start(bf16[336,128]{1,0:T(8,128)(2,1)S(1)} %get-tuple-element.36), channel_id=1, source_target_pairs={{0,48},{16,32},{32,16},{48,0},{64,112},{80,96},{96,80},{112,64},{1... | collective-permute-start | bytes 258056 | tf_op jit(solution)/shard_map/ppermute | solution.py:583
  81.5 6.7 %collective-permute-start.9 = (bf16[336,128]{1,0:T(8,128)(2,1)S(1)}, bf16[336,128]{1,0:T(8,128)(2,1)S(1)}, u32[]{:S(2)}, u32[]{:S(2)}) collective-permute-start(bf16[336,128]{1,0:T(8,128)(2,1)S(1)} %get-tuple-element.34), channel_id=1, source_target_pairs={{0,16},{16,0},{32,48},{48,32},{64,80},{80,64},{96,112},{112,96},{1... | collective-permute-start | bytes 258056 | tf_op jit(solution)/shard_map/ppermute | solution.py:583
